TPU v7x, 32 devices: a whole 2x2x4 slice. The times are simulated.
32 devices in a mesh: blk: 8 (over z, y), rhs: 4 (over x, core).
Axes of the slice: x: 2, y: 2, z: 4, core: 2. Of those that a mesh axis runs over, the one named last changes fastest.
Arguments:
- charges: bfloat16 [64, 16384], P('rhs', 'blk'), may hold values from -6 to 6
- counts: int32 [128], P('blk'), may hold values from 32 to 128
- self_tiles: bfloat16 [128, 128, 128], P('blk'), may hold values from -0.5 to 0.5
- basis: bfloat16 [128, 128, 64], P('blk'), may hold values from -0.5 to 0.5
- near_first: int32 [4096], P('blk'), may hold values from 0 to 127, as said below
- near_second: int32 [4096], P('blk'), may hold values from 0 to 127, as said below
- near_tiles: bfloat16 [4096, 128, 128], P(('blk', 'rhs')), may hold values from -0.125 to 0.125
- far_source: int32 [4096], P('blk'), may hold values from 0 to 127, as said below
- far_target: int32 [4096], P('blk'), may hold values from 0 to 127, as said below
- far_tiles: bfloat16 [4096, 64, 64], P('blk'), may hold values from -0.09375 to 0.09375
Outputs:
- potentials: float32 [64, 16384], P('rhs', 'blk')
Inputs may be any that keep to these rules, and one draw needn't show every extreme that they name: Block c holds counts[c] real panels in its first slots; the others are padding. `near_first`: the first block of a pair is one of the 16 blocks of the blk index that holds the pair. `near_second`: the second block lies within 48 blocks of the first, counted cyclically. `far_source`: any cell. `far_target`: the target cell is one of the 16 cells of the blk index that holds the interaction.
All inputs are finite; a program needn't handle non-finite values.
Results may differ from a plain program's by a relative error of at most 0.0012.
Values may be sent and summed in bfloat16 or wider, within the bound.
No kernel may reach another device: no remote copies, remote signals or barrier semaphores. Data moves between devices by JAX's collectives and lax.ppermute only.
A program may use at most 128 MiB of HBM per device.

v0:
```python
import jax
import jax.numpy as jnp
from jax import lax
from jax.sharding import PartitionSpec as P


def select_blocks(blocks, indices):
    onehot = (indices[:, None] == jnp.arange(blocks.shape[1], dtype=jnp.int32)[None, :]).astype(
        blocks.dtype
    )
    picked = jnp.einsum("rcj,nc->rnj", blocks, onehot, preferred_element_type=jnp.float32)
    return picked.astype(blocks.dtype)


def place_blocks(values, indices, out_total):
    onehot = (indices[:, None] == jnp.arange(out_total, dtype=jnp.int32)[None, :]).astype(
        jnp.float32
    )
    return jnp.einsum(
        "rnj,nc->rcj",
        values,
        onehot,
        precision=lax.Precision.HIGHEST,
        preferred_element_type=jnp.float32,
    )


def pair_sums(blocks, first, second, tiles, out_first, out_second, out_total):
    from_second = select_blocks(blocks, second)
    from_first = select_blocks(blocks, first)
    to_first = jnp.einsum("rnj,nij->rni", from_second, tiles, preferred_element_type=jnp.float32)
    to_second = jnp.einsum("rni,nij->rnj", from_first, tiles, preferred_element_type=jnp.float32)
    return place_blocks(to_first, out_first, out_total) + place_blocks(
        to_second, out_second, out_total
    )


def body(
    charges,
    counts,
    self_tiles,
    basis,
    near_first,
    near_second,
    near_tiles,
    far_source,
    far_target,
    far_tiles,
):
    block_size = self_tiles.shape[1]
    blk_dev = self_tiles.shape[0]
    terms = basis.shape[2]
    rows = charges.shape[0]
    valid = (jnp.arange(block_size)[None, :] < counts[:, None]).reshape(-1)
    masked = jnp.where(valid[None, :], charges, jnp.zeros_like(charges))
    local_blocks = masked.reshape(rows, blk_dev, block_size)
    moments = jnp.einsum(
        "rcb,cbp->rcp", local_blocks, basis, preferred_element_type=jnp.float32
    ).astype(jnp.bfloat16)
    all_charges, all_moments = (
        lax.all_gather(masked, "blk", axis=1, tiled=True),
        lax.all_gather(moments.reshape(rows, blk_dev * terms), "blk", axis=1, tiled=True),
    )
    blocks_total = all_charges.shape[1] // block_size
    charge_blocks = all_charges.reshape(rows, blocks_total, block_size)
    moment_blocks = all_moments.reshape(rows, blocks_total, terms)
    tiles_all = lax.all_gather(near_tiles, "rhs", axis=0, tiled=True)
    first, second = (near_first, near_second)
    out_first = jnp.mod(first, blocks_total)
    out_second = jnp.mod(second, blocks_total)
    near = pair_sums(charge_blocks, first, second, tiles_all, out_first, out_second, blocks_total)
    far_sums = pair_sums(
        moment_blocks, far_target, far_source, far_tiles, far_target, far_source, blocks_total
    )
    near_mine, field_mine = (
        lax.psum_scatter(near.reshape(rows, -1), "blk", scatter_dimension=1, tiled=True),
        lax.psum_scatter(far_sums.reshape(rows, -1), "blk", scatter_dimension=1, tiled=True),
    )
    fields = field_mine.astype(jnp.bfloat16).reshape(rows, blk_dev, terms)
    far_part = jnp.einsum(
        "rcp,cbp->rcb", fields, basis, preferred_element_type=jnp.float32
    ).reshape(rows, -1)
    self_part = jnp.einsum(
        "rcj,cij->rci", local_blocks, self_tiles, preferred_element_type=jnp.float32
    ).reshape(rows, -1)
    total = near_mine + far_part + self_part
    return jnp.where(valid[None, :], total, jnp.zeros_like(total))


def solution(mesh):
    in_specs = (
        P("rhs", "blk"),
        P("blk"),
        P("blk", None, None),
        P("blk", None, None),
        P("blk"),
        P("blk"),
        P(("blk", "rhs"), None, None),
        P("blk"),
        P("blk"),
        P("blk", None, None),
    )
    out_specs = P("rhs", "blk")
    return jax.shard_map(body, mesh=mesh, in_specs=in_specs, out_specs=out_specs, check_vma=False)
```

profile of v0, /device:TPU:0, one launch (start us, length us, event | category | flops | bytes accessed | tf_op | source)
XLA Modules:
  0.0 233.9 jit_solution(18310313946707509744)
XLA Ops:
  7.4 0.0 copy-start
  7.4 0.0 all-gather.2.cloned.1.call-start
  7.4 0.7 all-gather.2.cloned.1.call-update
  8.1 0.0 reduce-scatter.5.cloned.1.call-start
  8.2 0.1 fusion.36
  8.3 0.0 copy-done.3
  8.3 0.1 copy-done.2
  8.4 0.2 fusion.9
  8.7 0.1 reshape.51
  8.8 32.5 %all_gather.11 = bf16[16,8192]{1,0:T(8,128)(2,1)S(1)} all-gather(bf16[16,1024]{1,0:T(8,128)(2,1)S(1)} %reshape.51), channel_id=1, replica_groups=mesh['blk'=8,'rhs'=4] {'blk'}, dimensions={1}, use_global_device_ids=true | all-gather | bytes 294912 | tf_op jit(solution)/shard_map/all_gather | solution.py:62
  41.3 0.5 reshape.52
  41.9 0.2 copy.26
  42.1 0.5 fusion.11
  42.7 1.1 convert_bitcast_fusion.3
  43.8 3.0 %copy.27 = bf16[16,512,64]{2,0,1:T(8,128)(2,1)S(1)} copy(bf16[16,512,64]{1,2,0:T(8,128)(2,1)} %convert_bitcast_fusion.3) | data formatting | bytes 2097152 | tf_op jit(solution)/shard_map/convert_element_type | solution.py:12
  46.8 13.0 %copy.28 = bf16[512,64,64]{2,1,0:T(8,128)(2,1)} copy(bf16[512,64,64]{0,2,1:T(8,128)(2,1)} %param.19) | data formatting | bytes 8388608 | tf_op args[9]
  59.7 9.9 %convolution_bitcast_fusion.1 = f32[16,512,64]{2,0,1:T(8,128)} fusion(bf16[16,512,64]{2,0,1:T(8,128)(2,1)S(1)} %copy.27, bf16[512,64,64]{2,1,0:T(8,128)(2,1)} %copy.28), kind=kOutput, calls=%fused_computation.5 | convolution fusion | flops 67108864 | bytes 7340032 | tf_op jit(solution)/shard_map/rnj,nij->rni/dot_general | solution.py:31
  69.7 3.8 %copy.29 = f32[16,512,64]{1,2,0:T(8,128)} copy(f32[16,512,64]{2,0,1:T(8,128)} %convolution_bitcast_fusion.1) | data formatting | bytes 4194304 | tf_op jit(solution)/shard_map/rnj,nij->rni/transpose | solution.py:31
  73.5 0.5 fusion.12
  74.0 1.2 convert_bitcast_fusion.2
  75.2 3.0 %copy.31 = bf16[16,512,64]{2,0,1:T(8,128)(2,1)S(1)} copy(bf16[16,512,64]{1,2,0:T(8,128)(2,1)} %convert_bitcast_fusion.2) | data formatting | bytes 2097152 | tf_op jit(solution)/shard_map/convert_element_type | solution.py:12
  78.2 7.6 %convolution_bitcast_fusion = f32[16,512,64]{2,0,1:T(8,128)} fusion(bf16[16,512,64]{2,0,1:T(8,128)(2,1)S(1)} %copy.31, bf16[512,64,64]{2,1,0:T(8,128)(2,1)} %copy.28), kind=kOutput, calls=%fused_computation.4 | convolution fusion | flops 67108864 | bytes 7340032 | tf_op jit(solution)/shard_map/rni,nij->rnj/dot_general | solution.py:32
  85.9 4.0 %copy.33 = f32[16,512,64]{1,2,0:T(8,128)} copy(f32[16,512,64]{2,0,1:T(8,128)} %convolution_bitcast_fusion) | data formatting | bytes 4194304 | tf_op jit(solution)/shard_map/rni,nij->rnj/transpose | solution.py:32
  89.9 1.2 fusion.13
  91.0 0.0 copy-start.4
  91.0 2.7 %fusion.10 = f32[128,1024]{0,1:S(1)} fusion(f32[512,1024]{0,1:T(8,128)} %bitcast.97, s32[512]{0:T(512)S(1)} %copy-done.7), kind=kOutput, calls=%fused_computation.22 | convolution fusion | flops 805371904 | bytes 2623488
  93.8 0.1 add_bitcast_fusion
  93.9 0.0 copy-start.5
  93.9 0.3 copy.34
  94.2 1.2 reshape.53
  95.4 0.0 reduce-scatter.5.cloned.1.call-update
  95.4 0.0 reduce-scatter.3.cloned.1.call-start
  95.5 31.9 %all_gather.9 = bf16[16,16384]{1,0:T(8,128)(2,1)S(1)} all-gather(bf16[16,2048]{1,0:T(8,128)(2,1)S(1)} %broadcast_select_fusion), channel_id=1, replica_groups=mesh['blk'=8,'rhs'=4] {'blk'}, dimensions={1}, use_global_device_ids=true | all-gather | bytes 589824 | tf_op jit(solution)/shard_map/all_gather | solution.py:61
  127.4 0.1 copy.42
  127.5 0.8 convert_bitcast_fusion.1
  128.3 2.1 convert_bitcast_fusion
  130.3 8.8 %convolution_bitcast_fusion.2 = f32[16,512,128]{2,0,1:T(8,128)S(1)} fusion(bf16[512,128,128]{2,1,0:T(8,128)(2,1)} %all-gather.2.cloned.1.call-done, bf16[16,512,128]{2,1,0:T(8,128)(2,1)} %convert_bitcast_fusion), kind=kOutput, calls=%fused_computation.6 | convolution fusion | flops 268435456 | bytes 23068672 | tf_op jit(solution)/shard_map/rni,nij->rnj/dot_general | solution.py:32
  139.1 11.9 %convolution_bitcast_fusion.3 = f32[16,512,128]{2,0,1:T(8,128)S(1)} fusion(bf16[512,128,128]{2,1,0:T(8,128)(2,1)} %all-gather.2.cloned.1.call-done, bf16[16,512,128]{2,1,0:T(8,128)(2,1)S(1)} %convert_bitcast_fusion.1), kind=kOutput, calls=%fused_computation.7 | convolution fusion | flops 268435456 | bytes 23068672 | tf_op jit(solution)/shard_map/rnj,nij->rni/dot_general | solution.py:31
  151.1 2.8 %fusion = f32[128,16,128]{2,0,1:T(8,128)S(1)} fusion(f32[16,512,128]{2,0,1:T(8,128)S(1)} %convolution_bitcast_fusion.2, s32[512]{0:T(512)S(1)} %add_select_fusion), kind=kOutput, calls=%fused_computation | convolution fusion | flops 1610678272 | bytes 5244928 | tf_op jit(solution)/shard_map/rnj,nc->rcj/dot_general | solution.py:19
  153.9 2.8 %fusion.6 = f32[128,16,128]{2,0,1:T(8,128)S(1)} fusion(f32[128,16,128]{2,0,1:T(8,128)S(1)} %fusion, f32[16,512,128]{2,0,1:T(8,128)S(1)} %convolution_bitcast_fusion.3, s32[512]{0:T(512)S(1)} %add_select_fusion.1), kind=kOutput, calls=%fused_computation.12 | convolution fusion | flops 1610940416 | bytes 6293504 | tf_op jit(solution)/shard_map/rnj,nc->rcj/dot_general | solution.py:19
  156.7 1.6 copy.67
  158.3 0.0 reduce-scatter.3.cloned.1.call-update
  158.3 0.4 convolution_bitcast_fusion.4
  158.7 0.9 convert_element_type.51
  159.6 0.1 reshape.54
  159.7 0.2 convolution_bitcast_fusion.5
  159.9 65.0 %reduce-scatter.3.cloned.1.call-done = f32[16,2048]{1,0:T(8,128)} async-done(((f32[16,16384]{1,0:T(8,128)}), f32[16,2048]{1,0:T(8,128)}) %reduce-scatter.3.cloned.1.call-update) | async-done | bytes 131088 | tf_op jit(solution)/shard_map/reduce_scatter | solution.py:76
  224.8 1.6 fusion.22
  (19 shorter events, 0.1 us)
Async XLA Ops:
  7.4 151.0 %copy-start = (bf16[16,128,128]{2,1,0:T(8,128)(2,1)S(1)}, bf16[16,128,128]{2,1,0:T(8,128)(2,1)}, u32[]{:S(2)}) copy-start(bf16[16,128,128]{2,1,0:T(8,128)(2,1)} %param.12) | copy-start | bytes 1572868
  7.4 0.8 copy-start.8
  7.4 0.9 copy-start.3
  7.4 1.1 copy-start.2
  7.4 34.7 %copy-start.7 = (s32[512]{0:T(512)S(1)}, s32[512]{0:T(512)}, u32[]{:S(2)}) copy-start(s32[512]{0:T(512)} %param.17) | copy-start | bytes 6148
  7.4 123.0 %all-gather.2.cloned.1.call-start = ((), (), s32[]{:S(2)}) async-start(), calls=%async_computation.2 | async-start | bytes 20971520 | tf_op jit(solution)/shard_map/all_gather | solution.py:67
  8.1 150.6 %reduce-scatter.5.cloned.1.call-start = ((), (), s32[]{:S(2)}) async-start(), calls=%async_computation.4 | async-start | bytes 589824 | tf_op jit(solution)/shard_map/reduce_scatter | solution.py:77
  69.7 3.8 %copy-start.6 = (s32[512]{0:T(512)S(1)}, s32[512]{0:T(512)}, u32[]{:S(2)}) copy-start(s32[512]{0:T(512)} %param.18) | copy-start | bytes 6148
  85.9 4.0 %copy-start.1 = (f32[16,512,64]{1,2,0:T(8,128)S(1)}, f32[16,512,64]{1,2,0:T(8,128)}, u32[]{:S(2)}) copy-start(f32[16,512,64]{1,2,0:T(8,128)} %copy.29) | copy-start | bytes 6291460
  91.0 36.4 %copy-start.4 = (s32[512]{0:T(512)S(1)}, s32[512]{0:T(512)}, u32[]{:S(2)}) copy-start(s32[512]{0:T(512)} %param.15) | copy-start | bytes 6148
  93.9 34.4 %copy-start.5 = (s32[512]{0:T(512)S(1)}, s32[512]{0:T(512)}, u32[]{:S(2)}) copy-start(s32[512]{0:T(512)} %param.14) | copy-start | bytes 6148
  95.4 129.4 %reduce-scatter.3.cloned.1.call-start = ((), (), s32[]{:S(2)}) async-start(), calls=%async_computation.3 | async-start | bytes 1179648 | tf_op jit(solution)/shard_map/reduce_scatter | solution.py:76
Sparse Core Ops, SparseCore 0:
  9.8 108.6 all-gather.1
Sparse Core Ops, SparseCore 1:
  95.5 63.1 reduce-scatter.4
  162.3 62.5 reduce-scatter.2
where the time goes:
time: 234 us
  waiting for transfers between devices  65.7 us (28%)
  blocking collectives  64.4 us (28%)
  matrix products  52.5 us (22%)
  local copies, waits for them, and re-layouts  31.1 us (13%)
  between operations  15 us (6%)
  other arithmetic  4.94 us (2%)
    reduce_scatter x1, waiting for transfers between devices, body(): lax.psum_scatter(near.reshape(rows, -1), 'blk', scatter_dimension=1, tile...  65 us
    all_gather x1, blocking collectives, body(): lax.all_gather(moments.reshape(rows, blk_dev * terms), 'blk', axis=1, til...  32.5 us
    all_gather x1, blocking collectives, body(): lax.all_gather(masked, 'blk', axis=1, tiled=True)  31.9 us
    dot_general x2, matrix products, pair_sums(): jnp.einsum('rnj,nij->rni', from_second, tiles, preferred_element_type=jnp...  21.9 us
    dot_general x2, matrix products, pair_sums(): jnp.einsum('rni,nij->rnj', from_first, tiles, preferred_element_type=jnp....  16.4 us
    unnamed x21, local copies, waits for them, and re-layouts  14.8 us
    convert_element_type x2, local copies, waits for them, and re-layouts, select_blocks(): return picked.astype(blocks.dtype)  5.96 us
    dot_general x2, matrix products, place_blocks(): jnp.einsum('rnj,nc->rcj', values, onehot, precision=lax.Precision.HIGHEST...  5.62 us
  transfers between devices with their start and end apart: 3, of which 1 were waited for; matrix products, arithmetic and copies ran while one was open for 37% of the time, Pallas kernels for 0%

commit v1 on v0

v1 whole, which is shorter than its diff:
```python
import functools

import jax
import jax.numpy as jnp
from jax import lax
from jax.experimental import pallas as pl
from jax.experimental.pallas import tpu as pltpu
from jax.sharding import PartitionSpec as P

F32, BF16, I16, I32 = jnp.float32, jnp.bfloat16, jnp.int16, jnp.int32
GROUP = 16
TOP = 32767.0
VMEM = pl.BlockSpec(memory_space=pltpu.VMEM)
SMEM = pl.BlockSpec(memory_space=pltpu.SMEM)
NAT = (((1,), (0,)), ((), ()))
TRN = (((1,), (1,)), ((), ()))


def params(mib):
    return pltpu.CompilerParams(vmem_limit_bytes=mib << 20)


def dot(lhs, rhs, dims):
    return lax.dot_general(lhs, rhs, dims, preferred_element_type=F32)


def scale_blocks(count):
    return -(-count // GROUP)


def encode(src, out, count, peak, inv):
    peak[...] = jnp.zeros_like(peak)

    def find(b, _):
        peak[pl.ds(b, 1), :] = jnp.max(jnp.abs(src[b]), axis=0, keepdims=True)
        return 0

    lax.fori_loop(0, count, find, 0, unroll=8)
    code = jnp.ceil(jnp.log2(jnp.maximum(peak[...], 1e-30)) * 8.0) + 1.0
    inv[...] = TOP * jnp.exp2(code * -0.125)
    for s in range(scale_blocks(count)):
        out[count + s] = code[s * GROUP : (s + 1) * GROUP].astype(I32).astype(I16)

    def put(b, _):
        out[b] = jnp.round(src[b] * inv[pl.ds(b, 1), :]).astype(I32).astype(I16)
        return 0

    lax.fori_loop(0, count, put, 0, unroll=8)


def decode_scales(coded, count, scale):
    for s in range(scale_blocks(count)):
        code = coded[count + s].astype(I32).astype(F32)
        scale[s * GROUP : (s + 1) * GROUP, :] = jnp.exp2(code * 0.125) * (1.0 / TOP)


def decode(coded, scale, b):
    return coded[b].astype(I32).astype(F32) * scale[pl.ds(b, 1), :]


def prep_kernel(counts, charges, basis_t, out):
    cells, terms, size = basis_t.shape
    rows = charges.shape[0]
    lane = lax.broadcasted_iota(I32, (rows, size), 1)
    moments = []
    for c in range(cells):
        x = charges[:, c * size : (c + 1) * size]
        x = jnp.where(lane < counts[c], x, jnp.zeros_like(x))
        out[c] = x
        moments.append(dot(x, basis_t[c], TRN))
    for k in range(cells // 2):
        out[cells + k] = jnp.concatenate(moments[2 * k : 2 * k + 2], axis=1).astype(BF16)


def far_source_kernel(tgt, pos, mine, tiles, turned, out, flip, lhs, acc):
    step = pl.program_id(0)
    half = mine.shape[2] // 2
    quarter = half // 2
    chunk = tiles.shape[1]
    pairs = half // 2
    cells = 2 * mine.shape[0]

    @pl.when(step == 0)
    def _():
        acc[...] = jnp.zeros_like(acc)
        for k in range(cells // 2):
            x = mine[k]
            for h in range(2):
                y = x[:, h * half : (h + 1) * half]
                lhs[2 * k + h] = jnp.concatenate([y[:, :quarter], y[:, quarter:]], axis=0)

    for i in range(pairs):
        both = jnp.concatenate(
            [tiles[i * half : (i + 1) * half, :], tiles[(i + pairs) * half : (i + pairs + 1) * half, :]], axis=0
        )
        flip[i * chunk : (i + 1) * chunk, :] = both.astype(F32).T

    unroll = 16

    def work(g, _):
        sums = []
        for u in range(unroll):
            e = g * unroll + u
            w = flip[pl.ds(e, pairs, stride=chunk), :].astype(BF16)
            turned[e] = w
            sums.append(dot(lhs[tgt[step * chunk + e]], w, NAT))
        for u in range(unroll):
            acc[pos[step * chunk + g * unroll + u]] += sums[u]
        return 0

    lax.fori_loop(0, chunk // unroll, work, 0)

    @pl.when(step == pl.num_programs(0) - 1)
    def _():
        rows = mine.shape[1]

        def fold(k, _):
            a, b = acc[2 * k], acc[2 * k + 1]
            out[k] = jnp.concatenate(
                [a[:rows, :half] + a[rows:, half:], b[:rows, :half] + b[rows:, half:]], axis=1
            )
            return 0

        lax.fori_loop(0, out.shape[0], fold, 0)


def far_target_kernel(stride, cells, tgt, pos, everyone, turned, out, lhs, acc):
    step = pl.program_id(0)
    rows, lanes = everyone.shape[1], everyone.shape[2]
    half = lanes // 2
    chunk = turned.shape[0]
    owners = everyone.shape[0] // stride

    @pl.when(step == 0)
    def _():
        acc[...] = jnp.zeros_like(acc)
        low = lax.broadcasted_iota(I32, (rows, lanes), 1) < half

        def spread(o, _):
            for k in range(cells // 2):
                x = everyone[o * stride + cells + k]
                y = jnp.concatenate([x[:, half:], x[:, :half]], axis=1)
                zero = jnp.zeros_like(x)
                at = o * cells + 2 * k
                lhs[at] = jnp.concatenate([jnp.where(low, x, zero), jnp.where(low, zero, y)], axis=0)
                lhs[at + 1] = jnp.concatenate([jnp.where(low, y, zero), jnp.where(low, zero, x)], axis=0)
            return 0

        lax.fori_loop(0, owners, spread, 0)

    unroll = 16

    def work(g, _):
        sums = []
        for u in range(unroll):
            e = g * unroll + u
            sums.append(dot(lhs[pos[step * chunk + e]], turned[e], TRN))
        for u in range(unroll):
            acc[tgt[step * chunk + g * unroll + u]] += sums[u]
        return 0

    lax.fori_loop(0, chunk // unroll, work, 0)

    @pl.when(step == pl.num_programs(0) - 1)
    def _():
        for k in range(cells // 2):
            a, b = acc[2 * k], acc[2 * k + 1]
            out[k] = jnp.concatenate([a[:rows], a[rows:], b[:rows], b[rows:]], axis=1)


def near_loop(step, chunk, base, lhs, lhs_at, tiles, dims, acc, acc_at):
    unroll = 16

    def work(g, _):
        sums = []
        for u in range(unroll):
            n = g * unroll + u
            sums.append(dot(lhs[lhs_at[base + n]], tiles[n], dims))
        for u in range(unroll):
            acc[acc_at[base + g * unroll + u]] += sums[u]
        return 0

    lax.fori_loop(0, chunk // unroll, work, 0)


def near_second_kernel(first, second, mine, theirs, tiles, other, keep, send, lhs, acc, peak, inv):
    step = pl.program_id(0)
    steps = pl.num_programs(0) // 2
    rows = mine.shape[1]
    chunk = tiles.shape[0]
    total = keep.shape[0]

    @pl.when(step == 0)
    def _():
        acc[...] = jnp.zeros_like(acc)
        for c in range(lhs.shape[0]):
            lhs[c] = jnp.concatenate([mine[c], theirs[c]], axis=0)

    @pl.when(step < steps)
    def _():
        near_loop(step, chunk, step * chunk, lhs, first, tiles, NAT, acc, second)

    @pl.when(step >= steps)
    def _():
        near_loop(step, chunk, step * chunk, lhs, first, other, NAT, acc, second)

    @pl.when(step == 2 * steps - 1)
    def _():
        def split(b, _):
            keep[b] = acc[b, :rows, :]
            return 0

        lax.fori_loop(0, total, split, 0, unroll=8)
        encode(acc.at[:, rows:, :], send, total, peak, inv)


def near_first_kernel(stride, cells, first, second, everyone, theirs, tiles, other, keep, send, lhs, acc):
    step = pl.program_id(0)
    steps = pl.num_programs(0) // 2
    rows = everyone.shape[1]
    chunk = tiles.shape[0]

    @pl.when(step == 0)
    def _():
        acc[...] = jnp.zeros_like(acc)

        def fill(o, _):
            for c in range(cells):
                lhs[o * cells + c] = jnp.concatenate([everyone[o * stride + c], theirs[o * cells + c]], axis=0)
            return 0

        lax.fori_loop(0, everyone.shape[0] // stride, fill, 0)

    @pl.when(step < steps)
    def _():
        near_loop(step, chunk, step * chunk, lhs, second, tiles, TRN, acc, first)

    @pl.when(step >= steps)
    def _():
        near_loop(step, chunk, step * chunk, lhs, second, other, TRN, acc, first)

    @pl.when(step == 2 * steps - 1)
    def _():
        for c in range(cells):
            keep[c] = acc[c, :rows, :]
            send[c] = acc[c, rows:, :]


def meet_kernel(cells, mine, coded, far, keep, send, acc, scale, peak, inv):
    total = mine.shape[0]
    near_b, far_b = cells, cells // 2
    stride = near_b + far_b
    owners = total // cells
    decode_scales(coded, total, scale)

    def owner(o, dst, at):
        def near_part(c, _):
            b = o * near_b + c
            dst[at * stride + c] = mine[b] + decode(coded, scale, b)
            return 0

        lax.fori_loop(0, near_b, near_part, 0, unroll=8)
        for c in range(far_b):
            dst[at * stride + near_b + c] = far[o * far_b + c]

    for o in range(owners // 2):
        owner(o, keep, o)
        owner(o + owners // 2, acc, o)
    encode(acc, send, acc.shape[0], peak, inv)


def add_kernel(mine, coded, keep, send, acc, scale, peak, inv):
    total = mine.shape[0]
    half = total // 2
    decode_scales(coded, total, scale)

    def one(b, _):
        keep[b] = mine[b] + decode(coded, scale, b)
        acc[b] = mine[half + b] + decode(coded, scale, half + b)
        return 0

    lax.fori_loop(0, half, one, 0, unroll=8)
    encode(acc, send, half, peak, inv)


def final_kernel(counts, mine, coded, first, first_other, target, moved, self_tiles, basis_t, out, scale):
    cells, terms, size = basis_t.shape
    rows = out.shape[0]
    decode_scales(coded, mine.shape[0], scale)
    lane = lax.broadcasted_iota(I32, (rows, size), 1)
    for k in range(cells // 2):
        b = cells + k
        fields = (mine[b] + decode(coded, scale, b) + target[k]).astype(BF16)
        for h in range(2):
            c = 2 * k + h
            near = mine[c] + decode(coded, scale, c) + first[c] + first_other[c]
            far = dot(fields[:, h * terms : (h + 1) * terms], basis_t[c], NAT)
            own = dot(moved[c], self_tiles[c], TRN)
            total = near + far + own
            out[:, c * size : (c + 1) * size] = jnp.where(lane < counts[c], total, jnp.zeros_like(total))


def body(
    charges,
    counts,
    self_tiles,
    basis,
    near_first,
    near_second,
    near_tiles,
    far_source,
    far_target,
    far_tiles,
):
    blks = lax.axis_size("blk")
    ranks = lax.axis_size("rhs")
    me = lax.axis_index("blk")
    rank = lax.axis_index("rhs")
    cells, size, _ = self_tiles.shape
    terms = basis.shape[2]
    rows = charges.shape[0]
    pairs = near_tiles.shape[0]
    fars = far_tiles.shape[0]
    bits = blks.bit_length() - 1
    order = [*range(1, bits), 0]
    halfc = cells // 2
    stride = cells + halfc
    total = blks * cells

    def swap_rank(x, d):
        return lax.ppermute(x, "rhs", [(i, i ^ d) for i in range(ranks)])

    def swap_blk(x, bit):
        return lax.ppermute(x, "blk", [(i, i ^ (1 << bit)) for i in range(blks)])

    def place(block):
        other = (block // cells) ^ me
        at = sum(((other >> bit) & 1) << s for s, bit in enumerate(order))
        return at * cells + block % cells

    def shape(n, dtype, r=rows):
        return jax.ShapeDtypeStruct((n, r, size), dtype)

    def scratch(n, r=rows):
        return pltpu.VMEM((n, r, size), F32)

    def scales(n):
        return pltpu.VMEM((scale_blocks(n) * GROUP, size), F32)

    other_tiles = swap_rank(near_tiles, 1)
    basis_t = jnp.swapaxes(basis, 1, 2)

    own = pl.pallas_call(
        prep_kernel,
        in_specs=[SMEM, VMEM, VMEM],
        out_specs=VMEM,
        out_shape=shape(stride, BF16),
        compiler_params=params(16),
        name="prep",
    )(counts, charges, basis_t)
    charge_own = own[:cells]
    charge_other = swap_rank(charge_own, 2)

    gathered = own
    for bit in order:
        gathered = jnp.concatenate([gathered, swap_blk(gathered, bit)], axis=0)

    def pick(x):
        return jnp.concatenate(
            [lax.dynamic_slice(x, (r * pairs,), (pairs,)) for r in (rank, rank ^ 1)]
        )

    first = pick(near_first % cells)
    second = pick(place(near_second))
    tgt = far_target % cells
    src = place(far_source)

    fchunk = 128
    tiles_ij = jnp.transpose(far_tiles, (1, 2, 0)).reshape(terms * terms, fars)
    turned, far_part = pl.pallas_call(
        far_source_kernel,
        grid_spec=pltpu.PrefetchScalarGridSpec(
            num_scalar_prefetch=2,
            grid=(fars // fchunk,),
            in_specs=[
                pl.BlockSpec((halfc, rows, size), lambda i, *_: (0, 0, 0)),
                pl.BlockSpec((terms * terms, fchunk), lambda i, *_: (0, i)),
            ],
            out_specs=[
                pl.BlockSpec((fchunk, terms // 2, size), lambda i, *_: (i, 0, 0)),
                pl.BlockSpec((total // 2, rows, size), lambda i, *_: (0, 0, 0)),
            ],
            scratch_shapes=[
                pltpu.VMEM((terms // 2 * fchunk, size), F32),
                pltpu.VMEM((cells, 2 * rows, terms // 2), BF16),
                scratch(total, 2 * rows),
            ],
        ),
        out_shape=[shape(fars, BF16, terms // 2), shape(total // 2, F32)],
        compiler_params=params(32),
        cost_estimate=pl.CostEstimate(flops=2 * fars * rows * terms * terms, bytes_accessed=10 << 20, transcendentals=0),
        name="far_source",
    )(tgt, src, own[cells:], tiles_ij)

    chunk = 32
    steps = pairs // chunk

    def whole(n, r=rows):
        return pl.BlockSpec((n, r, size), lambda i, *_: (0, 0, 0))

    tile_specs = [
        pl.BlockSpec((chunk, size, size), lambda i, *_: (jnp.minimum(i, steps - 1), 0, 0)),
        pl.BlockSpec((chunk, size, size), lambda i, *_: (jnp.maximum(i - steps, 0), 0, 0)),
    ]
    near_cost = pl.CostEstimate(flops=8 * pairs * rows * size * size, bytes_accessed=12 << 20, transcendentals=0)
    keep, send = pl.pallas_call(
        near_second_kernel,
        grid_spec=pltpu.PrefetchScalarGridSpec(
            num_scalar_prefetch=2,
            grid=(2 * steps,),
            in_specs=[whole(cells), whole(cells), *tile_specs],
            out_specs=[whole(total), whole(total + scale_blocks(total))],
            scratch_shapes=[
                pltpu.VMEM((cells, 2 * rows, size), BF16),
                scratch(total, 2 * rows),
                scales(total),
                scales(total),
            ],
        ),
        out_shape=[shape(total, F32), shape(total + scale_blocks(total), I16)],
        compiler_params=params(48),
        cost_estimate=near_cost,
        name="near_second",
    )(first, second, charge_own, charge_other, near_tiles, other_tiles)

    coded = swap_rank(send, 2)
    half = blks // 2 * stride
    keep, send = pl.pallas_call(
        functools.partial(meet_kernel, cells),
        in_specs=[VMEM] * 3,
        out_specs=[VMEM] * 2,
        out_shape=[shape(half, F32), shape(half + scale_blocks(half), I16)],
        scratch_shapes=[scratch(half), scales(total), scales(half), scales(half)],
        compiler_params=params(48),
        name="meet",
    )(keep, coded, far_part)
    coded = swap_blk(send, order[-1])

    for bit in reversed(order[:-1]):
        now, half = half, half // 2
        keep, send = pl.pallas_call(
            add_kernel,
            in_specs=[VMEM] * 2,
            out_specs=[VMEM] * 2,
            out_shape=[shape(half, F32), shape(half + scale_blocks(half), I16)],
            scratch_shapes=[scratch(half), scales(now), scales(half), scales(half)],
            compiler_params=params(32),
            name="add",
        )(keep, coded)
        coded = swap_blk(send, bit)

    charge_all_other = swap_rank(
        gathered.reshape(blks, stride, rows, size)[:, :cells].reshape(total, rows, size), 2
    )
    target_part = pl.pallas_call(
        functools.partial(far_target_kernel, stride, cells),
        grid_spec=pltpu.PrefetchScalarGridSpec(
            num_scalar_prefetch=2,
            grid=(fars // fchunk,),
            in_specs=[
                whole(blks * stride),
                pl.BlockSpec((fchunk, terms // 2, size), lambda i, *_: (i, 0, 0)),
            ],
            out_specs=whole(halfc),
            scratch_shapes=[
                pltpu.VMEM((total, 2 * rows, size), BF16),
                pltpu.VMEM((cells, 2 * rows, terms // 2), F32),
            ],
        ),
        out_shape=shape(halfc, F32),
        compiler_params=params(32),
        cost_estimate=pl.CostEstimate(flops=2 * fars * rows * terms * terms, bytes_accessed=6 << 20, transcendentals=0),
        name="far_target",
    )(tgt, src, gathered, turned)

    first_own, first_send = pl.pallas_call(
        functools.partial(near_first_kernel, stride, cells),
        grid_spec=pltpu.PrefetchScalarGridSpec(
            num_scalar_prefetch=2,
            grid=(2 * steps,),
            in_specs=[whole(blks * stride), whole(total), *tile_specs],
            out_specs=[whole(cells), whole(cells)],
            scratch_shapes=[
                pltpu.VMEM((total, 2 * rows, size), BF16),
                scratch(cells, 2 * rows),
            ],
        ),
        out_shape=[shape(cells, F32), shape(cells, F32)],
        compiler_params=params(32),
        cost_estimate=near_cost,
        name="near_first",
    )(first, second, gathered, charge_all_other, near_tiles, other_tiles)
    first_other = swap_rank(first_send, 2)

    return pl.pallas_call(
        final_kernel,
        in_specs=[SMEM] + [VMEM] * 8,
        out_specs=VMEM,
        out_shape=jax.ShapeDtypeStruct(charges.shape, F32),
        scratch_shapes=[scales(stride)],
        compiler_params=params(16),
        name="final",
    )(counts, keep, coded, first_own, first_other, target_part, charge_own, self_tiles, basis_t)


def solution(mesh):
    in_specs = (
        P("rhs", "blk"),
        P("blk"),
        P("blk", None, None),
        P("blk", None, None),
        P("blk"),
        P("blk"),
        P(("blk", "rhs"), None, None),
        P("blk"),
        P("blk"),
        P("blk", None, None),
    )
    out_specs = P("rhs", "blk")
    return jax.shard_map(body, mesh=mesh, in_specs=in_specs, out_specs=out_specs, check_vma=False)
```

time: 234 us -> 86.8 us (0.37)
  blocking collectives: 64.4 us -> 0 us
  waiting for transfers between devices: 65.7 us -> 11.6 us
  matrix products: 52.5 us -> 0 us
  Pallas kernels: 0 us -> 51.1 us
  local copies, waits for them, and re-layouts: 31.1 us -> 5.84 us
  between operations: 15 us -> 0.22 us
  starting transfers between devices: 0.13 us -> 14.3 us
    reduce_scatter x2 -> x0, waiting for transfers between devices: 65 us -> none  [the longest x1 65 us: body(): lax.psum_scatter(near.reshape(rows, -1), 'blk', scatter_dimension=1, tile...]
    all_gather x2 -> x0, blocking collectives: 64.4 us -> none  [the longest x1 32.5 us: body(): lax.all_gather(moments.reshape(rows, blk_dev * terms), 'blk', axis=1, til...]
    pallas_call x0 -> x9, Pallas kernels: none -> 51.1 us  [the longest x1 20.7 us: body(): pl.pallas_call(far_source_kernel, grid_spec=pltpu.PrefetchScalarGridSpec(...]
    dot_general x11 -> x0, matrix products: 47.6 us -> none  [the longest x2 21.9 us: pair_sums(): jnp.einsum('rnj,nij->rni', from_second, tiles, preferred_element_type=jnp...]
    ppermute x0 -> x11, starting transfers between devices: none -> 14.3 us  [the longest x6 9.66 us: swap_blk(): return lax.ppermute(x, 'blk', [(i, i ^ 1 << bit) for i in range(blks)])]
    ppermute x0 -> x11, waiting for transfers between devices: none -> 11.6 us  [the longest x6 8.65 us: swap_blk(): return lax.ppermute(x, 'blk', [(i, i ^ 1 << bit) for i in range(blks)])]
    unnamed x21 -> x32, local copies, waits for them, and re-layouts: 14.8 us -> 5.72 us
    transpose x2 -> x0, local copies, waits for them, and re-layouts: 7.77 us -> none  [the longest x1 3.97 us: pair_sums(): jnp.einsum('rni,nij->rnj', from_first, tiles, preferred_element_type=jnp....]
  transfers between devices with their start and end apart: 3 -> 11, of which waited for: 1 -> 3; matrix products, arithmetic and copies ran while one was open for 37% -> 4% of each run, Pallas kernels for 0% -> 57%
where the time goes in v1:
time: 86.8 us; the launch traced here: 86.4 us
  Pallas kernels  51.1 us (59%)
  starting transfers between devices  14.3 us (16%)
  waiting for transfers between devices  11.6 us (13%)
  local copies, waits for them, and re-layouts  5.84 us (7%)
  other arithmetic  3.41 us (4%)
    pallas_call x1, Pallas kernels, body(): pl.pallas_call(far_source_kernel, grid_spec=pltpu.PrefetchScalarGridSpec(...  20.7 us
    ppermute x6, starting transfers between devices, swap_blk(): return lax.ppermute(x, 'blk', [(i, i ^ 1 << bit) for i in range(blks)])  9.66 us
    pallas_call x1, Pallas kernels, body(): pl.pallas_call(functools.partial(near_first_kernel, stride, cells), grid_...  9.27 us
    pallas_call x1, Pallas kernels, body(): pl.pallas_call(near_second_kernel, grid_spec=pltpu.PrefetchScalarGridSpec...  9.27 us
    ppermute x6, waiting for transfers between devices, swap_blk(): return lax.ppermute(x, 'blk', [(i, i ^ 1 << bit) for i in range(blks)])  8.65 us
    pallas_call x1, Pallas kernels, body(): pl.pallas_call(functools.partial(far_target_kernel, stride, cells), grid_...  8.06 us
    unnamed x32, local copies, waits for them, and re-layouts  5.72 us
    ppermute x5, starting transfers between devices, swap_rank(): return lax.ppermute(x, 'rhs', [(i, i ^ d) for i in range(ranks)])  4.6 us
  transfers between devices with their start and end apart: 11, of which 3 were waited for; matrix products, arithmetic and copies ran while one was open for 4% of the time, Pallas kernels for 57%

profile of v1, /device:TPU:0, one launch (start us, length us, event | category | flops | bytes accessed | tf_op | source)
XLA Modules:
  0.0 86.4 jit_solution(5966338920898494803)
XLA Ops:
  0.0 0.5 collective-permute-start.1
  0.5 0.9 %copy-done.5 = bf16[16,128,64]{1,2,0:T(8,128)(2,1)S(1)} copy-done((bf16[16,128,64]{1,2,0:T(8,128)(2,1)S(1)}, bf16[16,128,64]{1,2,0:T(8,128)(2,1)}, u32[]{:S(2)}) %copy-start.5) | copy-done | bytes 262168
  1.4 0.8 copy-done.8
  2.2 0.7 copy-done.9
  2.9 0.8 prep.1
  3.7 2.6 %collective-permute-start.6 = (bf16[24,16,128]{2,1,0:T(8,128)(2,1)S(1)}, bf16[24,16,128]{2,1,0:T(8,128)(2,1)S(1)}, u32[]{:S(2)}, u32[]{:S(2)}) collective-permute-start(bf16[24,16,128]{2,1,0:T(8,128)(2,1)S(1)} %prep.1), channel_id=1, source_target_pairs={{0,8},{4,12},{8,0},{12,4},{16,24},{20,28},{24,16},{28,20},{1,9},{5... | collective-permute-start | bytes 294920 | tf_op jit(solution)/shard_map/ppermute | solution.py:334
  6.4 1.5 %collective-permute-start = (bf16[16,16,128]{2,1,0:T(8,128)(2,1)S(1)}, bf16[16,16,128]{2,1,0:T(8,128)(2,1)S(1)}, u32[]{:S(2)}, u32[]{:S(2)}) collective-permute-start(bf16[16,16,128]{2,1,0:T(8,128)(2,1)S(1)} %slice.12.mine.moved), channel_id=1, source_target_pairs={{0,2},{1,3},{2,0},{3,1},{4,6},{5,7},{6,4},{7,5},{8,10},{9,11},{10,... | collective-permute-start | bytes 196616 | tf_op jit(solution)/shard_map/ppermute | solution.py:331
  7.9 0.7 add_select_fusion.5
  8.6 0.7 fusion.2
  9.2 0.1 fusion.10
  9.3 0.5 collective-permute-done.6
  9.9 2.8 %collective-permute-start.7 = (bf16[48,16,128]{2,1,0:T(8,128)(2,1)S(1)}, bf16[48,16,128]{2,1,0:T(8,128)(2,1)S(1)}, u32[]{:S(2)}, u32[]{:S(2)}) collective-permute-start(bf16[48,16,128]{2,1,0:T(8,128)(2,1)S(1)} %pad_maximum_fusion.2), channel_id=1, source_target_pairs={{0,16},{4,20},{8,24},{12,28},{16,0},{20,4},{24,8},{28,12},{1,17},{... | collective-permute-start | bytes 589832 | tf_op jit(solution)/shard_map/ppermute | solution.py:334
  12.7 0.0 collective-permute-done.theirs
  12.7 0.0 collective-permute-done.1.other
  12.7 0.0 copy-start
  12.7 2.2 %copy-done = bf16[128,128,128]{2,1,0:T(8,128)(2,1)S(1)} copy-done((bf16[128,128,128]{2,1,0:T(8,128)(2,1)S(1)}, bf16[128,128,128]{2,1,0:T(8,128)(2,1)}, u32[]{:S(2)}) %copy-start) | copy-done | bytes 4194328
  14.9 9.3 %near_second.1 = (f32[128,16,128]{2,1,0:T(8,128)S(1)}, s16[136,16,128]{2,1,0:T(8,128)(2,1)}) custom-call(s32[256]{0:T(256)S(1)} %pad_add_fusion.first, s32[256]{0:T(256)S(1)} %pad_add_fusion.1.second, bf16[16,16,128]{2,1,0:T(8,128)(2,1)S(1)} %slice.12.mine.moved, bf16[16,16,128]{2,1,0:T(8,128)(2,1)S(1)} %collective-permute-done.theirs, ...), custom_call_target="tpu_custom_call" | custom-call | flops 268435456 | bytes 12582912 | tf_op jit(solution)/shard_map/near_second/pallas_call | solution.py:416
  24.2 1.0 %copy-done.3 = f32[128,16,128]{2,1,0:T(8,128)} copy-done((f32[128,16,128]{2,1,0:T(8,128)}, f32[128,16,128]{2,1,0:T(8,128)S(1)}, u32[]{:S(2)}) %copy-start.3) | copy-done | bytes 1048600
  25.2 1.5 %collective-permute-start.2 = (s16[136,16,128]{2,1,0:T(8,128)(2,1)}, s16[136,16,128]{2,1,0:T(8,128)(2,1)S(1)}, u32[]{:S(2)}, u32[]{:S(2)}) collective-permute-start(s16[136,16,128]{2,1,0:T(8,128)(2,1)} %get-tuple-element.18), channel_id=1, source_target_pairs={{0,2},{1,3},{2,0},{3,1},{4,6},{5,7},{6,4},{7,5},{8,10},{9,11},{10,... | collective-permute-start | bytes 1671176 | tf_op jit(solution)/shard_map/ppermute | solution.py:331
  26.7 0.0 collective-permute-done.7
  26.7 0.8 pad_maximum_fusion.1
  27.6 1.5 %collective-permute-start.8 = (bf16[96,16,128]{2,1,0:T(8,128)(2,1)}, bf16[96,16,128]{2,1,0:T(8,128)(2,1)}, u32[]{:S(2)}, u32[]{:S(2)}) collective-permute-start(bf16[96,16,128]{2,1,0:T(8,128)(2,1)} %pad_maximum_fusion.1), channel_id=1, source_target_pairs={{0,4},{4,0},{8,12},{12,8},{16,20},{20,16},{24,28},{28,24},{1,5},{5... | collective-permute-start | bytes 1179656 | tf_op jit(solution)/shard_map/ppermute | solution.py:334
  29.1 0.0 copy-done.13
  29.1 0.0 copy-done.2
  29.2 0.0 copy-start.1
  29.2 20.7 %far_source.1 = (bf16[512,32,128]{2,1,0:T(8,128)(2,1)S(1)}, f32[64,16,128]{2,1,0:T(8,128)S(1)}) custom-call(s32[512]{0:T(512)S(1)} %get-tuple-element.35.tgt, s32[512]{0:T(512)S(1)} %get-tuple-element.36.pos, bf16[8,16,128]{2,1,0:T(8,128)(2,1)S(1)} %slice.13.mine, bf16[4096,512]{1,0:T(8,128)(2,1)S(1)} %bitcast.7), custom_call_target="tpu_custom_call" | custom-call | flops 67108864 | bytes 10485760 | tf_op jit(solution)/shard_map/far_source/pallas_call | solution.py:380
  49.9 0.0 collective-permute-done.2.coded
  49.9 0.7 meet.1
  50.6 0.6 collective-permute-start.3
  51.1 0.0 collective-permute-done.8
  51.1 1.1 %pad_maximum_fusion.everyone = bf16[192,16,128]{2,1,0:T(8,128)(2,1)S(1)} fusion(bf16[96,16,128]{2,1,0:T(8,128)(2,1)} %collective-permute-done.8, bf16[48,16,128]{2,1,0:T(8,128)(2,1)} %copy-done.13, bf16[24,16,128]{2,1,0:T(8,128)(2,1)S(1)} %copy-done.12, bf16[24,16,128]{2,1,0:T(8,128)(2,1)S(1)} %prep.1), kind=kLoop, calls=%fused_computation | loop fusion | flops 1179648 | bytes 1572864 | tf_op jit(solution)/shard_map/concatenate | solution.py:366
  52.3 0.6 collective-permute-start.9
  52.9 8.1 %collective-permute-done.3.coded = s16[102,16,128]{2,1,0:T(8,128)(2,1)S(1)} collective-permute-done((s16[102,16,128]{2,1,0:T(8,128)(2,1)S(1)}, s16[102,16,128]{2,1,0:T(8,128)(2,1)S(1)}, u32[]{:S(2)}, u32[]{:S(2)}) %collective-permute-start.3) | collective-permute-done | bytes 417824 | tf_op jit(solution)/shard_map/ppermute | solution.py:334
  61.0 0.3 add.78
  61.4 0.5 collective-permute-start.4
  61.9 2.9 %collective-permute-done.9.theirs = bf16[128,16,128]{2,1,0:T(8,128)(2,1)S(1)} collective-permute-done((bf16[128,16,128]{2,1,0:T(8,128)(2,1)S(1)}, bf16[128,16,128]{2,1,0:T(8,128)(2,1)S(1)}, u32[]{:S(2)}, u32[]{:S(2)}) %collective-permute-start.9) | collective-permute-done | bytes 524320 | tf_op jit(solution)/shard_map/ppermute | solution.py:331
  64.8 9.3 %near_first.1 = (f32[16,16,128]{2,1,0:T(8,128)S(1)}, f32[16,16,128]{2,1,0:T(8,128)S(1)}) custom-call(s32[256]{0:T(256)S(1)} %pad_add_fusion.first, s32[256]{0:T(256)S(1)} %pad_add_fusion.1.second, bf16[192,16,128]{2,1,0:T(8,128)(2,1)S(1)} %pad_maximum_fusion.everyone, bf16[128,16,128]{2,1,0:T(8,128)(2,1)S(1)} %collective-permute-done.9.theirs, ...), custom_call_target="tpu_custom_call" | custom-call | flops 268435456 | bytes 12582912 | tf_op jit(solution)/shard_map/near_first/pallas_call | solution.py:486
  74.1 0.0 copy-start.6
  74.1 0.0 copy-start.7
  74.1 0.0 copy-start.10
  74.1 0.6 collective-permute-start.10
  74.7 0.0 collective-permute-done.4.coded
  74.7 0.2 add.79
  74.9 1.6 %collective-permute-start.5 = (s16[26,16,128]{2,1,0:T(8,128)(2,1)S(1)}, s16[26,16,128]{2,1,0:T(8,128)(2,1)S(1)}, u32[]{:S(2)}, u32[]{:S(2)}) collective-permute-start(s16[26,16,128]{2,1,0:T(8,128)(2,1)S(1)} %get-tuple-element.25), channel_id=1, source_target_pairs={{0,8},{4,12},{8,0},{12,4},{16,24},{20,28},{24,16},{28,20},{1,9},{5... | collective-permute-start | bytes 319496 | tf_op jit(solution)/shard_map/ppermute | solution.py:334
  76.5 8.1 %far_target.1.target = f32[8,16,128]{2,1,0:T(8,128)S(1)} custom-call(s32[512]{0:T(512)S(1)} %get-tuple-element.35.tgt, s32[512]{0:T(512)S(1)} %get-tuple-element.36.pos, bf16[192,16,128]{2,1,0:T(8,128)(2,1)S(1)} %pad_maximum_fusion.everyone, bf16[512,32,128]{2,1,0:T(8,128)(2,1)S(1)} %get-tuple-element.28.turned), custom_call_target="tpu_custom_call" | custom-call | flops 67108864 | bytes 6291456 | tf_op jit(solution)/shard_map/far_target/pallas_call | solution.py:465
  84.6 0.0 collective-permute-done.10.first_other
  84.6 0.0 collective-permute-done.5.coded
  84.6 1.8 %final.1 = f32[16,2048]{1,0:T(8,128)} custom-call(s32[16]{0:T(128)S(1)} %copy-done.10, f32[24,16,128]{2,1,0:T(8,128)S(1)} %get-tuple-element.24.mine, s16[26,16,128]{2,1,0:T(8,128)(2,1)S(1)} %collective-permute-done.5.coded, f32[16,16,128]{2,1,0:T(8,128)S(1)} %get-tuple-element.26.first, f32[16,16,128]{2,1,0:T(8,128)S(1)} %collective-permute-done.10.first_other, ...), custom_call_target="tpu_custom_call" | custom-call | tf_op jit(solution)/shard_map/final/pallas_call | solution.py:505
  (27 shorter events, 0.1 us)
Async XLA Ops:
  0.0 12.7 %collective-permute-start.1 = (bf16[128,128,128]{2,1,0:T(8,128)(2,1)}, bf16[128,128,128]{2,1,0:T(8,128)(2,1)}, u32[]{:S(2)}, u32[]{:S(2)}) collective-permute-start(bf16[128,128,128]{2,1,0:T(8,128)(2,1)} %tiles.3), channel_id=1, source_target_pairs={{0,1},{1,0},{2,3},{3,2},{4,5},{5,4},{6,7},{7,6},{8,9},{9,8},{10,11... | collective-permute-start | bytes 12582920 | tf_op jit(solution)/shard_map/ppermute | solution.py:331
  0.5 0.9 %copy-start.5 = (bf16[16,128,64]{1,2,0:T(8,128)(2,1)S(1)}, bf16[16,128,64]{1,2,0:T(8,128)(2,1)}, u32[]{:S(2)}) copy-start(bf16[16,128,64]{1,2,0:T(8,128)(2,1)} %param.13) | copy-start | bytes 786436
  1.4 0.8 copy-start.8
  2.2 0.7 copy-start.9
  3.7 6.1 %collective-permute-start.6 = (bf16[24,16,128]{2,1,0:T(8,128)(2,1)S(1)}, bf16[24,16,128]{2,1,0:T(8,128)(2,1)S(1)}, u32[]{:S(2)}, u32[]{:S(2)}) collective-permute-start(bf16[24,16,128]{2,1,0:T(8,128)(2,1)S(1)} %prep.1), channel_id=1, source_target_pairs={{0,8},{4,12},{8,0},{12,4},{16,24},{20,28},{24,16},{28,20},{1,9},{5... | collective-permute-start | bytes 294920 | tf_op jit(solution)/shard_map/ppermute | solution.py:334
  6.4 6.3 %collective-permute-start = (bf16[16,16,128]{2,1,0:T(8,128)(2,1)S(1)}, bf16[16,16,128]{2,1,0:T(8,128)(2,1)S(1)}, u32[]{:S(2)}, u32[]{:S(2)}) collective-permute-start(bf16[16,16,128]{2,1,0:T(8,128)(2,1)S(1)} %slice.12.mine.moved), channel_id=1, source_target_pairs={{0,2},{1,3},{2,0},{3,1},{4,6},{5,7},{6,4},{7,5},{8,10},{9,11},{10,... | collective-permute-start | bytes 196616 | tf_op jit(solution)/shard_map/ppermute | solution.py:331
  9.8 16.9 %copy-start.11 = (bf16[24,16,128]{2,1,0:T(8,128)(2,1)}, bf16[24,16,128]{2,1,0:T(8,128)(2,1)S(1)}, u32[]{:S(2)}) copy-start(bf16[24,16,128]{2,1,0:T(8,128)(2,1)S(1)} %collective-permute-done.6) | copy-start | bytes 294916
  9.9 16.9 %collective-permute-start.7 = (bf16[48,16,128]{2,1,0:T(8,128)(2,1)S(1)}, bf16[48,16,128]{2,1,0:T(8,128)(2,1)S(1)}, u32[]{:S(2)}, u32[]{:S(2)}) collective-permute-start(bf16[48,16,128]{2,1,0:T(8,128)(2,1)S(1)} %pad_maximum_fusion.2), channel_id=1, source_target_pairs={{0,16},{4,20},{8,24},{12,28},{16,0},{20,4},{24,8},{28,12},{1,17},{... | collective-permute-start | bytes 589832 | tf_op jit(solution)/shard_map/ppermute | solution.py:334
  12.7 16.4 %copy-start.14 = (s32[512]{0:T(512)S(1)}, s32[512]{0:T(512)}, u32[]{:S(2)}) copy-start(s32[512]{0:T(512)} %param.18) | copy-start | bytes 6148
  12.7 2.2 %copy-start = (bf16[128,128,128]{2,1,0:T(8,128)(2,1)S(1)}, bf16[128,128,128]{2,1,0:T(8,128)(2,1)}, u32[]{:S(2)}) copy-start(bf16[128,128,128]{2,1,0:T(8,128)(2,1)} %tiles.3) | copy-start | bytes 12582916
  14.9 14.2 %copy-start.15 = (s32[512]{0:T(512)S(1)}, s32[512]{0:T(512)}, u32[]{:S(2)}) copy-start(s32[512]{0:T(512)} %param.17) | copy-start | bytes 6148
  14.9 14.2 %copy-start.2 = (bf16[512,64,64]{0,2,1:T(8,128)(2,1)S(1)}, bf16[512,64,64]{0,2,1:T(8,128)(2,1)}, u32[]{:S(2)}) copy-start(bf16[512,64,64]{0,2,1:T(8,128)(2,1)} %param.19) | copy-start | bytes 12582916
  24.2 1.0 %copy-start.3 = (f32[128,16,128]{2,1,0:T(8,128)}, f32[128,16,128]{2,1,0:T(8,128)S(1)}, u32[]{:S(2)}) copy-start(f32[128,16,128]{2,1,0:T(8,128)S(1)} %get-tuple-element.17.mine) | copy-start | bytes 3145732
  25.2 24.6 %copy-start.4 = (f32[128,16,128]{2,1,0:T(8,128)S(1)}, f32[128,16,128]{2,1,0:T(8,128)}, u32[]{:S(2)}) copy-start(f32[128,16,128]{2,1,0:T(8,128)} %copy-done.3) | copy-start | bytes 3145732
  25.2 24.6 %collective-permute-start.2 = (s16[136,16,128]{2,1,0:T(8,128)(2,1)}, s16[136,16,128]{2,1,0:T(8,128)(2,1)S(1)}, u32[]{:S(2)}, u32[]{:S(2)}) collective-permute-start(s16[136,16,128]{2,1,0:T(8,128)(2,1)} %get-tuple-element.18), channel_id=1, source_target_pairs={{0,2},{1,3},{2,0},{3,1},{4,6},{5,7},{6,4},{7,5},{8,10},{9,11},{10,... | collective-permute-start | bytes 1671176 | tf_op jit(solution)/shard_map/ppermute | solution.py:331
  26.7 2.4 %copy-start.13 = (bf16[48,16,128]{2,1,0:T(8,128)(2,1)}, bf16[48,16,128]{2,1,0:T(8,128)(2,1)S(1)}, u32[]{:S(2)}) copy-start(bf16[48,16,128]{2,1,0:T(8,128)(2,1)S(1)} %collective-permute-done.7) | copy-start | bytes 589828
  27.6 23.6 %copy-start.12 = (bf16[24,16,128]{2,1,0:T(8,128)(2,1)S(1)}, bf16[24,16,128]{2,1,0:T(8,128)(2,1)}, u32[]{:S(2)}) copy-start(bf16[24,16,128]{2,1,0:T(8,128)(2,1)} %copy-done.11) | copy-start | bytes 294916
  27.6 23.6 %collective-permute-start.8 = (bf16[96,16,128]{2,1,0:T(8,128)(2,1)}, bf16[96,16,128]{2,1,0:T(8,128)(2,1)}, u32[]{:S(2)}, u32[]{:S(2)}) collective-permute-start(bf16[96,16,128]{2,1,0:T(8,128)(2,1)} %pad_maximum_fusion.1), channel_id=1, source_target_pairs={{0,4},{4,0},{8,12},{12,8},{16,20},{20,16},{24,28},{28,24},{1,5},{5... | collective-permute-start | bytes 1179656 | tf_op jit(solution)/shard_map/ppermute | solution.py:334
  29.2 35.7 %copy-start.1 = (bf16[128,128,128]{2,1,0:T(8,128)(2,1)S(1)}, bf16[128,128,128]{2,1,0:T(8,128)(2,1)}, u32[]{:S(2)}) copy-start(bf16[128,128,128]{2,1,0:T(8,128)(2,1)} %tiles.3) | copy-start | bytes 12582916
  50.6 10.5 %collective-permute-start.3 = (s16[102,16,128]{2,1,0:T(8,128)(2,1)S(1)}, s16[102,16,128]{2,1,0:T(8,128)(2,1)S(1)}, u32[]{:S(2)}, u32[]{:S(2)}) collective-permute-start(s16[102,16,128]{2,1,0:T(8,128)(2,1)S(1)} %get-tuple-element.21), channel_id=1, source_target_pairs={{0,4},{4,0},{8,12},{12,8},{16,20},{20,16},{24,28},{28,24},{1,5},{5... | collective-permute-start | bytes 1253384 | tf_op jit(solution)/shard_map/ppermute | solution.py:334
  52.3 12.5 %collective-permute-start.9 = (bf16[128,16,128]{2,1,0:T(8,128)(2,1)S(1)}, bf16[128,16,128]{2,1,0:T(8,128)(2,1)S(1)}, u32[]{:S(2)}, u32[]{:S(2)}) collective-permute-start(bf16[128,16,128]{2,1,0:T(8,128)(2,1)S(1)} %bitcast.10), channel_id=1, source_target_pairs={{0,2},{1,3},{2,0},{3,1},{4,6},{5,7},{6,4},{7,5},{8,10},{9,11},{10,... | collective-permute-start | bytes 1572872 | tf_op jit(solution)/shard_map/ppermute | solution.py:331
  61.4 13.3 %collective-permute-start.4 = (s16[51,16,128]{2,1,0:T(8,128)(2,1)S(1)}, s16[51,16,128]{2,1,0:T(8,128)(2,1)S(1)}, u32[]{:S(2)}, u32[]{:S(2)}) collective-permute-start(s16[51,16,128]{2,1,0:T(8,128)(2,1)S(1)} %get-tuple-element.23), channel_id=1, source_target_pairs={{0,16},{4,20},{8,24},{12,28},{16,0},{20,4},{24,8},{28,12},{1,17},{... | collective-permute-start | bytes 626696 | tf_op jit(solution)/shard_map/ppermute | solution.py:334
  74.1 10.5 %copy-start.6 = (bf16[16,128,64]{1,2,0:T(8,128)(2,1)S(1)}, bf16[16,128,64]{1,2,0:T(8,128)(2,1)}, u32[]{:S(2)}) copy-start(bf16[16,128,64]{1,2,0:T(8,128)(2,1)} %param.13) | copy-start | bytes 786436
  74.1 10.5 %copy-start.7 = (bf16[16,128,128]{2,1,0:T(8,128)(2,1)S(1)}, bf16[16,128,128]{2,1,0:T(8,128)(2,1)}, u32[]{:S(2)}) copy-start(bf16[16,128,128]{2,1,0:T(8,128)(2,1)} %self_tiles.1) | copy-start | bytes 1572868
  74.1 10.5 %copy-start.10 = (s32[16]{0:T(128)S(1)}, s32[16]{0:T(128)}, u32[]{:S(2)}) copy-start(s32[16]{0:T(128)} %counts.3) | copy-start | bytes 196
  74.1 10.5 %collective-permute-start.10 = (f32[16,16,128]{2,1,0:T(8,128)S(1)}, f32[16,16,128]{2,1,0:T(8,128)S(1)}, u32[]{:S(2)}, u32[]{:S(2)}) collective-permute-start(f32[16,16,128]{2,1,0:T(8,128)S(1)} %get-tuple-element.27), channel_id=1, source_target_pairs={{0,2},{1,3},{2,0},{3,1},{4,6},{5,7},{6,4},{7,5},{8,10},{9,11},{10,... | collective-permute-start | bytes 393224 | tf_op jit(solution)/shard_map/ppermute | solution.py:331
  74.9 9.7 %collective-permute-start.5 = (s16[26,16,128]{2,1,0:T(8,128)(2,1)S(1)}, s16[26,16,128]{2,1,0:T(8,128)(2,1)S(1)}, u32[]{:S(2)}, u32[]{:S(2)}) collective-permute-start(s16[26,16,128]{2,1,0:T(8,128)(2,1)S(1)} %get-tuple-element.25), channel_id=1, source_target_pairs={{0,8},{4,12},{8,0},{12,4},{16,24},{20,28},{24,16},{28,20},{1,9},{5... | collective-permute-start | bytes 319496 | tf_op jit(solution)/shard_map/ppermute | solution.py:334

commit v2 on v1

v2 whole, which is shorter than its diff:
```python
import functools

import jax
import jax.numpy as jnp
from jax import lax
from jax.experimental import pallas as pl
from jax.experimental.pallas import tpu as pltpu
from jax.sharding import PartitionSpec as P

F32, BF16, I16, I32 = jnp.float32, jnp.bfloat16, jnp.int16, jnp.int32
GROUP = 16
TOP = 32767.0
VMEM = pl.BlockSpec(memory_space=pltpu.VMEM)
SMEM = pl.BlockSpec(memory_space=pltpu.SMEM)
HBM = pl.BlockSpec(memory_space=pltpu.HBM)
NAT = (((1,), (0,)), ((), ()))
TRN = (((1,), (1,)), ((), ()))


def params(mib):
    return pltpu.CompilerParams(vmem_limit_bytes=mib << 20)


def dot(lhs, rhs, dims):
    return lax.dot_general(lhs, rhs, dims, preferred_element_type=F32)


def scale_blocks(count):
    return -(-count // GROUP)


def encode(src, out, count, peak, inv):
    peak[...] = jnp.zeros_like(peak)

    def find(b, _):
        peak[pl.ds(b, 1), :] = jnp.max(jnp.abs(src[b]), axis=0, keepdims=True)
        return 0

    lax.fori_loop(0, count, find, 0, unroll=8)
    code = jnp.ceil(jnp.log2(jnp.maximum(peak[...], 1e-30)) * 8.0) + 1.0
    inv[...] = TOP * jnp.exp2(code * -0.125)
    for s in range(scale_blocks(count)):
        out[count + s] = code[s * GROUP : (s + 1) * GROUP].astype(I32).astype(I16)

    def put(b, _):
        out[b] = jnp.round(src[b] * inv[pl.ds(b, 1), :]).astype(I32).astype(I16)
        return 0

    lax.fori_loop(0, count, put, 0, unroll=8)


def decode_scales(coded, count, scale):
    for s in range(scale_blocks(count)):
        code = coded[count + s].astype(I32).astype(F32)
        scale[s * GROUP : (s + 1) * GROUP, :] = jnp.exp2(code * 0.125) * (1.0 / TOP)


def decode(coded, scale, b):
    return coded[b].astype(I32).astype(F32) * scale[pl.ds(b, 1), :]


def prep_kernel(counts_in, charges_in, basis_in, out, counts, charges, basis_t, sems):
    copies = [
        pltpu.make_async_copy(src, dst, sems.at[i])
        for i, (src, dst) in enumerate(((counts_in, counts), (charges_in, charges), (basis_in, basis_t)))
    ]
    for copy in copies:
        copy.start()
    for copy in copies:
        copy.wait()
    cells, terms, size = basis_t.shape
    rows = charges.shape[0]
    lane = lax.broadcasted_iota(I32, (rows, size), 1)
    moments = []
    for c in range(cells):
        x = charges[:, c * size : (c + 1) * size]
        x = jnp.where(lane < counts[c], x, jnp.zeros_like(x))
        out[c] = x
        moments.append(dot(x, basis_t[c], TRN))
    for k in range(cells // 2):
        out[cells + k] = jnp.concatenate(moments[2 * k : 2 * k + 2], axis=1).astype(BF16)


PITCH = 136
FAR_UNROLL = 32


def far_source_kernel(offs, tgt, pos, mine, theirs, tiles, turned, keep, send, flip, lhs, acc):
    step = pl.program_id(0)
    rows, lanes = mine.shape[1:]
    half = lanes // 2
    pairs = half // 2
    chunk = tiles.shape[1]
    base = (offs[0] * pl.num_programs(0) + step) * chunk

    @pl.when(step == 0)
    def _():
        acc[...] = jnp.zeros_like(acc)
        for k in range(mine.shape[0]):
            x, y = mine[k], theirs[k]
            for h in range(2):
                at = h * half
                parts = [z[:, at + q * pairs : at + (q + 1) * pairs] for q in range(2) for z in (x, y)]
                lhs[2 * k + h] = jnp.concatenate(parts, axis=0)

    for i in range(pairs):
        both = jnp.concatenate(
            [tiles[i * half : (i + 1) * half, :], tiles[(i + pairs) * half : (i + pairs + 1) * half, :]], axis=0
        )
        flip[i * PITCH : i * PITCH + chunk, :] = both.astype(F32).T

    def work(g, _):
        sums = []
        for u in range(FAR_UNROLL):
            e = g * FAR_UNROLL + u
            w = flip[pl.ds(e, pairs, stride=PITCH), :].astype(BF16)
            turned[e] = w
            sums.append(dot(lhs[tgt[base + e]], w, NAT))
        for u in range(FAR_UNROLL):
            acc[pos[base + g * FAR_UNROLL + u]] += sums[u]
        return 0

    lax.fori_loop(0, chunk // FAR_UNROLL, work, 0)

    @pl.when(step == pl.num_programs(0) - 1)
    def _():
        def fold(k, _):
            a, b = acc[2 * k], acc[2 * k + 1]
            for r, out in enumerate((keep, send)):
                low, high = r * rows, (2 + r) * rows
                out[k] = jnp.concatenate(
                    [x[low : low + rows, :half] + x[high : high + rows, half:] for x in (a, b)], axis=1
                )
            return 0

        lax.fori_loop(0, keep.shape[0], fold, 0, unroll=4)


def far_target_kernel(stride, cells, offs, tgt, pos, everyone, theirs, turned, keep, send, lhs, acc):
    step = pl.program_id(0)
    rows, lanes = everyone.shape[1], everyone.shape[2]
    half = lanes // 2
    chunk = turned.shape[0]
    owners = everyone.shape[0] // stride
    base = (offs[0] * pl.num_programs(0) + step) * chunk

    @pl.when(step == 0)
    def _():
        acc[...] = jnp.zeros_like(acc)
        low = lax.broadcasted_iota(I32, (2 * rows, lanes), 1) < half

        def spread(o, _):
            for k in range(cells // 2):
                x = jnp.concatenate([everyone[o * stride + cells + k], theirs[o * (cells // 2) + k]], axis=0)
                y = jnp.concatenate([x[:, half:], x[:, :half]], axis=1)
                zero = jnp.zeros_like(x)
                at = o * cells + 2 * k
                lhs[at] = jnp.concatenate([jnp.where(low, x, zero), jnp.where(low, zero, y)], axis=0)
                lhs[at + 1] = jnp.concatenate([jnp.where(low, y, zero), jnp.where(low, zero, x)], axis=0)
            return 0

        lax.fori_loop(0, owners, spread, 0)

    def work(g, _):
        sums = []
        for u in range(FAR_UNROLL):
            e = g * FAR_UNROLL + u
            sums.append(dot(lhs[pos[base + e]], turned[e], TRN))
        for u in range(FAR_UNROLL):
            acc[tgt[base + g * FAR_UNROLL + u]] += sums[u]
        return 0

    lax.fori_loop(0, chunk // FAR_UNROLL, work, 0)

    @pl.when(step == pl.num_programs(0) - 1)
    def _():
        for k in range(cells // 2):
            a, b = acc[2 * k], acc[2 * k + 1]
            for r, out in enumerate((keep, send)):
                low, high = r * rows, (2 + r) * rows
                out[k] = jnp.concatenate([x[i : i + rows] for x in (a, b) for i in (low, high)], axis=1)


def near_loop(offs, lhs, lhs_at, tiles, other, dims, acc, acc_at, buf, sems, setup):
    chunk = buf.shape[1]
    each = tiles.shape[0] // chunk
    steps = 2 * each
    copies = [
        pltpu.make_async_copy((tiles, other)[k // each].at[pl.ds(k % each * chunk, chunk)], buf.at[k], sems.at[k])
        for k in range(steps)
    ]
    for copy in copies:
        copy.start()
    setup()
    for k in range(steps):
        copies[k].wait()
        base = offs[k // each] + k % each * chunk
        sums = [dot(lhs[lhs_at[base + n]], buf[k, n], dims) for n in range(chunk)]
        for n in range(chunk):
            acc[acc_at[base + n]] += sums[n]


def near_second_kernel(offs, first, second, mine, theirs, tiles, other, keep, send, lhs, acc, buf, peak, inv, sems):
    rows = mine.shape[1]
    total = keep.shape[0]

    def setup():
        acc[...] = jnp.zeros_like(acc)
        for c in range(lhs.shape[0]):
            lhs[c] = jnp.concatenate([mine[c], theirs[c]], axis=0)

    near_loop(offs, lhs, first, tiles, other, NAT, acc, second, buf, sems, setup)

    def split(b, _):
        keep[b] = acc[b, :rows, :]
        return 0

    lax.fori_loop(0, total, split, 0, unroll=8)
    encode(acc.at[:, rows:, :], send, total, peak, inv)


def near_first_kernel(stride, cells, offs, first, second, everyone, *refs):
    *parts, tiles, other, keep, send, lhs, acc, buf, sems = refs
    rows = everyone.shape[1]

    def setup():
        acc[...] = jnp.zeros_like(acc)
        start = 0
        for part in parts:
            count = part.shape[0] // cells

            def fill(o, _, part=part, start=start):
                for c in range(cells):
                    at = start + o
                    lhs[at * cells + c] = jnp.concatenate(
                        [everyone[at * stride + c], part[o * cells + c]], axis=0
                    )
                return 0

            lax.fori_loop(0, count, fill, 0)
            start += count

    near_loop(offs, lhs, second, tiles, other, TRN, acc, first, buf, sems, setup)
    for c in range(cells):
        keep[c] = acc[c, :rows, :]
        send[c] = acc[c, rows:, :]


def meet_kernel(cells, mine, coded, far, far_other, keep, send, acc, scale, peak, inv):
    total = mine.shape[0]
    near_b, far_b = cells, cells // 2
    stride = near_b + far_b
    owners = total // cells
    decode_scales(coded, total, scale)

    def owner(o, dst, at):
        def near_part(c, _):
            b = o * near_b + c
            dst[at * stride + c] = mine[b] + decode(coded, scale, b)
            return 0

        lax.fori_loop(0, near_b, near_part, 0, unroll=8)
        for c in range(far_b):
            dst[at * stride + near_b + c] = far[o * far_b + c] + far_other[o * far_b + c]

    for o in range(owners // 2):
        owner(o, keep, o)
        owner(o + owners // 2, acc, o)
    encode(acc, send, acc.shape[0], peak, inv)


def add_kernel(mine, coded, keep, send, acc, scale, peak, inv):
    total = mine.shape[0]
    half = total // 2
    decode_scales(coded, total, scale)

    def one(b, _):
        keep[b] = mine[b] + decode(coded, scale, b)
        acc[b] = mine[half + b] + decode(coded, scale, half + b)
        return 0

    lax.fori_loop(0, half, one, 0, unroll=8)
    encode(acc, send, half, peak, inv)


def final_kernel(
    counts, mine, coded, first, first_other, target, target_other, moved, self_tiles, basis_t, out, scale
):
    cells, terms, size = basis_t.shape
    rows = out.shape[0]
    decode_scales(coded, mine.shape[0], scale)
    lane = lax.broadcasted_iota(I32, (rows, size), 1)
    for k in range(cells // 2):
        b = cells + k
        fields = (mine[b] + decode(coded, scale, b) + target[k] + target_other[k]).astype(BF16)
        for h in range(2):
            c = 2 * k + h
            near = mine[c] + decode(coded, scale, c) + first[c] + first_other[c]
            far = dot(fields[:, h * terms : (h + 1) * terms], basis_t[c], NAT)
            own = dot(moved[c], self_tiles[c], TRN)
            total = near + far + own
            out[:, c * size : (c + 1) * size] = jnp.where(lane < counts[c], total, jnp.zeros_like(total))


def body(
    charges,
    counts,
    self_tiles,
    basis,
    near_first,
    near_second,
    near_tiles,
    far_source,
    far_target,
    far_tiles,
):
    blks = lax.axis_size("blk")
    ranks = lax.axis_size("rhs")
    me = lax.axis_index("blk")
    rank = lax.axis_index("rhs")
    cells, size, _ = self_tiles.shape
    terms = basis.shape[2]
    rows = charges.shape[0]
    pairs = near_tiles.shape[0]
    fars = far_tiles.shape[0]
    bits = blks.bit_length() - 1
    order = [*reversed(range(bits))]
    halfc = cells // 2
    stride = cells + halfc
    total = blks * cells

    def swap_rank(x, d):
        return lax.ppermute(x, "rhs", [(i, i ^ d) for i in range(ranks)])

    def swap_blk(x, bit):
        return lax.ppermute(x, "blk", [(i, i ^ (1 << bit)) for i in range(blks)])

    def place(block):
        other = (block // cells) ^ me
        at = sum(((other >> bit) & 1) << s for s, bit in enumerate(order))
        return at * cells + block % cells

    def shape(n, dtype, r=rows):
        return jax.ShapeDtypeStruct((n, r, size), dtype)

    def scratch(n, r=rows, dtype=F32):
        return pltpu.VMEM((n, r, size), dtype)

    def scales(n):
        return pltpu.VMEM((scale_blocks(n) * GROUP, size), F32)

    def whole(n, r=rows):
        return pl.BlockSpec((n, r, size), lambda i, *_: (0, 0, 0))

    def owners(x, low, high, begin, end):
        return x.reshape(-1, stride, rows, size)[low:high, begin:end].reshape(-1, rows, size)

    other_tiles = swap_rank(near_tiles, 1)
    basis_t = jnp.swapaxes(basis, 1, 2)

    own = pl.pallas_call(
        prep_kernel,
        in_specs=[HBM] * 3,
        out_specs=VMEM,
        out_shape=shape(stride, BF16),
        scratch_shapes=[
            pltpu.SMEM(counts.shape, I32),
            pltpu.VMEM(charges.shape, BF16),
            pltpu.VMEM(basis_t.shape, BF16),
            pltpu.SemaphoreType.DMA((3,)),
        ],
        compiler_params=params(8),
        name="prep",
    )(counts, charges, basis_t)
    charge_own = own[:cells]
    moment_own = own[cells:]
    moment_pair = swap_rank(moment_own, 1)

    gathered = own
    others = [swap_rank(charge_own, 2)]
    sent = 1
    for s, bit in enumerate(order):
        gathered = jnp.concatenate([gathered, swap_blk(gathered, bit)], axis=0)
        if s >= bits - 2:
            others.append(swap_rank(owners(gathered, sent, 2 << s, 0, cells), 2))
            sent = 2 << s

    first = near_first % cells
    second = place(near_second)
    tgt = far_target % cells
    src = place(far_source)
    offs = jnp.stack([rank * pairs, (rank ^ 1) * pairs])
    part = (rank & 1).reshape(1)

    fchunk = min(128, fars // 2)
    fsteps = fars // 2 // fchunk
    far_cost = pl.CostEstimate(flops=2 * fars * rows * terms * terms, bytes_accessed=6 << 20, transcendentals=0)
    tiles_ij = jnp.transpose(far_tiles, (1, 2, 0)).reshape(terms * terms, fars)
    turned, far_keep, far_send = pl.pallas_call(
        far_source_kernel,
        grid_spec=pltpu.PrefetchScalarGridSpec(
            num_scalar_prefetch=3,
            grid=(fsteps,),
            in_specs=[
                whole(halfc),
                whole(halfc),
                pl.BlockSpec((terms * terms, fchunk), lambda i, at, *_: (0, at[0] * fsteps + i)),
            ],
            out_specs=[
                pl.BlockSpec((fchunk, terms // 2, size), lambda i, *_: (i, 0, 0)),
                whole(total // 2),
                whole(total // 2),
            ],
            scratch_shapes=[
                pltpu.VMEM((terms // 2 * PITCH, size), F32),
                pltpu.VMEM((cells, 4 * rows, terms // 2), BF16),
                scratch(total, 4 * rows),
            ],
        ),
        out_shape=[shape(fars // 2, BF16, terms // 2), shape(total // 2, F32), shape(total // 2, F32)],
        compiler_params=params(16 + total // 16),
        cost_estimate=far_cost,
        name="far_source",
    )(part, tgt, src, moment_own, moment_pair, tiles_ij)
    far_other = swap_rank(far_send, 1)

    chunk = min(64, pairs)
    steps = 2 * pairs // chunk
    near_cost = pl.CostEstimate(flops=8 * pairs * rows * size * size, bytes_accessed=12 << 20, transcendentals=0)
    buffers = [pltpu.VMEM((steps, chunk, size, size), BF16)]
    keep, send = pl.pallas_call(
        near_second_kernel,
        in_specs=[SMEM, SMEM, SMEM, VMEM, VMEM, HBM, HBM],
        out_specs=[VMEM, VMEM],
        out_shape=[shape(total, F32), shape(total + scale_blocks(total), I16)],
        scratch_shapes=[
            scratch(cells, 2 * rows, BF16),
            scratch(total, 2 * rows),
            *buffers,
            scales(total),
            scales(total),
            pltpu.SemaphoreType.DMA((steps,)),
        ],
        compiler_params=params(16 + total // 16),
        cost_estimate=near_cost,
        name="near_second",
    )(offs, first, second, charge_own, others[0], near_tiles, other_tiles)

    coded = swap_rank(send, 2)
    half = blks // 2 * stride
    keep, send = pl.pallas_call(
        functools.partial(meet_kernel, cells),
        in_specs=[VMEM] * 4,
        out_specs=[VMEM] * 2,
        out_shape=[shape(half, F32), shape(half + scale_blocks(half), I16)],
        scratch_shapes=[scratch(half), scales(total), scales(half), scales(half)],
        compiler_params=params(8 + total // 16),
        name="meet",
    )(keep, coded, far_keep, far_other)
    coded = swap_blk(send, order[-1])

    for bit in reversed(order[:-1]):
        now, half = half, half // 2
        keep, send = pl.pallas_call(
            add_kernel,
            in_specs=[VMEM] * 2,
            out_specs=[VMEM] * 2,
            out_shape=[shape(half, F32), shape(half + scale_blocks(half), I16)],
            scratch_shapes=[scratch(half), scales(now), scales(half), scales(half)],
            compiler_params=params(8 + total // 16),
            name="add",
        )(keep, coded)
        coded = swap_blk(send, bit)

    moment_all_pair = swap_rank(owners(gathered, 0, blks, cells, stride), 1)
    target_keep, target_send = pl.pallas_call(
        functools.partial(far_target_kernel, stride, cells),
        grid_spec=pltpu.PrefetchScalarGridSpec(
            num_scalar_prefetch=3,
            grid=(fsteps,),
            in_specs=[
                whole(blks * stride),
                whole(total // 2),
                pl.BlockSpec((fchunk, terms // 2, size), lambda i, *_: (i, 0, 0)),
            ],
            out_specs=[whole(halfc), whole(halfc)],
            scratch_shapes=[
                scratch(total, 4 * rows, BF16),
                pltpu.VMEM((cells, 4 * rows, terms // 2), F32),
            ],
        ),
        out_shape=[shape(halfc, F32), shape(halfc, F32)],
        compiler_params=params(12 + total // 16),
        cost_estimate=far_cost,
        name="far_target",
    )(part, tgt, src, gathered, moment_all_pair, turned)
    target_other = swap_rank(target_send, 1)

    first_keep, first_send = pl.pallas_call(
        functools.partial(near_first_kernel, stride, cells),
        in_specs=[SMEM] * 3 + [VMEM] * (1 + len(others)) + [HBM] * 2,
        out_specs=[VMEM, VMEM],
        out_shape=[shape(cells, F32), shape(cells, F32)],
        scratch_shapes=[
            scratch(total, 2 * rows, BF16),
            scratch(cells, 2 * rows),
            *buffers,
            pltpu.SemaphoreType.DMA((steps,)),
        ],
        compiler_params=params(16 + total // 16),
        cost_estimate=near_cost,
        name="near_first",
    )(offs, first, second, gathered, *others, near_tiles, other_tiles)
    first_other = swap_rank(first_send, 2)

    return pl.pallas_call(
        final_kernel,
        in_specs=[SMEM] + [VMEM] * 9,
        out_specs=VMEM,
        out_shape=jax.ShapeDtypeStruct(charges.shape, F32),
        scratch_shapes=[scales(stride)],
        compiler_params=params(8),
        name="final",
    )(
        counts, keep, coded, first_keep, first_other, target_keep, target_other, charge_own, self_tiles, basis_t
    )


def solution(mesh):
    in_specs = (
        P("rhs", "blk"),
        P("blk"),
        P("blk", None, None),
        P("blk", None, None),
        P("blk"),
        P("blk"),
        P(("blk", "rhs"), None, None),
        P("blk"),
        P("blk"),
        P("blk", None, None),
    )
    out_specs = P("rhs", "blk")
    return jax.shard_map(body, mesh=mesh, in_specs=in_specs, out_specs=out_specs, check_vma=False)
```

time: 86.8 us -> 68.8 us (0.79)
  Pallas kernels: 51.1 us -> 26 us
  waiting for transfers between devices: 11.6 us -> 20.2 us
  other arithmetic: 3.41 us -> 1.66 us
  starting transfers between devices: 14.3 us -> 15.8 us
  local copies, waits for them, and re-layouts: 5.84 us -> 4.72 us
    pallas_call x1, Pallas kernels: 20.7 us -> 7.24 us  [body(): pl.pallas_call(far_source_kernel, grid_spec=pltpu.PrefetchScalarGridSpec(...]
    pallas_call x5, Pallas kernels: 21.8 us -> 14.1 us  [the longest x1 6.03 us: body(): pl.pallas_call(functools.partial(near_first_kernel, stride, cells), in_sp...]
    ppermute x6, waiting for transfers between devices: 8.65 us -> 13.5 us  [swap_blk(): return lax.ppermute(x, 'blk', [(i, i ^ 1 << bit) for i in range(blks)])]
    pallas_call x1, Pallas kernels: 8.06 us -> 4.11 us  [body(): pl.pallas_call(functools.partial(far_target_kernel, stride, cells), grid_...]
    ppermute x5 -> x10, waiting for transfers between devices: 2.94 us -> 6.7 us  [swap_rank(): return lax.ppermute(x, 'rhs', [(i, i ^ d) for i in range(ranks)])]
    ppermute x5 -> x10, starting transfers between devices: 4.6 us -> 6.47 us  [swap_rank(): return lax.ppermute(x, 'rhs', [(i, i ^ d) for i in range(ranks)])]
    concatenate x3, other arithmetic: 1.98 us -> 0.14 us  [body(): gathered = jnp.concatenate([gathered, swap_blk(gathered, bit)], axis=0)]
    unnamed x32 -> x18, local copies, waits for them, and re-layouts: 5.72 us -> 4.66 us
  transfers between devices with their start and end apart: 11 -> 16, of which waited for: 3 -> 8; matrix products, arithmetic and copies ran while one was open for 4% -> 3% of each run, Pallas kernels for 57% -> 35%
where the time goes in v2:
time: 68.8 us; the launch traced here: 68.5 us
  Pallas kernels  26 us (38%)
  waiting for transfers between devices  20.2 us (29%)
  starting transfers between devices  15.8 us (23%)
  local copies, waits for them, and re-layouts  4.72 us (7%)
  other arithmetic  1.66 us (2%)
    ppermute x6, waiting for transfers between devices, swap_blk(): return lax.ppermute(x, 'blk', [(i, i ^ 1 << bit) for i in range(blks)])  13.5 us
    ppermute x6, starting transfers between devices, swap_blk(): return lax.ppermute(x, 'blk', [(i, i ^ 1 << bit) for i in range(blks)])  9.37 us
    pallas_call x1, Pallas kernels, body(): pl.pallas_call(far_source_kernel, grid_spec=pltpu.PrefetchScalarGridSpec(...  7.24 us
    ppermute x10, waiting for transfers between devices, swap_rank(): return lax.ppermute(x, 'rhs', [(i, i ^ d) for i in range(ranks)])  6.7 us
    ppermute x10, starting transfers between devices, swap_rank(): return lax.ppermute(x, 'rhs', [(i, i ^ d) for i in range(ranks)])  6.47 us
    pallas_call x1, Pallas kernels, body(): pl.pallas_call(functools.partial(near_first_kernel, stride, cells), in_sp...  6.03 us
    pallas_call x1, Pallas kernels, body(): pl.pallas_call(near_second_kernel, in_specs=[SMEM, SMEM, SMEM, VMEM, VMEM...  4.81 us
    unnamed x18, local copies, waits for them, and re-layouts  4.66 us
  transfers between devices with their start and end apart: 16, of which 8 were waited for; matrix products, arithmetic and copies ran while one was open for 3% of the time, Pallas kernels for 35%

profile of v2, /device:TPU:0, one launch (start us, length us, event | category | flops | bytes accessed | tf_op | source)
XLA Modules:
  0.0 68.5 jit_solution(14662445947074125856)
XLA Ops:
  0.0 0.5 collective-permute-start.1
  0.5 0.9 %copy-done.3 = bf16[16,128,64]{1,2,0:T(8,128)(2,1)S(1)} copy-done((bf16[16,128,64]{1,2,0:T(8,128)(2,1)S(1)}, bf16[16,128,64]{1,2,0:T(8,128)(2,1)}, u32[]{:S(2)}) %copy-start.3) | copy-done | bytes 262168
  1.4 0.8 %copy-done.6 = bf16[16,2048]{1,0:T(8,128)(2,1)S(1)} copy-done((bf16[16,2048]{1,0:T(8,128)(2,1)S(1)}, bf16[16,2048]{1,0:T(8,128)(2,1)}, u32[]{:S(2)}) %copy-start.6) | copy-done | bytes 65560
  2.2 0.7 copy-done.7
  2.9 0.9 %prep.1 = bf16[24,16,128]{2,1,0:T(8,128)(2,1)S(1)} custom-call(s32[16]{0:T(128)S(1)} %copy-done.7, bf16[16,2048]{1,0:T(8,128)(2,1)S(1)} %copy-done.6, bf16[16,64,128]{2,1,0:T(8,128)(2,1)S(1)} %bitcast.15), custom_call_target="tpu_custom_call" | custom-call | tf_op jit(solution)/shard_map/prep/pallas_call | solution.py:361
  3.8 3.7 %collective-permute-start.8 = (bf16[24,16,128]{2,1,0:T(8,128)(2,1)S(1)}, bf16[24,16,128]{2,1,0:T(8,128)(2,1)S(1)}, u32[]{:S(2)}, u32[]{:S(2)}) collective-permute-start(bf16[24,16,128]{2,1,0:T(8,128)(2,1)S(1)} %prep.1), channel_id=1, source_target_pairs={{0,16},{4,20},{8,24},{12,28},{16,0},{20,4},{24,8},{28,12},{1,17},{... | collective-permute-start | bytes 294920 | tf_op jit(solution)/shard_map/ppermute | solution.py:336
  7.5 1.5 %collective-permute-start = (bf16[16,16,128]{2,1,0:T(8,128)(2,1)S(1)}, bf16[16,16,128]{2,1,0:T(8,128)(2,1)S(1)}, u32[]{:S(2)}, u32[]{:S(2)}) collective-permute-start(bf16[16,16,128]{2,1,0:T(8,128)(2,1)S(1)} %slice.20.mine.moved), channel_id=1, source_target_pairs={{0,2},{1,3},{2,0},{3,1},{4,6},{5,7},{6,4},{7,5},{8,10},{9,11},{10,... | collective-permute-start | bytes 196616 | tf_op jit(solution)/shard_map/ppermute | solution.py:333
  9.0 0.0 collective-permute-start.3
  9.0 0.7 %add_select_fusion.5 = (s32[512]{0:T(512)S(1)}, s32[512]{0:T(512)S(1)}) fusion(s32[512]{0:T(512)} %param.14, s32[]{:T(128)S(6)} %axis_index.25, s32[512]{0:T(512)} %param.15), kind=kLoop, calls=%fused_computation.16 | loop fusion | flops 22528 | bytes 8196 | tf_op jit(solution)/shard_map/jit(remainder)/select_n | solution.py:388
  9.7 0.7 %add_select_fusion.2 = (s32[512]{0:T(512)S(1)}, s32[512]{0:T(512)S(1)}) fusion(s32[512]{0:T(512)} %param.18, s32[]{:T(128)S(6)} %axis_index.25, s32[512]{0:T(512)} %param.17), kind=kLoop, calls=%fused_computation.8 | loop fusion | flops 22528 | bytes 8196 | tf_op jit(solution)/shard_map/jit(remainder)/select_n | solution.py:390
  10.4 0.1 pad_add_fusion.offs
  10.5 1.3 %collective-permute-done.theirs.refs_0_ = bf16[16,16,128]{2,1,0:T(8,128)(2,1)S(1)} collective-permute-done((bf16[16,16,128]{2,1,0:T(8,128)(2,1)S(1)}, bf16[16,16,128]{2,1,0:T(8,128)(2,1)S(1)}, u32[]{:S(2)}, u32[]{:S(2)}) %collective-permute-start) | collective-permute-done | bytes 65568 | tf_op jit(solution)/shard_map/ppermute | solution.py:333
  11.7 0.0 collective-permute-done.1.other.refs_4_
  11.7 2.2 %copy-done = bf16[128,128,128]{2,1,0:T(8,128)(2,1)S(1)} copy-done((bf16[128,128,128]{2,1,0:T(8,128)(2,1)S(1)}, bf16[128,128,128]{2,1,0:T(8,128)(2,1)}, u32[]{:S(2)}) %copy-start) | copy-done | bytes 4194328
  13.9 4.8 %near_second.1 = (f32[128,16,128]{2,1,0:T(8,128)S(1)}, s16[136,16,128]{2,1,0:T(8,128)(2,1)S(1)}) custom-call(s32[2]{0:T(128)S(1)} %pad_add_fusion.offs, s32[512]{0:T(512)S(1)} %get-tuple-element.35.first, s32[512]{0:T(512)S(1)} %get-tuple-element.36.second, bf16[16,16,128]{2,1,0:T(8,128)(2,1)S(1)} %slice.20.mine.moved, ...), custom_call_target="tpu_custom_call" | custom-call | flops 268435456 | bytes 12582912 | tf_op jit(solution)/shard_map/near_second/pallas_call | solution.py:431
  18.7 1.6 %collective-permute-start.2 = (s16[136,16,128]{2,1,0:T(8,128)(2,1)S(1)}, s16[136,16,128]{2,1,0:T(8,128)(2,1)S(1)}, u32[]{:S(2)}, u32[]{:S(2)}) collective-permute-start(s16[136,16,128]{2,1,0:T(8,128)(2,1)S(1)} %get-tuple-element.21), channel_id=1, source_target_pairs={{0,2},{1,3},{2,0},{3,1},{4,6},{5,7},{6,4},{7,5},{8,10},{9,11},{10,... | collective-permute-start | bytes 1671176 | tf_op jit(solution)/shard_map/ppermute | solution.py:333
  20.3 0.0 collective-permute-done.8
  20.3 1.6 %collective-permute-start.9 = (bf16[48,16,128]{2,1,0:T(8,128)(2,1)S(1)}, bf16[48,16,128]{2,1,0:T(8,128)(2,1)S(1)}, u32[]{:S(2)}, u32[]{:S(2)}) collective-permute-start(bf16[48,16,128]{2,1,0:T(8,128)(2,1)S(1)} %pad_maximum_fusion.2), channel_id=1, source_target_pairs={{0,8},{4,12},{8,0},{12,4},{16,24},{20,28},{24,16},{28,20},{1,9},{5... | collective-permute-start | bytes 589832 | tf_op jit(solution)/shard_map/ppermute | solution.py:336
  22.0 0.0 collective-permute-done.3.theirs
  22.0 7.2 %far_source.1 = (bf16[256,32,128]{2,1,0:T(8,128)(2,1)S(1)}, f32[64,16,128]{2,1,0:T(8,128)S(1)}, f32[64,16,128]{2,1,0:T(8,128)S(1)}) custom-call(s32[1]{0:T(128)} %bitcast.3.offs, s32[512]{0:T(512)S(1)} %get-tuple-element.37.tgt, s32[512]{0:T(512)S(1)} %get-tuple-element.38.pos, bf16[8,16,128]{2,1,0:T(8,128)(2,1)S(1)} %slice.21.mine, ...), custom_call_target="tpu_custom_call" | custom-call | flops 67108864 | bytes 6291456 | tf_op jit(solution)/shard_map/far_source/pallas_call | solution.py:399
  29.2 0.0 copy-start.1
  29.2 0.1 collective-permute-start.4
  29.4 1.6 %collective-permute-start.10 = (bf16[96,16,128]{2,1,0:T(8,128)(2,1)S(1)}, bf16[96,16,128]{2,1,0:T(8,128)(2,1)S(1)}, u32[]{:S(2)}, u32[]{:S(2)}) collective-permute-start(bf16[96,16,128]{2,1,0:T(8,128)(2,1)S(1)} %pad_maximum_fusion.1), channel_id=1, source_target_pairs={{0,4},{4,0},{8,12},{12,8},{16,20},{20,16},{24,28},{28,24},{1,5},{5... | collective-permute-start | bytes 1179656 | tf_op jit(solution)/shard_map/ppermute | solution.py:336
  30.9 0.3 collective-permute-done.4.far_other
  31.2 1.5 %collective-permute-done.2.coded = s16[136,16,128]{2,1,0:T(8,128)(2,1)S(1)} collective-permute-done((s16[136,16,128]{2,1,0:T(8,128)(2,1)S(1)}, s16[136,16,128]{2,1,0:T(8,128)(2,1)S(1)}, u32[]{:S(2)}, u32[]{:S(2)}) %collective-permute-start.2) | collective-permute-done | bytes 557088 | tf_op jit(solution)/shard_map/ppermute | solution.py:333
  32.7 0.6 meet.1
  33.3 1.6 %collective-permute-start.5 = (s16[102,16,128]{2,1,0:T(8,128)(2,1)S(1)}, s16[102,16,128]{2,1,0:T(8,128)(2,1)S(1)}, u32[]{:S(2)}, u32[]{:S(2)}) collective-permute-start(s16[102,16,128]{2,1,0:T(8,128)(2,1)S(1)} %get-tuple-element.25), channel_id=1, source_target_pairs={{0,4},{4,0},{8,12},{12,8},{16,20},{20,16},{24,28},{28,24},{1,5},{5... | collective-permute-start | bytes 1253384 | tf_op jit(solution)/shard_map/ppermute | solution.py:336
  34.9 6.4 %collective-permute-done.10 = bf16[96,16,128]{2,1,0:T(8,128)(2,1)S(1)} collective-permute-done((bf16[96,16,128]{2,1,0:T(8,128)(2,1)S(1)}, bf16[96,16,128]{2,1,0:T(8,128)(2,1)S(1)}, u32[]{:S(2)}, u32[]{:S(2)}) %collective-permute-start.10) | collective-permute-done | bytes 393248 | tf_op jit(solution)/shard_map/ppermute | solution.py:336
  41.3 0.1 pad_maximum_fusion.everyone
  41.4 0.6 collective-permute-start.12
  42.1 1.6 %collective-permute-start.11 = (bf16[48,16,128]{2,1,0:T(8,128)(2,1)S(1)}, bf16[48,16,128]{2,1,0:T(8,128)(2,1)S(1)}, u32[]{:S(2)}, u32[]{:S(2)}) collective-permute-start(bf16[48,16,128]{2,1,0:T(8,128)(2,1)S(1)} %bitcast.20), channel_id=1, source_target_pairs={{0,2},{1,3},{2,0},{3,1},{4,6},{5,7},{6,4},{7,5},{8,10},{9,11},{10,... | collective-permute-start | bytes 589832 | tf_op jit(solution)/shard_map/ppermute | solution.py:333
  43.6 0.1 collective-permute-start.14
  43.7 6.2 %collective-permute-done.5.coded = s16[102,16,128]{2,1,0:T(8,128)(2,1)S(1)} collective-permute-done((s16[102,16,128]{2,1,0:T(8,128)(2,1)S(1)}, s16[102,16,128]{2,1,0:T(8,128)(2,1)S(1)}, u32[]{:S(2)}, u32[]{:S(2)}) %collective-permute-start.5) | collective-permute-done | bytes 417824 | tf_op jit(solution)/shard_map/ppermute | solution.py:336
  49.9 0.4 add.66
  50.2 0.0 copy-start.4
  50.3 0.0 copy-start.5
  50.3 0.0 copy-start.8
  50.3 0.5 collective-permute-start.6
  50.8 2.4 %collective-permute-done.11.refs_1_ = bf16[48,16,128]{2,1,0:T(8,128)(2,1)S(1)} collective-permute-done((bf16[48,16,128]{2,1,0:T(8,128)(2,1)S(1)}, bf16[48,16,128]{2,1,0:T(8,128)(2,1)S(1)}, u32[]{:S(2)}, u32[]{:S(2)}) %collective-permute-start.11) | collective-permute-done | bytes 196640 | tf_op jit(solution)/shard_map/ppermute | solution.py:333
  53.2 6.0 %near_first.1 = (f32[16,16,128]{2,1,0:T(8,128)S(1)}, f32[16,16,128]{2,1,0:T(8,128)S(1)}) custom-call(s32[2]{0:T(128)S(1)} %pad_add_fusion.offs, s32[512]{0:T(512)S(1)} %get-tuple-element.35.first, s32[512]{0:T(512)S(1)} %get-tuple-element.36.second, bf16[192,16,128]{2,1,0:T(8,128)(2,1)S(1)} %pad_maximum_fusion.everyone, ...), custom_call_target="tpu_custom_call" | custom-call | flops 268435456 | bytes 12582912 | tf_op jit(solution)/shard_map/near_first/pallas_call | solution.py:499
  59.3 0.6 collective-permute-start.13
  59.9 0.2 add.67
  60.1 0.4 collective-permute-start.7
  60.5 4.1 %far_target.1 = (f32[8,16,128]{2,1,0:T(8,128)S(1)}, f32[8,16,128]{2,1,0:T(8,128)S(1)}) custom-call(s32[1]{0:T(128)} %bitcast.3.offs, s32[512]{0:T(512)S(1)} %get-tuple-element.37.tgt, s32[512]{0:T(512)S(1)} %get-tuple-element.38.pos, bf16[192,16,128]{2,1,0:T(8,128)(2,1)S(1)} %pad_maximum_fusion.everyone, ...), custom_call_target="tpu_custom_call" | custom-call | flops 67108864 | bytes 6291456 | tf_op jit(solution)/shard_map/far_target/pallas_call | solution.py:476
  64.6 0.1 collective-permute-start.15
  64.7 1.2 %collective-permute-done.15.target_other = f32[8,16,128]{2,1,0:T(8,128)S(1)} collective-permute-done((f32[8,16,128]{2,1,0:T(8,128)S(1)}, f32[8,16,128]{2,1,0:T(8,128)S(1)}, u32[]{:S(2)}, u32[]{:S(2)}) %collective-permute-start.15) | collective-permute-done | bytes 65568 | tf_op jit(solution)/shard_map/ppermute | solution.py:333
  65.9 0.9 %collective-permute-done.7.coded = s16[26,16,128]{2,1,0:T(8,128)(2,1)S(1)} collective-permute-done((s16[26,16,128]{2,1,0:T(8,128)(2,1)S(1)}, s16[26,16,128]{2,1,0:T(8,128)(2,1)S(1)}, u32[]{:S(2)}, u32[]{:S(2)}) %collective-permute-start.7) | collective-permute-done | bytes 106528 | tf_op jit(solution)/shard_map/ppermute | solution.py:336
  66.8 1.8 %final.1 = f32[16,2048]{1,0:T(8,128)} custom-call(s32[16]{0:T(128)S(1)} %copy-done.8, f32[24,16,128]{2,1,0:T(8,128)S(1)} %get-tuple-element.28.mine, s16[26,16,128]{2,1,0:T(8,128)(2,1)S(1)} %collective-permute-done.7.coded, f32[16,16,128]{2,1,0:T(8,128)S(1)} %get-tuple-element.30.first, f32[16,16,128]{2,1,0:T(8,128)S(1)} %collective-permute-done.13.first_other, ...), custom_call_target="tpu_custom_call" | custom-call | tf_op jit(solution)/shard_map/final/pallas_call | solution.py:516
  (22 shorter events, 0.2 us)
Async XLA Ops:
  0.0 11.7 %collective-permute-start.1 = (bf16[128,128,128]{2,1,0:T(8,128)(2,1)}, bf16[128,128,128]{2,1,0:T(8,128)(2,1)}, u32[]{:S(2)}, u32[]{:S(2)}) collective-permute-start(bf16[128,128,128]{2,1,0:T(8,128)(2,1)} %refs_3_.1), channel_id=1, source_target_pairs={{0,1},{1,0},{2,3},{3,2},{4,5},{5,4},{6,7},{7,6},{8,9},{9,8},{10,11... | collective-permute-start | bytes 12582920 | tf_op jit(solution)/shard_map/ppermute | solution.py:333
  0.5 0.9 %copy-start.3 = (bf16[16,128,64]{1,2,0:T(8,128)(2,1)S(1)}, bf16[16,128,64]{1,2,0:T(8,128)(2,1)}, u32[]{:S(2)}) copy-start(bf16[16,128,64]{1,2,0:T(8,128)(2,1)} %param.13) | copy-start | bytes 786436
  1.4 0.8 %copy-start.6 = (bf16[16,2048]{1,0:T(8,128)(2,1)S(1)}, bf16[16,2048]{1,0:T(8,128)(2,1)}, u32[]{:S(2)}) copy-start(bf16[16,2048]{1,0:T(8,128)(2,1)} %charges_in.1) | copy-start | bytes 196612
  2.2 0.7 copy-start.7
  3.8 16.5 %collective-permute-start.8 = (bf16[24,16,128]{2,1,0:T(8,128)(2,1)S(1)}, bf16[24,16,128]{2,1,0:T(8,128)(2,1)S(1)}, u32[]{:S(2)}, u32[]{:S(2)}) collective-permute-start(bf16[24,16,128]{2,1,0:T(8,128)(2,1)S(1)} %prep.1), channel_id=1, source_target_pairs={{0,16},{4,20},{8,24},{12,28},{16,0},{20,4},{24,8},{28,12},{1,17},{... | collective-permute-start | bytes 294920 | tf_op jit(solution)/shard_map/ppermute | solution.py:336
  7.5 4.3 %collective-permute-start = (bf16[16,16,128]{2,1,0:T(8,128)(2,1)S(1)}, bf16[16,16,128]{2,1,0:T(8,128)(2,1)S(1)}, u32[]{:S(2)}, u32[]{:S(2)}) collective-permute-start(bf16[16,16,128]{2,1,0:T(8,128)(2,1)S(1)} %slice.20.mine.moved), channel_id=1, source_target_pairs={{0,2},{1,3},{2,0},{3,1},{4,6},{5,7},{6,4},{7,5},{8,10},{9,11},{10,... | collective-permute-start | bytes 196616 | tf_op jit(solution)/shard_map/ppermute | solution.py:333
  9.0 13.0 %collective-permute-start.3 = (bf16[8,16,128]{2,1,0:T(8,128)(2,1)S(1)}, bf16[8,16,128]{2,1,0:T(8,128)(2,1)S(1)}, u32[]{:S(2)}, u32[]{:S(2)}) collective-permute-start(bf16[8,16,128]{2,1,0:T(8,128)(2,1)S(1)} %slice.21.mine), channel_id=1, source_target_pairs={{0,1},{1,0},{2,3},{3,2},{4,5},{5,4},{6,7},{7,6},{8,9},{9,8},{10,11... | collective-permute-start | bytes 98312 | tf_op jit(solution)/shard_map/ppermute | solution.py:333
  11.7 2.2 %copy-start = (bf16[128,128,128]{2,1,0:T(8,128)(2,1)S(1)}, bf16[128,128,128]{2,1,0:T(8,128)(2,1)}, u32[]{:S(2)}) copy-start(bf16[128,128,128]{2,1,0:T(8,128)(2,1)} %refs_3_.1) | copy-start | bytes 12582916
  13.9 8.0 %copy-start.2 = (bf16[512,64,64]{0,2,1:T(8,128)(2,1)S(1)}, bf16[512,64,64]{0,2,1:T(8,128)(2,1)}, u32[]{:S(2)}) copy-start(bf16[512,64,64]{0,2,1:T(8,128)(2,1)} %param.19) | copy-start | bytes 12582916
  18.7 14.0 %collective-permute-start.2 = (s16[136,16,128]{2,1,0:T(8,128)(2,1)S(1)}, s16[136,16,128]{2,1,0:T(8,128)(2,1)S(1)}, u32[]{:S(2)}, u32[]{:S(2)}) collective-permute-start(s16[136,16,128]{2,1,0:T(8,128)(2,1)S(1)} %get-tuple-element.21), channel_id=1, source_target_pairs={{0,2},{1,3},{2,0},{3,1},{4,6},{5,7},{6,4},{7,5},{8,10},{9,11},{10,... | collective-permute-start | bytes 1671176 | tf_op jit(solution)/shard_map/ppermute | solution.py:333
  20.3 9.0 %collective-permute-start.9 = (bf16[48,16,128]{2,1,0:T(8,128)(2,1)S(1)}, bf16[48,16,128]{2,1,0:T(8,128)(2,1)S(1)}, u32[]{:S(2)}, u32[]{:S(2)}) collective-permute-start(bf16[48,16,128]{2,1,0:T(8,128)(2,1)S(1)} %pad_maximum_fusion.2), channel_id=1, source_target_pairs={{0,8},{4,12},{8,0},{12,4},{16,24},{20,28},{24,16},{28,20},{1,9},{5... | collective-permute-start | bytes 589832 | tf_op jit(solution)/shard_map/ppermute | solution.py:336
  29.2 24.0 %copy-start.1 = (bf16[128,128,128]{2,1,0:T(8,128)(2,1)S(1)}, bf16[128,128,128]{2,1,0:T(8,128)(2,1)}, u32[]{:S(2)}) copy-start(bf16[128,128,128]{2,1,0:T(8,128)(2,1)} %refs_3_.1) | copy-start | bytes 12582916
  29.2 2.0 %collective-permute-start.4 = (f32[64,16,128]{2,1,0:T(8,128)S(1)}, f32[64,16,128]{2,1,0:T(8,128)S(1)}, u32[]{:S(2)}, u32[]{:S(2)}) collective-permute-start(f32[64,16,128]{2,1,0:T(8,128)S(1)} %get-tuple-element.23), channel_id=1, source_target_pairs={{0,1},{1,0},{2,3},{3,2},{4,5},{5,4},{6,7},{7,6},{8,9},{9,8},{10,11... | collective-permute-start | bytes 1572872 | tf_op jit(solution)/shard_map/ppermute | solution.py:333
  29.4 12.0 %collective-permute-start.10 = (bf16[96,16,128]{2,1,0:T(8,128)(2,1)S(1)}, bf16[96,16,128]{2,1,0:T(8,128)(2,1)S(1)}, u32[]{:S(2)}, u32[]{:S(2)}) collective-permute-start(bf16[96,16,128]{2,1,0:T(8,128)(2,1)S(1)} %pad_maximum_fusion.1), channel_id=1, source_target_pairs={{0,4},{4,0},{8,12},{12,8},{16,20},{20,16},{24,28},{28,24},{1,5},{5... | collective-permute-start | bytes 1179656 | tf_op jit(solution)/shard_map/ppermute | solution.py:336
  33.3 16.6 %collective-permute-start.5 = (s16[102,16,128]{2,1,0:T(8,128)(2,1)S(1)}, s16[102,16,128]{2,1,0:T(8,128)(2,1)S(1)}, u32[]{:S(2)}, u32[]{:S(2)}) collective-permute-start(s16[102,16,128]{2,1,0:T(8,128)(2,1)S(1)} %get-tuple-element.25), channel_id=1, source_target_pairs={{0,4},{4,0},{8,12},{12,8},{16,20},{20,16},{24,28},{28,24},{1,5},{5... | collective-permute-start | bytes 1253384 | tf_op jit(solution)/shard_map/ppermute | solution.py:336
  41.4 11.8 %collective-permute-start.12 = (bf16[64,16,128]{2,1,0:T(8,128)(2,1)S(1)}, bf16[64,16,128]{2,1,0:T(8,128)(2,1)S(1)}, u32[]{:S(2)}, u32[]{:S(2)}) collective-permute-start(bf16[64,16,128]{2,1,0:T(8,128)(2,1)S(1)} %bitcast.19), channel_id=1, source_target_pairs={{0,2},{1,3},{2,0},{3,1},{4,6},{5,7},{6,4},{7,5},{8,10},{9,11},{10,... | collective-permute-start | bytes 786440 | tf_op jit(solution)/shard_map/ppermute | solution.py:333
  42.1 11.2 %collective-permute-start.11 = (bf16[48,16,128]{2,1,0:T(8,128)(2,1)S(1)}, bf16[48,16,128]{2,1,0:T(8,128)(2,1)S(1)}, u32[]{:S(2)}, u32[]{:S(2)}) collective-permute-start(bf16[48,16,128]{2,1,0:T(8,128)(2,1)S(1)} %bitcast.20), channel_id=1, source_target_pairs={{0,2},{1,3},{2,0},{3,1},{4,6},{5,7},{6,4},{7,5},{8,10},{9,11},{10,... | collective-permute-start | bytes 589832 | tf_op jit(solution)/shard_map/ppermute | solution.py:333
  43.6 16.8 %collective-permute-start.14 = (bf16[64,16,128]{2,1,0:T(8,128)(2,1)S(1)}, bf16[64,16,128]{2,1,0:T(8,128)(2,1)S(1)}, u32[]{:S(2)}, u32[]{:S(2)}) collective-permute-start(bf16[64,16,128]{2,1,0:T(8,128)(2,1)S(1)} %bitcast.18), channel_id=1, source_target_pairs={{0,1},{1,0},{2,3},{3,2},{4,5},{5,4},{6,7},{7,6},{8,9},{9,8},{10,11... | collective-permute-start | bytes 786440 | tf_op jit(solution)/shard_map/ppermute | solution.py:333
  50.2 16.5 %copy-start.4 = (bf16[16,128,64]{1,2,0:T(8,128)(2,1)S(1)}, bf16[16,128,64]{1,2,0:T(8,128)(2,1)}, u32[]{:S(2)}) copy-start(bf16[16,128,64]{1,2,0:T(8,128)(2,1)} %param.13) | copy-start | bytes 786436
  50.3 16.5 %copy-start.5 = (bf16[16,128,128]{2,1,0:T(8,128)(2,1)S(1)}, bf16[16,128,128]{2,1,0:T(8,128)(2,1)}, u32[]{:S(2)}) copy-start(bf16[16,128,128]{2,1,0:T(8,128)(2,1)} %self_tiles.1) | copy-start | bytes 1572868
  50.3 16.5 %copy-start.8 = (s32[16]{0:T(128)S(1)}, s32[16]{0:T(128)}, u32[]{:S(2)}) copy-start(s32[16]{0:T(128)} %counts.1) | copy-start | bytes 196
  50.3 9.6 %collective-permute-start.6 = (s16[51,16,128]{2,1,0:T(8,128)(2,1)S(1)}, s16[51,16,128]{2,1,0:T(8,128)(2,1)S(1)}, u32[]{:S(2)}, u32[]{:S(2)}) collective-permute-start(s16[51,16,128]{2,1,0:T(8,128)(2,1)S(1)} %get-tuple-element.27), channel_id=1, source_target_pairs={{0,8},{4,12},{8,0},{12,4},{16,24},{20,28},{24,16},{28,20},{1,9},{5... | collective-permute-start | bytes 626696 | tf_op jit(solution)/shard_map/ppermute | solution.py:336
  59.3 6.6 %collective-permute-start.13 = (f32[16,16,128]{2,1,0:T(8,128)S(1)}, f32[16,16,128]{2,1,0:T(8,128)S(1)}, u32[]{:S(2)}, u32[]{:S(2)}) collective-permute-start(f32[16,16,128]{2,1,0:T(8,128)S(1)} %get-tuple-element.31), channel_id=1, source_target_pairs={{0,2},{1,3},{2,0},{3,1},{4,6},{5,7},{6,4},{7,5},{8,10},{9,11},{10,... | collective-permute-start | bytes 393224 | tf_op jit(solution)/shard_map/ppermute | solution.py:333
  60.1 6.7 %collective-permute-start.7 = (s16[26,16,128]{2,1,0:T(8,128)(2,1)S(1)}, s16[26,16,128]{2,1,0:T(8,128)(2,1)S(1)}, u32[]{:S(2)}, u32[]{:S(2)}) collective-permute-start(s16[26,16,128]{2,1,0:T(8,128)(2,1)S(1)} %get-tuple-element.29), channel_id=1, source_target_pairs={{0,16},{4,20},{8,24},{12,28},{16,0},{20,4},{24,8},{28,12},{1,17},{... | collective-permute-start | bytes 319496 | tf_op jit(solution)/shard_map/ppermute | solution.py:336
  64.6 1.3 %collective-permute-start.15 = (f32[8,16,128]{2,1,0:T(8,128)S(1)}, f32[8,16,128]{2,1,0:T(8,128)S(1)}, u32[]{:S(2)}, u32[]{:S(2)}) collective-permute-start(f32[8,16,128]{2,1,0:T(8,128)S(1)} %get-tuple-element.34), channel_id=1, source_target_pairs={{0,1},{1,0},{2,3},{3,2},{4,5},{5,4},{6,7},{7,6},{8,9},{9,8},{10,11... | collective-permute-start | bytes 196616 | tf_op jit(solution)/shard_map/ppermute | solution.py:333

commit v3 on v0

v3 whole, which is shorter than its diff:
```python
import functools

import jax
import jax.numpy as jnp
from jax import lax
from jax.experimental import pallas as pl
from jax.experimental.pallas import tpu as pltpu
from jax.sharding import PartitionSpec as P

F32, BF16, I16, I32 = jnp.float32, jnp.bfloat16, jnp.int16, jnp.int32
REACH = 48
GROUP = 16
TOP = 32767.0
VMEM = pl.BlockSpec(memory_space=pltpu.VMEM)
SMEM = pl.BlockSpec(memory_space=pltpu.SMEM)
HBM = pl.BlockSpec(memory_space=pltpu.HBM)
NAT = (((1,), (0,)), ((), ()))
TRN = (((1,), (1,)), ((), ()))


def params(mib):
    return pltpu.CompilerParams(vmem_limit_bytes=mib << 20)


def in_hbm(x):
    return pltpu.with_memory_space_constraint(x, pltpu.HBM)


def dot(lhs, rhs, dims):
    return lax.dot_general(lhs, rhs, dims, preferred_element_type=F32)


def scale_blocks(count):
    return -(-count // GROUP)


def encode(get, out, outer, inner, peak, inv):
    count = outer * inner
    peak[...] = jnp.zeros_like(peak)

    def find(o, _):
        for i in range(inner):
            peak[pl.ds(o * inner + i, 1), :] = jnp.max(jnp.abs(get(o, i)), axis=0, keepdims=True)
        return 0

    lax.fori_loop(0, outer, find, 0)
    code = jnp.ceil(jnp.log2(jnp.maximum(peak[...], 1e-30)) * 8.0) + 1.0
    inv[...] = TOP * jnp.exp2(code * -0.125)
    for s in range(scale_blocks(count)):
        out[count + s] = code[s * GROUP : (s + 1) * GROUP].astype(I32).astype(I16)

    def put(o, _):
        for i in range(inner):
            b = o * inner + i
            out[b] = jnp.round(get(o, i) * inv[pl.ds(b, 1), :]).astype(I32).astype(I16)
        return 0

    lax.fori_loop(0, outer, put, 0)


def decode_scales(coded, count, scale):
    for s in range(scale_blocks(count)):
        code = coded[count + s].astype(I32).astype(F32)
        scale[s * GROUP : (s + 1) * GROUP, :] = jnp.exp2(code * 0.125) * (1.0 / TOP)


def decode(coded, scale, b):
    return coded[b].astype(I32).astype(F32) * scale[pl.ds(b, 1), :]


def prep_kernel(
    place, low, counts_in, charges_in, basis_in, near_first, near_second, far_source, far_target,
    out, idx, counts, charges, basis_t, lists, counts_row, sems,
):
    pairs = [(counts_in.at[0], counts), (charges_in, charges), (basis_in, basis_t), (counts_in, counts_row)]
    pairs += [
        (src, lists.at[pl.ds(i, 1)]) for i, src in enumerate((near_first, near_second, far_source, far_target))
    ]
    copies = [pltpu.make_async_copy(src, dst, sems.at[i]) for i, (src, dst) in enumerate(pairs)]
    for copy in copies:
        copy.start()
    for copy in copies:
        copy.wait()
    cells, terms, size = basis_t.shape
    rows = charges.shape[0]
    lane = lax.broadcasted_iota(I32, (rows, size), 1)
    moments = []
    for c in range(cells):
        x = charges[:, c * size : (c + 1) * size]
        x = jnp.where(lane < counts[c], x, jnp.zeros_like(x))
        out[c] = x
        moments.append(dot(x, basis_t[c], TRN))
    for k in range(cells // 2):
        out[cells + k] = jnp.concatenate(moments[2 * k : 2 * k + 2], axis=1).astype(BF16)
    first, second, source, target = (lists[i : i + 1, :] for i in range(4))
    reduce_at = place(second, 1)
    for row, value in (
        (FIRST, lax.rem(first, cells)),
        (SECOND, place(second, 0)),
        (SECOND_REDUCE, jnp.where(reduce_at < cells, reduce_at, reduce_at - (low - 1) * cells)),
        (SOURCE, place(source, 0)),
        (SOURCE_REDUCE, place(source, 1)),
        (TARGET, lax.rem(target, cells)),
    ):
        idx[row : row + 1, :] = value
    idx[COUNT : COUNT + 1, :cells] = counts_row[...]


FIRST, SECOND, SECOND_REDUCE, SOURCE, SOURCE_REDUCE, TARGET, COUNT = range(7)
PITCH = 136
FAR_UNROLL = 64
FAR_STEPS = 2
NEAR_UNROLL = 64
PARTS = 4


def far_source_kernel(idx, mine, theirs, tiles, turned, keep, *refs):
    *sends, flip, lhs, acc = refs
    rows, lanes = mine.shape[1:]
    half = lanes // 2
    pairs = half // 2
    total = turned.shape[0]
    chunk = total // FAR_STEPS
    acc[...] = jnp.zeros_like(acc)
    for k in range(mine.shape[0]):
        x, y = mine[k], theirs[k]
        for h in range(2):
            at = h * half
            lhs[2 * k + h] = jnp.concatenate([x[:, at : at + half], y[:, at : at + half]], axis=0)
    for step in range(FAR_STEPS):
        base = (lax.axis_index("rhs") & 1) * total + step * chunk
        span = pl.ds(pl.multiple_of(base, chunk), chunk)
        for i in range(pairs):
            both = [tiles[(i + h * pairs) * half : (i + h * pairs + 1) * half, span] for h in range(2)]
            flip[step, i * PITCH : i * PITCH + chunk, :] = jnp.concatenate(both, axis=0).astype(F32).T

        def work(g, _, step=step, base=base):
            sums = []
            at = g * FAR_UNROLL
            for u in range(FAR_UNROLL):
                w = flip[step, pl.ds(at + u, pairs, stride=PITCH), :]
                turned[step * chunk + at + u] = w.astype(BF16)
                moved = pltpu.roll(w, half, 1)
                w = jnp.concatenate([w[:, :half], moved[:, :half]], axis=0).astype(BF16)
                sums.append(dot(lhs[idx[TARGET, base + at + u]], w, NAT))
            for u in range(FAR_UNROLL):
                acc[idx[SOURCE_REDUCE, base + at + u]] += sums[u]
            return 0

        lax.fori_loop(0, chunk // FAR_UNROLL, work, 0)
    count = sends[0].shape[0]
    for q, send in enumerate(sends):

        def fold(k, _, q=q, send=send):
            for u in range(4):
                at = q * count + 4 * k + u
                both = jnp.concatenate([acc[2 * at], acc[2 * at + 1]], axis=1)
                keep[at] = both[:rows]
                send[4 * k + u] = both[rows:]
            return 0

        lax.fori_loop(0, count // 4, fold, 0)


def far_target_kernel(stride, cells, idx, everyone, theirs, turned, keep, send, lhs, acc):
    rows, lanes = everyone.shape[1], everyone.shape[2]
    half = lanes // 2
    chunk = turned.shape[0]
    owners = everyone.shape[0] // stride
    acc[...] = jnp.zeros_like(acc)
    low = lax.broadcasted_iota(I32, (2 * rows, lanes), 1) < half

    def spread(o, _):
        for k in range(cells // 2):
            x = jnp.concatenate([everyone[o * stride + cells + k], theirs[o * (cells // 2) + k]], axis=0)
            y = jnp.concatenate([x[:, half:], x[:, :half]], axis=1)
            zero = jnp.zeros_like(x)
            at = o * cells + 2 * k
            lhs[at] = jnp.concatenate([jnp.where(low, x, zero), jnp.where(low, zero, y)], axis=0)
            lhs[at + 1] = jnp.concatenate([jnp.where(low, y, zero), jnp.where(low, zero, x)], axis=0)
        return 0

    lax.fori_loop(0, owners, spread, 0)
    base = (lax.axis_index("rhs") & 1) * chunk

    def work(g, _):
        sums = []
        for u in range(FAR_UNROLL):
            e = g * FAR_UNROLL + u
            sums.append(dot(lhs[idx[SOURCE, base + e]], turned[e], TRN))
        for u in range(FAR_UNROLL):
            acc[idx[TARGET, base + g * FAR_UNROLL + u]] += sums[u]
        return 0

    lax.fori_loop(0, chunk // FAR_UNROLL, work, 0)
    for k in range(cells // 2):
        a, b = acc[2 * k], acc[2 * k + 1]
        for r, out in enumerate((keep, send)):
            at = (r * rows, (2 + r) * rows)
            out[k] = jnp.concatenate([x[i : i + rows] for x in (a, b) for i in at], axis=1)


def near_loop(idx, lhs, lhs_at, tiles, flip, dims, acc, acc_at):
    pairs = tiles.shape[0]
    base = (lax.axis_index("rhs") ^ flip) * pairs
    group = min(NEAR_UNROLL, pairs)
    for low in range(0, pairs, group):
        span = range(low, low + group)
        sums = [dot(lhs[idx[lhs_at, base + n]], tiles[n], dims) for n in span]
        for n in span:
            acc[idx[acc_at, base + n]] += sums[n - low]


def near_second_a_kernel(idx, mine, theirs, tiles, acc, both):
    rows, size = mine.shape[1:]

    acc[...] = jnp.zeros_like(acc)
    lane = lax.broadcasted_iota(I32, (rows, size), 1)
    for c in range(both.shape[0]):
        x = theirs[:, c * size : (c + 1) * size]
        x = jnp.where(lane < idx[COUNT, c], x, jnp.zeros_like(x))
        both[c] = jnp.concatenate([mine[c], x], axis=0)
    near_loop(idx, both, FIRST, tiles, 0, NAT, acc, SECOND_REDUCE)


def near_second_b_kernel(
    cells, idx, both, other, before, acc, keep_a, send_a, keep_b, send_b, peak, inv
):
    rows = both.shape[1] // 2
    half = cells // 2
    owners = acc.shape[0] // cells
    stay = keep_b.shape[0] // half
    near_loop(idx, both, FIRST, other, 1, NAT, acc, SECOND_REDUCE)
    encode(lambda o, c: acc[o * cells + c, rows:, :], send_a, owners, half, peak, inv)

    def part_b(o, i):
        return acc[(stay + o) * cells + half + i // 2, i % 2 * rows : (i % 2 + 1) * rows, :]

    encode(part_b, send_b, owners - stay, 2 * half, peak, inv)

    def own_a(o, _):
        for c in range(half):
            keep_a[o * half + c] = acc[o * cells + c, :rows, :]
        return 0

    def own_b(o, _):
        for c in range(half):
            keep_b[o * half + c] = acc[o * cells + half + c]
        return 0

    lax.fori_loop(0, owners, own_a, 0)
    lax.fori_loop(0, stay, own_b, 0)


def near_first_kernel(stride, cells, starts, idx, everyone, both, *refs):
    *parts, tiles, other, keep, send, lhs, acc = refs
    rows = everyone.shape[1]

    acc[...] = jnp.zeros_like(acc)
    lhs[:cells] = both[...]
    for start, part in zip(starts, parts):
        count = part.shape[0] // cells

        def fill(o, _, part=part, start=start):
            for c in range(cells):
                at = start + o
                lhs[at * cells + c] = jnp.concatenate([everyone[at * stride + c], part[o * cells + c]], axis=0)
            return 0

        lax.fori_loop(0, count, fill, 0)
    near_loop(idx, lhs, SECOND, tiles, 0, TRN, acc, FIRST)
    near_loop(idx, lhs, SECOND, other, 1, TRN, acc, FIRST)
    for c in range(cells):
        keep[c] = acc[c, :rows, :]
        send[c] = acc[c, rows:, :]


def join_kernel(mine, coded, out, scale):
    count = out.shape[0]
    decode_scales(coded, count, scale)

    def one(o, _):
        for i in range(8):
            b = o * 8 + i
            out[b] = mine[b] + decode(coded, scale, b)
        return 0

    lax.fori_loop(0, count // 8, one, 0)


def meet_a_kernel(half, low, mine, far, *refs):
    *far_others, keep, send, acc, peak, inv = refs
    count = far_others[0].shape[0]
    owners = far.shape[0] // half
    stay = owners // 2
    for p in range(owners):
        dst, at = (keep, p) if p < stay else (acc, p - stay)
        for c in range(half):
            if p == 0 or p >= low:
                near = mine[(p - low + 1 if p else 0) * half + c]
            else:
                near = jnp.zeros_like(mine[0])
            dst[at * 2 * half + c] = near
            b = p * half + c
            dst[at * 2 * half + half + c] = far[b] + far_others[b // count][b % count]
    encode(lambda o, i: acc[o * 8 + i], send, acc.shape[0] // 8, 8, peak, inv)


def meet_b_kernel(half, low, mine, coded, keep, send, acc, scale, peak, inv):
    rows = keep.shape[1]
    owners = keep.shape[0] // half
    decode_scales(coded, 2 * keep.shape[0], scale)
    for p in range(owners):
        for c in range(half):
            b = p * half + c
            both = [decode(coded, scale, 2 * b), decode(coded, scale, 2 * b + 1)]
            if p == 0 or p >= low:
                at = (p - low + 1 if p else 0) * half + c
                both = [both[0] + mine[at, :rows, :], both[1] + mine[at, rows:, :]]
            keep[b], acc[b] = both
    encode(lambda o, i: acc[o * 8 + i], send, acc.shape[0] // 8, 8, peak, inv)


def meet_kernel(half, mine_a, coded_a, mine_b, coded_b, keep, send, acc, scale_a, scale_b, peak, inv):
    owners = mine_b.shape[0] // half
    stay = owners // 2
    decode_scales(coded_a, mine_a.shape[0], scale_a)
    decode_scales(coded_b, mine_b.shape[0], scale_b)
    for p in range(owners):
        dst, at = (keep, p * 3) if p < stay else (acc, (p - stay) * 3)
        for c in range(half):
            a, b = p * 2 * half + c, p * half + c
            dst[at * half + c] = mine_a[a] + decode(coded_a, scale_a, a)
            dst[(at + 1) * half + c] = mine_b[b] + decode(coded_b, scale_b, b)
            a = a + half
            dst[(at + 2) * half + c] = mine_a[a] + decode(coded_a, scale_a, a)
    encode(lambda o, i: acc[o * 8 + i], send, acc.shape[0] // 8, 8, peak, inv)


def add_kernel(mine, coded, keep, send, acc, scale, peak, inv):
    total = mine.shape[0]
    half = total // 2
    decode_scales(coded, total, scale)

    def one(b, _):
        keep[b] = mine[b] + decode(coded, scale, b)
        acc[b] = mine[half + b] + decode(coded, scale, half + b)
        return 0

    lax.fori_loop(0, half, one, 0, unroll=8)
    encode(lambda o, i: acc[o * 8 + i], send, half // 8, 8, peak, inv)


def self_kernel(moved, self_tiles, out):
    for c in range(out.shape[0]):
        out[c] = dot(moved[c], self_tiles[c], TRN)


def final_kernel(
    counts, mine, coded, first, first_other, target, target_other, own, basis_t, out, scale
):
    cells, terms, size = basis_t.shape
    rows = out.shape[0]
    decode_scales(coded, mine.shape[0], scale)
    lane = lax.broadcasted_iota(I32, (rows, size), 1)
    for k in range(cells // 2):
        b = cells + k
        fields = (mine[b] + decode(coded, scale, b) + target[k] + target_other[k]).astype(BF16)
        for h in range(2):
            c = 2 * k + h
            near = mine[c] + decode(coded, scale, c) + first[c] + first_other[c]
            far = dot(fields[:, h * terms : (h + 1) * terms], basis_t[c], NAT)
            total = near + far + own[c]
            out[:, c * size : (c + 1) * size] = jnp.where(lane < counts[c], total, jnp.zeros_like(total))


def body(
    charges,
    counts,
    self_tiles,
    basis,
    near_first,
    near_second,
    near_tiles,
    far_source,
    far_target,
    far_tiles,
):
    blks = lax.axis_size("blk")
    ranks = lax.axis_size("rhs")
    me = lax.axis_index("blk")
    rank = lax.axis_index("rhs")
    cells, size, _ = self_tiles.shape
    terms = basis.shape[2]
    rows = charges.shape[0]
    pairs = near_tiles.shape[0]
    fars = far_tiles.shape[0]
    bits = blks.bit_length() - 1
    gather_order = [0, *range(bits - 1, 0, -1)]
    reduce_order = [*range(bits - 1, -1, -1)]
    halfc = cells // 2
    stride = cells + halfc
    total = blks * cells

    reach = -(-REACH // cells)
    masks = [sum(((p >> s) & 1) << bit for s, bit in enumerate(reduce_order)) for p in range(blks)]
    gaps = [min(min((o - (o ^ m)) % blks, ((o ^ m) - o) % blks) for o in range(blks)) for m in masks]
    low = 1
    kept = blks - low + 1

    def swap_rank(x, d):
        return lax.ppermute(x, "rhs", [(i, i ^ d) for i in range(ranks)])

    def swap_blk(x, bit):
        return lax.ppermute(x, "blk", [(i, i ^ (1 << bit)) for i in range(blks)])

    def place(block, reduce):
        other = lax.div(block, cells) ^ lax.axis_index("blk")
        order = reduce_order if reduce else gather_order
        at = sum(((other >> bit) & 1) << s for s, bit in enumerate(order))
        return at * cells + lax.rem(block, cells)

    def shape(n, dtype, r=rows):
        return jax.ShapeDtypeStruct((n, r, size), dtype)

    def scratch(n, r=rows, dtype=F32):
        return pltpu.VMEM((n, r, size), dtype)

    def scales(n):
        return pltpu.VMEM((scale_blocks(n) * GROUP, size), F32)

    def whole(n, r=rows):
        return pl.BlockSpec((n, r, size), lambda i, *_: (0, 0, 0))

    def owners(x, low, high, begin, end):
        return x.reshape(-1, stride, rows, size)[low:high, begin:end].reshape(-1, rows, size)

    other_tiles = swap_rank(near_tiles, 1)
    charge_other = swap_rank(charges, 2)
    basis_t = jnp.swapaxes(basis, 1, 2)

    width = max(near_first.shape[0], fars)
    lists = [x.reshape(1, -1) for x in (near_first, near_second, far_source, far_target)]
    own, idx = pl.pallas_call(
        functools.partial(prep_kernel, place, low),
        in_specs=[HBM] * 7,
        out_specs=[VMEM] * 2,
        out_shape=[shape(stride, BF16), jax.ShapeDtypeStruct((7, width), I32)],
        scratch_shapes=[
            pltpu.SMEM(counts.shape, I32),
            pltpu.VMEM(charges.shape, BF16),
            pltpu.VMEM(basis_t.shape, BF16),
            pltpu.VMEM((4, width), I32),
            pltpu.VMEM((1, cells), I32),
            pltpu.SemaphoreType.DMA((8,)),
        ],
        compiler_params=params(8),
        cost_estimate=pl.CostEstimate(flops=0, bytes_accessed=12 << 20, transcendentals=0),
        name="prep",
    )(*[in_hbm(x) for x in (counts.reshape(1, -1), charges, basis_t, *lists)])
    charge_own = own[:cells]
    moment_own = own[cells:]
    moment_pair = swap_rank(moment_own, 1)

    far_cost = pl.CostEstimate(flops=2 * fars * rows * terms * terms, bytes_accessed=12 << 20, transcendentals=0)
    tiles_ij = jnp.transpose(far_tiles, (1, 2, 0)).reshape(terms * terms, fars)
    near_cost = pl.CostEstimate(flops=4 * pairs * rows * size * size, bytes_accessed=10 << 20, transcendentals=0)
    first_cost = pl.CostEstimate(flops=8 * pairs * rows * size * size, bytes_accessed=20 << 20, transcendentals=0)
    coded_a = kept * halfc
    coded_b = blks // 2 * cells
    stay = kept - blks // 2
    near_acc = shape(kept * cells, F32, 2 * rows)
    near_sum, both = pl.pallas_call(
        near_second_a_kernel,
        in_specs=[SMEM, VMEM, VMEM, VMEM],
        out_specs=[VMEM] * 2,
        out_shape=[near_acc, shape(cells, BF16, 2 * rows)],
        compiler_params=params(4),
        cost_estimate=near_cost,
        name="near_second_a",
    )(idx, charge_own, charge_other, near_tiles)

    received = swap_blk(own, gather_order[0])
    received, near_sum = lax.optimization_barrier((received, near_sum))
    gathered = jnp.concatenate([own, received], axis=0)
    received = swap_blk(gathered, gather_order[1])
    near_sum, _ = lax.optimization_barrier((near_sum, gathered))

    _, keep_a, send_a, keep_b, send_b = pl.pallas_call(
        functools.partial(near_second_b_kernel, cells),
        in_specs=[SMEM, VMEM, VMEM, VMEM],
        out_specs=[VMEM] * 5,
        out_shape=[
            near_acc,
            shape(coded_a, F32),
            shape(coded_a + scale_blocks(coded_a), I16),
            shape(stay * halfc, F32, 2 * rows),
            shape(coded_b + scale_blocks(coded_b), I16),
        ],
        scratch_shapes=[
            scales(max(coded_a, coded_b)),
            scales(max(coded_a, coded_b)),
        ],
        input_output_aliases={3: 0},
        compiler_params=params(8),
        cost_estimate=near_cost,
        name="near_second_b",
    )(idx, both, other_tiles, near_sum)
    moment_late, _ = lax.optimization_barrier((moment_pair, send_a))
    turned, far_keep, *far_sends = pl.pallas_call(
        far_source_kernel,
        in_specs=[SMEM] + [VMEM] * 3,
        out_specs=[VMEM] * (2 + PARTS),
        out_shape=[
            shape(fars // 2, BF16, terms // 2),
            shape(total // 2, F32),
            *[shape(total // 2 // PARTS, F32)] * PARTS,
        ],
        scratch_shapes=[
            pltpu.VMEM((FAR_STEPS, terms // 2 * PITCH, size), F32),
            pltpu.VMEM((cells, 2 * rows, terms), BF16),
            pltpu.VMEM((total, 2 * rows, terms), F32),
        ],
        compiler_params=params(8 + total // 32),
        cost_estimate=far_cost,
        name="far_source",
    )(idx, moment_own, moment_late, tiles_ij)
    received, turned = lax.optimization_barrier((received, turned))
    others, starts = [], []
    for s, bit in enumerate(gather_order):
        if s > 1:
            received = swap_blk(gathered, bit)
        if s == bits - 1:
            received, others[0] = lax.optimization_barrier((received, others[0]))
            starts.append(1 << s)
            others.append(swap_rank(owners(received, 0, 1 << s, 0, cells), 2))
        if s > 0:
            gathered = jnp.concatenate([gathered, received], axis=0)
        if s == bits - 2:
            starts.append(1)
            others.append(swap_rank(owners(gathered, 1, 2 << s, 0, cells), 2))

    far_others = [swap_rank(x, 1) for x in far_sends]

    got_a = swap_rank(send_a, 2)
    got_b = swap_blk(send_b, reduce_order[-1])
    got_b, got_a = lax.optimization_barrier((got_b, got_a))
    half_a = blks // 2 * cells
    half_b = blks // 2 * halfc
    meet_cost = pl.CostEstimate(flops=0, bytes_accessed=3 << 20, transcendentals=0)
    keep_b, send_b = pl.pallas_call(
        functools.partial(meet_b_kernel, halfc, low),
        in_specs=[VMEM] * 2,
        out_specs=[VMEM] * 2,
        out_shape=[shape(half_b, F32), shape(half_b + scale_blocks(half_b), I16)],
        scratch_shapes=[scratch(half_b), scales(coded_b), scales(half_b), scales(half_b)],
        compiler_params=params(8 + total // 16),
        cost_estimate=meet_cost,
        name="meet_b",
    )(keep_b, got_b)
    keep_a, send_b = lax.optimization_barrier((keep_a, send_b))
    got_b = swap_rank(send_b, 2)
    joined = pl.pallas_call(
        join_kernel,
        in_specs=[VMEM] * 2,
        out_specs=VMEM,
        out_shape=shape(coded_a, F32),
        scratch_shapes=[scales(coded_a)],
        compiler_params=params(8),
        cost_estimate=pl.CostEstimate(flops=0, bytes_accessed=3 << 20, transcendentals=0),
        name="join",
    )(keep_a, got_a)
    keep_a, send_a = pl.pallas_call(
        functools.partial(meet_a_kernel, halfc, low),
        in_specs=[VMEM] * (2 + PARTS),
        out_specs=[VMEM] * 2,
        out_shape=[shape(half_a, F32), shape(half_a + scale_blocks(half_a), I16)],
        scratch_shapes=[scratch(half_a), scales(half_a), scales(half_a)],
        compiler_params=params(8 + total // 16),
        cost_estimate=meet_cost,
        name="meet_a",
    )(joined, far_keep, *far_others)
    got_a = swap_blk(send_a, reduce_order[-1])

    moment_all_pair = swap_rank(owners(gathered, 0, blks, cells, stride), 1)
    target_keep, target_send = pl.pallas_call(
        functools.partial(far_target_kernel, stride, cells),
        in_specs=[SMEM] + [VMEM] * 3,
        out_specs=[VMEM] * 2,
        out_shape=[shape(halfc, F32), shape(halfc, F32)],
        scratch_shapes=[
            scratch(total, 4 * rows, BF16),
            pltpu.VMEM((cells, 4 * rows, terms // 2), F32),
        ],
        compiler_params=params(6 + total // 32),
        cost_estimate=far_cost,
        name="far_target",
    )(idx, gathered, moment_all_pair, turned)
    target_other = swap_rank(target_send, 1)
    others[0], _ = lax.optimization_barrier((others[0], target_send))

    got_a, got_b, _ = lax.optimization_barrier((got_a, got_b, target_send))

    half = blks // 4 * stride
    keep, send = pl.pallas_call(
        functools.partial(meet_kernel, halfc),
        in_specs=[VMEM] * 4,
        out_specs=[VMEM] * 2,
        out_shape=[shape(half, F32), shape(half + scale_blocks(half), I16)],
        scratch_shapes=[scratch(half), scales(half_a), scales(half_b), scales(half), scales(half)],
        compiler_params=params(8 + total // 16),
        cost_estimate=meet_cost,
        name="meet",
    )(keep_a, got_a, keep_b, got_b)
    coded = swap_blk(send, reduce_order[-2])

    for bit in reversed(reduce_order[:-2]):
        now, half = half, half // 2
        keep, send = pl.pallas_call(
            add_kernel,
            in_specs=[VMEM] * 2,
            out_specs=[VMEM] * 2,
            out_shape=[shape(half, F32), shape(half + scale_blocks(half), I16)],
            scratch_shapes=[scratch(half), scales(now), scales(half), scales(half)],
            compiler_params=params(8 + total // 16),
            name="add",
        )(keep, coded)
        if bit != reduce_order[0]:
            coded = swap_blk(send, bit)

    first_keep, first_send = pl.pallas_call(
        functools.partial(near_first_kernel, stride, cells, starts),
        in_specs=[SMEM] + [VMEM] * (4 + len(others)),
        out_specs=[VMEM, VMEM],
        out_shape=[shape(cells, F32), shape(cells, F32)],
        scratch_shapes=[
            scratch(total, 2 * rows, BF16),
            scratch(cells, 2 * rows),
        ],
        compiler_params=params(4 + total // 32),
        cost_estimate=first_cost,
        name="near_first",
    )(idx, gathered, both, *others, near_tiles, other_tiles)
    first_send, send = lax.optimization_barrier((first_send, send))
    first_other = swap_rank(first_send, 2)
    coded = swap_blk(send, reduce_order[0])

    own_part = pl.pallas_call(
        self_kernel,
        in_specs=[VMEM] * 2,
        out_specs=VMEM,
        out_shape=shape(cells, F32),
        compiler_params=params(8),
        cost_estimate=meet_cost,
        name="self",
    )(charge_own, self_tiles)

    return pl.pallas_call(
        final_kernel,
        in_specs=[SMEM] + [VMEM] * 8,
        out_specs=VMEM,
        out_shape=jax.ShapeDtypeStruct(charges.shape, F32),
        scratch_shapes=[scales(stride)],
        compiler_params=params(8),
        name="final",
    )(
        counts, keep, coded, first_keep, first_other, target_keep, target_other, own_part, basis_t
    )


def solution(mesh):
    in_specs = (
        P("rhs", "blk"),
        P("blk"),
        P("blk", None, None),
        P("blk", None, None),
        P("blk"),
        P("blk"),
        P(("blk", "rhs"), None, None),
        P("blk"),
        P("blk"),
        P("blk", None, None),
    )
    out_specs = P("rhs", "blk")
    return jax.shard_map(body, mesh=mesh, in_specs=in_specs, out_specs=out_specs, check_vma=False)
```

time: 234 us -> 62.4 us (0.27)
  blocking collectives: 64.4 us -> 0 us
  matrix products: 52.5 us -> 0 us
  waiting for transfers between devices: 65.7 us -> 15.6 us
  local copies, waits for them, and re-layouts: 31.1 us -> 2.51 us
  Pallas kernels: 0 us -> 23.9 us
  starting transfers between devices: 0.13 us -> 20 us
  between operations: 15 us -> 0.23 us
  other arithmetic: 4.94 us -> 0 us
    reduce_scatter x2 -> x0, waiting for transfers between devices: 65 us -> none  [the longest x1 65 us: body(): lax.psum_scatter(near.reshape(rows, -1), 'blk', scatter_dimension=1, tile...]
    all_gather x2 -> x0, blocking collectives: 64.4 us -> none  [the longest x1 32.5 us: body(): lax.all_gather(moments.reshape(rows, blk_dev * terms), 'blk', axis=1, til...]
    dot_general x11 -> x0, matrix products: 47.6 us -> none  [the longest x2 21.9 us: pair_sums(): jnp.einsum('rnj,nij->rni', from_second, tiles, preferred_element_type=jnp...]
    pallas_call x0 -> x13, Pallas kernels: none -> 23.9 us  [the longest x1 5.53 us: body(): pl.pallas_call(functools.partial(near_first_kernel, stride, cells, starts...]
    ppermute x0 -> x21, starting transfers between devices: none -> 20 us  [the longest x7 11.5 us: swap_blk(): return lax.ppermute(x, 'blk', [(i, i ^ 1 << bit) for i in range(blks)])]
    ppermute x0 -> x21, waiting for transfers between devices: none -> 15.6 us  [the longest x14 9.03 us: swap_rank(): return lax.ppermute(x, 'rhs', [(i, i ^ d) for i in range(ranks)])]
    unnamed x21 -> x14, local copies, waits for them, and re-layouts: 14.8 us -> 2.32 us
    transpose x2 -> x0, local copies, waits for them, and re-layouts: 7.77 us -> none  [the longest x1 3.97 us: pair_sums(): jnp.einsum('rni,nij->rnj', from_first, tiles, preferred_element_type=jnp....]
  transfers between devices with their start and end apart: 3 -> 21, of which waited for: 1 -> 10; matrix products, arithmetic and copies ran while one was open for 37% -> 0% of each run, Pallas kernels for 0% -> 36%
where the time goes in v3:
time: 62.4 us; the launch traced here: 62.2 us
  Pallas kernels  23.9 us (38%)
  starting transfers between devices  20 us (32%)
  waiting for transfers between devices  15.6 us (25%)
  local copies, waits for them, and re-layouts  2.51 us (4%)
    ppermute x7, starting transfers between devices, swap_blk(): return lax.ppermute(x, 'blk', [(i, i ^ 1 << bit) for i in range(blks)])  11.5 us
    ppermute x14, waiting for transfers between devices, swap_rank(): return lax.ppermute(x, 'rhs', [(i, i ^ d) for i in range(ranks)])  9.03 us
    ppermute x14, starting transfers between devices, swap_rank(): return lax.ppermute(x, 'rhs', [(i, i ^ d) for i in range(ranks)])  8.52 us
    ppermute x7, waiting for transfers between devices, swap_blk(): return lax.ppermute(x, 'blk', [(i, i ^ 1 << bit) for i in range(blks)])  6.57 us
    pallas_call x1, Pallas kernels, body(): pl.pallas_call(functools.partial(near_first_kernel, stride, cells, starts...  5.53 us
    pallas_call x1, Pallas kernels, body(): pl.pallas_call(far_source_kernel, in_specs=[SMEM] + [VMEM] * 3, out_specs...  5.1 us
    pallas_call x1, Pallas kernels, body(): pl.pallas_call(functools.partial(far_target_kernel, stride, cells), in_sp...  4.22 us
    pallas_call x1, Pallas kernels, body(): pl.pallas_call(functools.partial(near_second_b_kernel, cells), in_specs=[...  2.59 us
  transfers between devices with their start and end apart: 21, of which 10 were waited for; matrix products, arithmetic and copies ran while one was open for 0% of the time, Pallas kernels for 36%

profile of v3, /device:TPU:0, one launch (start us, length us, event | category | flops | bytes accessed | tf_op | source)
XLA Modules:
  0.0 62.2 jit_solution(16828693377148132510)
XLA Ops:
  0.0 0.5 collective-permute-start.1
  0.5 2.5 %collective-permute-start = (bf16[16,2048]{1,0:T(8,128)(2,1)}, bf16[16,2048]{1,0:T(8,128)(2,1)S(1)}, u32[]{:S(2)}, u32[]{:S(2)}) collective-permute-start(bf16[16,2048]{1,0:T(8,128)(2,1)} %charges_in.1), channel_id=1, source_target_pairs={{0,2},{1,3},{2,0},{3,1},{4,6},{5,7},{6,4},{7,5},{8,10},{9,11},{10,... | collective-permute-start | bytes 196616 | tf_op jit(solution)/shard_map/ppermute | solution.py:412
  2.9 1.4 %prep.1 = (bf16[24,16,128]{2,1,0:T(8,128)(2,1)S(1)}, s32[7,512]{1,0:T(8,128)S(1)}) custom-call(s32[1,16]{1,0:T(1,128)} %bitcast.19, bf16[16,2048]{1,0:T(8,128)(2,1)} %charges_in.1, bf16[16,64,128]{2,1,0:T(8,128)(2,1)} %bitcast.17, s32[1,512]{1,0:T(1,128)} %bitcast.25, s32[1,512]{1,0:T(1,128)} %bitcast.26, s32[1,512]{1,0:T(1,128)} %bitcast.27, s32[1,512]{1,0:T(1,128)} %bitcast.28), custom_call_target="tpu_custom_call" | custom-call | bytes 12582912 | tf_op jit(solution)/shard_map/prep/pallas_call | solution.py:444
  4.3 1.6 %collective-permute-start.2 = (bf16[24,16,128]{2,1,0:T(8,128)(2,1)S(1)}, bf16[24,16,128]{2,1,0:T(8,128)(2,1)S(1)}, u32[]{:S(2)}, u32[]{:S(2)}) collective-permute-start(bf16[24,16,128]{2,1,0:T(8,128)(2,1)S(1)} %get-tuple-element.49), channel_id=1, source_target_pairs={{0,4},{4,0},{8,12},{12,8},{16,20},{20,16},{24,28},{28,24},{1,5},{5... | collective-permute-start | bytes 294920 | tf_op jit(solution)/shard_map/ppermute | solution.py:415
  6.0 0.0 copy-start
  6.0 2.2 %copy-done = bf16[128,128,128]{2,1,0:T(8,128)(2,1)S(1)} copy-done((bf16[128,128,128]{2,1,0:T(8,128)(2,1)S(1)}, bf16[128,128,128]{2,1,0:T(8,128)(2,1)}, u32[]{:S(2)}) %copy-start) | copy-done | bytes 4194328
  8.2 2.1 %near_second_a.1 = (f32[128,32,128]{2,1,0:T(8,128)S(1)}, bf16[16,32,128]{2,1,0:T(8,128)(2,1)S(1)}) custom-call(s32[7,512]{1,0:T(8,128)S(1)} %get-tuple-element.48.idx, bf16[16,16,128]{2,1,0:T(8,128)(2,1)S(1)} %slice.15.mine.moved, bf16[16,2048]{1,0:T(8,128)(2,1)S(1)} %collective-permute-done.theirs, bf16[128,128,128]{2,1,0:T(8,128)(2,1)S(1)} %copy-done), custom_call_target="tpu_custom_call" | custom-call | flops 134217728 | bytes 10485760 | tf_op jit(solution)/shard_map/near_second_a/pallas_call | solution.py:473
  10.3 0.1 constant_dynamic-update-slice_fusion.3
  10.4 2.8 %collective-permute-start.12 = (bf16[48,16,128]{2,1,0:T(8,128)(2,1)S(1)}, bf16[48,16,128]{2,1,0:T(8,128)(2,1)S(1)}, u32[]{:S(2)}, u32[]{:S(2)}) collective-permute-start(bf16[48,16,128]{2,1,0:T(8,128)(2,1)S(1)} %get-tuple-element.95), channel_id=1, source_target_pairs={{0,16},{4,20},{8,24},{12,28},{16,0},{20,4},{24,8},{28,12},{1,17},{... | collective-permute-start | bytes 589832 | tf_op jit(solution)/shard_map/ppermute | solution.py:415
  13.2 2.6 %near_second_b.1 = (f32[128,32,128]{2,1,0:T(8,128)S(1)}, f32[64,16,128]{2,1,0:T(8,128)S(1)}, s16[68,16,128]{2,1,0:T(8,128)(2,1)S(1)}, f32[32,32,128]{2,1,0:T(8,128)S(1)}, s16[68,16,128]{2,1,0:T(8,128)(2,1)S(1)}) custom-call(s32[7,512]{1,0:T(8,128)S(1)} %get-tuple-element.48.idx, ...), custom_call_target="tpu_custom_call", output_to_operand_aliasing={{0}: (3, {})} | custom-call | flops 134217728 | bytes 10485760 | tf_op jit(solution)/shard_map/near_second_b/pallas_call | solution.py:489
  15.8 1.6 %collective-permute-start.3 = (s16[68,16,128]{2,1,0:T(8,128)(2,1)S(1)}, s16[68,16,128]{2,1,0:T(8,128)(2,1)S(1)}, u32[]{:S(2)}, u32[]{:S(2)}) collective-permute-start(s16[68,16,128]{2,1,0:T(8,128)(2,1)S(1)} %get-tuple-element.57), channel_id=1, source_target_pairs={{0,4},{4,0},{8,12},{12,8},{16,20},{20,16},{24,28},{28,24},{1,5},{5... | collective-permute-start | bytes 835592 | tf_op jit(solution)/shard_map/ppermute | solution.py:415
  17.4 1.5 %collective-permute-start.4 = (s16[68,16,128]{2,1,0:T(8,128)(2,1)S(1)}, s16[68,16,128]{2,1,0:T(8,128)(2,1)S(1)}, u32[]{:S(2)}, u32[]{:S(2)}) collective-permute-start(s16[68,16,128]{2,1,0:T(8,128)(2,1)S(1)} %get-tuple-element.58), channel_id=1, source_target_pairs={{0,2},{1,3},{2,0},{3,1},{4,6},{5,7},{6,4},{7,5},{8,10},{9,11},{10,... | collective-permute-start | bytes 835592 | tf_op jit(solution)/shard_map/ppermute | solution.py:412
  18.9 5.1 %far_source.1 = (bf16[256,32,128]{2,1,0:T(8,128)(2,1)S(1)}, f32[64,16,128]{2,1,0:T(8,128)S(1)}, f32[16,16,128]{2,1,0:T(8,128)S(1)}, f32[16,16,128]{2,1,0:T(8,128...) custom-call(s32[7,512]{1,0:T(8,128)S(1)} %get-tuple-element.48.idx, bf16[8,16,128]{2,1,0:T(8,128)(2,1)S(1)} %slice.16.mine, ...), custom_call_target="tpu_custom_call" | custom-call | flops 67108864 | bytes 12582912 | tf_op jit(solution)/shard_map/far_source/pallas_call | solution.py:510
  24.0 0.1 constant_dynamic-update-slice_fusion.2
  24.1 1.7 %collective-permute-start.13 = (bf16[96,16,128]{2,1,0:T(8,128)(2,1)S(1)}, bf16[96,16,128]{2,1,0:T(8,128)(2,1)S(1)}, u32[]{:S(2)}, u32[]{:S(2)}) collective-permute-start(bf16[96,16,128]{2,1,0:T(8,128)(2,1)S(1)} %get-tuple-element.91), channel_id=1, source_target_pairs={{0,8},{4,12},{8,0},{12,4},{16,24},{20,28},{24,16},{28,20},{1,9},{5... | collective-permute-start | bytes 1179656 | tf_op jit(solution)/shard_map/ppermute | solution.py:415
  25.8 0.6 collective-permute-start.14
  26.4 0.7 %collective-permute-done.6.refs_0_ = f32[16,16,128]{2,1,0:T(8,128)S(1)} collective-permute-done((f32[16,16,128]{2,1,0:T(8,128)S(1)}, f32[16,16,128]{2,1,0:T(8,128)S(1)}, u32[]{:S(2)}, u32[]{:S(2)}) %collective-permute-start.6) | collective-permute-done | bytes 131104 | tf_op jit(solution)/shard_map/ppermute | solution.py:412
  27.1 0.1 collective-permute-start.7
  27.2 0.4 collective-permute-start.8
  27.6 0.1 collective-permute-start.9
  27.8 0.2 meet_b.1
  28.0 0.1 join.1.mine
  28.1 0.0 copy-start.1
  28.1 0.3 collective-permute-done.7.refs_1_
  28.4 0.2 collective-permute-done.8.refs_2_
  28.6 0.3 collective-permute-done.9.refs_3_
  29.0 0.3 meet_a.1
  29.3 0.6 collective-permute-start.10
  29.9 3.3 %collective-permute-done.14.refs_0_ = bf16[48,16,128]{2,1,0:T(8,128)(2,1)S(1)} collective-permute-done((bf16[48,16,128]{2,1,0:T(8,128)(2,1)S(1)}, bf16[48,16,128]{2,1,0:T(8,128)(2,1)S(1)}, u32[]{:S(2)}, u32[]{:S(2)}) %collective-permute-start.14) | collective-permute-done | bytes 196640 | tf_op jit(solution)/shard_map/ppermute | solution.py:412
  33.1 2.0 %collective-permute-done.13 = bf16[96,16,128]{2,1,0:T(8,128)(2,1)S(1)} collective-permute-done((bf16[96,16,128]{2,1,0:T(8,128)(2,1)S(1)}, bf16[96,16,128]{2,1,0:T(8,128)(2,1)S(1)}, u32[]{:S(2)}, u32[]{:S(2)}) %collective-permute-start.13) | collective-permute-done | bytes 393248 | tf_op jit(solution)/shard_map/ppermute | solution.py:415
  35.1 0.1 constant_dynamic-update-slice_fusion.5.everyone
  35.2 0.1 collective-permute-start.15
  35.3 0.6 collective-permute-start.11
  35.9 1.6 %collective-permute-start.17 = (bf16[64,16,128]{2,1,0:T(8,128)(2,1)S(1)}, bf16[64,16,128]{2,1,0:T(8,128)(2,1)S(1)}, u32[]{:S(2)}, u32[]{:S(2)}) collective-permute-start(bf16[64,16,128]{2,1,0:T(8,128)(2,1)S(1)} %bitcast.21), channel_id=1, source_target_pairs={{0,2},{1,3},{2,0},{3,1},{4,6},{5,7},{6,4},{7,5},{8,10},{9,11},{10,... | collective-permute-start | bytes 786440 | tf_op jit(solution)/shard_map/ppermute | solution.py:412
  37.5 4.2 %far_target.1 = (f32[8,16,128]{2,1,0:T(8,128)S(1)}, f32[8,16,128]{2,1,0:T(8,128)S(1)}) custom-call(s32[7,512]{1,0:T(8,128)S(1)} %get-tuple-element.48.idx, bf16[192,16,128]{2,1,0:T(8,128)(2,1)S(1)} %constant_dynamic-update-slice_fusion.5.everyone, bf16[64,16,128]{2,1,0:T(8,128)(2,1)S(1)} %collective-permute-done.15.theirs, ...), custom_call_target="tpu_custom_call" | custom-call | flops 67108864 | bytes 12582912 | tf_op jit(solution)/shard_map/far_target/pallas_call | solution.py:586
  41.7 0.1 collective-permute-done.11.coded_b
  41.8 0.3 meet.1
  42.1 0.0 copy-start.4
  42.2 1.7 %collective-permute-start.16 = (s16[51,16,128]{2,1,0:T(8,128)(2,1)S(1)}, s16[51,16,128]{2,1,0:T(8,128)(2,1)S(1)}, u32[]{:S(2)}, u32[]{:S(2)}) collective-permute-start(s16[51,16,128]{2,1,0:T(8,128)(2,1)S(1)} %get-tuple-element.81), channel_id=1, source_target_pairs={{0,8},{4,12},{8,0},{12,4},{16,24},{20,28},{24,16},{28,20},{1,9},{5... | collective-permute-start | bytes 626696 | tf_op jit(solution)/shard_map/ppermute | solution.py:415
  43.8 3.2 %collective-permute-done.17.refs_1_ = bf16[64,16,128]{2,1,0:T(8,128)(2,1)S(1)} collective-permute-done((bf16[64,16,128]{2,1,0:T(8,128)(2,1)S(1)}, bf16[64,16,128]{2,1,0:T(8,128)(2,1)S(1)}, u32[]{:S(2)}, u32[]{:S(2)}) %collective-permute-start.17) | collective-permute-done | bytes 262176 | tf_op jit(solution)/shard_map/ppermute | solution.py:412
  47.0 5.5 %near_first.1 = (f32[16,16,128]{2,1,0:T(8,128)S(1)}, f32[16,16,128]{2,1,0:T(8,128)S(1)}) custom-call(s32[7,512]{1,0:T(8,128)S(1)} %get-tuple-element.48.idx, bf16[192,16,128]{2,1,0:T(8,128)(2,1)S(1)} %constant_dynamic-update-slice_fusion.5.everyone, bf16[16,32,128]{2,1,0:T(8,128)(2,1)S(1)} %get-tuple-element.50.both, ...), custom_call_target="tpu_custom_call" | custom-call | flops 268435456 | bytes 20971520 | tf_op jit(solution)/shard_map/near_first/pallas_call | solution.py:631
  52.5 0.2 add.1
  52.7 0.6 collective-permute-start.19
  53.3 1.6 %collective-permute-start.18 = (s16[26,16,128]{2,1,0:T(8,128)(2,1)S(1)}, s16[26,16,128]{2,1,0:T(8,128)(2,1)S(1)}, u32[]{:S(2)}, u32[]{:S(2)}) collective-permute-start(s16[26,16,128]{2,1,0:T(8,128)(2,1)S(1)} %get-tuple-element.87), channel_id=1, source_target_pairs={{0,16},{4,20},{8,24},{12,28},{16,0},{20,4},{24,8},{28,12},{1,17},{... | collective-permute-start | bytes 319496 | tf_op jit(solution)/shard_map/ppermute | solution.py:415
  54.9 0.4 self.1.own
  55.3 0.9 %collective-permute-done.20.target_other = f32[8,16,128]{2,1,0:T(8,128)S(1)} collective-permute-done((f32[8,16,128]{2,1,0:T(8,128)S(1)}, f32[8,16,128]{2,1,0:T(8,128)S(1)}, u32[]{:S(2)}, u32[]{:S(2)}) %collective-permute-start.20) | collective-permute-done | bytes 65568 | tf_op jit(solution)/shard_map/ppermute | solution.py:412
  56.2 4.6 %collective-permute-done.18.coded = s16[26,16,128]{2,1,0:T(8,128)(2,1)S(1)} collective-permute-done((s16[26,16,128]{2,1,0:T(8,128)(2,1)S(1)}, s16[26,16,128]{2,1,0:T(8,128)(2,1)S(1)}, u32[]{:S(2)}, u32[]{:S(2)}) %collective-permute-start.18) | collective-permute-done | bytes 106528 | tf_op jit(solution)/shard_map/ppermute | solution.py:415
  60.8 1.5 %final.1 = f32[16,2048]{1,0:T(8,128)} custom-call(s32[16]{0:T(128)S(1)} %copy-done.5, f32[24,16,128]{2,1,0:T(8,128)S(1)} %get-tuple-element.82.mine, s16[26,16,128]{2,1,0:T(8,128)(2,1)S(1)} %collective-permute-done.18.coded, f32[16,16,128]{2,1,0:T(8,128)S(1)} %get-tuple-element.88.first, f32[16,16,128]{2,1,0:T(8,128)S(1)} %collective-permute-done.19.first_other, ...), custom_call_target="tpu_custom_call" | custom-call | tf_op jit(solution)/shard_map/final/pallas_call | solution.py:658
  (28 shorter events, 0.2 us)
Async XLA Ops:
  0.0 13.2 %collective-permute-start.1 = (bf16[128,128,128]{2,1,0:T(8,128)(2,1)}, bf16[128,128,128]{2,1,0:T(8,128)(2,1)S(1)}, u32[]{:S(2)}, u32[]{:S(2)}) collective-permute-start(bf16[128,128,128]{2,1,0:T(8,128)(2,1)} %refs_2_.1), channel_id=1, source_target_pairs={{0,1},{1,0},{2,3},{3,2},{4,5},{5,4},{6,7},{7,6},{8,9},{9,8},{10,11... | collective-permute-start | bytes 12582920 | tf_op jit(solution)/shard_map/ppermute | solution.py:412
  0.5 5.5 %collective-permute-start = (bf16[16,2048]{1,0:T(8,128)(2,1)}, bf16[16,2048]{1,0:T(8,128)(2,1)S(1)}, u32[]{:S(2)}, u32[]{:S(2)}) collective-permute-start(bf16[16,2048]{1,0:T(8,128)(2,1)} %charges_in.1), channel_id=1, source_target_pairs={{0,2},{1,3},{2,0},{3,1},{4,6},{5,7},{6,4},{7,5},{8,10},{9,11},{10,... | collective-permute-start | bytes 196616 | tf_op jit(solution)/shard_map/ppermute | solution.py:412
  4.3 5.9 %collective-permute-start.2 = (bf16[24,16,128]{2,1,0:T(8,128)(2,1)S(1)}, bf16[24,16,128]{2,1,0:T(8,128)(2,1)S(1)}, u32[]{:S(2)}, u32[]{:S(2)}) collective-permute-start(bf16[24,16,128]{2,1,0:T(8,128)(2,1)S(1)} %get-tuple-element.49), channel_id=1, source_target_pairs={{0,4},{4,0},{8,12},{12,8},{16,20},{20,16},{24,28},{28,24},{1,5},{5... | collective-permute-start | bytes 294920 | tf_op jit(solution)/shard_map/ppermute | solution.py:415
  6.0 2.2 %copy-start = (bf16[128,128,128]{2,1,0:T(8,128)(2,1)S(1)}, bf16[128,128,128]{2,1,0:T(8,128)(2,1)}, u32[]{:S(2)}) copy-start(bf16[128,128,128]{2,1,0:T(8,128)(2,1)} %refs_2_.1) | copy-start | bytes 12582916
  10.3 8.6 %copy-start.2 = (bf16[512,64,64]{0,2,1:T(8,128)(2,1)S(1)}, bf16[512,64,64]{0,2,1:T(8,128)(2,1)}, u32[]{:S(2)}) copy-start(bf16[512,64,64]{0,2,1:T(8,128)(2,1)} %param.19) | copy-start | bytes 12582916
  10.4 13.6 %collective-permute-start.12 = (bf16[48,16,128]{2,1,0:T(8,128)(2,1)S(1)}, bf16[48,16,128]{2,1,0:T(8,128)(2,1)S(1)}, u32[]{:S(2)}, u32[]{:S(2)}) collective-permute-start(bf16[48,16,128]{2,1,0:T(8,128)(2,1)S(1)} %get-tuple-element.95), channel_id=1, source_target_pairs={{0,16},{4,20},{8,24},{12,28},{16,0},{20,4},{24,8},{28,12},{1,17},{... | collective-permute-start | bytes 589832 | tf_op jit(solution)/shard_map/ppermute | solution.py:415
  13.2 5.7 %collective-permute-start.5 = (bf16[8,16,128]{2,1,0:T(8,128)(2,1)S(1)}, bf16[8,16,128]{2,1,0:T(8,128)(2,1)S(1)}, u32[]{:S(2)}, u32[]{:S(2)}) collective-permute-start(bf16[8,16,128]{2,1,0:T(8,128)(2,1)S(1)} %slice.16.mine), channel_id=1, source_target_pairs={{0,1},{1,0},{2,3},{3,2},{4,5},{5,4},{6,7},{7,6},{8,9},{9,8},{10,11... | collective-permute-start | bytes 98312 | tf_op jit(solution)/shard_map/ppermute | solution.py:412
  15.8 11.4 %collective-permute-start.3 = (s16[68,16,128]{2,1,0:T(8,128)(2,1)S(1)}, s16[68,16,128]{2,1,0:T(8,128)(2,1)S(1)}, u32[]{:S(2)}, u32[]{:S(2)}) collective-permute-start(s16[68,16,128]{2,1,0:T(8,128)(2,1)S(1)} %get-tuple-element.57), channel_id=1, source_target_pairs={{0,4},{4,0},{8,12},{12,8},{16,20},{20,16},{24,28},{28,24},{1,5},{5... | collective-permute-start | bytes 835592 | tf_op jit(solution)/shard_map/ppermute | solution.py:415
  17.4 10.2 %collective-permute-start.4 = (s16[68,16,128]{2,1,0:T(8,128)(2,1)S(1)}, s16[68,16,128]{2,1,0:T(8,128)(2,1)S(1)}, u32[]{:S(2)}, u32[]{:S(2)}) collective-permute-start(s16[68,16,128]{2,1,0:T(8,128)(2,1)S(1)} %get-tuple-element.58), channel_id=1, source_target_pairs={{0,2},{1,3},{2,0},{3,1},{4,6},{5,7},{6,4},{7,5},{8,10},{9,11},{10,... | collective-permute-start | bytes 835592 | tf_op jit(solution)/shard_map/ppermute | solution.py:412
  24.1 11.0 %collective-permute-start.13 = (bf16[96,16,128]{2,1,0:T(8,128)(2,1)S(1)}, bf16[96,16,128]{2,1,0:T(8,128)(2,1)S(1)}, u32[]{:S(2)}, u32[]{:S(2)}) collective-permute-start(bf16[96,16,128]{2,1,0:T(8,128)(2,1)S(1)} %get-tuple-element.91), channel_id=1, source_target_pairs={{0,8},{4,12},{8,0},{12,4},{16,24},{20,28},{24,16},{28,20},{1,9},{5... | collective-permute-start | bytes 1179656 | tf_op jit(solution)/shard_map/ppermute | solution.py:415
  25.7 1.3 %collective-permute-start.6 = (f32[16,16,128]{2,1,0:T(8,128)S(1)}, f32[16,16,128]{2,1,0:T(8,128)S(1)}, u32[]{:S(2)}, u32[]{:S(2)}) collective-permute-start(f32[16,16,128]{2,1,0:T(8,128)S(1)} %get-tuple-element.65), channel_id=1, source_target_pairs={{0,1},{1,0},{2,3},{3,2},{4,5},{5,4},{6,7},{7,6},{8,9},{9,8},{10,11... | collective-permute-start | bytes 393224 | tf_op jit(solution)/shard_map/ppermute | solution.py:412
  25.8 7.4 %collective-permute-start.14 = (bf16[48,16,128]{2,1,0:T(8,128)(2,1)S(1)}, bf16[48,16,128]{2,1,0:T(8,128)(2,1)S(1)}, u32[]{:S(2)}, u32[]{:S(2)}) collective-permute-start(bf16[48,16,128]{2,1,0:T(8,128)(2,1)S(1)} %bitcast.24), channel_id=1, source_target_pairs={{0,2},{1,3},{2,0},{3,1},{4,6},{5,7},{6,4},{7,5},{8,10},{9,11},{10,... | collective-permute-start | bytes 589832 | tf_op jit(solution)/shard_map/ppermute | solution.py:412
  27.1 1.3 %collective-permute-start.7 = (f32[16,16,128]{2,1,0:T(8,128)S(1)}, f32[16,16,128]{2,1,0:T(8,128)S(1)}, u32[]{:S(2)}, u32[]{:S(2)}) collective-permute-start(f32[16,16,128]{2,1,0:T(8,128)S(1)} %get-tuple-element.66), channel_id=1, source_target_pairs={{0,1},{1,0},{2,3},{3,2},{4,5},{5,4},{6,7},{7,6},{8,9},{9,8},{10,11... | collective-permute-start | bytes 393224 | tf_op jit(solution)/shard_map/ppermute | solution.py:412
  27.2 1.4 %collective-permute-start.8 = (f32[16,16,128]{2,1,0:T(8,128)S(1)}, f32[16,16,128]{2,1,0:T(8,128)S(1)}, u32[]{:S(2)}, u32[]{:S(2)}) collective-permute-start(f32[16,16,128]{2,1,0:T(8,128)S(1)} %get-tuple-element.67), channel_id=1, source_target_pairs={{0,1},{1,0},{2,3},{3,2},{4,5},{5,4},{6,7},{7,6},{8,9},{9,8},{10,11... | collective-permute-start | bytes 393224 | tf_op jit(solution)/shard_map/ppermute | solution.py:412
  27.6 1.3 %collective-permute-start.9 = (f32[16,16,128]{2,1,0:T(8,128)S(1)}, f32[16,16,128]{2,1,0:T(8,128)S(1)}, u32[]{:S(2)}, u32[]{:S(2)}) collective-permute-start(f32[16,16,128]{2,1,0:T(8,128)S(1)} %get-tuple-element.68), channel_id=1, source_target_pairs={{0,1},{1,0},{2,3},{3,2},{4,5},{5,4},{6,7},{7,6},{8,9},{9,8},{10,11... | collective-permute-start | bytes 393224 | tf_op jit(solution)/shard_map/ppermute | solution.py:412
  28.1 18.9 %copy-start.1 = (bf16[128,128,128]{2,1,0:T(8,128)(2,1)S(1)}, bf16[128,128,128]{2,1,0:T(8,128)(2,1)}, u32[]{:S(2)}) copy-start(bf16[128,128,128]{2,1,0:T(8,128)(2,1)} %refs_2_.1) | copy-start | bytes 12582916
  29.3 12.5 %collective-permute-start.10 = (s16[68,16,128]{2,1,0:T(8,128)(2,1)S(1)}, s16[68,16,128]{2,1,0:T(8,128)(2,1)S(1)}, u32[]{:S(2)}, u32[]{:S(2)}) collective-permute-start(s16[68,16,128]{2,1,0:T(8,128)(2,1)S(1)} %get-tuple-element.70), channel_id=1, source_target_pairs={{0,4},{4,0},{8,12},{12,8},{16,20},{20,16},{24,28},{28,24},{1,5},{5... | collective-permute-start | bytes 835592 | tf_op jit(solution)/shard_map/ppermute | solution.py:415
  35.2 2.3 %collective-permute-start.15 = (bf16[64,16,128]{2,1,0:T(8,128)(2,1)S(1)}, bf16[64,16,128]{2,1,0:T(8,128)(2,1)S(1)}, u32[]{:S(2)}, u32[]{:S(2)}) collective-permute-start(bf16[64,16,128]{2,1,0:T(8,128)(2,1)S(1)} %bitcast.22), channel_id=1, source_target_pairs={{0,1},{1,0},{2,3},{3,2},{4,5},{5,4},{6,7},{7,6},{8,9},{9,8},{10,11... | collective-permute-start | bytes 786440 | tf_op jit(solution)/shard_map/ppermute | solution.py:412
  35.3 6.5 %collective-permute-start.11 = (s16[34,16,128]{2,1,0:T(8,128)(2,1)S(1)}, s16[34,16,128]{2,1,0:T(8,128)(2,1)S(1)}, u32[]{:S(2)}, u32[]{:S(2)}) collective-permute-start(s16[34,16,128]{2,1,0:T(8,128)(2,1)S(1)} %get-tuple-element.71), channel_id=1, source_target_pairs={{0,2},{1,3},{2,0},{3,1},{4,6},{5,7},{6,4},{7,5},{8,10},{9,11},{10,... | collective-permute-start | bytes 417800 | tf_op jit(solution)/shard_map/ppermute | solution.py:412
  35.9 11.1 %collective-permute-start.17 = (bf16[64,16,128]{2,1,0:T(8,128)(2,1)S(1)}, bf16[64,16,128]{2,1,0:T(8,128)(2,1)S(1)}, u32[]{:S(2)}, u32[]{:S(2)}) collective-permute-start(bf16[64,16,128]{2,1,0:T(8,128)(2,1)S(1)} %bitcast.21), channel_id=1, source_target_pairs={{0,2},{1,3},{2,0},{3,1},{4,6},{5,7},{6,4},{7,5},{8,10},{9,11},{10,... | collective-permute-start | bytes 786440 | tf_op jit(solution)/shard_map/ppermute | solution.py:412
  42.1 12.8 %copy-start.4 = (bf16[16,128,128]{2,1,0:T(8,128)(2,1)S(1)}, bf16[16,128,128]{2,1,0:T(8,128)(2,1)}, u32[]{:S(2)}) copy-start(bf16[16,128,128]{2,1,0:T(8,128)(2,1)} %self_tiles.1) | copy-start | bytes 1572868
  42.1 18.6 %copy-start.3 = (bf16[16,128,64]{1,2,0:T(8,128)(2,1)S(1)}, bf16[16,128,64]{1,2,0:T(8,128)(2,1)}, u32[]{:S(2)}) copy-start(bf16[16,128,64]{1,2,0:T(8,128)(2,1)} %param.13) | copy-start | bytes 786436
  42.2 18.6 %copy-start.5 = (s32[16]{0:T(128)S(1)}, s32[16]{0:T(128)}, u32[]{:S(2)}) copy-start(s32[16]{0:T(128)} %counts.1) | copy-start | bytes 196
  42.2 10.4 %collective-permute-start.16 = (s16[51,16,128]{2,1,0:T(8,128)(2,1)S(1)}, s16[51,16,128]{2,1,0:T(8,128)(2,1)S(1)}, u32[]{:S(2)}, u32[]{:S(2)}) collective-permute-start(s16[51,16,128]{2,1,0:T(8,128)(2,1)S(1)} %get-tuple-element.81), channel_id=1, source_target_pairs={{0,8},{4,12},{8,0},{12,4},{16,24},{20,28},{24,16},{28,20},{1,9},{5... | collective-permute-start | bytes 626696 | tf_op jit(solution)/shard_map/ppermute | solution.py:415
  52.7 8.0 %collective-permute-start.19 = (f32[16,16,128]{2,1,0:T(8,128)S(1)}, f32[16,16,128]{2,1,0:T(8,128)S(1)}, u32[]{:S(2)}, u32[]{:S(2)}) collective-permute-start(f32[16,16,128]{2,1,0:T(8,128)S(1)} %get-tuple-element.89), channel_id=1, source_target_pairs={{0,2},{1,3},{2,0},{3,1},{4,6},{5,7},{6,4},{7,5},{8,10},{9,11},{10,... | collective-permute-start | bytes 393224 | tf_op jit(solution)/shard_map/ppermute | solution.py:412
  53.3 7.4 %collective-permute-start.18 = (s16[26,16,128]{2,1,0:T(8,128)(2,1)S(1)}, s16[26,16,128]{2,1,0:T(8,128)(2,1)S(1)}, u32[]{:S(2)}, u32[]{:S(2)}) collective-permute-start(s16[26,16,128]{2,1,0:T(8,128)(2,1)S(1)} %get-tuple-element.87), channel_id=1, source_target_pairs={{0,16},{4,20},{8,24},{12,28},{16,0},{20,4},{24,8},{28,12},{1,17},{... | collective-permute-start | bytes 319496 | tf_op jit(solution)/shard_map/ppermute | solution.py:415
  54.9 1.3 %collective-permute-start.20 = (f32[8,16,128]{2,1,0:T(8,128)S(1)}, f32[8,16,128]{2,1,0:T(8,128)S(1)}, u32[]{:S(2)}, u32[]{:S(2)}) collective-permute-start(f32[8,16,128]{2,1,0:T(8,128)S(1)} %get-tuple-element.76), channel_id=1, source_target_pairs={{0,1},{1,0},{2,3},{3,2},{4,5},{5,4},{6,7},{7,6},{8,9},{9,8},{10,11... | collective-permute-start | bytes 196616 | tf_op jit(solution)/shard_map/ppermute | solution.py:412

commit v4 on v3

--- a/solution.py
+++ b/solution.py
@@ -8,7 +8,6 @@
 from jax.sharding import PartitionSpec as P
 
 F32, BF16, I16, I32 = jnp.float32, jnp.bfloat16, jnp.int16, jnp.int32
-REACH = 48
 GROUP = 16
 TOP = 32767.0
 VMEM = pl.BlockSpec(memory_space=pltpu.VMEM)
@@ -69,17 +68,18 @@
 
 
 def prep_kernel(
-    place, low, counts_in, charges_in, basis_in, near_first, near_second, far_source, far_target,
-    out, idx, counts, charges, basis_t, lists, counts_row, sems,
+    place, counts_in, charges_in, basis_in, near_first, near_second, far_source, far_target, tiles_in,
+    out, idx, tiles, counts, charges, basis_t, lists, counts_row, sems,
 ):
     pairs = [(counts_in.at[0], counts), (charges_in, charges), (basis_in, basis_t), (counts_in, counts_row)]
     pairs += [
         (src, lists.at[pl.ds(i, 1)]) for i, src in enumerate((near_first, near_second, far_source, far_target))
     ]
+    pairs += [(tiles_in.at[pl.ds(0, tiles.shape[0])], tiles)]
     copies = [pltpu.make_async_copy(src, dst, sems.at[i]) for i, (src, dst) in enumerate(pairs)]
     for copy in copies:
         copy.start()
-    for copy in copies:
+    for copy in copies[:-1]:
         copy.wait()
     cells, terms, size = basis_t.shape
     rows = charges.shape[0]
@@ -93,17 +93,17 @@
     for k in range(cells // 2):
         out[cells + k] = jnp.concatenate(moments[2 * k : 2 * k + 2], axis=1).astype(BF16)
     first, second, source, target = (lists[i : i + 1, :] for i in range(4))
-    reduce_at = place(second, 1)
     for row, value in (
         (FIRST, lax.rem(first, cells)),
         (SECOND, place(second, 0)),
-        (SECOND_REDUCE, jnp.where(reduce_at < cells, reduce_at, reduce_at - (low - 1) * cells)),
+        (SECOND_REDUCE, place(second, 1)),
         (SOURCE, place(source, 0)),
         (SOURCE_REDUCE, place(source, 1)),
         (TARGET, lax.rem(target, cells)),
     ):
         idx[row : row + 1, :] = value
     idx[COUNT : COUNT + 1, :cells] = counts_row[...]
+    copies[-1].wait()
 
 
 FIRST, SECOND, SECOND_REDUCE, SOURCE, SOURCE_REDUCE, TARGET, COUNT = range(7)
@@ -200,27 +200,32 @@
             out[k] = jnp.concatenate([x[i : i + rows] for x in (a, b) for i in at], axis=1)
 
 
-def near_loop(idx, lhs, lhs_at, tiles, flip, dims, acc, acc_at):
-    pairs = tiles.shape[0]
-    base = (lax.axis_index("rhs") ^ flip) * pairs
-    group = min(NEAR_UNROLL, pairs)
-    for low in range(0, pairs, group):
+def near_loop(idx, lhs, lhs_at, tiles, flip, first, pairs, dims, acc, acc_at):
+    count = tiles.shape[0]
+    base = (lax.axis_index("rhs") ^ flip) * pairs + first
+    group = min(NEAR_UNROLL, count)
+    for low in range(0, count, group):
         span = range(low, low + group)
         sums = [dot(lhs[idx[lhs_at, base + n]], tiles[n], dims) for n in span]
         for n in span:
             acc[idx[acc_at, base + n]] += sums[n - low]
 
 
-def near_second_a_kernel(idx, mine, theirs, tiles, acc, both):
+def near_second_a_kernel(idx, mine, theirs, tiles, rest, acc, both, tiles_high, sem):
     rows, size = mine.shape[1:]
 
+    half, pairs = tiles.shape[0], rest.shape[0]
+    copy = pltpu.make_async_copy(rest.at[pl.ds(half, pairs - half)], tiles_high, sem)
+    copy.start()
     acc[...] = jnp.zeros_like(acc)
     lane = lax.broadcasted_iota(I32, (rows, size), 1)
     for c in range(both.shape[0]):
         x = theirs[:, c * size : (c + 1) * size]
         x = jnp.where(lane < idx[COUNT, c], x, jnp.zeros_like(x))
         both[c] = jnp.concatenate([mine[c], x], axis=0)
-    near_loop(idx, both, FIRST, tiles, 0, NAT, acc, SECOND_REDUCE)
+    near_loop(idx, both, FIRST, tiles, 0, 0, pairs, NAT, acc, SECOND_REDUCE)
+    copy.wait()
+    near_loop(idx, both, FIRST, tiles_high, 0, half, pairs, NAT, acc, SECOND_REDUCE)
 
 
 def near_second_b_kernel(
@@ -230,7 +235,7 @@
     half = cells // 2
     owners = acc.shape[0] // cells
     stay = keep_b.shape[0] // half
-    near_loop(idx, both, FIRST, other, 1, NAT, acc, SECOND_REDUCE)
+    near_loop(idx, both, FIRST, other, 1, 0, other.shape[0], NAT, acc, SECOND_REDUCE)
     encode(lambda o, c: acc[o * cells + c, rows:, :], send_a, owners, half, peak, inv)
 
     def part_b(o, i):
@@ -253,7 +258,7 @@
 
 
 def near_first_kernel(stride, cells, starts, idx, everyone, both, *refs):
-    *parts, tiles, other, keep, send, lhs, acc = refs
+    *parts, tiles, tiles_high, other, keep, send, lhs, acc = refs
     rows = everyone.shape[1]
 
     acc[...] = jnp.zeros_like(acc)
@@ -268,8 +273,10 @@
             return 0
 
         lax.fori_loop(0, count, fill, 0)
-    near_loop(idx, lhs, SECOND, tiles, 0, TRN, acc, FIRST)
-    near_loop(idx, lhs, SECOND, other, 1, TRN, acc, FIRST)
+    pairs = other.shape[0]
+    near_loop(idx, lhs, SECOND, tiles, 0, 0, pairs, TRN, acc, FIRST)
+    near_loop(idx, lhs, SECOND, tiles_high, 0, tiles.shape[0], pairs, TRN, acc, FIRST)
+    near_loop(idx, lhs, SECOND, other, 1, 0, pairs, TRN, acc, FIRST)
     for c in range(cells):
         keep[c] = acc[c, :rows, :]
         send[c] = acc[c, rows:, :]
@@ -288,7 +295,7 @@
     lax.fori_loop(0, count // 8, one, 0)
 
 
-def meet_a_kernel(half, low, mine, far, *refs):
+def meet_a_kernel(half, mine, far, *refs):
     *far_others, keep, send, acc, peak, inv = refs
     count = far_others[0].shape[0]
     owners = far.shape[0] // half
@@ -296,28 +303,21 @@
     for p in range(owners):
         dst, at = (keep, p) if p < stay else (acc, p - stay)
         for c in range(half):
-            if p == 0 or p >= low:
-                near = mine[(p - low + 1 if p else 0) * half + c]
-            else:
-                near = jnp.zeros_like(mine[0])
-            dst[at * 2 * half + c] = near
             b = p * half + c
+            dst[at * 2 * half + c] = mine[b]
             dst[at * 2 * half + half + c] = far[b] + far_others[b // count][b % count]
     encode(lambda o, i: acc[o * 8 + i], send, acc.shape[0] // 8, 8, peak, inv)
 
 
-def meet_b_kernel(half, low, mine, coded, keep, send, acc, scale, peak, inv):
+def meet_b_kernel(half, mine, coded, keep, send, acc, scale, peak, inv):
     rows = keep.shape[1]
     owners = keep.shape[0] // half
     decode_scales(coded, 2 * keep.shape[0], scale)
     for p in range(owners):
         for c in range(half):
             b = p * half + c
-            both = [decode(coded, scale, 2 * b), decode(coded, scale, 2 * b + 1)]
-            if p == 0 or p >= low:
-                at = (p - low + 1 if p else 0) * half + c
-                both = [both[0] + mine[at, :rows, :], both[1] + mine[at, rows:, :]]
-            keep[b], acc[b] = both
+            keep[b] = mine[b, :rows, :] + decode(coded, scale, 2 * b)
+            acc[b] = mine[b, rows:, :] + decode(coded, scale, 2 * b + 1)
     encode(lambda o, i: acc[o * 8 + i], send, acc.shape[0] // 8, 8, peak, inv)
 
 
@@ -402,12 +402,6 @@
     stride = cells + halfc
     total = blks * cells
 
-    reach = -(-REACH // cells)
-    masks = [sum(((p >> s) & 1) << bit for s, bit in enumerate(reduce_order)) for p in range(blks)]
-    gaps = [min(min((o - (o ^ m)) % blks, ((o ^ m) - o) % blks) for o in range(blks)) for m in masks]
-    low = 1
-    kept = blks - low + 1
-
     def swap_rank(x, d):
         return lax.ppermute(x, "rhs", [(i, i ^ d) for i in range(ranks)])
 
@@ -441,23 +435,27 @@
 
     width = max(near_first.shape[0], fars)
     lists = [x.reshape(1, -1) for x in (near_first, near_second, far_source, far_target)]
-    own, idx = pl.pallas_call(
-        functools.partial(prep_kernel, place, low),
-        in_specs=[HBM] * 7,
-        out_specs=[VMEM] * 2,
-        out_shape=[shape(stride, BF16), jax.ShapeDtypeStruct((7, width), I32)],
+    own, idx, tiles_low = pl.pallas_call(
+        functools.partial(prep_kernel, place),
+        in_specs=[HBM] * 8,
+        out_specs=[VMEM] * 3,
+        out_shape=[
+            shape(stride, BF16),
+            jax.ShapeDtypeStruct((7, width), I32),
+            shape(pairs // 2, BF16, size),
+        ],
         scratch_shapes=[
             pltpu.SMEM(counts.shape, I32),
             pltpu.VMEM(charges.shape, BF16),
             pltpu.VMEM(basis_t.shape, BF16),
             pltpu.VMEM((4, width), I32),
             pltpu.VMEM((1, cells), I32),
-            pltpu.SemaphoreType.DMA((8,)),
+            pltpu.SemaphoreType.DMA((9,)),
         ],
         compiler_params=params(8),
         cost_estimate=pl.CostEstimate(flops=0, bytes_accessed=12 << 20, transcendentals=0),
         name="prep",
-    )(*[in_hbm(x) for x in (counts.reshape(1, -1), charges, basis_t, *lists)])
+    )(*[in_hbm(x) for x in (counts.reshape(1, -1), charges, basis_t, *lists, near_tiles)])
     charge_own = own[:cells]
     moment_own = own[cells:]
     moment_pair = swap_rank(moment_own, 1)
@@ -466,19 +464,20 @@
     tiles_ij = jnp.transpose(far_tiles, (1, 2, 0)).reshape(terms * terms, fars)
     near_cost = pl.CostEstimate(flops=4 * pairs * rows * size * size, bytes_accessed=10 << 20, transcendentals=0)
     first_cost = pl.CostEstimate(flops=8 * pairs * rows * size * size, bytes_accessed=20 << 20, transcendentals=0)
-    coded_a = kept * halfc
+    coded_a = total // 2
     coded_b = blks // 2 * cells
-    stay = kept - blks // 2
-    near_acc = shape(kept * cells, F32, 2 * rows)
-    near_sum, both = pl.pallas_call(
+    stay = blks // 2
+    near_acc = shape(total, F32, 2 * rows)
+    near_sum, both, tiles_high = pl.pallas_call(
         near_second_a_kernel,
-        in_specs=[SMEM, VMEM, VMEM, VMEM],
-        out_specs=[VMEM] * 2,
-        out_shape=[near_acc, shape(cells, BF16, 2 * rows)],
+        in_specs=[SMEM, VMEM, VMEM, VMEM, HBM],
+        out_specs=[VMEM] * 3,
+        out_shape=[near_acc, shape(cells, BF16, 2 * rows), shape(pairs - pairs // 2, BF16, size)],
+        scratch_shapes=[pltpu.SemaphoreType.DMA],
         compiler_params=params(4),
         cost_estimate=near_cost,
         name="near_second_a",
-    )(idx, charge_own, charge_other, near_tiles)
+    )(idx, charge_own, charge_other, tiles_low, in_hbm(near_tiles))
 
     received = swap_blk(own, gather_order[0])
     received, near_sum = lax.optimization_barrier((received, near_sum))
@@ -530,16 +529,10 @@
     for s, bit in enumerate(gather_order):
         if s > 1:
             received = swap_blk(gathered, bit)
-        if s == bits - 1:
-            received, others[0] = lax.optimization_barrier((received, others[0]))
-            starts.append(1 << s)
-            others.append(swap_rank(owners(received, 0, 1 << s, 0, cells), 2))
-        if s > 0:
+        if 0 < s < bits - 1:
             gathered = jnp.concatenate([gathered, received], axis=0)
-        if s == bits - 2:
-            starts.append(1)
-            others.append(swap_rank(owners(gathered, 1, 2 << s, 0, cells), 2))
-
+    starts.append(1)
+    others.append(swap_rank(owners(gathered, 1, blks // 2, 0, cells), 2))
     far_others = [swap_rank(x, 1) for x in far_sends]
 
     got_a = swap_rank(send_a, 2)
@@ -547,9 +540,9 @@
     got_b, got_a = lax.optimization_barrier((got_b, got_a))
     half_a = blks // 2 * cells
     half_b = blks // 2 * halfc
-    meet_cost = pl.CostEstimate(flops=0, bytes_accessed=3 << 20, transcendentals=0)
+    meet_cost = pl.CostEstimate(flops=0, bytes_accessed=1 << 20, transcendentals=0)
     keep_b, send_b = pl.pallas_call(
-        functools.partial(meet_b_kernel, halfc, low),
+        functools.partial(meet_b_kernel, halfc),
         in_specs=[VMEM] * 2,
         out_specs=[VMEM] * 2,
         out_shape=[shape(half_b, F32), shape(half_b + scale_blocks(half_b), I16)],
@@ -560,6 +553,10 @@
     )(keep_b, got_b)
     keep_a, send_b = lax.optimization_barrier((keep_a, send_b))
     got_b = swap_rank(send_b, 2)
+    received, others[0], got_b = lax.optimization_barrier((received, others[0], got_b))
+    gathered = jnp.concatenate([gathered, received], axis=0)
+    starts.append(blks // 2)
+    others.append(swap_rank(owners(received, 0, blks // 2, 0, cells), 2))
     joined = pl.pallas_call(
         join_kernel,
         in_specs=[VMEM] * 2,
@@ -571,7 +568,7 @@
         name="join",
     )(keep_a, got_a)
     keep_a, send_a = pl.pallas_call(
-        functools.partial(meet_a_kernel, halfc, low),
+        functools.partial(meet_a_kernel, halfc),
         in_specs=[VMEM] * (2 + PARTS),
         out_specs=[VMEM] * 2,
         out_shape=[shape(half_a, F32), shape(half_a + scale_blocks(half_a), I16)],
@@ -593,7 +590,7 @@
             pltpu.VMEM((cells, 4 * rows, terms // 2), F32),
         ],
         compiler_params=params(6 + total // 32),
-        cost_estimate=far_cost,
+        cost_estimate=meet_cost,
         name="far_target",
     )(idx, gathered, moment_all_pair, turned)
     target_other = swap_rank(target_send, 1)
@@ -630,7 +627,7 @@
 
     first_keep, first_send = pl.pallas_call(
         functools.partial(near_first_kernel, stride, cells, starts),
-        in_specs=[SMEM] + [VMEM] * (4 + len(others)),
+        in_specs=[SMEM] + [VMEM] * (5 + len(others)),
         out_specs=[VMEM, VMEM],
         out_shape=[shape(cells, F32), shape(cells, F32)],
         scratch_shapes=[
@@ -640,7 +637,7 @@
         compiler_params=params(4 + total // 32),
         cost_estimate=first_cost,
         name="near_first",
-    )(idx, gathered, both, *others, near_tiles, other_tiles)
+    )(idx, gathered, both, *others, tiles_low, tiles_high, other_tiles)
     first_send, send = lax.optimization_barrier((first_send, send))
     first_other = swap_rank(first_send, 2)
     coded = swap_blk(send, reduce_order[0])

time: 62.4 us -> 60 us (0.962)
  local copies, waits for them, and re-layouts: 2.51 us -> 0.32 us
  Pallas kernels: 23.9 us -> 26 us
  waiting for transfers between devices: 15.6 us -> 14.4 us
  starting transfers between devices: 20 us -> 18.9 us
    unnamed x14 -> x11, local copies, waits for them, and re-layouts: 2.32 us -> 0.2 us
    pallas_call x4, Pallas kernels: 4.01 us -> 6.12 us  [the longest x1 3.7 us: body(): pl.pallas_call(near_second_a_kernel, in_specs=[SMEM, VMEM, VMEM, VMEM, HB...]
    ppermute x7, starting transfers between devices: 11.5 us -> 10 us  [swap_blk(): return lax.ppermute(x, 'blk', [(i, i ^ 1 << bit) for i in range(blks)])]
    ppermute x7, waiting for transfers between devices: 6.57 us -> 5.57 us  [swap_blk(): return lax.ppermute(x, 'blk', [(i, i ^ 1 << bit) for i in range(blks)])]
  transfers between devices with their start and end apart: 21 -> 21, of which waited for: 10 -> 9; matrix products, arithmetic and copies ran while one was open for 0% -> 0% of each run, Pallas kernels for 36% -> 41%
where the time goes in v4:
time: 60 us; the launch traced here: 59.8 us
  Pallas kernels  26 us (43%)
  starting transfers between devices  18.9 us (31%)
  waiting for transfers between devices  14.4 us (24%)
    ppermute x7, starting transfers between devices, swap_blk(): return lax.ppermute(x, 'blk', [(i, i ^ 1 << bit) for i in range(blks)])  10 us
    ppermute x14, starting transfers between devices, swap_rank(): return lax.ppermute(x, 'rhs', [(i, i ^ d) for i in range(ranks)])  8.89 us
    ppermute x14, waiting for transfers between devices, swap_rank(): return lax.ppermute(x, 'rhs', [(i, i ^ d) for i in range(ranks)])  8.84 us
    ppermute x7, waiting for transfers between devices, swap_blk(): return lax.ppermute(x, 'blk', [(i, i ^ 1 << bit) for i in range(blks)])  5.57 us
    pallas_call x1, Pallas kernels, body(): pl.pallas_call(functools.partial(near_first_kernel, stride, cells, starts...  5.53 us
    pallas_call x1, Pallas kernels, body(): pl.pallas_call(far_source_kernel, in_specs=[SMEM] + [VMEM] * 3, out_specs...  5.1 us
    pallas_call x1, Pallas kernels, body(): pl.pallas_call(functools.partial(far_target_kernel, stride, cells), in_sp...  4.23 us
    pallas_call x1, Pallas kernels, body(): pl.pallas_call(near_second_a_kernel, in_specs=[SMEM, VMEM, VMEM, VMEM, HB...  3.7 us
  transfers between devices with their start and end apart: 21, of which 9 were waited for; matrix products, arithmetic and copies ran while one was open for 0% of the time, Pallas kernels for 41%

profile of v4, /device:TPU:0, one launch (start us, length us, event | category | flops | bytes accessed | tf_op | source)
XLA Modules:
  0.0 59.8 jit_solution(3031328376488348260)
XLA Ops:
  0.0 0.5 collective-permute-start.1
  0.5 2.5 %collective-permute-start = (bf16[16,2048]{1,0:T(8,128)(2,1)}, bf16[16,2048]{1,0:T(8,128)(2,1)S(1)}, u32[]{:S(2)}, u32[]{:S(2)}) collective-permute-start(bf16[16,2048]{1,0:T(8,128)(2,1)} %charges_in.1), channel_id=1, source_target_pairs={{0,2},{1,3},{2,0},{3,1},{4,6},{5,7},{6,4},{7,5},{8,10},{9,11},{10,... | collective-permute-start | bytes 196616 | tf_op jit(solution)/shard_map/ppermute | solution.py:406
  2.9 1.9 %prep.1 = (bf16[24,16,128]{2,1,0:T(8,128)(2,1)S(1)}, s32[7,512]{1,0:T(8,128)S(1)}, bf16[64,128,128]{2,1,0:T(8,128)(2,1)S(1)}) custom-call(s32[1,16]{1,0:T(1,128)} %bitcast.19, bf16[16,2048]{1,0:T(8,128)(2,1)} %charges_in.1, bf16[16,64,128]{2,1,0:T(8,128)(2,1)} %bitcast.17, s32[1,512]{1,0:T(1,128)} %bitcast.25, s32[1,512]{1,0:T(1,128)} %bitcast.26, ...), custom_call_target="tpu_custom_call" | custom-call | bytes 12582912 | tf_op jit(solution)/shard_map/prep/pallas_call | solution.py:438
  4.8 1.6 %collective-permute-start.2 = (bf16[24,16,128]{2,1,0:T(8,128)(2,1)S(1)}, bf16[24,16,128]{2,1,0:T(8,128)(2,1)S(1)}, u32[]{:S(2)}, u32[]{:S(2)}) collective-permute-start(bf16[24,16,128]{2,1,0:T(8,128)(2,1)S(1)} %get-tuple-element.52), channel_id=1, source_target_pairs={{0,4},{4,0},{8,12},{12,8},{16,20},{20,16},{24,28},{28,24},{1,5},{5... | collective-permute-start | bytes 294920 | tf_op jit(solution)/shard_map/ppermute | solution.py:409
  6.5 0.0 collective-permute-done.theirs
  6.5 3.7 %near_second_a.1 = (f32[128,32,128]{2,1,0:T(8,128)S(1)}, bf16[16,32,128]{2,1,0:T(8,128)(2,1)S(1)}, bf16[64,128,128]{2,1,0:T(8,128)(2,1)S(1)}) custom-call(s32[7,512]{1,0:T(8,128)S(1)} %get-tuple-element.51.idx, bf16[16,16,128]{2,1,0:T(8,128)(2,1)S(1)} %slice.15.mine.moved, bf16[16,2048]{1,0:T(8,128)(2,1)S(1)} %collective-permute-done.theirs, ...), custom_call_target="tpu_custom_call" | custom-call | flops 134217728 | bytes 10485760 | tf_op jit(solution)/shard_map/near_second_a/pallas_call | solution.py:471
  10.2 0.1 constant_dynamic-update-slice_fusion.7
  10.3 2.7 %collective-permute-start.11 = (bf16[48,16,128]{2,1,0:T(8,128)(2,1)S(1)}, bf16[48,16,128]{2,1,0:T(8,128)(2,1)S(1)}, u32[]{:S(2)}, u32[]{:S(2)}) collective-permute-start(bf16[48,16,128]{2,1,0:T(8,128)(2,1)S(1)} %get-tuple-element.101), channel_id=1, source_target_pairs={{0,16},{4,20},{8,24},{12,28},{16,0},{20,4},{24,8},{28,12},{1,17},{... | collective-permute-start | bytes 589832 | tf_op jit(solution)/shard_map/ppermute | solution.py:409
  12.9 0.0 collective-permute-start.5
  12.9 0.0 collective-permute-done.1.other.refs_4_
  12.9 0.0 copy-start
  12.9 2.6 %near_second_b.1 = (f32[128,32,128]{2,1,0:T(8,128)S(1)}, f32[64,16,128]{2,1,0:T(8,128)S(1)}, s16[68,16,128]{2,1,0:T(8,128)(2,1)S(1)}, f32[32,32,128]{2,1,0:T(8,128)S(1)}, s16[68,16,128]{2,1,0:T(8,128)(2,1)S(1)}) custom-call(s32[7,512]{1,0:T(8,128)S(1)} %get-tuple-element.51.idx, ...), custom_call_target="tpu_custom_call", output_to_operand_aliasing={{0}: (3, {})} | custom-call | flops 134217728 | bytes 10485760 | tf_op jit(solution)/shard_map/near_second_b/pallas_call | solution.py:488
  15.5 1.3 %collective-permute-start.3 = (s16[68,16,128]{2,1,0:T(8,128)(2,1)S(1)}, s16[68,16,128]{2,1,0:T(8,128)(2,1)S(1)}, u32[]{:S(2)}, u32[]{:S(2)}) collective-permute-start(s16[68,16,128]{2,1,0:T(8,128)(2,1)S(1)} %get-tuple-element.61), channel_id=1, source_target_pairs={{0,4},{4,0},{8,12},{12,8},{16,20},{20,16},{24,28},{28,24},{1,5},{5... | collective-permute-start | bytes 835592 | tf_op jit(solution)/shard_map/ppermute | solution.py:409
  16.8 1.5 %collective-permute-start.4 = (s16[68,16,128]{2,1,0:T(8,128)(2,1)S(1)}, s16[68,16,128]{2,1,0:T(8,128)(2,1)S(1)}, u32[]{:S(2)}, u32[]{:S(2)}) collective-permute-start(s16[68,16,128]{2,1,0:T(8,128)(2,1)S(1)} %get-tuple-element.62), channel_id=1, source_target_pairs={{0,2},{1,3},{2,0},{3,1},{4,6},{5,7},{6,4},{7,5},{8,10},{9,11},{10,... | collective-permute-start | bytes 835592 | tf_op jit(solution)/shard_map/ppermute | solution.py:406
  18.3 0.0 collective-permute-done.5.theirs
  18.3 5.1 %far_source.1 = (bf16[256,32,128]{2,1,0:T(8,128)(2,1)S(1)}, f32[64,16,128]{2,1,0:T(8,128)S(1)}, f32[16,16,128]{2,1,0:T(8,128)S(1)}, f32[16,16,128]{2,1,0:T(8,128...) custom-call(s32[7,512]{1,0:T(8,128)S(1)} %get-tuple-element.51.idx, bf16[8,16,128]{2,1,0:T(8,128)(2,1)S(1)} %slice.16.mine, ...), custom_call_target="tpu_custom_call" | custom-call | flops 67108864 | bytes 12582912 | tf_op jit(solution)/shard_map/far_source/pallas_call | solution.py:509
  23.4 0.1 constant_dynamic-update-slice_fusion.6
  23.5 1.6 %collective-permute-start.12 = (bf16[96,16,128]{2,1,0:T(8,128)(2,1)S(1)}, bf16[96,16,128]{2,1,0:T(8,128)(2,1)S(1)}, u32[]{:S(2)}, u32[]{:S(2)}) collective-permute-start(bf16[96,16,128]{2,1,0:T(8,128)(2,1)S(1)} %get-tuple-element.98), channel_id=1, source_target_pairs={{0,8},{4,12},{8,0},{12,4},{16,24},{20,28},{24,16},{28,20},{1,9},{5... | collective-permute-start | bytes 1179656 | tf_op jit(solution)/shard_map/ppermute | solution.py:409
  25.2 0.5 collective-permute-start.7
  25.7 0.0 collective-permute-done.3.coded
  25.7 0.6 %collective-permute-start.13 = (bf16[48,16,128]{2,1,0:T(8,128)(2,1)S(1)}, bf16[48,16,128]{2,1,0:T(8,128)(2,1)S(1)}, u32[]{:S(2)}, u32[]{:S(2)}) collective-permute-start(bf16[48,16,128]{2,1,0:T(8,128)(2,1)S(1)} %bitcast.24), channel_id=1, source_target_pairs={{0,2},{1,3},{2,0},{3,1},{4,6},{5,7},{6,4},{7,5},{8,10},{9,11},{10,... | collective-permute-start | bytes 589832 | tf_op jit(solution)/shard_map/ppermute | solution.py:406
  26.3 0.2 meet_b.1
  26.5 1.6 %collective-permute-start.14 = (s16[34,16,128]{2,1,0:T(8,128)(2,1)S(1)}, s16[34,16,128]{2,1,0:T(8,128)(2,1)S(1)}, u32[]{:S(2)}, u32[]{:S(2)}) collective-permute-start(s16[34,16,128]{2,1,0:T(8,128)(2,1)S(1)} %get-tuple-element.77), channel_id=1, source_target_pairs={{0,2},{1,3},{2,0},{3,1},{4,6},{5,7},{6,4},{7,5},{8,10},{9,11},{10,... | collective-permute-start | bytes 417800 | tf_op jit(solution)/shard_map/ppermute | solution.py:406
  28.1 0.5 collective-permute-start.9
  28.6 0.1 join.1.mine
  28.7 0.7 %collective-permute-done.8.refs_2_ = f32[16,16,128]{2,1,0:T(8,128)S(1)} collective-permute-done((f32[16,16,128]{2,1,0:T(8,128)S(1)}, f32[16,16,128]{2,1,0:T(8,128)S(1)}, u32[]{:S(2)}, u32[]{:S(2)}) %collective-permute-start.8) | collective-permute-done | bytes 131104 | tf_op jit(solution)/shard_map/ppermute | solution.py:406
  29.4 0.2 collective-permute-done.9.refs_3_
  29.6 0.3 meet_a.1
  29.9 0.6 collective-permute-start.10
  30.5 3.0 %collective-permute-done.13.refs_0_ = bf16[48,16,128]{2,1,0:T(8,128)(2,1)S(1)} collective-permute-done((bf16[48,16,128]{2,1,0:T(8,128)(2,1)S(1)}, bf16[48,16,128]{2,1,0:T(8,128)(2,1)S(1)}, u32[]{:S(2)}, u32[]{:S(2)}) %collective-permute-start.13) | collective-permute-done | bytes 196640 | tf_op jit(solution)/shard_map/ppermute | solution.py:406
  33.5 1.0 %collective-permute-done.12 = bf16[96,16,128]{2,1,0:T(8,128)(2,1)S(1)} collective-permute-done((bf16[96,16,128]{2,1,0:T(8,128)(2,1)S(1)}, bf16[96,16,128]{2,1,0:T(8,128)(2,1)S(1)}, u32[]{:S(2)}, u32[]{:S(2)}) %collective-permute-start.12) | collective-permute-done | bytes 393248 | tf_op jit(solution)/shard_map/ppermute | solution.py:409
  34.5 1.0 %collective-permute-done.14.coded_b = s16[34,16,128]{2,1,0:T(8,128)(2,1)S(1)} collective-permute-done((s16[34,16,128]{2,1,0:T(8,128)(2,1)S(1)}, s16[34,16,128]{2,1,0:T(8,128)(2,1)S(1)}, u32[]{:S(2)}, u32[]{:S(2)}) %collective-permute-start.14) | collective-permute-done | bytes 139296 | tf_op jit(solution)/shard_map/ppermute | solution.py:406
  35.6 0.1 constant_dynamic-update-slice_fusion.5.everyone
  35.6 0.1 collective-permute-start.15
  35.7 0.6 %collective-permute-start.17 = (bf16[64,16,128]{2,1,0:T(8,128)(2,1)S(1)}, bf16[64,16,128]{2,1,0:T(8,128)(2,1)S(1)}, u32[]{:S(2)}, u32[]{:S(2)}) collective-permute-start(bf16[64,16,128]{2,1,0:T(8,128)(2,1)S(1)} %bitcast.21), channel_id=1, source_target_pairs={{0,2},{1,3},{2,0},{3,1},{4,6},{5,7},{6,4},{7,5},{8,10},{9,11},{10,... | collective-permute-start | bytes 786440 | tf_op jit(solution)/shard_map/ppermute | solution.py:406
  36.3 0.9 %collective-permute-done.15.theirs = bf16[64,16,128]{2,1,0:T(8,128)(2,1)S(1)} collective-permute-done((bf16[64,16,128]{2,1,0:T(8,128)(2,1)S(1)}, bf16[64,16,128]{2,1,0:T(8,128)(2,1)S(1)}, u32[]{:S(2)}, u32[]{:S(2)}) %collective-permute-start.15) | collective-permute-done | bytes 262176 | tf_op jit(solution)/shard_map/ppermute | solution.py:406
  37.2 4.2 %far_target.1 = (f32[8,16,128]{2,1,0:T(8,128)S(1)}, f32[8,16,128]{2,1,0:T(8,128)S(1)}) custom-call(s32[7,512]{1,0:T(8,128)S(1)} %get-tuple-element.51.idx, bf16[192,16,128]{2,1,0:T(8,128)(2,1)S(1)} %constant_dynamic-update-slice_fusion.5.everyone, bf16[64,16,128]{2,1,0:T(8,128)(2,1)S(1)} %collective-permute-done.15.theirs, ...), custom_call_target="tpu_custom_call" | custom-call | bytes 1048576 | tf_op jit(solution)/shard_map/far_target/pallas_call | solution.py:583
  41.5 0.3 meet.1
  41.8 0.6 %collective-permute-start.16 = (s16[51,16,128]{2,1,0:T(8,128)(2,1)S(1)}, s16[51,16,128]{2,1,0:T(8,128)(2,1)S(1)}, u32[]{:S(2)}, u32[]{:S(2)}) collective-permute-start(s16[51,16,128]{2,1,0:T(8,128)(2,1)S(1)} %get-tuple-element.86), channel_id=1, source_target_pairs={{0,8},{4,12},{8,0},{12,4},{16,24},{20,28},{24,16},{28,20},{1,9},{5... | collective-permute-start | bytes 626696 | tf_op jit(solution)/shard_map/ppermute | solution.py:409
  42.4 2.1 %collective-permute-done.17.refs_1_ = bf16[64,16,128]{2,1,0:T(8,128)(2,1)S(1)} collective-permute-done((bf16[64,16,128]{2,1,0:T(8,128)(2,1)S(1)}, bf16[64,16,128]{2,1,0:T(8,128)(2,1)S(1)}, u32[]{:S(2)}, u32[]{:S(2)}) %collective-permute-start.17) | collective-permute-done | bytes 262176 | tf_op jit(solution)/shard_map/ppermute | solution.py:406
  44.5 5.5 %near_first.1 = (f32[16,16,128]{2,1,0:T(8,128)S(1)}, f32[16,16,128]{2,1,0:T(8,128)S(1)}) custom-call(s32[7,512]{1,0:T(8,128)S(1)} %get-tuple-element.51.idx, bf16[192,16,128]{2,1,0:T(8,128)(2,1)S(1)} %constant_dynamic-update-slice_fusion.5.everyone, bf16[16,32,128]{2,1,0:T(8,128)(2,1)S(1)} %get-tuple-element.54.both, ...), custom_call_target="tpu_custom_call" | custom-call | flops 268435456 | bytes 20971520 | tf_op jit(solution)/shard_map/near_first/pallas_call | solution.py:628
  50.1 0.2 add.1
  50.2 0.6 %collective-permute-start.19 = (f32[16,16,128]{2,1,0:T(8,128)S(1)}, f32[16,16,128]{2,1,0:T(8,128)S(1)}, u32[]{:S(2)}, u32[]{:S(2)}) collective-permute-start(f32[16,16,128]{2,1,0:T(8,128)S(1)} %get-tuple-element.95), channel_id=1, source_target_pairs={{0,2},{1,3},{2,0},{3,1},{4,6},{5,7},{6,4},{7,5},{8,10},{9,11},{10,... | collective-permute-start | bytes 393224 | tf_op jit(solution)/shard_map/ppermute | solution.py:406
  50.9 1.7 %collective-permute-start.18 = (s16[26,16,128]{2,1,0:T(8,128)(2,1)S(1)}, s16[26,16,128]{2,1,0:T(8,128)(2,1)S(1)}, u32[]{:S(2)}, u32[]{:S(2)}) collective-permute-start(s16[26,16,128]{2,1,0:T(8,128)(2,1)S(1)} %get-tuple-element.93), channel_id=1, source_target_pairs={{0,16},{4,20},{8,24},{12,28},{16,0},{20,4},{24,8},{28,12},{1,17},{... | collective-permute-start | bytes 319496 | tf_op jit(solution)/shard_map/ppermute | solution.py:409
  52.5 0.4 self.1.own
  52.9 0.9 %collective-permute-done.20.target_other = f32[8,16,128]{2,1,0:T(8,128)S(1)} collective-permute-done((f32[8,16,128]{2,1,0:T(8,128)S(1)}, f32[8,16,128]{2,1,0:T(8,128)S(1)}, u32[]{:S(2)}, u32[]{:S(2)}) %collective-permute-start.20) | collective-permute-done | bytes 65568 | tf_op jit(solution)/shard_map/ppermute | solution.py:406
  53.8 4.6 %collective-permute-done.18.coded = s16[26,16,128]{2,1,0:T(8,128)(2,1)S(1)} collective-permute-done((s16[26,16,128]{2,1,0:T(8,128)(2,1)S(1)}, s16[26,16,128]{2,1,0:T(8,128)(2,1)S(1)}, u32[]{:S(2)}, u32[]{:S(2)}) %collective-permute-start.18) | collective-permute-done | bytes 106528 | tf_op jit(solution)/shard_map/ppermute | solution.py:409
  58.4 1.5 %final.1 = f32[16,2048]{1,0:T(8,128)} custom-call(s32[16]{0:T(128)S(1)} %copy-done.3, f32[24,16,128]{2,1,0:T(8,128)S(1)} %get-tuple-element.87.mine, s16[26,16,128]{2,1,0:T(8,128)(2,1)S(1)} %collective-permute-done.18.coded, f32[16,16,128]{2,1,0:T(8,128)S(1)} %get-tuple-element.94.first, f32[16,16,128]{2,1,0:T(8,128)S(1)} %collective-permute-done.19.first_other, ...), custom_call_target="tpu_custom_call" | custom-call | tf_op jit(solution)/shard_map/final/pallas_call | solution.py:655
  (24 shorter events, 0.1 us)
Async XLA Ops:
  0.0 12.9 %collective-permute-start.1 = (bf16[128,128,128]{2,1,0:T(8,128)(2,1)}, bf16[128,128,128]{2,1,0:T(8,128)(2,1)S(1)}, u32[]{:S(2)}, u32[]{:S(2)}) collective-permute-start(bf16[128,128,128]{2,1,0:T(8,128)(2,1)} %rest.1), channel_id=1, source_target_pairs={{0,1},{1,0},{2,3},{3,2},{4,5},{5,4},{6,7},{7,6},{8,9},{9,8},{10,11... | collective-permute-start | bytes 12582920 | tf_op jit(solution)/shard_map/ppermute | solution.py:406
  0.5 6.0 %collective-permute-start = (bf16[16,2048]{1,0:T(8,128)(2,1)}, bf16[16,2048]{1,0:T(8,128)(2,1)S(1)}, u32[]{:S(2)}, u32[]{:S(2)}) collective-permute-start(bf16[16,2048]{1,0:T(8,128)(2,1)} %charges_in.1), channel_id=1, source_target_pairs={{0,2},{1,3},{2,0},{3,1},{4,6},{5,7},{6,4},{7,5},{8,10},{9,11},{10,... | collective-permute-start | bytes 196616 | tf_op jit(solution)/shard_map/ppermute | solution.py:406
  4.8 5.4 %collective-permute-start.2 = (bf16[24,16,128]{2,1,0:T(8,128)(2,1)S(1)}, bf16[24,16,128]{2,1,0:T(8,128)(2,1)S(1)}, u32[]{:S(2)}, u32[]{:S(2)}) collective-permute-start(bf16[24,16,128]{2,1,0:T(8,128)(2,1)S(1)} %get-tuple-element.52), channel_id=1, source_target_pairs={{0,4},{4,0},{8,12},{12,8},{16,20},{20,16},{24,28},{28,24},{1,5},{5... | collective-permute-start | bytes 294920 | tf_op jit(solution)/shard_map/ppermute | solution.py:409
  10.3 13.1 %collective-permute-start.11 = (bf16[48,16,128]{2,1,0:T(8,128)(2,1)S(1)}, bf16[48,16,128]{2,1,0:T(8,128)(2,1)S(1)}, u32[]{:S(2)}, u32[]{:S(2)}) collective-permute-start(bf16[48,16,128]{2,1,0:T(8,128)(2,1)S(1)} %get-tuple-element.101), channel_id=1, source_target_pairs={{0,16},{4,20},{8,24},{12,28},{16,0},{20,4},{24,8},{28,12},{1,17},{... | collective-permute-start | bytes 589832 | tf_op jit(solution)/shard_map/ppermute | solution.py:409
  12.9 5.4 %collective-permute-start.5 = (bf16[8,16,128]{2,1,0:T(8,128)(2,1)S(1)}, bf16[8,16,128]{2,1,0:T(8,128)(2,1)S(1)}, u32[]{:S(2)}, u32[]{:S(2)}) collective-permute-start(bf16[8,16,128]{2,1,0:T(8,128)(2,1)S(1)} %slice.16.mine), channel_id=1, source_target_pairs={{0,1},{1,0},{2,3},{3,2},{4,5},{5,4},{6,7},{7,6},{8,9},{9,8},{10,11... | collective-permute-start | bytes 98312 | tf_op jit(solution)/shard_map/ppermute | solution.py:406
  12.9 5.4 %copy-start = (bf16[512,64,64]{0,2,1:T(8,128)(2,1)S(1)}, bf16[512,64,64]{0,2,1:T(8,128)(2,1)}, u32[]{:S(2)}) copy-start(bf16[512,64,64]{0,2,1:T(8,128)(2,1)} %param.19) | copy-start | bytes 12582916
  15.5 10.2 %collective-permute-start.3 = (s16[68,16,128]{2,1,0:T(8,128)(2,1)S(1)}, s16[68,16,128]{2,1,0:T(8,128)(2,1)S(1)}, u32[]{:S(2)}, u32[]{:S(2)}) collective-permute-start(s16[68,16,128]{2,1,0:T(8,128)(2,1)S(1)} %get-tuple-element.61), channel_id=1, source_target_pairs={{0,4},{4,0},{8,12},{12,8},{16,20},{20,16},{24,28},{28,24},{1,5},{5... | collective-permute-start | bytes 835592 | tf_op jit(solution)/shard_map/ppermute | solution.py:409
  16.8 9.5 %collective-permute-start.4 = (s16[68,16,128]{2,1,0:T(8,128)(2,1)S(1)}, s16[68,16,128]{2,1,0:T(8,128)(2,1)S(1)}, u32[]{:S(2)}, u32[]{:S(2)}) collective-permute-start(s16[68,16,128]{2,1,0:T(8,128)(2,1)S(1)} %get-tuple-element.62), channel_id=1, source_target_pairs={{0,2},{1,3},{2,0},{3,1},{4,6},{5,7},{6,4},{7,5},{8,10},{9,11},{10,... | collective-permute-start | bytes 835592 | tf_op jit(solution)/shard_map/ppermute | solution.py:406
  23.5 11.0 %collective-permute-start.12 = (bf16[96,16,128]{2,1,0:T(8,128)(2,1)S(1)}, bf16[96,16,128]{2,1,0:T(8,128)(2,1)S(1)}, u32[]{:S(2)}, u32[]{:S(2)}) collective-permute-start(bf16[96,16,128]{2,1,0:T(8,128)(2,1)S(1)} %get-tuple-element.98), channel_id=1, source_target_pairs={{0,8},{4,12},{8,0},{12,4},{16,24},{20,28},{24,16},{28,20},{1,9},{5... | collective-permute-start | bytes 1179656 | tf_op jit(solution)/shard_map/ppermute | solution.py:409
  25.2 2.9 %collective-permute-start.6 = (f32[16,16,128]{2,1,0:T(8,128)S(1)}, f32[16,16,128]{2,1,0:T(8,128)S(1)}, u32[]{:S(2)}, u32[]{:S(2)}) collective-permute-start(f32[16,16,128]{2,1,0:T(8,128)S(1)} %get-tuple-element.69), channel_id=1, source_target_pairs={{0,1},{1,0},{2,3},{3,2},{4,5},{5,4},{6,7},{7,6},{8,9},{9,8},{10,11... | collective-permute-start | bytes 393224 | tf_op jit(solution)/shard_map/ppermute | solution.py:406
  25.2 2.9 %collective-permute-start.7 = (f32[16,16,128]{2,1,0:T(8,128)S(1)}, f32[16,16,128]{2,1,0:T(8,128)S(1)}, u32[]{:S(2)}, u32[]{:S(2)}) collective-permute-start(f32[16,16,128]{2,1,0:T(8,128)S(1)} %get-tuple-element.70), channel_id=1, source_target_pairs={{0,1},{1,0},{2,3},{3,2},{4,5},{5,4},{6,7},{7,6},{8,9},{9,8},{10,11... | collective-permute-start | bytes 393224 | tf_op jit(solution)/shard_map/ppermute | solution.py:406
  25.7 7.8 %collective-permute-start.13 = (bf16[48,16,128]{2,1,0:T(8,128)(2,1)S(1)}, bf16[48,16,128]{2,1,0:T(8,128)(2,1)S(1)}, u32[]{:S(2)}, u32[]{:S(2)}) collective-permute-start(bf16[48,16,128]{2,1,0:T(8,128)(2,1)S(1)} %bitcast.24), channel_id=1, source_target_pairs={{0,2},{1,3},{2,0},{3,1},{4,6},{5,7},{6,4},{7,5},{8,10},{9,11},{10,... | collective-permute-start | bytes 589832 | tf_op jit(solution)/shard_map/ppermute | solution.py:406
  26.5 9.0 %collective-permute-start.14 = (s16[34,16,128]{2,1,0:T(8,128)(2,1)S(1)}, s16[34,16,128]{2,1,0:T(8,128)(2,1)S(1)}, u32[]{:S(2)}, u32[]{:S(2)}) collective-permute-start(s16[34,16,128]{2,1,0:T(8,128)(2,1)S(1)} %get-tuple-element.77), channel_id=1, source_target_pairs={{0,2},{1,3},{2,0},{3,1},{4,6},{5,7},{6,4},{7,5},{8,10},{9,11},{10,... | collective-permute-start | bytes 417800 | tf_op jit(solution)/shard_map/ppermute | solution.py:406
  28.1 1.3 %collective-permute-start.8 = (f32[16,16,128]{2,1,0:T(8,128)S(1)}, f32[16,16,128]{2,1,0:T(8,128)S(1)}, u32[]{:S(2)}, u32[]{:S(2)}) collective-permute-start(f32[16,16,128]{2,1,0:T(8,128)S(1)} %get-tuple-element.71), channel_id=1, source_target_pairs={{0,1},{1,0},{2,3},{3,2},{4,5},{5,4},{6,7},{7,6},{8,9},{9,8},{10,11... | collective-permute-start | bytes 393224 | tf_op jit(solution)/shard_map/ppermute | solution.py:406
  28.1 1.5 %collective-permute-start.9 = (f32[16,16,128]{2,1,0:T(8,128)S(1)}, f32[16,16,128]{2,1,0:T(8,128)S(1)}, u32[]{:S(2)}, u32[]{:S(2)}) collective-permute-start(f32[16,16,128]{2,1,0:T(8,128)S(1)} %get-tuple-element.72), channel_id=1, source_target_pairs={{0,1},{1,0},{2,3},{3,2},{4,5},{5,4},{6,7},{7,6},{8,9},{9,8},{10,11... | collective-permute-start | bytes 393224 | tf_op jit(solution)/shard_map/ppermute | solution.py:406
  29.9 11.5 %collective-permute-start.10 = (s16[68,16,128]{2,1,0:T(8,128)(2,1)S(1)}, s16[68,16,128]{2,1,0:T(8,128)(2,1)S(1)}, u32[]{:S(2)}, u32[]{:S(2)}) collective-permute-start(s16[68,16,128]{2,1,0:T(8,128)(2,1)S(1)} %get-tuple-element.74), channel_id=1, source_target_pairs={{0,4},{4,0},{8,12},{12,8},{16,20},{20,16},{24,28},{28,24},{1,5},{5... | collective-permute-start | bytes 835592 | tf_op jit(solution)/shard_map/ppermute | solution.py:409
  35.6 1.6 %collective-permute-start.15 = (bf16[64,16,128]{2,1,0:T(8,128)(2,1)S(1)}, bf16[64,16,128]{2,1,0:T(8,128)(2,1)S(1)}, u32[]{:S(2)}, u32[]{:S(2)}) collective-permute-start(bf16[64,16,128]{2,1,0:T(8,128)(2,1)S(1)} %bitcast.22), channel_id=1, source_target_pairs={{0,1},{1,0},{2,3},{3,2},{4,5},{5,4},{6,7},{7,6},{8,9},{9,8},{10,11... | collective-permute-start | bytes 786440 | tf_op jit(solution)/shard_map/ppermute | solution.py:406
  35.7 8.8 %collective-permute-start.17 = (bf16[64,16,128]{2,1,0:T(8,128)(2,1)S(1)}, bf16[64,16,128]{2,1,0:T(8,128)(2,1)S(1)}, u32[]{:S(2)}, u32[]{:S(2)}) collective-permute-start(bf16[64,16,128]{2,1,0:T(8,128)(2,1)S(1)} %bitcast.21), channel_id=1, source_target_pairs={{0,2},{1,3},{2,0},{3,1},{4,6},{5,7},{6,4},{7,5},{8,10},{9,11},{10,... | collective-permute-start | bytes 786440 | tf_op jit(solution)/shard_map/ppermute | solution.py:406
  41.8 8.3 %collective-permute-start.16 = (s16[51,16,128]{2,1,0:T(8,128)(2,1)S(1)}, s16[51,16,128]{2,1,0:T(8,128)(2,1)S(1)}, u32[]{:S(2)}, u32[]{:S(2)}) collective-permute-start(s16[51,16,128]{2,1,0:T(8,128)(2,1)S(1)} %get-tuple-element.86), channel_id=1, source_target_pairs={{0,8},{4,12},{8,0},{12,4},{16,24},{20,28},{24,16},{28,20},{1,9},{5... | collective-permute-start | bytes 626696 | tf_op jit(solution)/shard_map/ppermute | solution.py:409
  44.5 8.0 %copy-start.2 = (bf16[16,128,128]{2,1,0:T(8,128)(2,1)S(1)}, bf16[16,128,128]{2,1,0:T(8,128)(2,1)}, u32[]{:S(2)}) copy-start(bf16[16,128,128]{2,1,0:T(8,128)(2,1)} %self_tiles.1) | copy-start | bytes 1572868
  44.5 13.8 %copy-start.1 = (bf16[16,128,64]{1,2,0:T(8,128)(2,1)S(1)}, bf16[16,128,64]{1,2,0:T(8,128)(2,1)}, u32[]{:S(2)}) copy-start(bf16[16,128,64]{1,2,0:T(8,128)(2,1)} %param.13) | copy-start | bytes 786436
  44.5 13.8 %copy-start.3 = (s32[16]{0:T(128)S(1)}, s32[16]{0:T(128)}, u32[]{:S(2)}) copy-start(s32[16]{0:T(128)} %counts.1) | copy-start | bytes 196
  50.2 8.1 %collective-permute-start.19 = (f32[16,16,128]{2,1,0:T(8,128)S(1)}, f32[16,16,128]{2,1,0:T(8,128)S(1)}, u32[]{:S(2)}, u32[]{:S(2)}) collective-permute-start(f32[16,16,128]{2,1,0:T(8,128)S(1)} %get-tuple-element.95), channel_id=1, source_target_pairs={{0,2},{1,3},{2,0},{3,1},{4,6},{5,7},{6,4},{7,5},{8,10},{9,11},{10,... | collective-permute-start | bytes 393224 | tf_op jit(solution)/shard_map/ppermute | solution.py:406
  50.9 7.5 %collective-permute-start.18 = (s16[26,16,128]{2,1,0:T(8,128)(2,1)S(1)}, s16[26,16,128]{2,1,0:T(8,128)(2,1)S(1)}, u32[]{:S(2)}, u32[]{:S(2)}) collective-permute-start(s16[26,16,128]{2,1,0:T(8,128)(2,1)S(1)} %get-tuple-element.93), channel_id=1, source_target_pairs={{0,16},{4,20},{8,24},{12,28},{16,0},{20,4},{24,8},{28,12},{1,17},{... | collective-permute-start | bytes 319496 | tf_op jit(solution)/shard_map/ppermute | solution.py:409
  52.5 1.3 %collective-permute-start.20 = (f32[8,16,128]{2,1,0:T(8,128)S(1)}, f32[8,16,128]{2,1,0:T(8,128)S(1)}, u32[]{:S(2)}, u32[]{:S(2)}) collective-permute-start(f32[8,16,128]{2,1,0:T(8,128)S(1)} %get-tuple-element.81), channel_id=1, source_target_pairs={{0,1},{1,0},{2,3},{3,2},{4,5},{5,4},{6,7},{7,6},{8,9},{9,8},{10,11... | collective-permute-start | bytes 196616 | tf_op jit(solution)/shard_map/ppermute | solution.py:406

commit v5 on v4

--- a/solution.py
+++ b/solution.py
@@ -8,6 +8,7 @@
 from jax.sharding import PartitionSpec as P
 
 F32, BF16, I16, I32 = jnp.float32, jnp.bfloat16, jnp.int16, jnp.int32
+REACH = 48
 GROUP = 16
 TOP = 32767.0
 VMEM = pl.BlockSpec(memory_space=pltpu.VMEM)
@@ -69,14 +70,14 @@
 
 def prep_kernel(
     place, counts_in, charges_in, basis_in, near_first, near_second, far_source, far_target, tiles_in,
-    out, idx, tiles, counts, charges, basis_t, lists, counts_row, sems,
+    out, at_second, at_first, at_source, at_target, tiles, near_zero, counts, charges, basis_t, lists, counts_row, sems,
 ):
-    pairs = [(counts_in.at[0], counts), (charges_in, charges), (basis_in, basis_t), (counts_in, counts_row)]
-    pairs += [
+    moves = [(counts_in.at[0], counts), (charges_in, charges), (basis_in, basis_t), (counts_in, counts_row)]
+    moves += [
         (src, lists.at[pl.ds(i, 1)]) for i, src in enumerate((near_first, near_second, far_source, far_target))
     ]
-    pairs += [(tiles_in.at[pl.ds(0, tiles.shape[0])], tiles)]
-    copies = [pltpu.make_async_copy(src, dst, sems.at[i]) for i, (src, dst) in enumerate(pairs)]
+    moves += [(tiles_in.at[pl.ds(0, tiles.shape[0])], tiles)]
+    copies = [pltpu.make_async_copy(src, dst, sems.at[i]) for i, (src, dst) in enumerate(moves)]
     for copy in copies:
         copy.start()
     for copy in copies[:-1]:
@@ -92,62 +93,72 @@
         moments.append(dot(x, basis_t[c], TRN))
     for k in range(cells // 2):
         out[cells + k] = jnp.concatenate(moments[2 * k : 2 * k + 2], axis=1).astype(BF16)
-    first, second, source, target = (lists[i : i + 1, :] for i in range(4))
-    for row, value in (
-        (FIRST, lax.rem(first, cells)),
-        (SECOND, place(second, 0)),
-        (SECOND_REDUCE, place(second, 1)),
-        (SOURCE, place(source, 0)),
-        (SOURCE_REDUCE, place(source, 1)),
-        (TARGET, lax.rem(target, cells)),
-    ):
-        idx[row : row + 1, :] = value
-    idx[COUNT : COUNT + 1, :cells] = counts_row[...]
+    rank = lax.axis_index("rhs")
+    pairs = tiles_in.shape[0]
+    for flip in range(2):
+        span = pl.ds(pl.multiple_of((rank ^ flip) * pairs, pairs), pairs)
+        to = slice(flip * pairs, (flip + 1) * pairs)
+        first, second = lists[0:1, span], lists[1:2, span]
+        for at in (at_second, at_first):
+            at[0:1, to] = lax.rem(first, cells)
+        at_second[1:2, to] = place(second, 1)
+        at_first[1:2, to] = place(second, 0)
+    at_second[2:3, :cells] = counts_row[...]
+    half = lists.shape[1] // 2
+    span = pl.ds(pl.multiple_of((rank & 1) * half, half), half)
+    source, target = lists[2:3, span], lists[3:4, span]
+    for at, reduce in ((at_source, 1), (at_target, 0)):
+        at[0:1, :] = lax.rem(target, cells)
+        at[1:2, :] = place(source, reduce)
+    near_zero[...] = jnp.zeros_like(near_zero)
     copies[-1].wait()
 
 
-FIRST, SECOND, SECOND_REDUCE, SOURCE, SOURCE_REDUCE, TARGET, COUNT = range(7)
 PITCH = 136
 FAR_UNROLL = 64
-FAR_STEPS = 2
 NEAR_UNROLL = 64
 PARTS = 4
 
 
-def far_source_kernel(idx, mine, theirs, tiles, turned, keep, *refs):
-    *sends, flip, lhs, acc = refs
-    rows, lanes = mine.shape[1:]
-    half = lanes // 2
+def far_sources(step, idx, mine, theirs, tiles, turned, acc, flip, lhs):
+    half = mine.shape[2] // 2
     pairs = half // 2
-    total = turned.shape[0]
-    chunk = total // FAR_STEPS
-    acc[...] = jnp.zeros_like(acc)
+    chunk = turned.shape[0]
     for k in range(mine.shape[0]):
         x, y = mine[k], theirs[k]
         for h in range(2):
             at = h * half
             lhs[2 * k + h] = jnp.concatenate([x[:, at : at + half], y[:, at : at + half]], axis=0)
-    for step in range(FAR_STEPS):
-        base = (lax.axis_index("rhs") & 1) * total + step * chunk
-        span = pl.ds(pl.multiple_of(base, chunk), chunk)
-        for i in range(pairs):
-            both = [tiles[(i + h * pairs) * half : (i + h * pairs + 1) * half, span] for h in range(2)]
-            flip[step, i * PITCH : i * PITCH + chunk, :] = jnp.concatenate(both, axis=0).astype(F32).T
-
-        def work(g, _, step=step, base=base):
-            sums = []
-            at = g * FAR_UNROLL
-            for u in range(FAR_UNROLL):
-                w = flip[step, pl.ds(at + u, pairs, stride=PITCH), :]
-                turned[step * chunk + at + u] = w.astype(BF16)
-                moved = pltpu.roll(w, half, 1)
-                w = jnp.concatenate([w[:, :half], moved[:, :half]], axis=0).astype(BF16)
-                sums.append(dot(lhs[idx[TARGET, base + at + u]], w, NAT))
-            for u in range(FAR_UNROLL):
-                acc[idx[SOURCE_REDUCE, base + at + u]] += sums[u]
-            return 0
-
-        lax.fori_loop(0, chunk // FAR_UNROLL, work, 0)
+    span = pl.ds(pl.multiple_of((lax.axis_index("rhs") & 1) * 2 * chunk + step * chunk, chunk), chunk)
+    for i in range(pairs):
+        both = [tiles[(i + h * pairs) * half : (i + h * pairs + 1) * half, span] for h in range(2)]
+        flip[i * PITCH : i * PITCH + chunk, :] = jnp.concatenate(both, axis=0).astype(F32).T
+
+    def work(g, _):
+        sums = []
+        at = g * FAR_UNROLL
+        for u in range(FAR_UNROLL):
+            w = flip[pl.ds(at + u, pairs, stride=PITCH), :]
+            turned[at + u] = w.astype(BF16)
+            moved = pltpu.roll(w, half, 1)
+            w = jnp.concatenate([w[:, :half], moved[:, :half]], axis=0).astype(BF16)
+            sums.append(dot(lhs[idx[0, step * chunk + at + u]], w, NAT))
+        for u in range(FAR_UNROLL):
+            acc[idx[1, step * chunk + at + u]] += sums[u]
+        return 0
+
+    lax.fori_loop(0, chunk // FAR_UNROLL, work, 0)
+
+
+def far_source_a_kernel(idx, mine, theirs, tiles, turned, acc, flip, lhs):
+    acc[...] = jnp.zeros_like(acc)
+    far_sources(0, idx, mine, theirs, tiles, turned, acc, flip, lhs)
+
+
+def far_source_b_kernel(idx, mine, theirs, tiles, before, turned, acc, keep, *refs):
+    *sends, flip, lhs = refs
+    rows = mine.shape[1]
+    far_sources(1, idx, mine, theirs, tiles, turned, acc, flip, lhs)
     count = sends[0].shape[0]
     for q, send in enumerate(sends):
 
@@ -162,10 +173,10 @@
         lax.fori_loop(0, count // 4, fold, 0)
 
 
-def far_target_kernel(stride, cells, idx, everyone, theirs, turned, keep, send, lhs, acc):
+def far_target_kernel(stride, cells, idx, everyone, theirs, turned_a, turned_b, keep, send, lhs, acc):
     rows, lanes = everyone.shape[1], everyone.shape[2]
     half = lanes // 2
-    chunk = turned.shape[0]
+    chunk = turned_a.shape[0]
     owners = everyone.shape[0] // stride
     acc[...] = jnp.zeros_like(acc)
     low = lax.broadcasted_iota(I32, (2 * rows, lanes), 1) < half
@@ -181,18 +192,18 @@
         return 0
 
     lax.fori_loop(0, owners, spread, 0)
-    base = (lax.axis_index("rhs") & 1) * chunk
-
-    def work(g, _):
-        sums = []
-        for u in range(FAR_UNROLL):
-            e = g * FAR_UNROLL + u
-            sums.append(dot(lhs[idx[SOURCE, base + e]], turned[e], TRN))
-        for u in range(FAR_UNROLL):
-            acc[idx[TARGET, base + g * FAR_UNROLL + u]] += sums[u]
-        return 0
-
-    lax.fori_loop(0, chunk // FAR_UNROLL, work, 0)
+    for step, turned in enumerate((turned_a, turned_b)):
+
+        def work(g, _, base=step * chunk, turned=turned):
+            sums = []
+            for u in range(FAR_UNROLL):
+                e = g * FAR_UNROLL + u
+                sums.append(dot(lhs[idx[1, base + e]], turned[e], TRN))
+            for u in range(FAR_UNROLL):
+                acc[idx[0, base + g * FAR_UNROLL + u]] += sums[u]
+            return 0
+
+        lax.fori_loop(0, chunk // FAR_UNROLL, work, 0)
     for k in range(cells // 2):
         a, b = acc[2 * k], acc[2 * k + 1]
         for r, out in enumerate((keep, send)):
@@ -200,32 +211,30 @@
             out[k] = jnp.concatenate([x[i : i + rows] for x in (a, b) for i in at], axis=1)
 
 
-def near_loop(idx, lhs, lhs_at, tiles, flip, first, pairs, dims, acc, acc_at):
+def near_loop(idx, lhs, lhs_at, tiles, first, dims, acc, acc_at):
     count = tiles.shape[0]
-    base = (lax.axis_index("rhs") ^ flip) * pairs + first
     group = min(NEAR_UNROLL, count)
     for low in range(0, count, group):
-        span = range(low, low + group)
-        sums = [dot(lhs[idx[lhs_at, base + n]], tiles[n], dims) for n in span]
+        span = range(low, min(low + group, count))
+        sums = [dot(lhs[idx[lhs_at, first + n]], tiles[n], dims) for n in span]
         for n in span:
-            acc[idx[acc_at, base + n]] += sums[n - low]
-
-
-def near_second_a_kernel(idx, mine, theirs, tiles, rest, acc, both, tiles_high, sem):
+            acc[idx[acc_at, first + n]] += sums[n - low]
+
+
+def near_second_a_kernel(idx, mine, theirs, tiles, rest, zero, acc, both, tiles_high, sem):
     rows, size = mine.shape[1:]
 
     half, pairs = tiles.shape[0], rest.shape[0]
     copy = pltpu.make_async_copy(rest.at[pl.ds(half, pairs - half)], tiles_high, sem)
     copy.start()
-    acc[...] = jnp.zeros_like(acc)
     lane = lax.broadcasted_iota(I32, (rows, size), 1)
     for c in range(both.shape[0]):
         x = theirs[:, c * size : (c + 1) * size]
-        x = jnp.where(lane < idx[COUNT, c], x, jnp.zeros_like(x))
+        x = jnp.where(lane < idx[2, c], x, jnp.zeros_like(x))
         both[c] = jnp.concatenate([mine[c], x], axis=0)
-    near_loop(idx, both, FIRST, tiles, 0, 0, pairs, NAT, acc, SECOND_REDUCE)
+    near_loop(idx, both, 0, tiles, 0, NAT, acc, 1)
     copy.wait()
-    near_loop(idx, both, FIRST, tiles_high, 0, half, pairs, NAT, acc, SECOND_REDUCE)
+    near_loop(idx, both, 0, tiles_high, half, NAT, acc, 1)
 
 
 def near_second_b_kernel(
@@ -235,7 +244,7 @@
     half = cells // 2
     owners = acc.shape[0] // cells
     stay = keep_b.shape[0] // half
-    near_loop(idx, both, FIRST, other, 1, 0, other.shape[0], NAT, acc, SECOND_REDUCE)
+    near_loop(idx, both, 0, other, other.shape[0], NAT, acc, 1)
     encode(lambda o, c: acc[o * cells + c, rows:, :], send_a, owners, half, peak, inv)
 
     def part_b(o, i):
@@ -257,29 +266,22 @@
     lax.fori_loop(0, stay, own_b, 0)
 
 
-def near_first_kernel(stride, cells, starts, idx, everyone, both, *refs):
-    *parts, tiles, tiles_high, other, keep, send, lhs, acc = refs
+def near_first_kernel(stride, cells, places, idx, everyone, both, *refs):
+    *parts, tiles, tiles_high, other, keep, send, lhs, acc, peak, inv = refs
     rows = everyone.shape[1]
 
     acc[...] = jnp.zeros_like(acc)
     lhs[:cells] = both[...]
-    for start, part in zip(starts, parts):
-        count = part.shape[0] // cells
-
-        def fill(o, _, part=part, start=start):
+    for part, at in zip(parts, places):
+        for i, p in enumerate(at):
             for c in range(cells):
-                at = start + o
-                lhs[at * cells + c] = jnp.concatenate([everyone[at * stride + c], part[o * cells + c]], axis=0)
-            return 0
-
-        lax.fori_loop(0, count, fill, 0)
-    pairs = other.shape[0]
-    near_loop(idx, lhs, SECOND, tiles, 0, 0, pairs, TRN, acc, FIRST)
-    near_loop(idx, lhs, SECOND, tiles_high, 0, tiles.shape[0], pairs, TRN, acc, FIRST)
-    near_loop(idx, lhs, SECOND, other, 1, 0, pairs, TRN, acc, FIRST)
+                lhs[p * cells + c] = jnp.concatenate([everyone[p * stride + c], part[i * cells + c]], axis=0)
+    near_loop(idx, lhs, 1, tiles, 0, TRN, acc, 0)
+    near_loop(idx, lhs, 1, tiles_high, tiles.shape[0], TRN, acc, 0)
+    near_loop(idx, lhs, 1, other, other.shape[0], TRN, acc, 0)
     for c in range(cells):
         keep[c] = acc[c, :rows, :]
-        send[c] = acc[c, rows:, :]
+    encode(lambda o, c: acc[c, rows:, :], send, 1, cells, peak, inv)
 
 
 def join_kernel(mine, coded, out, scale):
@@ -357,18 +359,19 @@
 
 
 def final_kernel(
-    counts, mine, coded, first, first_other, target, target_other, own, basis_t, out, scale
+    counts, mine, coded, first, first_other, target, target_other, own, basis_t, out, scale, first_scale
 ):
     cells, terms, size = basis_t.shape
     rows = out.shape[0]
     decode_scales(coded, mine.shape[0], scale)
+    decode_scales(first_other, cells, first_scale)
     lane = lax.broadcasted_iota(I32, (rows, size), 1)
     for k in range(cells // 2):
         b = cells + k
         fields = (mine[b] + decode(coded, scale, b) + target[k] + target_other[k]).astype(BF16)
         for h in range(2):
             c = 2 * k + h
-            near = mine[c] + decode(coded, scale, c) + first[c] + first_other[c]
+            near = mine[c] + decode(coded, scale, c) + first[c] + decode(first_other, first_scale, c)
             far = dot(fields[:, h * terms : (h + 1) * terms], basis_t[c], NAT)
             total = near + far + own[c]
             out[:, c * size : (c + 1) * size] = jnp.where(lane < counts[c], total, jnp.zeros_like(total))
@@ -402,6 +405,14 @@
     stride = cells + halfc
     total = blks * cells
 
+    def reached(at):
+        mask = sum(((at >> s) & 1) << bit for s, bit in enumerate(gather_order))
+        gaps = [(o ^ mask) - o for o in range(blks)]
+        return min(min(g % blks, -g % blks) for g in gaps) <= -(-REACH // cells)
+
+    early = [at for at in range(1, blks // 2) if reached(at)]
+    late = [at for at in range(blks // 2, blks) if reached(at)]
+
     def swap_rank(x, d):
         return lax.ppermute(x, "rhs", [(i, i ^ d) for i in range(ranks)])
 
@@ -426,23 +437,32 @@
     def whole(n, r=rows):
         return pl.BlockSpec((n, r, size), lambda i, *_: (0, 0, 0))
 
-    def owners(x, low, high, begin, end):
-        return x.reshape(-1, stride, rows, size)[low:high, begin:end].reshape(-1, rows, size)
-
+    def owners(x, places, begin, end):
+        x = x.reshape(-1, stride, rows, size)
+        runs = []
+        for at in places:
+            if runs and runs[-1][1] == at:
+                runs[-1][1] = at + 1
+            else:
+                runs.append([at, at + 1])
+        return jnp.concatenate([x[low:high, begin:end] for low, high in runs], axis=0).reshape(-1, rows, size)
+
+    near_acc = shape(total, F32, 2 * rows)
     other_tiles = swap_rank(near_tiles, 1)
     charge_other = swap_rank(charges, 2)
     basis_t = jnp.swapaxes(basis, 1, 2)
 
     width = max(near_first.shape[0], fars)
     lists = [x.reshape(1, -1) for x in (near_first, near_second, far_source, far_target)]
-    own, idx, tiles_low = pl.pallas_call(
+    own, at_second, at_first, at_source, at_target, tiles_low, near_zero = pl.pallas_call(
         functools.partial(prep_kernel, place),
         in_specs=[HBM] * 8,
-        out_specs=[VMEM] * 3,
+        out_specs=[VMEM] * 7,
         out_shape=[
             shape(stride, BF16),
-            jax.ShapeDtypeStruct((7, width), I32),
+            *[jax.ShapeDtypeStruct((r, n), I32) for r, n in ((3, 2 * pairs), (2, 2 * pairs), (2, fars // 2), (2, fars // 2))],
             shape(pairs // 2, BF16, size),
+            near_acc,
         ],
         scratch_shapes=[
             pltpu.SMEM(counts.shape, I32),
@@ -467,17 +487,17 @@
     coded_a = total // 2
     coded_b = blks // 2 * cells
     stay = blks // 2
-    near_acc = shape(total, F32, 2 * rows)
     near_sum, both, tiles_high = pl.pallas_call(
         near_second_a_kernel,
-        in_specs=[SMEM, VMEM, VMEM, VMEM, HBM],
+        in_specs=[SMEM, VMEM, VMEM, VMEM, HBM, VMEM],
+        input_output_aliases={5: 0},
         out_specs=[VMEM] * 3,
         out_shape=[near_acc, shape(cells, BF16, 2 * rows), shape(pairs - pairs // 2, BF16, size)],
         scratch_shapes=[pltpu.SemaphoreType.DMA],
         compiler_params=params(4),
         cost_estimate=near_cost,
         name="near_second_a",
-    )(idx, charge_own, charge_other, tiles_low, in_hbm(near_tiles))
+    )(at_second, charge_own, charge_other, tiles_low, in_hbm(near_tiles), near_zero)
 
     received = swap_blk(own, gather_order[0])
     received, near_sum = lax.optimization_barrier((received, near_sum))
@@ -504,35 +524,49 @@
         compiler_params=params(8),
         cost_estimate=near_cost,
         name="near_second_b",
-    )(idx, both, other_tiles, near_sum)
+    )(at_second, both, other_tiles, near_sum)
     moment_late, _ = lax.optimization_barrier((moment_pair, send_a))
-    turned, far_keep, *far_sends = pl.pallas_call(
-        far_source_kernel,
+    far_scratch = [
+        pltpu.VMEM((terms // 2 * PITCH, size), F32),
+        pltpu.VMEM((cells, 2 * rows, terms), BF16),
+    ]
+    far_sums = jax.ShapeDtypeStruct((total, 2 * rows, terms), F32)
+    turned_a, far_acc = pl.pallas_call(
+        far_source_a_kernel,
         in_specs=[SMEM] + [VMEM] * 3,
-        out_specs=[VMEM] * (2 + PARTS),
-        out_shape=[
-            shape(fars // 2, BF16, terms // 2),
-            shape(total // 2, F32),
-            *[shape(total // 2 // PARTS, F32)] * PARTS,
-        ],
-        scratch_shapes=[
-            pltpu.VMEM((FAR_STEPS, terms // 2 * PITCH, size), F32),
-            pltpu.VMEM((cells, 2 * rows, terms), BF16),
-            pltpu.VMEM((total, 2 * rows, terms), F32),
-        ],
-        compiler_params=params(8 + total // 32),
+        out_specs=[VMEM] * 2,
+        out_shape=[shape(fars // 4, BF16, terms // 2), far_sums],
+        scratch_shapes=far_scratch,
+        compiler_params=params(6),
         cost_estimate=far_cost,
-        name="far_source",
-    )(idx, moment_own, moment_late, tiles_ij)
-    received, turned = lax.optimization_barrier((received, turned))
-    others, starts = [], []
+        name="far_source_a",
+    )(at_source, moment_own, moment_late, tiles_ij)
+    received, far_acc = lax.optimization_barrier((received, far_acc))
+    others, places = [], []
     for s, bit in enumerate(gather_order):
         if s > 1:
             received = swap_blk(gathered, bit)
         if 0 < s < bits - 1:
             gathered = jnp.concatenate([gathered, received], axis=0)
-    starts.append(1)
-    others.append(swap_rank(owners(gathered, 1, blks // 2, 0, cells), 2))
+    places.append(early)
+    others.append(swap_rank(owners(gathered, early, 0, cells), 2))
+    far_acc, _ = lax.optimization_barrier((far_acc, gathered))
+    turned_b, _, far_keep, *far_sends = pl.pallas_call(
+        far_source_b_kernel,
+        in_specs=[SMEM] + [VMEM] * 4,
+        out_specs=[VMEM] * (3 + PARTS),
+        out_shape=[
+            shape(fars // 4, BF16, terms // 2),
+            far_sums,
+            shape(total // 2, F32),
+            *[shape(total // 2 // PARTS, F32)] * PARTS,
+        ],
+        scratch_shapes=far_scratch,
+        input_output_aliases={4: 1},
+        compiler_params=params(6),
+        cost_estimate=far_cost,
+        name="far_source_b",
+    )(at_source, moment_own, moment_late, tiles_ij, far_acc)
     far_others = [swap_rank(x, 1) for x in far_sends]
 
     got_a = swap_rank(send_a, 2)
@@ -551,12 +585,12 @@
         cost_estimate=meet_cost,
         name="meet_b",
     )(keep_b, got_b)
-    keep_a, send_b = lax.optimization_barrier((keep_a, send_b))
+    keep_a, _, others[0] = lax.optimization_barrier((keep_a, send_b, others[0]))
     got_b = swap_rank(send_b, 2)
-    received, others[0], got_b = lax.optimization_barrier((received, others[0], got_b))
+    received, got_b = lax.optimization_barrier((received, got_b))
     gathered = jnp.concatenate([gathered, received], axis=0)
-    starts.append(blks // 2)
-    others.append(swap_rank(owners(received, 0, blks // 2, 0, cells), 2))
+    places.append(late)
+    others.append(swap_rank(owners(received, [at - blks // 2 for at in late], 0, cells), 2))
     joined = pl.pallas_call(
         join_kernel,
         in_specs=[VMEM] * 2,
@@ -579,10 +613,10 @@
     )(joined, far_keep, *far_others)
     got_a = swap_blk(send_a, reduce_order[-1])
 
-    moment_all_pair = swap_rank(owners(gathered, 0, blks, cells, stride), 1)
+    moment_all_pair = swap_rank(owners(gathered, range(blks), cells, stride), 1)
     target_keep, target_send = pl.pallas_call(
         functools.partial(far_target_kernel, stride, cells),
-        in_specs=[SMEM] + [VMEM] * 3,
+        in_specs=[SMEM] + [VMEM] * 4,
         out_specs=[VMEM] * 2,
         out_shape=[shape(halfc, F32), shape(halfc, F32)],
         scratch_shapes=[
@@ -592,7 +626,7 @@
         compiler_params=params(6 + total // 32),
         cost_estimate=meet_cost,
         name="far_target",
-    )(idx, gathered, moment_all_pair, turned)
+    )(at_target, gathered, moment_all_pair, turned_a, turned_b)
     target_other = swap_rank(target_send, 1)
     others[0], _ = lax.optimization_barrier((others[0], target_send))
 
@@ -626,18 +660,20 @@
             coded = swap_blk(send, bit)
 
     first_keep, first_send = pl.pallas_call(
-        functools.partial(near_first_kernel, stride, cells, starts),
+        functools.partial(near_first_kernel, stride, cells, places),
         in_specs=[SMEM] + [VMEM] * (5 + len(others)),
         out_specs=[VMEM, VMEM],
-        out_shape=[shape(cells, F32), shape(cells, F32)],
+        out_shape=[shape(cells, F32), shape(cells + scale_blocks(cells), I16)],
         scratch_shapes=[
             scratch(total, 2 * rows, BF16),
             scratch(cells, 2 * rows),
+            scales(cells),
+            scales(cells),
         ],
         compiler_params=params(4 + total // 32),
         cost_estimate=first_cost,
         name="near_first",
-    )(idx, gathered, both, *others, tiles_low, tiles_high, other_tiles)
+    )(at_first, gathered, both, *others, tiles_low, tiles_high, other_tiles)
     first_send, send = lax.optimization_barrier((first_send, send))
     first_other = swap_rank(first_send, 2)
     coded = swap_blk(send, reduce_order[0])
@@ -657,7 +693,7 @@
         in_specs=[SMEM] + [VMEM] * 8,
         out_specs=VMEM,
         out_shape=jax.ShapeDtypeStruct(charges.shape, F32),
-        scratch_shapes=[scales(stride)],
+        scratch_shapes=[scales(stride), scales(cells)],
         compiler_params=params(8),
         name="final",
     )(

time: 60 us -> 58.3 us (0.972)
  waiting for transfers between devices: 14.4 us -> 10.5 us
  starting transfers between devices: 18.9 us -> 21.8 us
  Pallas kernels: 26 us -> 25.3 us
    ppermute x7, starting transfers between devices: 10 us -> 12.4 us  [swap_blk(): return lax.ppermute(x, 'blk', [(i, i ^ 1 << bit) for i in range(blks)])]
    ppermute x14, waiting for transfers between devices: 8.84 us -> 6.86 us  [swap_rank(): return lax.ppermute(x, 'rhs', [(i, i ^ d) for i in range(ranks)])]
    ppermute x7, waiting for transfers between devices: 5.57 us -> 3.63 us  [swap_blk(): return lax.ppermute(x, 'blk', [(i, i ^ 1 << bit) for i in range(blks)])]
    pallas_call x2 -> x3, Pallas kernels: 10.6 us -> 10.7 us  [the longest x1 5.25 us: body(): pl.pallas_call(functools.partial(near_first_kernel, stride, cells, places...]
  transfers between devices with their start and end apart: 21 -> 21, of which waited for: 9 -> 12; matrix products, arithmetic and copies ran while one was open for 0% -> 1% of each run, Pallas kernels for 41% -> 41%
where the time goes in v5:
time: 58.3 us; the launch traced here: 58.1 us
  Pallas kernels  25.3 us (43%)
  starting transfers between devices  21.8 us (37%)
  waiting for transfers between devices  10.5 us (18%)
    ppermute x7, starting transfers between devices, swap_blk(): return lax.ppermute(x, 'blk', [(i, i ^ 1 << bit) for i in range(blks)])  12.4 us
    ppermute x14, starting transfers between devices, swap_rank(): return lax.ppermute(x, 'rhs', [(i, i ^ d) for i in range(ranks)])  9.45 us
    ppermute x14, waiting for transfers between devices, swap_rank(): return lax.ppermute(x, 'rhs', [(i, i ^ d) for i in range(ranks)])  6.86 us
    pallas_call x1, Pallas kernels, body(): pl.pallas_call(functools.partial(near_first_kernel, stride, cells, places...  5.25 us
    pallas_call x1, Pallas kernels, body(): pl.pallas_call(functools.partial(far_target_kernel, stride, cells), in_sp...  3.67 us
    ppermute x7, waiting for transfers between devices, swap_blk(): return lax.ppermute(x, 'blk', [(i, i ^ 1 << bit) for i in range(blks)])  3.63 us
    pallas_call x1, Pallas kernels, body(): pl.pallas_call(near_second_a_kernel, in_specs=[SMEM, VMEM, VMEM, VMEM, HB...  3.45 us
    pallas_call x1, Pallas kernels, body(): pl.pallas_call(far_source_b_kernel, in_specs=[SMEM] + [VMEM] * 4, out_spe...  3.35 us
  transfers between devices with their start and end apart: 21, of which 12 were waited for; matrix products, arithmetic and copies ran while one was open for 1% of the time, Pallas kernels for 41%

profile of v5, /device:TPU:0, one launch (start us, length us, event | category | flops | bytes accessed | tf_op | source)
XLA Modules:
  0.0 58.1 jit_solution(10301821649252983167)
XLA Ops:
  0.0 0.5 collective-permute-start.1
  0.5 2.5 %collective-permute-start = (bf16[16,2048]{1,0:T(8,128)(2,1)}, bf16[16,2048]{1,0:T(8,128)(2,1)S(1)}, u32[]{:S(2)}, u32[]{:S(2)}) collective-permute-start(bf16[16,2048]{1,0:T(8,128)(2,1)} %charges_in.1), channel_id=1, source_target_pairs={{0,2},{1,3},{2,0},{3,1},{4,6},{5,7},{6,4},{7,5},{8,10},{9,11},{10,... | collective-permute-start | bytes 196616 | tf_op jit(solution)/shard_map/ppermute | solution.py:417
  2.9 1.9 %prep.1 = (bf16[24,16,128]{2,1,0:T(8,128)(2,1)S(1)}, s32[3,256]{1,0:T(4,128)S(1)}, s32[2,256]{1,0:T(2,128)S(1)}, s32[2,256]{1,0:T(2,128)S(1)}, s32[2,256]{1,0:T(...) custom-call(s32[1,16]{1,0:T(1,128)} %bitcast.20, bf16[16,2048]{1,0:T(8,128)(2,1)} %charges_in.1, ...), custom_call_target="tpu_custom_call" | custom-call | bytes 12582912 | tf_op jit(solution)/shard_map/prep/pallas_call | solution.py:457
  4.8 1.6 %collective-permute-start.2 = (bf16[24,16,128]{2,1,0:T(8,128)(2,1)S(1)}, bf16[24,16,128]{2,1,0:T(8,128)(2,1)S(1)}, u32[]{:S(2)}, u32[]{:S(2)}) collective-permute-start(bf16[24,16,128]{2,1,0:T(8,128)(2,1)S(1)} %get-tuple-element.58), channel_id=1, source_target_pairs={{0,4},{4,0},{8,12},{12,8},{16,20},{20,16},{24,28},{28,24},{1,5},{5... | collective-permute-start | bytes 294920 | tf_op jit(solution)/shard_map/ppermute | solution.py:420
  6.5 3.5 %near_second_a.1 = (f32[128,32,128]{2,1,0:T(8,128)S(1)}, bf16[16,32,128]{2,1,0:T(8,128)(2,1)S(1)}, bf16[64,128,128]{2,1,0:T(8,128)(2,1)S(1)}) custom-call(s32[3,256]{1,0:T(4,128)S(1)} %get-tuple-element.57.idx, bf16[16,16,128]{2,1,0:T(8,128)(2,1)S(1)} %slice.18.mine.moved, ...), custom_call_target="tpu_custom_call", output_to_operand_aliasing={{0}: (5, {})} | custom-call | flops 134217728 | bytes 10485760 | tf_op jit(solution)/shard_map/near_second_a/pallas_call | solution.py:490
  9.9 0.1 constant_dynamic-update-slice_fusion.7
  10.0 2.6 %collective-permute-start.5 = (bf16[48,16,128]{2,1,0:T(8,128)(2,1)S(1)}, bf16[48,16,128]{2,1,0:T(8,128)(2,1)S(1)}, u32[]{:S(2)}, u32[]{:S(2)}) collective-permute-start(bf16[48,16,128]{2,1,0:T(8,128)(2,1)S(1)} %get-tuple-element.115), channel_id=1, source_target_pairs={{0,16},{4,20},{8,24},{12,28},{16,0},{20,4},{24,8},{28,12},{1,17},{... | collective-permute-start | bytes 589832 | tf_op jit(solution)/shard_map/ppermute | solution.py:420
  12.7 2.5 %near_second_b.1 = (f32[128,32,128]{2,1,0:T(8,128)S(1)}, f32[64,16,128]{2,1,0:T(8,128)S(1)}, s16[68,16,128]{2,1,0:T(8,128)(2,1)S(1)}, f32[32,32,128]{2,1,0:T(8,128)S(1)}, s16[68,16,128]{2,1,0:T(8,128)(2,1)S(1)}) custom-call(s32[3,256]{1,0:T(4,128)S(1)} %get-tuple-element.57.idx, ...), custom_call_target="tpu_custom_call", output_to_operand_aliasing={{0}: (3, {})} | custom-call | flops 134217728 | bytes 10485760 | tf_op jit(solution)/shard_map/near_second_b/pallas_call | solution.py:508
  15.2 1.5 %collective-permute-start.3 = (s16[68,16,128]{2,1,0:T(8,128)(2,1)S(1)}, s16[68,16,128]{2,1,0:T(8,128)(2,1)S(1)}, u32[]{:S(2)}, u32[]{:S(2)}) collective-permute-start(s16[68,16,128]{2,1,0:T(8,128)(2,1)S(1)} %get-tuple-element.68), channel_id=1, source_target_pairs={{0,4},{4,0},{8,12},{12,8},{16,20},{20,16},{24,28},{28,24},{1,5},{5... | collective-permute-start | bytes 835592 | tf_op jit(solution)/shard_map/ppermute | solution.py:420
  16.7 1.3 %collective-permute-start.4 = (s16[68,16,128]{2,1,0:T(8,128)(2,1)S(1)}, s16[68,16,128]{2,1,0:T(8,128)(2,1)S(1)}, u32[]{:S(2)}, u32[]{:S(2)}) collective-permute-start(s16[68,16,128]{2,1,0:T(8,128)(2,1)S(1)} %get-tuple-element.69), channel_id=1, source_target_pairs={{0,2},{1,3},{2,0},{3,1},{4,6},{5,7},{6,4},{7,5},{8,10},{9,11},{10,... | collective-permute-start | bytes 835592 | tf_op jit(solution)/shard_map/ppermute | solution.py:417
  18.0 2.1 %far_source_a.1 = (bf16[128,32,128]{2,1,0:T(8,128)(2,1)S(1)}, f32[128,32,64]{2,1,0:T(8,128)S(1)}) custom-call(s32[2,256]{1,0:T(2,128)S(1)} %get-tuple-element.72.idx, bf16[8,16,128]{2,1,0:T(8,128)(2,1)S(1)} %slice.19.mine, bf16[8,16,128]{2,1,0:T(8,128)(2,1)S(1)} %collective-permute-done.6.theirs, bf16[4096,512]{1,0:T(8,128)(2,1)S(1)} %bitcast.15), custom_call_target="tpu_custom_call" | custom-call | flops 67108864 | bytes 12582912 | tf_op jit(solution)/shard_map/far_source_a/pallas_call | solution.py:534
  20.1 1.8 %collective-permute-done.5 = bf16[48,16,128]{2,1,0:T(8,128)(2,1)S(1)} collective-permute-done((bf16[48,16,128]{2,1,0:T(8,128)(2,1)S(1)}, bf16[48,16,128]{2,1,0:T(8,128)(2,1)S(1)}, u32[]{:S(2)}, u32[]{:S(2)}) %collective-permute-start.5) | collective-permute-done | bytes 196640 | tf_op jit(solution)/shard_map/ppermute | solution.py:420
  21.9 0.1 constant_dynamic-update-slice_fusion.6
  22.0 0.7 %collective-permute-start.13 = (bf16[96,16,128]{2,1,0:T(8,128)(2,1)S(1)}, bf16[96,16,128]{2,1,0:T(8,128)(2,1)S(1)}, u32[]{:S(2)}, u32[]{:S(2)}) collective-permute-start(bf16[96,16,128]{2,1,0:T(8,128)(2,1)S(1)} %get-tuple-element.112), channel_id=1, source_target_pairs={{0,8},{4,12},{8,0},{12,4},{16,24},{20,28},{24,16},{28,20},{1,9},{5... | collective-permute-start | bytes 1179656 | tf_op jit(solution)/shard_map/ppermute | solution.py:420
  22.8 1.0 %collective-permute-start.7 = (bf16[32,16,128]{2,1,0:T(8,128)(2,1)S(1)}, bf16[32,16,128]{2,1,0:T(8,128)(2,1)S(1)}, u32[]{:S(2)}, u32[]{:S(2)}) collective-permute-start(bf16[32,16,128]{2,1,0:T(8,128)(2,1)S(1)} %bitcast.25), channel_id=1, source_target_pairs={{0,2},{1,3},{2,0},{3,1},{4,6},{5,7},{6,4},{7,5},{8,10},{9,11},{10,... | collective-permute-start | bytes 393224 | tf_op jit(solution)/shard_map/ppermute | solution.py:417
  23.8 3.4 %far_source_b.1 = (bf16[128,32,128]{2,1,0:T(8,128)(2,1)S(1)}, f32[128,32,64]{2,1,0:T(8,128)S(1)}, f32[64,16,128]{2,1,0:T(8,128)S(1)}, f32[16,16,128]{2,1,0:T(8,1...) custom-call(s32[2,256]{1,0:T(2,128)S(1)} %get-tuple-element.72.idx, ...), custom_call_target="tpu_custom_call", output_to_operand_aliasing={{1}: (4, {})} | custom-call | flops 67108864 | bytes 12582912 | tf_op jit(solution)/shard_map/far_source_b/pallas_call | solution.py:554
  27.2 0.1 collective-permute-start.8
  27.3 0.2 meet_b.1
  27.5 1.1 %collective-permute-start.14 = (s16[34,16,128]{2,1,0:T(8,128)(2,1)S(1)}, s16[34,16,128]{2,1,0:T(8,128)(2,1)S(1)}, u32[]{:S(2)}, u32[]{:S(2)}) collective-permute-start(s16[34,16,128]{2,1,0:T(8,128)(2,1)S(1)} %get-tuple-element.71), channel_id=1, source_target_pairs={{0,2},{1,3},{2,0},{3,1},{4,6},{5,7},{6,4},{7,5},{8,10},{9,11},{10,... | collective-permute-start | bytes 417800 | tf_op jit(solution)/shard_map/ppermute | solution.py:417
  28.6 0.2 collective-permute-start.9
  28.8 0.3 collective-permute-start.10
  29.2 0.2 collective-permute-start.11
  29.4 0.1 join.1.mine
  29.5 0.5 collective-permute-done.9.refs_1_
  30.0 0.2 collective-permute-done.10.refs_2_
  30.2 0.3 collective-permute-done.11.refs_3_
  30.5 0.3 meet_a.1
  30.9 1.1 %collective-permute-start.12 = (s16[68,16,128]{2,1,0:T(8,128)(2,1)S(1)}, s16[68,16,128]{2,1,0:T(8,128)(2,1)S(1)}, u32[]{:S(2)}, u32[]{:S(2)}) collective-permute-start(s16[68,16,128]{2,1,0:T(8,128)(2,1)S(1)} %get-tuple-element.86), channel_id=1, source_target_pairs={{0,4},{4,0},{8,12},{12,8},{16,20},{20,16},{24,28},{28,24},{1,5},{5... | collective-permute-start | bytes 835592 | tf_op jit(solution)/shard_map/ppermute | solution.py:420
  31.9 0.3 collective-permute-done.13
  32.2 1.4 %collective-permute-done.14.coded_b = s16[34,16,128]{2,1,0:T(8,128)(2,1)S(1)} collective-permute-done((s16[34,16,128]{2,1,0:T(8,128)(2,1)S(1)}, s16[34,16,128]{2,1,0:T(8,128)(2,1)S(1)}, u32[]{:S(2)}, u32[]{:S(2)}) %collective-permute-start.14) | collective-permute-done | bytes 139296 | tf_op jit(solution)/shard_map/ppermute | solution.py:417
  33.6 0.1 constant_dynamic-update-slice_fusion.5.everyone
  33.7 0.1 collective-permute-start.15
  33.8 1.1 %collective-permute-start.17 = (bf16[64,16,128]{2,1,0:T(8,128)(2,1)S(1)}, bf16[64,16,128]{2,1,0:T(8,128)(2,1)S(1)}, u32[]{:S(2)}, u32[]{:S(2)}) collective-permute-start(bf16[64,16,128]{2,1,0:T(8,128)(2,1)S(1)} %bitcast.22), channel_id=1, source_target_pairs={{0,2},{1,3},{2,0},{3,1},{4,6},{5,7},{6,4},{7,5},{8,10},{9,11},{10,... | collective-permute-start | bytes 786440 | tf_op jit(solution)/shard_map/ppermute | solution.py:417
  35.0 0.4 collective-permute-done.15.theirs
  35.3 3.7 %far_target.1 = (f32[8,16,128]{2,1,0:T(8,128)S(1)}, f32[8,16,128]{2,1,0:T(8,128)S(1)}) custom-call(s32[2,256]{1,0:T(2,128)S(1)} %get-tuple-element.88.idx, bf16[192,16,128]{2,1,0:T(8,128)(2,1)S(1)} %constant_dynamic-update-slice_fusion.5.everyone, bf16[64,16,128]{2,1,0:T(8,128)(2,1)S(1)} %collective-permute-done.15.theirs, ...), custom_call_target="tpu_custom_call" | custom-call | bytes 1048576 | tf_op jit(solution)/shard_map/far_target/pallas_call | solution.py:617
  39.0 0.7 %collective-permute-done.12.coded_a = s16[68,16,128]{2,1,0:T(8,128)(2,1)S(1)} collective-permute-done((s16[68,16,128]{2,1,0:T(8,128)(2,1)S(1)}, s16[68,16,128]{2,1,0:T(8,128)(2,1)S(1)}, u32[]{:S(2)}, u32[]{:S(2)}) %collective-permute-start.12) | collective-permute-done | bytes 278560 | tf_op jit(solution)/shard_map/ppermute | solution.py:420
  39.7 0.3 meet.1
  40.0 1.4 %collective-permute-start.16 = (s16[51,16,128]{2,1,0:T(8,128)(2,1)S(1)}, s16[51,16,128]{2,1,0:T(8,128)(2,1)S(1)}, u32[]{:S(2)}, u32[]{:S(2)}) collective-permute-start(s16[51,16,128]{2,1,0:T(8,128)(2,1)S(1)} %get-tuple-element.97), channel_id=1, source_target_pairs={{0,8},{4,12},{8,0},{12,4},{16,24},{20,28},{24,16},{28,20},{1,9},{5... | collective-permute-start | bytes 626696 | tf_op jit(solution)/shard_map/ppermute | solution.py:420
  41.4 1.2 %collective-permute-done.17.refs_1_ = bf16[64,16,128]{2,1,0:T(8,128)(2,1)S(1)} collective-permute-done((bf16[64,16,128]{2,1,0:T(8,128)(2,1)S(1)}, bf16[64,16,128]{2,1,0:T(8,128)(2,1)S(1)}, u32[]{:S(2)}, u32[]{:S(2)}) %collective-permute-start.17) | collective-permute-done | bytes 262176 | tf_op jit(solution)/shard_map/ppermute | solution.py:417
  42.6 5.2 %near_first.1 = (f32[16,16,128]{2,1,0:T(8,128)S(1)}, s16[17,16,128]{2,1,0:T(8,128)(2,1)S(1)}) custom-call(s32[2,256]{1,0:T(2,128)S(1)} %get-tuple-element.99.idx, bf16[192,16,128]{2,1,0:T(8,128)(2,1)S(1)} %constant_dynamic-update-slice_fusion.5.everyone, bf16[16,32,128]{2,1,0:T(8,128)(2,1)S(1)} %get-tuple-element.61.both, ...), custom_call_target="tpu_custom_call" | custom-call | flops 268435456 | bytes 20971520 | tf_op jit(solution)/shard_map/near_first/pallas_call | solution.py:662
  47.9 0.2 add.1
  48.1 3.4 %collective-permute-start.18 = (s16[26,16,128]{2,1,0:T(8,128)(2,1)S(1)}, s16[26,16,128]{2,1,0:T(8,128)(2,1)S(1)}, u32[]{:S(2)}, u32[]{:S(2)}) collective-permute-start(s16[26,16,128]{2,1,0:T(8,128)(2,1)S(1)} %get-tuple-element.105), channel_id=1, source_target_pairs={{0,16},{4,20},{8,24},{12,28},{16,0},{20,4},{24,8},{28,12},{1,17},{... | collective-permute-start | bytes 319496 | tf_op jit(solution)/shard_map/ppermute | solution.py:420
  51.5 1.1 %collective-permute-start.19 = (s16[17,16,128]{2,1,0:T(8,128)(2,1)S(1)}, s16[17,16,128]{2,1,0:T(8,128)(2,1)S(1)}, u32[]{:S(2)}, u32[]{:S(2)}) collective-permute-start(s16[17,16,128]{2,1,0:T(8,128)(2,1)S(1)} %get-tuple-element.107), channel_id=1, source_target_pairs={{0,2},{1,3},{2,0},{3,1},{4,6},{5,7},{6,4},{7,5},{8,10},{9,11},{10,... | collective-permute-start | bytes 208904 | tf_op jit(solution)/shard_map/ppermute | solution.py:417
  52.6 0.4 self.1.own
  52.9 0.9 %collective-permute-done.20.target_other = f32[8,16,128]{2,1,0:T(8,128)S(1)} collective-permute-done((f32[8,16,128]{2,1,0:T(8,128)S(1)}, f32[8,16,128]{2,1,0:T(8,128)S(1)}, u32[]{:S(2)}, u32[]{:S(2)}) %collective-permute-start.20) | collective-permute-done | bytes 65568 | tf_op jit(solution)/shard_map/ppermute | solution.py:417
  53.8 2.0 %collective-permute-done.19.first_other = s16[17,16,128]{2,1,0:T(8,128)(2,1)S(1)} collective-permute-done((s16[17,16,128]{2,1,0:T(8,128)(2,1)S(1)}, s16[17,16,128]{2,1,0:T(8,128)(2,1)S(1)}, u32[]{:S(2)}, u32[]{:S(2)}) %collective-permute-start.19) | collective-permute-done | bytes 69664 | tf_op jit(solution)/shard_map/ppermute | solution.py:417
  55.8 0.8 %collective-permute-done.18.coded = s16[26,16,128]{2,1,0:T(8,128)(2,1)S(1)} collective-permute-done((s16[26,16,128]{2,1,0:T(8,128)(2,1)S(1)}, s16[26,16,128]{2,1,0:T(8,128)(2,1)S(1)}, u32[]{:S(2)}, u32[]{:S(2)}) %collective-permute-start.18) | collective-permute-done | bytes 106528 | tf_op jit(solution)/shard_map/ppermute | solution.py:420
  56.6 1.5 %final.1 = f32[16,2048]{1,0:T(8,128)} custom-call(s32[16]{0:T(128)S(1)} %copy-done.3, f32[24,16,128]{2,1,0:T(8,128)S(1)} %get-tuple-element.98.mine, s16[26,16,128]{2,1,0:T(8,128)(2,1)S(1)} %collective-permute-done.18.coded, f32[16,16,128]{2,1,0:T(8,128)S(1)} %get-tuple-element.106.first, s16[17,16,128]{2,1,0:T(8,128)(2,1)S(1)} %collective-permute-done.19.first_other, ...), custom_call_target="tpu_custom_call" | custom-call | tf_op jit(solution)/shard_map/final/pallas_call | solution.py:691
  (26 shorter events, 0.2 us)
Async XLA Ops:
  0.0 12.7 %collective-permute-start.1 = (bf16[128,128,128]{2,1,0:T(8,128)(2,1)}, bf16[128,128,128]{2,1,0:T(8,128)(2,1)S(1)}, u32[]{:S(2)}, u32[]{:S(2)}) collective-permute-start(bf16[128,128,128]{2,1,0:T(8,128)(2,1)} %rest.1), channel_id=1, source_target_pairs={{0,1},{1,0},{2,3},{3,2},{4,5},{5,4},{6,7},{7,6},{8,9},{9,8},{10,11... | collective-permute-start | bytes 12582920 | tf_op jit(solution)/shard_map/ppermute | solution.py:417
  0.5 6.0 %collective-permute-start = (bf16[16,2048]{1,0:T(8,128)(2,1)}, bf16[16,2048]{1,0:T(8,128)(2,1)S(1)}, u32[]{:S(2)}, u32[]{:S(2)}) collective-permute-start(bf16[16,2048]{1,0:T(8,128)(2,1)} %charges_in.1), channel_id=1, source_target_pairs={{0,2},{1,3},{2,0},{3,1},{4,6},{5,7},{6,4},{7,5},{8,10},{9,11},{10,... | collective-permute-start | bytes 196616 | tf_op jit(solution)/shard_map/ppermute | solution.py:417
  4.8 5.1 %collective-permute-start.2 = (bf16[24,16,128]{2,1,0:T(8,128)(2,1)S(1)}, bf16[24,16,128]{2,1,0:T(8,128)(2,1)S(1)}, u32[]{:S(2)}, u32[]{:S(2)}) collective-permute-start(bf16[24,16,128]{2,1,0:T(8,128)(2,1)S(1)} %get-tuple-element.58), channel_id=1, source_target_pairs={{0,4},{4,0},{8,12},{12,8},{16,20},{20,16},{24,28},{28,24},{1,5},{5... | collective-permute-start | bytes 294920 | tf_op jit(solution)/shard_map/ppermute | solution.py:420
  10.0 11.9 %collective-permute-start.5 = (bf16[48,16,128]{2,1,0:T(8,128)(2,1)S(1)}, bf16[48,16,128]{2,1,0:T(8,128)(2,1)S(1)}, u32[]{:S(2)}, u32[]{:S(2)}) collective-permute-start(bf16[48,16,128]{2,1,0:T(8,128)(2,1)S(1)} %get-tuple-element.115), channel_id=1, source_target_pairs={{0,16},{4,20},{8,24},{12,28},{16,0},{20,4},{24,8},{28,12},{1,17},{... | collective-permute-start | bytes 589832 | tf_op jit(solution)/shard_map/ppermute | solution.py:420
  12.7 5.3 %collective-permute-start.6 = (bf16[8,16,128]{2,1,0:T(8,128)(2,1)S(1)}, bf16[8,16,128]{2,1,0:T(8,128)(2,1)S(1)}, u32[]{:S(2)}, u32[]{:S(2)}) collective-permute-start(bf16[8,16,128]{2,1,0:T(8,128)(2,1)S(1)} %slice.19.mine), channel_id=1, source_target_pairs={{0,1},{1,0},{2,3},{3,2},{4,5},{5,4},{6,7},{7,6},{8,9},{9,8},{10,11... | collective-permute-start | bytes 98312 | tf_op jit(solution)/shard_map/ppermute | solution.py:417
  12.7 5.3 %copy-start = (bf16[512,64,64]{0,2,1:T(8,128)(2,1)S(1)}, bf16[512,64,64]{0,2,1:T(8,128)(2,1)}, u32[]{:S(2)}) copy-start(bf16[512,64,64]{0,2,1:T(8,128)(2,1)} %param.19) | copy-start | bytes 12582916
  15.2 12.1 %collective-permute-start.3 = (s16[68,16,128]{2,1,0:T(8,128)(2,1)S(1)}, s16[68,16,128]{2,1,0:T(8,128)(2,1)S(1)}, u32[]{:S(2)}, u32[]{:S(2)}) collective-permute-start(s16[68,16,128]{2,1,0:T(8,128)(2,1)S(1)} %get-tuple-element.68), channel_id=1, source_target_pairs={{0,4},{4,0},{8,12},{12,8},{16,20},{20,16},{24,28},{28,24},{1,5},{5... | collective-permute-start | bytes 835592 | tf_op jit(solution)/shard_map/ppermute | solution.py:420
  16.7 10.6 %collective-permute-start.4 = (s16[68,16,128]{2,1,0:T(8,128)(2,1)S(1)}, s16[68,16,128]{2,1,0:T(8,128)(2,1)S(1)}, u32[]{:S(2)}, u32[]{:S(2)}) collective-permute-start(s16[68,16,128]{2,1,0:T(8,128)(2,1)S(1)} %get-tuple-element.69), channel_id=1, source_target_pairs={{0,2},{1,3},{2,0},{3,1},{4,6},{5,7},{6,4},{7,5},{8,10},{9,11},{10,... | collective-permute-start | bytes 835592 | tf_op jit(solution)/shard_map/ppermute | solution.py:417
  22.0 10.2 %collective-permute-start.13 = (bf16[96,16,128]{2,1,0:T(8,128)(2,1)S(1)}, bf16[96,16,128]{2,1,0:T(8,128)(2,1)S(1)}, u32[]{:S(2)}, u32[]{:S(2)}) collective-permute-start(bf16[96,16,128]{2,1,0:T(8,128)(2,1)S(1)} %get-tuple-element.112), channel_id=1, source_target_pairs={{0,8},{4,12},{8,0},{12,4},{16,24},{20,28},{24,16},{28,20},{1,9},{5... | collective-permute-start | bytes 1179656 | tf_op jit(solution)/shard_map/ppermute | solution.py:420
  22.8 6.0 %collective-permute-start.7 = (bf16[32,16,128]{2,1,0:T(8,128)(2,1)S(1)}, bf16[32,16,128]{2,1,0:T(8,128)(2,1)S(1)}, u32[]{:S(2)}, u32[]{:S(2)}) collective-permute-start(bf16[32,16,128]{2,1,0:T(8,128)(2,1)S(1)} %bitcast.25), channel_id=1, source_target_pairs={{0,2},{1,3},{2,0},{3,1},{4,6},{5,7},{6,4},{7,5},{8,10},{9,11},{10,... | collective-permute-start | bytes 393224 | tf_op jit(solution)/shard_map/ppermute | solution.py:417
  27.2 2.0 %collective-permute-start.8 = (f32[16,16,128]{2,1,0:T(8,128)S(1)}, f32[16,16,128]{2,1,0:T(8,128)S(1)}, u32[]{:S(2)}, u32[]{:S(2)}) collective-permute-start(f32[16,16,128]{2,1,0:T(8,128)S(1)} %get-tuple-element.81), channel_id=1, source_target_pairs={{0,1},{1,0},{2,3},{3,2},{4,5},{5,4},{6,7},{7,6},{8,9},{9,8},{10,11... | collective-permute-start | bytes 393224 | tf_op jit(solution)/shard_map/ppermute | solution.py:417
  27.5 6.1 %collective-permute-start.14 = (s16[34,16,128]{2,1,0:T(8,128)(2,1)S(1)}, s16[34,16,128]{2,1,0:T(8,128)(2,1)S(1)}, u32[]{:S(2)}, u32[]{:S(2)}) collective-permute-start(s16[34,16,128]{2,1,0:T(8,128)(2,1)S(1)} %get-tuple-element.71), channel_id=1, source_target_pairs={{0,2},{1,3},{2,0},{3,1},{4,6},{5,7},{6,4},{7,5},{8,10},{9,11},{10,... | collective-permute-start | bytes 417800 | tf_op jit(solution)/shard_map/ppermute | solution.py:417
  28.6 1.3 %collective-permute-start.9 = (f32[16,16,128]{2,1,0:T(8,128)S(1)}, f32[16,16,128]{2,1,0:T(8,128)S(1)}, u32[]{:S(2)}, u32[]{:S(2)}) collective-permute-start(f32[16,16,128]{2,1,0:T(8,128)S(1)} %get-tuple-element.82), channel_id=1, source_target_pairs={{0,1},{1,0},{2,3},{3,2},{4,5},{5,4},{6,7},{7,6},{8,9},{9,8},{10,11... | collective-permute-start | bytes 393224 | tf_op jit(solution)/shard_map/ppermute | solution.py:417
  28.8 1.3 %collective-permute-start.10 = (f32[16,16,128]{2,1,0:T(8,128)S(1)}, f32[16,16,128]{2,1,0:T(8,128)S(1)}, u32[]{:S(2)}, u32[]{:S(2)}) collective-permute-start(f32[16,16,128]{2,1,0:T(8,128)S(1)} %get-tuple-element.83), channel_id=1, source_target_pairs={{0,1},{1,0},{2,3},{3,2},{4,5},{5,4},{6,7},{7,6},{8,9},{9,8},{10,11... | collective-permute-start | bytes 393224 | tf_op jit(solution)/shard_map/ppermute | solution.py:417
  29.2 1.3 %collective-permute-start.11 = (f32[16,16,128]{2,1,0:T(8,128)S(1)}, f32[16,16,128]{2,1,0:T(8,128)S(1)}, u32[]{:S(2)}, u32[]{:S(2)}) collective-permute-start(f32[16,16,128]{2,1,0:T(8,128)S(1)} %get-tuple-element.84), channel_id=1, source_target_pairs={{0,1},{1,0},{2,3},{3,2},{4,5},{5,4},{6,7},{7,6},{8,9},{9,8},{10,11... | collective-permute-start | bytes 393224 | tf_op jit(solution)/shard_map/ppermute | solution.py:417
  30.9 8.8 %collective-permute-start.12 = (s16[68,16,128]{2,1,0:T(8,128)(2,1)S(1)}, s16[68,16,128]{2,1,0:T(8,128)(2,1)S(1)}, u32[]{:S(2)}, u32[]{:S(2)}) collective-permute-start(s16[68,16,128]{2,1,0:T(8,128)(2,1)S(1)} %get-tuple-element.86), channel_id=1, source_target_pairs={{0,4},{4,0},{8,12},{12,8},{16,20},{20,16},{24,28},{28,24},{1,5},{5... | collective-permute-start | bytes 835592 | tf_op jit(solution)/shard_map/ppermute | solution.py:420
  33.7 1.6 %collective-permute-start.15 = (bf16[64,16,128]{2,1,0:T(8,128)(2,1)S(1)}, bf16[64,16,128]{2,1,0:T(8,128)(2,1)S(1)}, u32[]{:S(2)}, u32[]{:S(2)}) collective-permute-start(bf16[64,16,128]{2,1,0:T(8,128)(2,1)S(1)} %bitcast.23), channel_id=1, source_target_pairs={{0,1},{1,0},{2,3},{3,2},{4,5},{5,4},{6,7},{7,6},{8,9},{9,8},{10,11... | collective-permute-start | bytes 786440 | tf_op jit(solution)/shard_map/ppermute | solution.py:417
  33.8 8.8 %collective-permute-start.17 = (bf16[64,16,128]{2,1,0:T(8,128)(2,1)S(1)}, bf16[64,16,128]{2,1,0:T(8,128)(2,1)S(1)}, u32[]{:S(2)}, u32[]{:S(2)}) collective-permute-start(bf16[64,16,128]{2,1,0:T(8,128)(2,1)S(1)} %bitcast.22), channel_id=1, source_target_pairs={{0,2},{1,3},{2,0},{3,1},{4,6},{5,7},{6,4},{7,5},{8,10},{9,11},{10,... | collective-permute-start | bytes 786440 | tf_op jit(solution)/shard_map/ppermute | solution.py:417
  40.0 7.8 %collective-permute-start.16 = (s16[51,16,128]{2,1,0:T(8,128)(2,1)S(1)}, s16[51,16,128]{2,1,0:T(8,128)(2,1)S(1)}, u32[]{:S(2)}, u32[]{:S(2)}) collective-permute-start(s16[51,16,128]{2,1,0:T(8,128)(2,1)S(1)} %get-tuple-element.97), channel_id=1, source_target_pairs={{0,8},{4,12},{8,0},{12,4},{16,24},{20,28},{24,16},{28,20},{1,9},{5... | collective-permute-start | bytes 626696 | tf_op jit(solution)/shard_map/ppermute | solution.py:420
  42.6 10.0 %copy-start.2 = (bf16[16,128,128]{2,1,0:T(8,128)(2,1)S(1)}, bf16[16,128,128]{2,1,0:T(8,128)(2,1)}, u32[]{:S(2)}) copy-start(bf16[16,128,128]{2,1,0:T(8,128)(2,1)} %self_tiles.1) | copy-start | bytes 1572868
  42.6 14.0 %copy-start.1 = (bf16[16,128,64]{1,2,0:T(8,128)(2,1)S(1)}, bf16[16,128,64]{1,2,0:T(8,128)(2,1)}, u32[]{:S(2)}) copy-start(bf16[16,128,64]{1,2,0:T(8,128)(2,1)} %param.13) | copy-start | bytes 786436
  42.6 14.0 %copy-start.3 = (s32[16]{0:T(128)S(1)}, s32[16]{0:T(128)}, u32[]{:S(2)}) copy-start(s32[16]{0:T(128)} %counts.1) | copy-start | bytes 196
  48.1 8.6 %collective-permute-start.18 = (s16[26,16,128]{2,1,0:T(8,128)(2,1)S(1)}, s16[26,16,128]{2,1,0:T(8,128)(2,1)S(1)}, u32[]{:S(2)}, u32[]{:S(2)}) collective-permute-start(s16[26,16,128]{2,1,0:T(8,128)(2,1)S(1)} %get-tuple-element.105), channel_id=1, source_target_pairs={{0,16},{4,20},{8,24},{12,28},{16,0},{20,4},{24,8},{28,12},{1,17},{... | collective-permute-start | bytes 319496 | tf_op jit(solution)/shard_map/ppermute | solution.py:420
  51.5 4.3 %collective-permute-start.19 = (s16[17,16,128]{2,1,0:T(8,128)(2,1)S(1)}, s16[17,16,128]{2,1,0:T(8,128)(2,1)S(1)}, u32[]{:S(2)}, u32[]{:S(2)}) collective-permute-start(s16[17,16,128]{2,1,0:T(8,128)(2,1)S(1)} %get-tuple-element.107), channel_id=1, source_target_pairs={{0,2},{1,3},{2,0},{3,1},{4,6},{5,7},{6,4},{7,5},{8,10},{9,11},{10,... | collective-permute-start | bytes 208904 | tf_op jit(solution)/shard_map/ppermute | solution.py:417
  52.6 1.3 %collective-permute-start.20 = (f32[8,16,128]{2,1,0:T(8,128)S(1)}, f32[8,16,128]{2,1,0:T(8,128)S(1)}, u32[]{:S(2)}, u32[]{:S(2)}) collective-permute-start(f32[8,16,128]{2,1,0:T(8,128)S(1)} %get-tuple-element.92), channel_id=1, source_target_pairs={{0,1},{1,0},{2,3},{3,2},{4,5},{5,4},{6,7},{7,6},{8,9},{9,8},{10,11... | collective-permute-start | bytes 196616 | tf_op jit(solution)/shard_map/ppermute | solution.py:417

commit v6 on v5

--- a/solution.py
+++ b/solution.py
@@ -76,11 +76,13 @@
     moves += [
         (src, lists.at[pl.ds(i, 1)]) for i, src in enumerate((near_first, near_second, far_source, far_target))
     ]
-    moves += [(tiles_in.at[pl.ds(0, tiles.shape[0])], tiles)]
+    count = tiles.shape[0] // TILE_COPIES
+    spans = [pl.ds(i * count, count) for i in range(TILE_COPIES)]
+    moves += [(tiles_in.at[span], tiles.at[span]) for span in spans]
     copies = [pltpu.make_async_copy(src, dst, sems.at[i]) for i, (src, dst) in enumerate(moves)]
     for copy in copies:
         copy.start()
-    for copy in copies[:-1]:
+    for copy in copies[:-TILE_COPIES]:
         copy.wait()
     cells, terms, size = basis_t.shape
     rows = charges.shape[0]
@@ -111,9 +113,11 @@
         at[0:1, :] = lax.rem(target, cells)
         at[1:2, :] = place(source, reduce)
     near_zero[...] = jnp.zeros_like(near_zero)
-    copies[-1].wait()
-
-
+    for copy in copies[-TILE_COPIES:]:
+        copy.wait()
+
+
+TILE_COPIES = 4
 PITCH = 136
 FAR_UNROLL = 64
 NEAR_UNROLL = 64
@@ -212,28 +216,48 @@
 
 
 def near_loop(idx, lhs, lhs_at, tiles, first, dims, acc, acc_at):
-    count = tiles.shape[0]
+    count, size = tiles.shape[:2]
+    rows = lhs.shape[1]
     group = min(NEAR_UNROLL, count)
+    zero = jnp.zeros((rows, size), lhs.dtype)
     for low in range(0, count, group):
-        span = range(low, min(low + group, count))
-        sums = [dot(lhs[idx[lhs_at, first + n]], tiles[n], dims) for n in span]
-        for n in span:
+        high = min(low + group, count)
+        sums = []
+        for n in range(low, high, 2):
+            a, b = (lhs[idx[lhs_at, first + n + i]] for i in range(2))
+            both = jnp.concatenate([tiles[n], tiles[n + 1]], axis=0)
+            if dims is TRN:
+                out = dot(jnp.concatenate([a, b], axis=0), both, TRN)
+                sums += [out[:rows, :size], out[rows:, size:]]
+            else:
+                wide = [jnp.concatenate(x, axis=1) for x in ((a, zero), (zero, b))]
+                out = dot(jnp.concatenate(wide, axis=0), both, NAT)
+                sums += [out[:rows], out[rows:]]
+        for n in range(low, high):
             acc[idx[acc_at, first + n]] += sums[n - low]
 
 
-def near_second_a_kernel(idx, mine, theirs, tiles, rest, zero, acc, both, tiles_high, sem):
+def near_second_a_kernel(idx, mine, theirs, tiles, rest, zero, acc, both, tiles_high, sems):
     rows, size = mine.shape[1:]
 
     half, pairs = tiles.shape[0], rest.shape[0]
-    copy = pltpu.make_async_copy(rest.at[pl.ds(half, pairs - half)], tiles_high, sem)
-    copy.start()
+    count = (pairs - half) // TILE_COPIES
+    copies = [
+        pltpu.make_async_copy(
+            rest.at[pl.ds(half + i * count, count)], tiles_high.at[pl.ds(i * count, count)], sems.at[i]
+        )
+        for i in range(TILE_COPIES)
+    ]
+    for copy in copies:
+        copy.start()
     lane = lax.broadcasted_iota(I32, (rows, size), 1)
     for c in range(both.shape[0]):
         x = theirs[:, c * size : (c + 1) * size]
         x = jnp.where(lane < idx[2, c], x, jnp.zeros_like(x))
         both[c] = jnp.concatenate([mine[c], x], axis=0)
     near_loop(idx, both, 0, tiles, 0, NAT, acc, 1)
-    copy.wait()
+    for copy in copies:
+        copy.wait()
     near_loop(idx, both, 0, tiles_high, half, NAT, acc, 1)
 
 
@@ -470,7 +494,7 @@
             pltpu.VMEM(basis_t.shape, BF16),
             pltpu.VMEM((4, width), I32),
             pltpu.VMEM((1, cells), I32),
-            pltpu.SemaphoreType.DMA((9,)),
+            pltpu.SemaphoreType.DMA((8 + TILE_COPIES,)),
         ],
         compiler_params=params(8),
         cost_estimate=pl.CostEstimate(flops=0, bytes_accessed=12 << 20, transcendentals=0),
@@ -493,7 +517,7 @@
         input_output_aliases={5: 0},
         out_specs=[VMEM] * 3,
         out_shape=[near_acc, shape(cells, BF16, 2 * rows), shape(pairs - pairs // 2, BF16, size)],
-        scratch_shapes=[pltpu.SemaphoreType.DMA],
+        scratch_shapes=[pltpu.SemaphoreType.DMA((TILE_COPIES,))],
         compiler_params=params(4),
         cost_estimate=near_cost,
         name="near_second_a",

time: 58.3 us -> 56.5 us (0.969)
  Pallas kernels: 25.3 us -> 23 us
  waiting for transfers between devices: 10.5 us -> 11.1 us
    pallas_call x1, Pallas kernels: 5.25 us -> 3.79 us  [body(): pl.pallas_call(functools.partial(near_first_kernel, stride, cells, places...]
  transfers between devices with their start and end apart: 21 -> 21, of which waited for: 12 -> 13; matrix products, arithmetic and copies ran while one was open for 1% -> 1% of each run, Pallas kernels for 41% -> 38%
where the time goes in v6:
time: 56.5 us; the launch traced here: 56.4 us
  Pallas kernels  23 us (41%)
  starting transfers between devices  21.7 us (38%)
  waiting for transfers between devices  11.1 us (20%)
    ppermute x7, starting transfers between devices, swap_blk(): return lax.ppermute(x, 'blk', [(i, i ^ 1 << bit) for i in range(blks)])  12.6 us
    ppermute x14, starting transfers between devices, swap_rank(): return lax.ppermute(x, 'rhs', [(i, i ^ d) for i in range(ranks)])  9.09 us
    ppermute x14, waiting for transfers between devices, swap_rank(): return lax.ppermute(x, 'rhs', [(i, i ^ d) for i in range(ranks)])  7.25 us
    ppermute x7, waiting for transfers between devices, swap_blk(): return lax.ppermute(x, 'blk', [(i, i ^ 1 << bit) for i in range(blks)])  3.86 us
    pallas_call x1, Pallas kernels, body(): pl.pallas_call(functools.partial(near_first_kernel, stride, cells, places...  3.79 us
    pallas_call x1, Pallas kernels, body(): pl.pallas_call(functools.partial(far_target_kernel, stride, cells), in_sp...  3.66 us
    pallas_call x1, Pallas kernels, body(): pl.pallas_call(far_source_b_kernel, in_specs=[SMEM] + [VMEM] * 4, out_spe...  3.36 us
    pallas_call x1, Pallas kernels, body(): pl.pallas_call(near_second_a_kernel, in_specs=[SMEM, VMEM, VMEM, VMEM, HB...  3.15 us
  transfers between devices with their start and end apart: 21, of which 13 were waited for; matrix products, arithmetic and copies ran while one was open for 1% of the time, Pallas kernels for 38%

profile of v6, /device:TPU:0, one launch (start us, length us, event | category | flops | bytes accessed | tf_op | source)
XLA Modules:
  0.0 56.4 jit_solution(15557760570652842988)
XLA Ops:
  0.0 0.5 collective-permute-start.1
  0.5 2.5 %collective-permute-start = (bf16[16,2048]{1,0:T(8,128)(2,1)}, bf16[16,2048]{1,0:T(8,128)(2,1)S(1)}, u32[]{:S(2)}, u32[]{:S(2)}) collective-permute-start(bf16[16,2048]{1,0:T(8,128)(2,1)} %charges_in.1), channel_id=1, source_target_pairs={{0,2},{1,3},{2,0},{3,1},{4,6},{5,7},{6,4},{7,5},{8,10},{9,11},{10,... | collective-permute-start | bytes 196616 | tf_op jit(solution)/shard_map/ppermute | solution.py:441
  2.9 1.8 %prep.1 = (bf16[24,16,128]{2,1,0:T(8,128)(2,1)S(1)}, s32[3,256]{1,0:T(4,128)S(1)}, s32[2,256]{1,0:T(2,128)S(1)}, s32[2,256]{1,0:T(2,128)S(1)}, s32[2,256]{1,0:T(...) custom-call(s32[1,16]{1,0:T(1,128)} %bitcast.20, bf16[16,2048]{1,0:T(8,128)(2,1)} %charges_in.1, ...), custom_call_target="tpu_custom_call" | custom-call | bytes 12582912 | tf_op jit(solution)/shard_map/prep/pallas_call | solution.py:481
  4.8 1.6 %collective-permute-start.2 = (bf16[24,16,128]{2,1,0:T(8,128)(2,1)S(1)}, bf16[24,16,128]{2,1,0:T(8,128)(2,1)S(1)}, u32[]{:S(2)}, u32[]{:S(2)}) collective-permute-start(bf16[24,16,128]{2,1,0:T(8,128)(2,1)S(1)} %get-tuple-element.58), channel_id=1, source_target_pairs={{0,4},{4,0},{8,12},{12,8},{16,20},{20,16},{24,28},{28,24},{1,5},{5... | collective-permute-start | bytes 294920 | tf_op jit(solution)/shard_map/ppermute | solution.py:444
  6.4 3.1 %near_second_a.1 = (f32[128,32,128]{2,1,0:T(8,128)S(1)}, bf16[16,32,128]{2,1,0:T(8,128)(2,1)S(1)}, bf16[64,128,128]{2,1,0:T(8,128)(2,1)S(1)}) custom-call(s32[3,256]{1,0:T(4,128)S(1)} %get-tuple-element.57.idx, bf16[16,16,128]{2,1,0:T(8,128)(2,1)S(1)} %slice.18.mine.moved, ...), custom_call_target="tpu_custom_call", output_to_operand_aliasing={{0}: (5, {})} | custom-call | flops 134217728 | bytes 10485760 | tf_op jit(solution)/shard_map/near_second_a/pallas_call | solution.py:514
  9.6 0.2 collective-permute-done.2
  9.8 0.1 constant_dynamic-update-slice_fusion.7
  9.8 2.7 %collective-permute-start.5 = (bf16[48,16,128]{2,1,0:T(8,128)(2,1)S(1)}, bf16[48,16,128]{2,1,0:T(8,128)(2,1)S(1)}, u32[]{:S(2)}, u32[]{:S(2)}) collective-permute-start(bf16[48,16,128]{2,1,0:T(8,128)(2,1)S(1)} %get-tuple-element.115), channel_id=1, source_target_pairs={{0,16},{4,20},{8,24},{12,28},{16,0},{20,4},{24,8},{28,12},{1,17},{... | collective-permute-start | bytes 589832 | tf_op jit(solution)/shard_map/ppermute | solution.py:444
  12.5 2.1 %near_second_b.1 = (f32[128,32,128]{2,1,0:T(8,128)S(1)}, f32[64,16,128]{2,1,0:T(8,128)S(1)}, s16[68,16,128]{2,1,0:T(8,128)(2,1)S(1)}, f32[32,32,128]{2,1,0:T(8,128)S(1)}, s16[68,16,128]{2,1,0:T(8,128)(2,1)S(1)}) custom-call(s32[3,256]{1,0:T(4,128)S(1)} %get-tuple-element.57.idx, ...), custom_call_target="tpu_custom_call", output_to_operand_aliasing={{0}: (3, {})} | custom-call | flops 134217728 | bytes 10485760 | tf_op jit(solution)/shard_map/near_second_b/pallas_call | solution.py:532
  14.6 1.6 %collective-permute-start.3 = (s16[68,16,128]{2,1,0:T(8,128)(2,1)S(1)}, s16[68,16,128]{2,1,0:T(8,128)(2,1)S(1)}, u32[]{:S(2)}, u32[]{:S(2)}) collective-permute-start(s16[68,16,128]{2,1,0:T(8,128)(2,1)S(1)} %get-tuple-element.68), channel_id=1, source_target_pairs={{0,4},{4,0},{8,12},{12,8},{16,20},{20,16},{24,28},{28,24},{1,5},{5... | collective-permute-start | bytes 835592 | tf_op jit(solution)/shard_map/ppermute | solution.py:444
  16.2 1.1 %collective-permute-start.4 = (s16[68,16,128]{2,1,0:T(8,128)(2,1)S(1)}, s16[68,16,128]{2,1,0:T(8,128)(2,1)S(1)}, u32[]{:S(2)}, u32[]{:S(2)}) collective-permute-start(s16[68,16,128]{2,1,0:T(8,128)(2,1)S(1)} %get-tuple-element.69), channel_id=1, source_target_pairs={{0,2},{1,3},{2,0},{3,1},{4,6},{5,7},{6,4},{7,5},{8,10},{9,11},{10,... | collective-permute-start | bytes 835592 | tf_op jit(solution)/shard_map/ppermute | solution.py:441
  17.3 2.1 %far_source_a.1 = (bf16[128,32,128]{2,1,0:T(8,128)(2,1)S(1)}, f32[128,32,64]{2,1,0:T(8,128)S(1)}) custom-call(s32[2,256]{1,0:T(2,128)S(1)} %get-tuple-element.72.idx, bf16[8,16,128]{2,1,0:T(8,128)(2,1)S(1)} %slice.19.mine, bf16[8,16,128]{2,1,0:T(8,128)(2,1)S(1)} %collective-permute-done.6.theirs, bf16[4096,512]{1,0:T(8,128)(2,1)S(1)} %bitcast.15), custom_call_target="tpu_custom_call" | custom-call | flops 67108864 | bytes 12582912 | tf_op jit(solution)/shard_map/far_source_a/pallas_call | solution.py:558
  19.4 2.2 %collective-permute-done.5 = bf16[48,16,128]{2,1,0:T(8,128)(2,1)S(1)} collective-permute-done((bf16[48,16,128]{2,1,0:T(8,128)(2,1)S(1)}, bf16[48,16,128]{2,1,0:T(8,128)(2,1)S(1)}, u32[]{:S(2)}, u32[]{:S(2)}) %collective-permute-start.5) | collective-permute-done | bytes 196640 | tf_op jit(solution)/shard_map/ppermute | solution.py:444
  21.6 0.1 constant_dynamic-update-slice_fusion.6
  21.7 0.7 %collective-permute-start.13 = (bf16[96,16,128]{2,1,0:T(8,128)(2,1)S(1)}, bf16[96,16,128]{2,1,0:T(8,128)(2,1)S(1)}, u32[]{:S(2)}, u32[]{:S(2)}) collective-permute-start(bf16[96,16,128]{2,1,0:T(8,128)(2,1)S(1)} %get-tuple-element.112), channel_id=1, source_target_pairs={{0,8},{4,12},{8,0},{12,4},{16,24},{20,28},{24,16},{28,20},{1,9},{5... | collective-permute-start | bytes 1179656 | tf_op jit(solution)/shard_map/ppermute | solution.py:444
  22.4 1.1 %collective-permute-start.7 = (bf16[32,16,128]{2,1,0:T(8,128)(2,1)S(1)}, bf16[32,16,128]{2,1,0:T(8,128)(2,1)S(1)}, u32[]{:S(2)}, u32[]{:S(2)}) collective-permute-start(bf16[32,16,128]{2,1,0:T(8,128)(2,1)S(1)} %bitcast.25), channel_id=1, source_target_pairs={{0,2},{1,3},{2,0},{3,1},{4,6},{5,7},{6,4},{7,5},{8,10},{9,11},{10,... | collective-permute-start | bytes 393224 | tf_op jit(solution)/shard_map/ppermute | solution.py:441
  23.5 3.4 %far_source_b.1 = (bf16[128,32,128]{2,1,0:T(8,128)(2,1)S(1)}, f32[128,32,64]{2,1,0:T(8,128)S(1)}, f32[64,16,128]{2,1,0:T(8,128)S(1)}, f32[16,16,128]{2,1,0:T(8,1...) custom-call(s32[2,256]{1,0:T(2,128)S(1)} %get-tuple-element.72.idx, ...), custom_call_target="tpu_custom_call", output_to_operand_aliasing={{1}: (4, {})} | custom-call | flops 67108864 | bytes 12582912 | tf_op jit(solution)/shard_map/far_source_b/pallas_call | solution.py:578
  26.9 0.1 collective-permute-start.8
  27.0 0.2 meet_b.1
  27.2 1.1 %collective-permute-start.14 = (s16[34,16,128]{2,1,0:T(8,128)(2,1)S(1)}, s16[34,16,128]{2,1,0:T(8,128)(2,1)S(1)}, u32[]{:S(2)}, u32[]{:S(2)}) collective-permute-start(s16[34,16,128]{2,1,0:T(8,128)(2,1)S(1)} %get-tuple-element.71), channel_id=1, source_target_pairs={{0,2},{1,3},{2,0},{3,1},{4,6},{5,7},{6,4},{7,5},{8,10},{9,11},{10,... | collective-permute-start | bytes 417800 | tf_op jit(solution)/shard_map/ppermute | solution.py:441
  28.3 0.2 collective-permute-start.9
  28.5 0.3 collective-permute-start.10
  28.8 0.2 collective-permute-start.11
  29.0 0.1 join.1.mine
  29.1 0.5 collective-permute-done.9.refs_1_
  29.6 0.2 collective-permute-done.10.refs_2_
  29.8 0.3 collective-permute-done.11.refs_3_
  30.1 0.3 meet_a.1
  30.5 1.2 %collective-permute-start.12 = (s16[68,16,128]{2,1,0:T(8,128)(2,1)S(1)}, s16[68,16,128]{2,1,0:T(8,128)(2,1)S(1)}, u32[]{:S(2)}, u32[]{:S(2)}) collective-permute-start(s16[68,16,128]{2,1,0:T(8,128)(2,1)S(1)} %get-tuple-element.86), channel_id=1, source_target_pairs={{0,4},{4,0},{8,12},{12,8},{16,20},{20,16},{24,28},{28,24},{1,5},{5... | collective-permute-start | bytes 835592 | tf_op jit(solution)/shard_map/ppermute | solution.py:444
  31.7 1.6 %collective-permute-done.14.coded_b = s16[34,16,128]{2,1,0:T(8,128)(2,1)S(1)} collective-permute-done((s16[34,16,128]{2,1,0:T(8,128)(2,1)S(1)}, s16[34,16,128]{2,1,0:T(8,128)(2,1)S(1)}, u32[]{:S(2)}, u32[]{:S(2)}) %collective-permute-start.14) | collective-permute-done | bytes 139296 | tf_op jit(solution)/shard_map/ppermute | solution.py:441
  33.4 0.1 collective-permute-start.15
  33.5 1.1 %collective-permute-start.17 = (bf16[64,16,128]{2,1,0:T(8,128)(2,1)S(1)}, bf16[64,16,128]{2,1,0:T(8,128)(2,1)S(1)}, u32[]{:S(2)}, u32[]{:S(2)}) collective-permute-start(bf16[64,16,128]{2,1,0:T(8,128)(2,1)S(1)} %bitcast.22), channel_id=1, source_target_pairs={{0,2},{1,3},{2,0},{3,1},{4,6},{5,7},{6,4},{7,5},{8,10},{9,11},{10,... | collective-permute-start | bytes 786440 | tf_op jit(solution)/shard_map/ppermute | solution.py:441
  34.6 0.4 collective-permute-done.15.theirs
  35.0 3.7 %far_target.1 = (f32[8,16,128]{2,1,0:T(8,128)S(1)}, f32[8,16,128]{2,1,0:T(8,128)S(1)}) custom-call(s32[2,256]{1,0:T(2,128)S(1)} %get-tuple-element.88.idx, bf16[192,16,128]{2,1,0:T(8,128)(2,1)S(1)} %constant_dynamic-update-slice_fusion.5.everyone, bf16[64,16,128]{2,1,0:T(8,128)(2,1)S(1)} %collective-permute-done.15.theirs, ...), custom_call_target="tpu_custom_call" | custom-call | bytes 1048576 | tf_op jit(solution)/shard_map/far_target/pallas_call | solution.py:641
  38.7 0.6 %collective-permute-done.12.coded_a = s16[68,16,128]{2,1,0:T(8,128)(2,1)S(1)} collective-permute-done((s16[68,16,128]{2,1,0:T(8,128)(2,1)S(1)}, s16[68,16,128]{2,1,0:T(8,128)(2,1)S(1)}, u32[]{:S(2)}, u32[]{:S(2)}) %collective-permute-start.12) | collective-permute-done | bytes 278560 | tf_op jit(solution)/shard_map/ppermute | solution.py:444
  39.3 0.3 meet.1
  39.6 1.4 %collective-permute-start.16 = (s16[51,16,128]{2,1,0:T(8,128)(2,1)S(1)}, s16[51,16,128]{2,1,0:T(8,128)(2,1)S(1)}, u32[]{:S(2)}, u32[]{:S(2)}) collective-permute-start(s16[51,16,128]{2,1,0:T(8,128)(2,1)S(1)} %get-tuple-element.97), channel_id=1, source_target_pairs={{0,8},{4,12},{8,0},{12,4},{16,24},{20,28},{24,16},{28,20},{1,9},{5... | collective-permute-start | bytes 626696 | tf_op jit(solution)/shard_map/ppermute | solution.py:444
  41.1 1.2 %collective-permute-done.17.refs_1_ = bf16[64,16,128]{2,1,0:T(8,128)(2,1)S(1)} collective-permute-done((bf16[64,16,128]{2,1,0:T(8,128)(2,1)S(1)}, bf16[64,16,128]{2,1,0:T(8,128)(2,1)S(1)}, u32[]{:S(2)}, u32[]{:S(2)}) %collective-permute-start.17) | collective-permute-done | bytes 262176 | tf_op jit(solution)/shard_map/ppermute | solution.py:441
  42.3 3.8 %near_first.1 = (f32[16,16,128]{2,1,0:T(8,128)S(1)}, s16[17,16,128]{2,1,0:T(8,128)(2,1)S(1)}) custom-call(s32[2,256]{1,0:T(2,128)S(1)} %get-tuple-element.99.idx, bf16[192,16,128]{2,1,0:T(8,128)(2,1)S(1)} %constant_dynamic-update-slice_fusion.5.everyone, bf16[16,32,128]{2,1,0:T(8,128)(2,1)S(1)} %get-tuple-element.61.both, ...), custom_call_target="tpu_custom_call" | custom-call | flops 268435456 | bytes 20971520 | tf_op jit(solution)/shard_map/near_first/pallas_call | solution.py:686
  46.1 0.2 collective-permute-done.16.coded
  46.3 0.2 add.1
  46.5 3.4 %collective-permute-start.18 = (s16[26,16,128]{2,1,0:T(8,128)(2,1)S(1)}, s16[26,16,128]{2,1,0:T(8,128)(2,1)S(1)}, u32[]{:S(2)}, u32[]{:S(2)}) collective-permute-start(s16[26,16,128]{2,1,0:T(8,128)(2,1)S(1)} %get-tuple-element.105), channel_id=1, source_target_pairs={{0,16},{4,20},{8,24},{12,28},{16,0},{20,4},{24,8},{28,12},{1,17},{... | collective-permute-start | bytes 319496 | tf_op jit(solution)/shard_map/ppermute | solution.py:444
  49.9 1.0 %collective-permute-start.19 = (s16[17,16,128]{2,1,0:T(8,128)(2,1)S(1)}, s16[17,16,128]{2,1,0:T(8,128)(2,1)S(1)}, u32[]{:S(2)}, u32[]{:S(2)}) collective-permute-start(s16[17,16,128]{2,1,0:T(8,128)(2,1)S(1)} %get-tuple-element.107), channel_id=1, source_target_pairs={{0,2},{1,3},{2,0},{3,1},{4,6},{5,7},{6,4},{7,5},{8,10},{9,11},{10,... | collective-permute-start | bytes 208904 | tf_op jit(solution)/shard_map/ppermute | solution.py:441
  50.9 0.4 self.1.own
  51.3 0.9 %collective-permute-done.20.target_other = f32[8,16,128]{2,1,0:T(8,128)S(1)} collective-permute-done((f32[8,16,128]{2,1,0:T(8,128)S(1)}, f32[8,16,128]{2,1,0:T(8,128)S(1)}, u32[]{:S(2)}, u32[]{:S(2)}) %collective-permute-start.20) | collective-permute-done | bytes 65568 | tf_op jit(solution)/shard_map/ppermute | solution.py:441
  52.2 2.1 %collective-permute-done.19.first_other = s16[17,16,128]{2,1,0:T(8,128)(2,1)S(1)} collective-permute-done((s16[17,16,128]{2,1,0:T(8,128)(2,1)S(1)}, s16[17,16,128]{2,1,0:T(8,128)(2,1)S(1)}, u32[]{:S(2)}, u32[]{:S(2)}) %collective-permute-start.19) | collective-permute-done | bytes 69664 | tf_op jit(solution)/shard_map/ppermute | solution.py:441
  54.2 0.6 %collective-permute-done.18.coded = s16[26,16,128]{2,1,0:T(8,128)(2,1)S(1)} collective-permute-done((s16[26,16,128]{2,1,0:T(8,128)(2,1)S(1)}, s16[26,16,128]{2,1,0:T(8,128)(2,1)S(1)}, u32[]{:S(2)}, u32[]{:S(2)}) %collective-permute-start.18) | collective-permute-done | bytes 106528 | tf_op jit(solution)/shard_map/ppermute | solution.py:444
  54.9 1.5 %final.1 = f32[16,2048]{1,0:T(8,128)} custom-call(s32[16]{0:T(128)S(1)} %copy-done.3, f32[24,16,128]{2,1,0:T(8,128)S(1)} %get-tuple-element.98.mine, s16[26,16,128]{2,1,0:T(8,128)(2,1)S(1)} %collective-permute-done.18.coded, f32[16,16,128]{2,1,0:T(8,128)S(1)} %get-tuple-element.106.first, s16[17,16,128]{2,1,0:T(8,128)(2,1)S(1)} %collective-permute-done.19.first_other, ...), custom_call_target="tpu_custom_call" | custom-call | tf_op jit(solution)/shard_map/final/pallas_call | solution.py:715
  (26 shorter events, 0.2 us)
Async XLA Ops:
  0.0 12.5 %collective-permute-start.1 = (bf16[128,128,128]{2,1,0:T(8,128)(2,1)}, bf16[128,128,128]{2,1,0:T(8,128)(2,1)S(1)}, u32[]{:S(2)}, u32[]{:S(2)}) collective-permute-start(bf16[128,128,128]{2,1,0:T(8,128)(2,1)} %rest.1), channel_id=1, source_target_pairs={{0,1},{1,0},{2,3},{3,2},{4,5},{5,4},{6,7},{7,6},{8,9},{9,8},{10,11... | collective-permute-start | bytes 12582920 | tf_op jit(solution)/shard_map/ppermute | solution.py:441
  0.5 5.9 %collective-permute-start = (bf16[16,2048]{1,0:T(8,128)(2,1)}, bf16[16,2048]{1,0:T(8,128)(2,1)S(1)}, u32[]{:S(2)}, u32[]{:S(2)}) collective-permute-start(bf16[16,2048]{1,0:T(8,128)(2,1)} %charges_in.1), channel_id=1, source_target_pairs={{0,2},{1,3},{2,0},{3,1},{4,6},{5,7},{6,4},{7,5},{8,10},{9,11},{10,... | collective-permute-start | bytes 196616 | tf_op jit(solution)/shard_map/ppermute | solution.py:441
  4.8 5.0 %collective-permute-start.2 = (bf16[24,16,128]{2,1,0:T(8,128)(2,1)S(1)}, bf16[24,16,128]{2,1,0:T(8,128)(2,1)S(1)}, u32[]{:S(2)}, u32[]{:S(2)}) collective-permute-start(bf16[24,16,128]{2,1,0:T(8,128)(2,1)S(1)} %get-tuple-element.58), channel_id=1, source_target_pairs={{0,4},{4,0},{8,12},{12,8},{16,20},{20,16},{24,28},{28,24},{1,5},{5... | collective-permute-start | bytes 294920 | tf_op jit(solution)/shard_map/ppermute | solution.py:444
  9.8 11.7 %collective-permute-start.5 = (bf16[48,16,128]{2,1,0:T(8,128)(2,1)S(1)}, bf16[48,16,128]{2,1,0:T(8,128)(2,1)S(1)}, u32[]{:S(2)}, u32[]{:S(2)}) collective-permute-start(bf16[48,16,128]{2,1,0:T(8,128)(2,1)S(1)} %get-tuple-element.115), channel_id=1, source_target_pairs={{0,16},{4,20},{8,24},{12,28},{16,0},{20,4},{24,8},{28,12},{1,17},{... | collective-permute-start | bytes 589832 | tf_op jit(solution)/shard_map/ppermute | solution.py:444
  12.5 4.8 %collective-permute-start.6 = (bf16[8,16,128]{2,1,0:T(8,128)(2,1)S(1)}, bf16[8,16,128]{2,1,0:T(8,128)(2,1)S(1)}, u32[]{:S(2)}, u32[]{:S(2)}) collective-permute-start(bf16[8,16,128]{2,1,0:T(8,128)(2,1)S(1)} %slice.19.mine), channel_id=1, source_target_pairs={{0,1},{1,0},{2,3},{3,2},{4,5},{5,4},{6,7},{7,6},{8,9},{9,8},{10,11... | collective-permute-start | bytes 98312 | tf_op jit(solution)/shard_map/ppermute | solution.py:441
  12.5 4.8 %copy-start = (bf16[512,64,64]{0,2,1:T(8,128)(2,1)S(1)}, bf16[512,64,64]{0,2,1:T(8,128)(2,1)}, u32[]{:S(2)}) copy-start(bf16[512,64,64]{0,2,1:T(8,128)(2,1)} %param.19) | copy-start | bytes 12582916
  14.6 12.4 %collective-permute-start.3 = (s16[68,16,128]{2,1,0:T(8,128)(2,1)S(1)}, s16[68,16,128]{2,1,0:T(8,128)(2,1)S(1)}, u32[]{:S(2)}, u32[]{:S(2)}) collective-permute-start(s16[68,16,128]{2,1,0:T(8,128)(2,1)S(1)} %get-tuple-element.68), channel_id=1, source_target_pairs={{0,4},{4,0},{8,12},{12,8},{16,20},{20,16},{24,28},{28,24},{1,5},{5... | collective-permute-start | bytes 835592 | tf_op jit(solution)/shard_map/ppermute | solution.py:444
  16.2 10.8 %collective-permute-start.4 = (s16[68,16,128]{2,1,0:T(8,128)(2,1)S(1)}, s16[68,16,128]{2,1,0:T(8,128)(2,1)S(1)}, u32[]{:S(2)}, u32[]{:S(2)}) collective-permute-start(s16[68,16,128]{2,1,0:T(8,128)(2,1)S(1)} %get-tuple-element.69), channel_id=1, source_target_pairs={{0,2},{1,3},{2,0},{3,1},{4,6},{5,7},{6,4},{7,5},{8,10},{9,11},{10,... | collective-permute-start | bytes 835592 | tf_op jit(solution)/shard_map/ppermute | solution.py:441
  21.7 10.1 %collective-permute-start.13 = (bf16[96,16,128]{2,1,0:T(8,128)(2,1)S(1)}, bf16[96,16,128]{2,1,0:T(8,128)(2,1)S(1)}, u32[]{:S(2)}, u32[]{:S(2)}) collective-permute-start(bf16[96,16,128]{2,1,0:T(8,128)(2,1)S(1)} %get-tuple-element.112), channel_id=1, source_target_pairs={{0,8},{4,12},{8,0},{12,4},{16,24},{20,28},{24,16},{28,20},{1,9},{5... | collective-permute-start | bytes 1179656 | tf_op jit(solution)/shard_map/ppermute | solution.py:444
  22.4 6.0 %collective-permute-start.7 = (bf16[32,16,128]{2,1,0:T(8,128)(2,1)S(1)}, bf16[32,16,128]{2,1,0:T(8,128)(2,1)S(1)}, u32[]{:S(2)}, u32[]{:S(2)}) collective-permute-start(bf16[32,16,128]{2,1,0:T(8,128)(2,1)S(1)} %bitcast.25), channel_id=1, source_target_pairs={{0,2},{1,3},{2,0},{3,1},{4,6},{5,7},{6,4},{7,5},{8,10},{9,11},{10,... | collective-permute-start | bytes 393224 | tf_op jit(solution)/shard_map/ppermute | solution.py:441
  26.9 1.9 %collective-permute-start.8 = (f32[16,16,128]{2,1,0:T(8,128)S(1)}, f32[16,16,128]{2,1,0:T(8,128)S(1)}, u32[]{:S(2)}, u32[]{:S(2)}) collective-permute-start(f32[16,16,128]{2,1,0:T(8,128)S(1)} %get-tuple-element.81), channel_id=1, source_target_pairs={{0,1},{1,0},{2,3},{3,2},{4,5},{5,4},{6,7},{7,6},{8,9},{9,8},{10,11... | collective-permute-start | bytes 393224 | tf_op jit(solution)/shard_map/ppermute | solution.py:441
  27.2 6.1 %collective-permute-start.14 = (s16[34,16,128]{2,1,0:T(8,128)(2,1)S(1)}, s16[34,16,128]{2,1,0:T(8,128)(2,1)S(1)}, u32[]{:S(2)}, u32[]{:S(2)}) collective-permute-start(s16[34,16,128]{2,1,0:T(8,128)(2,1)S(1)} %get-tuple-element.71), channel_id=1, source_target_pairs={{0,2},{1,3},{2,0},{3,1},{4,6},{5,7},{6,4},{7,5},{8,10},{9,11},{10,... | collective-permute-start | bytes 417800 | tf_op jit(solution)/shard_map/ppermute | solution.py:441
  28.3 1.3 %collective-permute-start.9 = (f32[16,16,128]{2,1,0:T(8,128)S(1)}, f32[16,16,128]{2,1,0:T(8,128)S(1)}, u32[]{:S(2)}, u32[]{:S(2)}) collective-permute-start(f32[16,16,128]{2,1,0:T(8,128)S(1)} %get-tuple-element.82), channel_id=1, source_target_pairs={{0,1},{1,0},{2,3},{3,2},{4,5},{5,4},{6,7},{7,6},{8,9},{9,8},{10,11... | collective-permute-start | bytes 393224 | tf_op jit(solution)/shard_map/ppermute | solution.py:441
  28.5 1.3 %collective-permute-start.10 = (f32[16,16,128]{2,1,0:T(8,128)S(1)}, f32[16,16,128]{2,1,0:T(8,128)S(1)}, u32[]{:S(2)}, u32[]{:S(2)}) collective-permute-start(f32[16,16,128]{2,1,0:T(8,128)S(1)} %get-tuple-element.83), channel_id=1, source_target_pairs={{0,1},{1,0},{2,3},{3,2},{4,5},{5,4},{6,7},{7,6},{8,9},{9,8},{10,11... | collective-permute-start | bytes 393224 | tf_op jit(solution)/shard_map/ppermute | solution.py:441
  28.8 1.3 %collective-permute-start.11 = (f32[16,16,128]{2,1,0:T(8,128)S(1)}, f32[16,16,128]{2,1,0:T(8,128)S(1)}, u32[]{:S(2)}, u32[]{:S(2)}) collective-permute-start(f32[16,16,128]{2,1,0:T(8,128)S(1)} %get-tuple-element.84), channel_id=1, source_target_pairs={{0,1},{1,0},{2,3},{3,2},{4,5},{5,4},{6,7},{7,6},{8,9},{9,8},{10,11... | collective-permute-start | bytes 393224 | tf_op jit(solution)/shard_map/ppermute | solution.py:441
  30.5 8.8 %collective-permute-start.12 = (s16[68,16,128]{2,1,0:T(8,128)(2,1)S(1)}, s16[68,16,128]{2,1,0:T(8,128)(2,1)S(1)}, u32[]{:S(2)}, u32[]{:S(2)}) collective-permute-start(s16[68,16,128]{2,1,0:T(8,128)(2,1)S(1)} %get-tuple-element.86), channel_id=1, source_target_pairs={{0,4},{4,0},{8,12},{12,8},{16,20},{20,16},{24,28},{28,24},{1,5},{5... | collective-permute-start | bytes 835592 | tf_op jit(solution)/shard_map/ppermute | solution.py:444
  33.4 1.6 %collective-permute-start.15 = (bf16[64,16,128]{2,1,0:T(8,128)(2,1)S(1)}, bf16[64,16,128]{2,1,0:T(8,128)(2,1)S(1)}, u32[]{:S(2)}, u32[]{:S(2)}) collective-permute-start(bf16[64,16,128]{2,1,0:T(8,128)(2,1)S(1)} %bitcast.23), channel_id=1, source_target_pairs={{0,1},{1,0},{2,3},{3,2},{4,5},{5,4},{6,7},{7,6},{8,9},{9,8},{10,11... | collective-permute-start | bytes 786440 | tf_op jit(solution)/shard_map/ppermute | solution.py:441
  33.5 8.8 %collective-permute-start.17 = (bf16[64,16,128]{2,1,0:T(8,128)(2,1)S(1)}, bf16[64,16,128]{2,1,0:T(8,128)(2,1)S(1)}, u32[]{:S(2)}, u32[]{:S(2)}) collective-permute-start(bf16[64,16,128]{2,1,0:T(8,128)(2,1)S(1)} %bitcast.22), channel_id=1, source_target_pairs={{0,2},{1,3},{2,0},{3,1},{4,6},{5,7},{6,4},{7,5},{8,10},{9,11},{10,... | collective-permute-start | bytes 786440 | tf_op jit(solution)/shard_map/ppermute | solution.py:441
  39.6 6.7 %collective-permute-start.16 = (s16[51,16,128]{2,1,0:T(8,128)(2,1)S(1)}, s16[51,16,128]{2,1,0:T(8,128)(2,1)S(1)}, u32[]{:S(2)}, u32[]{:S(2)}) collective-permute-start(s16[51,16,128]{2,1,0:T(8,128)(2,1)S(1)} %get-tuple-element.97), channel_id=1, source_target_pairs={{0,8},{4,12},{8,0},{12,4},{16,24},{20,28},{24,16},{28,20},{1,9},{5... | collective-permute-start | bytes 626696 | tf_op jit(solution)/shard_map/ppermute | solution.py:444
  42.3 8.6 %copy-start.2 = (bf16[16,128,128]{2,1,0:T(8,128)(2,1)S(1)}, bf16[16,128,128]{2,1,0:T(8,128)(2,1)}, u32[]{:S(2)}) copy-start(bf16[16,128,128]{2,1,0:T(8,128)(2,1)} %self_tiles.1) | copy-start | bytes 1572868
  42.3 12.6 %copy-start.1 = (bf16[16,128,64]{1,2,0:T(8,128)(2,1)S(1)}, bf16[16,128,64]{1,2,0:T(8,128)(2,1)}, u32[]{:S(2)}) copy-start(bf16[16,128,64]{1,2,0:T(8,128)(2,1)} %param.13) | copy-start | bytes 786436
  42.3 12.6 %copy-start.3 = (s32[16]{0:T(128)S(1)}, s32[16]{0:T(128)}, u32[]{:S(2)}) copy-start(s32[16]{0:T(128)} %counts.1) | copy-start | bytes 196
  46.5 8.4 %collective-permute-start.18 = (s16[26,16,128]{2,1,0:T(8,128)(2,1)S(1)}, s16[26,16,128]{2,1,0:T(8,128)(2,1)S(1)}, u32[]{:S(2)}, u32[]{:S(2)}) collective-permute-start(s16[26,16,128]{2,1,0:T(8,128)(2,1)S(1)} %get-tuple-element.105), channel_id=1, source_target_pairs={{0,16},{4,20},{8,24},{12,28},{16,0},{20,4},{24,8},{28,12},{1,17},{... | collective-permute-start | bytes 319496 | tf_op jit(solution)/shard_map/ppermute | solution.py:444
  49.9 4.3 %collective-permute-start.19 = (s16[17,16,128]{2,1,0:T(8,128)(2,1)S(1)}, s16[17,16,128]{2,1,0:T(8,128)(2,1)S(1)}, u32[]{:S(2)}, u32[]{:S(2)}) collective-permute-start(s16[17,16,128]{2,1,0:T(8,128)(2,1)S(1)} %get-tuple-element.107), channel_id=1, source_target_pairs={{0,2},{1,3},{2,0},{3,1},{4,6},{5,7},{6,4},{7,5},{8,10},{9,11},{10,... | collective-permute-start | bytes 208904 | tf_op jit(solution)/shard_map/ppermute | solution.py:441
  50.9 1.3 %collective-permute-start.20 = (f32[8,16,128]{2,1,0:T(8,128)S(1)}, f32[8,16,128]{2,1,0:T(8,128)S(1)}, u32[]{:S(2)}, u32[]{:S(2)}) collective-permute-start(f32[8,16,128]{2,1,0:T(8,128)S(1)} %get-tuple-element.92), channel_id=1, source_target_pairs={{0,1},{1,0},{2,3},{3,2},{4,5},{5,4},{6,7},{7,6},{8,9},{9,8},{10,11... | collective-permute-start | bytes 196616 | tf_op jit(solution)/shard_map/ppermute | solution.py:441

commit v7 on v6

--- a/solution.py
+++ b/solution.py
@@ -124,45 +124,41 @@
 PARTS = 4
 
 
-def far_sources(step, idx, mine, theirs, tiles, turned, acc, flip, lhs):
+def far_source_kernel(idx, mine, theirs, tiles, turned, acc, flip, lhs):
     half = mine.shape[2] // 2
     pairs = half // 2
-    chunk = turned.shape[0]
+    end = turned.shape[0]
+    chunk = end // 2
+    acc[...] = jnp.zeros_like(acc)
     for k in range(mine.shape[0]):
         x, y = mine[k], theirs[k]
         for h in range(2):
             at = h * half
             lhs[2 * k + h] = jnp.concatenate([x[:, at : at + half], y[:, at : at + half]], axis=0)
-    span = pl.ds(pl.multiple_of((lax.axis_index("rhs") & 1) * 2 * chunk + step * chunk, chunk), chunk)
-    for i in range(pairs):
-        both = [tiles[(i + h * pairs) * half : (i + h * pairs + 1) * half, span] for h in range(2)]
-        flip[i * PITCH : i * PITCH + chunk, :] = jnp.concatenate(both, axis=0).astype(F32).T
-
-    def work(g, _):
-        sums = []
-        at = g * FAR_UNROLL
-        for u in range(FAR_UNROLL):
-            w = flip[pl.ds(at + u, pairs, stride=PITCH), :]
-            turned[at + u] = w.astype(BF16)
-            moved = pltpu.roll(w, half, 1)
-            w = jnp.concatenate([w[:, :half], moved[:, :half]], axis=0).astype(BF16)
-            sums.append(dot(lhs[idx[0, step * chunk + at + u]], w, NAT))
-        for u in range(FAR_UNROLL):
-            acc[idx[1, step * chunk + at + u]] += sums[u]
-        return 0
-
-    lax.fori_loop(0, chunk // FAR_UNROLL, work, 0)
-
-
-def far_source_a_kernel(idx, mine, theirs, tiles, turned, acc, flip, lhs):
-    acc[...] = jnp.zeros_like(acc)
-    far_sources(0, idx, mine, theirs, tiles, turned, acc, flip, lhs)
-
-
-def far_source_b_kernel(idx, mine, theirs, tiles, before, turned, acc, keep, *refs):
-    *sends, flip, lhs = refs
-    rows = mine.shape[1]
-    far_sources(1, idx, mine, theirs, tiles, turned, acc, flip, lhs)
+    for low in range(0, end, chunk):
+        span = pl.ds(pl.multiple_of((lax.axis_index("rhs") & 1) * end + low, chunk), chunk)
+        for i in range(pairs):
+            both = [tiles[(i + h * pairs) * half : (i + h * pairs + 1) * half, span] for h in range(2)]
+            flip[i * PITCH : i * PITCH + chunk, :] = jnp.concatenate(both, axis=0).astype(F32).T
+
+        def work(g, _, low=low):
+            sums = []
+            at = low + g * FAR_UNROLL
+            for u in range(FAR_UNROLL):
+                w = flip[pl.ds(at - low + u, pairs, stride=PITCH), :]
+                turned[at + u] = w.astype(BF16)
+                moved = pltpu.roll(w, half, 1)
+                w = jnp.concatenate([w[:, :half], moved[:, :half]], axis=0).astype(BF16)
+                sums.append(dot(lhs[idx[0, at + u]], w, NAT))
+            for u in range(FAR_UNROLL):
+                acc[idx[1, at + u]] += sums[u]
+            return 0
+
+        lax.fori_loop(0, chunk // FAR_UNROLL, work, 0)
+
+
+def far_fold_kernel(acc, keep, *sends):
+    rows = keep.shape[1]
     count = sends[0].shape[0]
     for q, send in enumerate(sends):
 
@@ -177,10 +173,9 @@
         lax.fori_loop(0, count // 4, fold, 0)
 
 
-def far_target_kernel(stride, cells, idx, everyone, theirs, turned_a, turned_b, keep, send, lhs, acc):
+def far_target_kernel(stride, cells, idx, everyone, theirs, turned, keep, send, lhs, acc):
     rows, lanes = everyone.shape[1], everyone.shape[2]
     half = lanes // 2
-    chunk = turned_a.shape[0]
     owners = everyone.shape[0] // stride
     acc[...] = jnp.zeros_like(acc)
     low = lax.broadcasted_iota(I32, (2 * rows, lanes), 1) < half
@@ -196,18 +191,17 @@
         return 0
 
     lax.fori_loop(0, owners, spread, 0)
-    for step, turned in enumerate((turned_a, turned_b)):
-
-        def work(g, _, base=step * chunk, turned=turned):
-            sums = []
-            for u in range(FAR_UNROLL):
-                e = g * FAR_UNROLL + u
-                sums.append(dot(lhs[idx[1, base + e]], turned[e], TRN))
-            for u in range(FAR_UNROLL):
-                acc[idx[0, base + g * FAR_UNROLL + u]] += sums[u]
-            return 0
-
-        lax.fori_loop(0, chunk // FAR_UNROLL, work, 0)
+
+    def work(g, _):
+        sums = []
+        for u in range(FAR_UNROLL):
+            e = g * FAR_UNROLL + u
+            sums.append(dot(lhs[idx[1, e]], turned[e], TRN))
+        for u in range(FAR_UNROLL):
+            acc[idx[0, g * FAR_UNROLL + u]] += sums[u]
+        return 0
+
+    lax.fori_loop(0, turned.shape[0] // FAR_UNROLL, work, 0)
     for k in range(cells // 2):
         a, b = acc[2 * k], acc[2 * k + 1]
         for r, out in enumerate((keep, send)):
@@ -555,15 +549,15 @@
         pltpu.VMEM((cells, 2 * rows, terms), BF16),
     ]
     far_sums = jax.ShapeDtypeStruct((total, 2 * rows, terms), F32)
-    turned_a, far_acc = pl.pallas_call(
-        far_source_a_kernel,
+    turned, far_acc = pl.pallas_call(
+        far_source_kernel,
         in_specs=[SMEM] + [VMEM] * 3,
         out_specs=[VMEM] * 2,
-        out_shape=[shape(fars // 4, BF16, terms // 2), far_sums],
+        out_shape=[shape(fars // 2, BF16, terms // 2), far_sums],
         scratch_shapes=far_scratch,
         compiler_params=params(6),
         cost_estimate=far_cost,
-        name="far_source_a",
+        name="far_source",
     )(at_source, moment_own, moment_late, tiles_ij)
     received, far_acc = lax.optimization_barrier((received, far_acc))
     others, places = [], []
@@ -575,22 +569,15 @@
     places.append(early)
     others.append(swap_rank(owners(gathered, early, 0, cells), 2))
     far_acc, _ = lax.optimization_barrier((far_acc, gathered))
-    turned_b, _, far_keep, *far_sends = pl.pallas_call(
-        far_source_b_kernel,
-        in_specs=[SMEM] + [VMEM] * 4,
-        out_specs=[VMEM] * (3 + PARTS),
-        out_shape=[
-            shape(fars // 4, BF16, terms // 2),
-            far_sums,
-            shape(total // 2, F32),
-            *[shape(total // 2 // PARTS, F32)] * PARTS,
-        ],
-        scratch_shapes=far_scratch,
-        input_output_aliases={4: 1},
-        compiler_params=params(6),
+    far_keep, *far_sends = pl.pallas_call(
+        far_fold_kernel,
+        in_specs=[VMEM],
+        out_specs=[VMEM] * (1 + PARTS),
+        out_shape=[shape(total // 2, F32), *[shape(total // 2 // PARTS, F32)] * PARTS],
+        compiler_params=params(4),
         cost_estimate=far_cost,
-        name="far_source_b",
-    )(at_source, moment_own, moment_late, tiles_ij, far_acc)
+        name="far_fold",
+    )(far_acc)
     far_others = [swap_rank(x, 1) for x in far_sends]
 
     got_a = swap_rank(send_a, 2)
@@ -640,7 +627,7 @@
     moment_all_pair = swap_rank(owners(gathered, range(blks), cells, stride), 1)
     target_keep, target_send = pl.pallas_call(
         functools.partial(far_target_kernel, stride, cells),
-        in_specs=[SMEM] + [VMEM] * 4,
+        in_specs=[SMEM] + [VMEM] * 3,
         out_specs=[VMEM] * 2,
         out_shape=[shape(halfc, F32), shape(halfc, F32)],
         scratch_shapes=[
@@ -650,7 +637,7 @@
         compiler_params=params(6 + total // 32),
         cost_estimate=meet_cost,
         name="far_target",
-    )(at_target, gathered, moment_all_pair, turned_a, turned_b)
+    )(at_target, gathered, moment_all_pair, turned)
     target_other = swap_rank(target_send, 1)
     others[0], _ = lax.optimization_barrier((others[0], target_send))
 

time: 56.5 us -> 55.1 us (0.975)
  waiting for transfers between devices: 11.1 us -> 10.1 us
  Pallas kernels: 23 us -> 22.4 us
    ppermute x14, waiting for transfers between devices: 7.25 us -> 5.78 us  [swap_rank(): return lax.ppermute(x, 'rhs', [(i, i ^ d) for i in range(ranks)])]
    pallas_call x2, Pallas kernels: 5.5 us -> 4.88 us  [the longest x1 3.54 us: body(): pl.pallas_call(far_source_kernel, in_specs=[SMEM] + [VMEM] * 3, out_specs...]
  transfers between devices with their start and end apart: 21 -> 21, of which waited for: 13 -> 12; matrix products, arithmetic and copies ran while one was open for 1% -> 1% of each run, Pallas kernels for 38% -> 38%
where the time goes in v7:
time: 55.1 us; the launch traced here: 54.9 us
  Pallas kernels  22.4 us (41%)
  starting transfers between devices  21.8 us (40%)
  waiting for transfers between devices  10.1 us (18%)
    ppermute x7, starting transfers between devices, swap_blk(): return lax.ppermute(x, 'blk', [(i, i ^ 1 << bit) for i in range(blks)])  12.8 us
    ppermute x14, starting transfers between devices, swap_rank(): return lax.ppermute(x, 'rhs', [(i, i ^ d) for i in range(ranks)])  9.07 us
    ppermute x14, waiting for transfers between devices, swap_rank(): return lax.ppermute(x, 'rhs', [(i, i ^ d) for i in range(ranks)])  5.78 us
    ppermute x7, waiting for transfers between devices, swap_blk(): return lax.ppermute(x, 'blk', [(i, i ^ 1 << bit) for i in range(blks)])  4.34 us
    pallas_call x1, Pallas kernels, body(): pl.pallas_call(functools.partial(near_first_kernel, stride, cells, places...  3.78 us
    pallas_call x1, Pallas kernels, body(): pl.pallas_call(functools.partial(far_target_kernel, stride, cells), in_sp...  3.65 us
    pallas_call x1, Pallas kernels, body(): pl.pallas_call(far_source_kernel, in_specs=[SMEM] + [VMEM] * 3, out_specs...  3.54 us
    pallas_call x1, Pallas kernels, body(): pl.pallas_call(near_second_a_kernel, in_specs=[SMEM, VMEM, VMEM, VMEM, HB...  3.16 us
  transfers between devices with their start and end apart: 21, of which 12 were waited for; matrix products, arithmetic and copies ran while one was open for 1% of the time, Pallas kernels for 38%

profile of v7, /device:TPU:0, one launch (start us, length us, event | category | flops | bytes accessed | tf_op | source)
XLA Modules:
  0.0 54.9 jit_solution(351472255024921732)
XLA Ops:
  0.0 0.5 collective-permute-start.1
  0.5 2.5 %collective-permute-start = (bf16[16,2048]{1,0:T(8,128)(2,1)}, bf16[16,2048]{1,0:T(8,128)(2,1)S(1)}, u32[]{:S(2)}, u32[]{:S(2)}) collective-permute-start(bf16[16,2048]{1,0:T(8,128)(2,1)} %charges_in.1), channel_id=1, source_target_pairs={{0,2},{1,3},{2,0},{3,1},{4,6},{5,7},{6,4},{7,5},{8,10},{9,11},{10,... | collective-permute-start | bytes 196616 | tf_op jit(solution)/shard_map/ppermute | solution.py:435
  2.9 1.8 %prep.1 = (bf16[24,16,128]{2,1,0:T(8,128)(2,1)S(1)}, s32[3,256]{1,0:T(4,128)S(1)}, s32[2,256]{1,0:T(2,128)S(1)}, s32[2,256]{1,0:T(2,128)S(1)}, s32[2,256]{1,0:T(...) custom-call(s32[1,16]{1,0:T(1,128)} %bitcast.19, bf16[16,2048]{1,0:T(8,128)(2,1)} %charges_in.1, ...), custom_call_target="tpu_custom_call" | custom-call | bytes 12582912 | tf_op jit(solution)/shard_map/prep/pallas_call | solution.py:475
  4.8 1.6 %collective-permute-start.2 = (bf16[24,16,128]{2,1,0:T(8,128)(2,1)S(1)}, bf16[24,16,128]{2,1,0:T(8,128)(2,1)S(1)}, u32[]{:S(2)}, u32[]{:S(2)}) collective-permute-start(bf16[24,16,128]{2,1,0:T(8,128)(2,1)S(1)} %get-tuple-element.57), channel_id=1, source_target_pairs={{0,4},{4,0},{8,12},{12,8},{16,20},{20,16},{24,28},{28,24},{1,5},{5... | collective-permute-start | bytes 294920 | tf_op jit(solution)/shard_map/ppermute | solution.py:438
  6.4 3.2 %near_second_a.1 = (f32[128,32,128]{2,1,0:T(8,128)S(1)}, bf16[16,32,128]{2,1,0:T(8,128)(2,1)S(1)}, bf16[64,128,128]{2,1,0:T(8,128)(2,1)S(1)}) custom-call(s32[3,256]{1,0:T(4,128)S(1)} %get-tuple-element.56.idx, bf16[16,16,128]{2,1,0:T(8,128)(2,1)S(1)} %slice.18.mine.moved, ...), custom_call_target="tpu_custom_call", output_to_operand_aliasing={{0}: (5, {})} | custom-call | flops 134217728 | bytes 10485760 | tf_op jit(solution)/shard_map/near_second_a/pallas_call | solution.py:508
  9.6 0.2 collective-permute-done.2
  9.8 0.1 constant_dynamic-update-slice_fusion.7
  9.8 2.7 %collective-permute-start.5 = (bf16[48,16,128]{2,1,0:T(8,128)(2,1)S(1)}, bf16[48,16,128]{2,1,0:T(8,128)(2,1)S(1)}, u32[]{:S(2)}, u32[]{:S(2)}) collective-permute-start(bf16[48,16,128]{2,1,0:T(8,128)(2,1)S(1)} %get-tuple-element.113), channel_id=1, source_target_pairs={{0,16},{4,20},{8,24},{12,28},{16,0},{20,4},{24,8},{28,12},{1,17},{... | collective-permute-start | bytes 589832 | tf_op jit(solution)/shard_map/ppermute | solution.py:438
  12.5 0.0 copy-start
  12.5 2.1 %near_second_b.1 = (f32[128,32,128]{2,1,0:T(8,128)S(1)}, f32[64,16,128]{2,1,0:T(8,128)S(1)}, s16[68,16,128]{2,1,0:T(8,128)(2,1)S(1)}, f32[32,32,128]{2,1,0:T(8,128)S(1)}, s16[68,16,128]{2,1,0:T(8,128)(2,1)S(1)}) custom-call(s32[3,256]{1,0:T(4,128)S(1)} %get-tuple-element.56.idx, ...), custom_call_target="tpu_custom_call", output_to_operand_aliasing={{0}: (3, {})} | custom-call | flops 134217728 | bytes 10485760 | tf_op jit(solution)/shard_map/near_second_b/pallas_call | solution.py:526
  14.6 1.6 %collective-permute-start.3 = (s16[68,16,128]{2,1,0:T(8,128)(2,1)S(1)}, s16[68,16,128]{2,1,0:T(8,128)(2,1)S(1)}, u32[]{:S(2)}, u32[]{:S(2)}) collective-permute-start(s16[68,16,128]{2,1,0:T(8,128)(2,1)S(1)} %get-tuple-element.67), channel_id=1, source_target_pairs={{0,4},{4,0},{8,12},{12,8},{16,20},{20,16},{24,28},{28,24},{1,5},{5... | collective-permute-start | bytes 835592 | tf_op jit(solution)/shard_map/ppermute | solution.py:438
  16.2 1.1 %collective-permute-start.4 = (s16[68,16,128]{2,1,0:T(8,128)(2,1)S(1)}, s16[68,16,128]{2,1,0:T(8,128)(2,1)S(1)}, u32[]{:S(2)}, u32[]{:S(2)}) collective-permute-start(s16[68,16,128]{2,1,0:T(8,128)(2,1)S(1)} %get-tuple-element.68), channel_id=1, source_target_pairs={{0,2},{1,3},{2,0},{3,1},{4,6},{5,7},{6,4},{7,5},{8,10},{9,11},{10,... | collective-permute-start | bytes 835592 | tf_op jit(solution)/shard_map/ppermute | solution.py:435
  17.3 3.5 %far_source.1 = (bf16[256,32,128]{2,1,0:T(8,128)(2,1)S(1)}, f32[128,32,64]{2,1,0:T(8,128)S(1)}) custom-call(s32[2,256]{1,0:T(2,128)S(1)} %get-tuple-element.71.idx, bf16[8,16,128]{2,1,0:T(8,128)(2,1)S(1)} %slice.19.mine, bf16[8,16,128]{2,1,0:T(8,128)(2,1)S(1)} %collective-permute-done.6.theirs, bf16[4096,512]{1,0:T(8,128)(2,1)S(1)} %bitcast.16), custom_call_target="tpu_custom_call" | custom-call | flops 67108864 | bytes 12582912 | tf_op jit(solution)/shard_map/far_source/pallas_call | solution.py:552
  20.8 0.7 %collective-permute-done.5 = bf16[48,16,128]{2,1,0:T(8,128)(2,1)S(1)} collective-permute-done((bf16[48,16,128]{2,1,0:T(8,128)(2,1)S(1)}, bf16[48,16,128]{2,1,0:T(8,128)(2,1)S(1)}, u32[]{:S(2)}, u32[]{:S(2)}) %collective-permute-start.5) | collective-permute-done | bytes 196640 | tf_op jit(solution)/shard_map/ppermute | solution.py:438
  21.6 0.1 constant_dynamic-update-slice_fusion.6
  21.7 0.9 %collective-permute-start.13 = (bf16[96,16,128]{2,1,0:T(8,128)(2,1)S(1)}, bf16[96,16,128]{2,1,0:T(8,128)(2,1)S(1)}, u32[]{:S(2)}, u32[]{:S(2)}) collective-permute-start(bf16[96,16,128]{2,1,0:T(8,128)(2,1)S(1)} %get-tuple-element.110), channel_id=1, source_target_pairs={{0,8},{4,12},{8,0},{12,4},{16,24},{20,28},{24,16},{28,20},{1,9},{5... | collective-permute-start | bytes 1179656 | tf_op jit(solution)/shard_map/ppermute | solution.py:438
  22.6 1.0 %collective-permute-start.7 = (bf16[32,16,128]{2,1,0:T(8,128)(2,1)S(1)}, bf16[32,16,128]{2,1,0:T(8,128)(2,1)S(1)}, u32[]{:S(2)}, u32[]{:S(2)}) collective-permute-start(bf16[32,16,128]{2,1,0:T(8,128)(2,1)S(1)} %bitcast.24), channel_id=1, source_target_pairs={{0,2},{1,3},{2,0},{3,1},{4,6},{5,7},{6,4},{7,5},{8,10},{9,11},{10,... | collective-permute-start | bytes 393224 | tf_op jit(solution)/shard_map/ppermute | solution.py:435
  23.6 1.3 %far_fold.1 = (f32[64,16,128]{2,1,0:T(8,128)S(1)}, f32[16,16,128]{2,1,0:T(8,128)S(1)}, f32[16,16,128]{2,1,0:T(8,128)S(1)}, f32[16,16,128]{2,1,0:T(8,128)S(1)}, f32[16,16,128]{2,1,0:T(8,128)S(1)}) custom-call(f32[128,32,64]{2,1,0:T(8,128)S(1)} %get-tuple-element.78.acc), custom_call_target="tpu_custom_call" | custom-call | flops 67108864 | bytes 12582912 | tf_op jit(solution)/shard_map/far_fold/pallas_call | solution.py:572
  25.0 0.1 collective-permute-start.8
  25.1 0.2 meet_b.1
  25.3 1.2 %collective-permute-start.14 = (s16[34,16,128]{2,1,0:T(8,128)(2,1)S(1)}, s16[34,16,128]{2,1,0:T(8,128)(2,1)S(1)}, u32[]{:S(2)}, u32[]{:S(2)}) collective-permute-start(s16[34,16,128]{2,1,0:T(8,128)(2,1)S(1)} %get-tuple-element.70), channel_id=1, source_target_pairs={{0,2},{1,3},{2,0},{3,1},{4,6},{5,7},{6,4},{7,5},{8,10},{9,11},{10,... | collective-permute-start | bytes 417800 | tf_op jit(solution)/shard_map/ppermute | solution.py:435
  26.5 0.2 collective-permute-start.9
  26.6 1.2 %collective-permute-done.7.refs_0_ = bf16[32,16,128]{2,1,0:T(8,128)(2,1)S(1)} collective-permute-done((bf16[32,16,128]{2,1,0:T(8,128)(2,1)S(1)}, bf16[32,16,128]{2,1,0:T(8,128)(2,1)S(1)}, u32[]{:S(2)}, u32[]{:S(2)}) %collective-permute-start.7) | collective-permute-done | bytes 131104 | tf_op jit(solution)/shard_map/ppermute | solution.py:435
  27.8 0.5 collective-permute-start.11
  28.3 0.1 join.1.mine
  28.4 0.7 %collective-permute-done.10.refs_2_ = f32[16,16,128]{2,1,0:T(8,128)S(1)} collective-permute-done((f32[16,16,128]{2,1,0:T(8,128)S(1)}, f32[16,16,128]{2,1,0:T(8,128)S(1)}, u32[]{:S(2)}, u32[]{:S(2)}) %collective-permute-start.10) | collective-permute-done | bytes 131104 | tf_op jit(solution)/shard_map/ppermute | solution.py:435
  29.1 0.2 collective-permute-done.11.refs_3_
  29.3 0.3 meet_a.1
  29.7 1.1 %collective-permute-start.12 = (s16[68,16,128]{2,1,0:T(8,128)(2,1)S(1)}, s16[68,16,128]{2,1,0:T(8,128)(2,1)S(1)}, u32[]{:S(2)}, u32[]{:S(2)}) collective-permute-start(s16[68,16,128]{2,1,0:T(8,128)(2,1)S(1)} %get-tuple-element.85), channel_id=1, source_target_pairs={{0,4},{4,0},{8,12},{12,8},{16,20},{20,16},{24,28},{28,24},{1,5},{5... | collective-permute-start | bytes 835592 | tf_op jit(solution)/shard_map/ppermute | solution.py:438
  30.7 1.2 %collective-permute-done.13 = bf16[96,16,128]{2,1,0:T(8,128)(2,1)S(1)} collective-permute-done((bf16[96,16,128]{2,1,0:T(8,128)(2,1)S(1)}, bf16[96,16,128]{2,1,0:T(8,128)(2,1)S(1)}, u32[]{:S(2)}, u32[]{:S(2)}) %collective-permute-start.13) | collective-permute-done | bytes 393248 | tf_op jit(solution)/shard_map/ppermute | solution.py:438
  31.9 0.1 constant_dynamic-update-slice_fusion.5.everyone
  32.0 0.1 collective-permute-start.15
  32.1 1.0 %collective-permute-start.17 = (bf16[64,16,128]{2,1,0:T(8,128)(2,1)S(1)}, bf16[64,16,128]{2,1,0:T(8,128)(2,1)S(1)}, u32[]{:S(2)}, u32[]{:S(2)}) collective-permute-start(bf16[64,16,128]{2,1,0:T(8,128)(2,1)S(1)} %bitcast.21), channel_id=1, source_target_pairs={{0,2},{1,3},{2,0},{3,1},{4,6},{5,7},{6,4},{7,5},{8,10},{9,11},{10,... | collective-permute-start | bytes 786440 | tf_op jit(solution)/shard_map/ppermute | solution.py:435
  33.1 0.5 collective-permute-done.15.theirs
  33.6 3.7 %far_target.1 = (f32[8,16,128]{2,1,0:T(8,128)S(1)}, f32[8,16,128]{2,1,0:T(8,128)S(1)}) custom-call(s32[2,256]{1,0:T(2,128)S(1)} %get-tuple-element.87.idx, bf16[192,16,128]{2,1,0:T(8,128)(2,1)S(1)} %constant_dynamic-update-slice_fusion.5.everyone, bf16[64,16,128]{2,1,0:T(8,128)(2,1)S(1)} %collective-permute-done.15.theirs, ...), custom_call_target="tpu_custom_call" | custom-call | bytes 1048576 | tf_op jit(solution)/shard_map/far_target/pallas_call | solution.py:628
  37.3 1.3 %collective-permute-done.12.coded_a = s16[68,16,128]{2,1,0:T(8,128)(2,1)S(1)} collective-permute-done((s16[68,16,128]{2,1,0:T(8,128)(2,1)S(1)}, s16[68,16,128]{2,1,0:T(8,128)(2,1)S(1)}, u32[]{:S(2)}, u32[]{:S(2)}) %collective-permute-start.12) | collective-permute-done | bytes 278560 | tf_op jit(solution)/shard_map/ppermute | solution.py:438
  38.6 0.3 meet.1
  38.9 1.6 %collective-permute-start.16 = (s16[51,16,128]{2,1,0:T(8,128)(2,1)S(1)}, s16[51,16,128]{2,1,0:T(8,128)(2,1)S(1)}, u32[]{:S(2)}, u32[]{:S(2)}) collective-permute-start(s16[51,16,128]{2,1,0:T(8,128)(2,1)S(1)} %get-tuple-element.95), channel_id=1, source_target_pairs={{0,8},{4,12},{8,0},{12,4},{16,24},{20,28},{24,16},{28,20},{1,9},{5... | collective-permute-start | bytes 626696 | tf_op jit(solution)/shard_map/ppermute | solution.py:438
  40.6 0.3 collective-permute-done.17.refs_1_
  40.9 3.8 %near_first.1 = (f32[16,16,128]{2,1,0:T(8,128)S(1)}, s16[17,16,128]{2,1,0:T(8,128)(2,1)S(1)}) custom-call(s32[2,256]{1,0:T(2,128)S(1)} %get-tuple-element.97.idx, bf16[192,16,128]{2,1,0:T(8,128)(2,1)S(1)} %constant_dynamic-update-slice_fusion.5.everyone, bf16[16,32,128]{2,1,0:T(8,128)(2,1)S(1)} %get-tuple-element.60.both, ...), custom_call_target="tpu_custom_call" | custom-call | flops 268435456 | bytes 20971520 | tf_op jit(solution)/shard_map/near_first/pallas_call | solution.py:673
  44.7 0.9 %collective-permute-done.16.coded = s16[51,16,128]{2,1,0:T(8,128)(2,1)S(1)} collective-permute-done((s16[51,16,128]{2,1,0:T(8,128)(2,1)S(1)}, s16[51,16,128]{2,1,0:T(8,128)(2,1)S(1)}, u32[]{:S(2)}, u32[]{:S(2)}) %collective-permute-start.16) | collective-permute-done | bytes 208928 | tf_op jit(solution)/shard_map/ppermute | solution.py:438
  45.6 0.2 add.1
  45.8 3.3 %collective-permute-start.18 = (s16[26,16,128]{2,1,0:T(8,128)(2,1)S(1)}, s16[26,16,128]{2,1,0:T(8,128)(2,1)S(1)}, u32[]{:S(2)}, u32[]{:S(2)}) collective-permute-start(s16[26,16,128]{2,1,0:T(8,128)(2,1)S(1)} %get-tuple-element.103), channel_id=1, source_target_pairs={{0,16},{4,20},{8,24},{12,28},{16,0},{20,4},{24,8},{28,12},{1,17},{... | collective-permute-start | bytes 319496 | tf_op jit(solution)/shard_map/ppermute | solution.py:438
  49.1 1.0 %collective-permute-start.19 = (s16[17,16,128]{2,1,0:T(8,128)(2,1)S(1)}, s16[17,16,128]{2,1,0:T(8,128)(2,1)S(1)}, u32[]{:S(2)}, u32[]{:S(2)}) collective-permute-start(s16[17,16,128]{2,1,0:T(8,128)(2,1)S(1)} %get-tuple-element.105), channel_id=1, source_target_pairs={{0,2},{1,3},{2,0},{3,1},{4,6},{5,7},{6,4},{7,5},{8,10},{9,11},{10,... | collective-permute-start | bytes 208904 | tf_op jit(solution)/shard_map/ppermute | solution.py:435
  50.1 0.4 self.1.own
  50.5 0.9 %collective-permute-done.20.target_other = f32[8,16,128]{2,1,0:T(8,128)S(1)} collective-permute-done((f32[8,16,128]{2,1,0:T(8,128)S(1)}, f32[8,16,128]{2,1,0:T(8,128)S(1)}, u32[]{:S(2)}, u32[]{:S(2)}) %collective-permute-start.20) | collective-permute-done | bytes 65568 | tf_op jit(solution)/shard_map/ppermute | solution.py:435
  51.4 2.0 %collective-permute-done.19.first_other = s16[17,16,128]{2,1,0:T(8,128)(2,1)S(1)} collective-permute-done((s16[17,16,128]{2,1,0:T(8,128)(2,1)S(1)}, s16[17,16,128]{2,1,0:T(8,128)(2,1)S(1)}, u32[]{:S(2)}, u32[]{:S(2)}) %collective-permute-start.19) | collective-permute-done | bytes 69664 | tf_op jit(solution)/shard_map/ppermute | solution.py:435
  53.4 1.5 %final.1 = f32[16,2048]{1,0:T(8,128)} custom-call(s32[16]{0:T(128)S(1)} %copy-done.3, f32[24,16,128]{2,1,0:T(8,128)S(1)} %get-tuple-element.96.mine, s16[26,16,128]{2,1,0:T(8,128)(2,1)S(1)} %collective-permute-done.18.coded, f32[16,16,128]{2,1,0:T(8,128)S(1)} %get-tuple-element.104.first, s16[17,16,128]{2,1,0:T(8,128)(2,1)S(1)} %collective-permute-done.19.first_other, ...), custom_call_target="tpu_custom_call" | custom-call | tf_op jit(solution)/shard_map/final/pallas_call | solution.py:702
  (26 shorter events, 0.2 us)
Async XLA Ops:
  0.0 12.5 %collective-permute-start.1 = (bf16[128,128,128]{2,1,0:T(8,128)(2,1)}, bf16[128,128,128]{2,1,0:T(8,128)(2,1)S(1)}, u32[]{:S(2)}, u32[]{:S(2)}) collective-permute-start(bf16[128,128,128]{2,1,0:T(8,128)(2,1)} %rest.1), channel_id=1, source_target_pairs={{0,1},{1,0},{2,3},{3,2},{4,5},{5,4},{6,7},{7,6},{8,9},{9,8},{10,11... | collective-permute-start | bytes 12582920 | tf_op jit(solution)/shard_map/ppermute | solution.py:435
  0.5 5.9 %collective-permute-start = (bf16[16,2048]{1,0:T(8,128)(2,1)}, bf16[16,2048]{1,0:T(8,128)(2,1)S(1)}, u32[]{:S(2)}, u32[]{:S(2)}) collective-permute-start(bf16[16,2048]{1,0:T(8,128)(2,1)} %charges_in.1), channel_id=1, source_target_pairs={{0,2},{1,3},{2,0},{3,1},{4,6},{5,7},{6,4},{7,5},{8,10},{9,11},{10,... | collective-permute-start | bytes 196616 | tf_op jit(solution)/shard_map/ppermute | solution.py:435
  4.8 5.0 %collective-permute-start.2 = (bf16[24,16,128]{2,1,0:T(8,128)(2,1)S(1)}, bf16[24,16,128]{2,1,0:T(8,128)(2,1)S(1)}, u32[]{:S(2)}, u32[]{:S(2)}) collective-permute-start(bf16[24,16,128]{2,1,0:T(8,128)(2,1)S(1)} %get-tuple-element.57), channel_id=1, source_target_pairs={{0,4},{4,0},{8,12},{12,8},{16,20},{20,16},{24,28},{28,24},{1,5},{5... | collective-permute-start | bytes 294920 | tf_op jit(solution)/shard_map/ppermute | solution.py:438
  9.8 11.8 %collective-permute-start.5 = (bf16[48,16,128]{2,1,0:T(8,128)(2,1)S(1)}, bf16[48,16,128]{2,1,0:T(8,128)(2,1)S(1)}, u32[]{:S(2)}, u32[]{:S(2)}) collective-permute-start(bf16[48,16,128]{2,1,0:T(8,128)(2,1)S(1)} %get-tuple-element.113), channel_id=1, source_target_pairs={{0,16},{4,20},{8,24},{12,28},{16,0},{20,4},{24,8},{28,12},{1,17},{... | collective-permute-start | bytes 589832 | tf_op jit(solution)/shard_map/ppermute | solution.py:438
  12.5 4.8 %collective-permute-start.6 = (bf16[8,16,128]{2,1,0:T(8,128)(2,1)S(1)}, bf16[8,16,128]{2,1,0:T(8,128)(2,1)S(1)}, u32[]{:S(2)}, u32[]{:S(2)}) collective-permute-start(bf16[8,16,128]{2,1,0:T(8,128)(2,1)S(1)} %slice.19.mine), channel_id=1, source_target_pairs={{0,1},{1,0},{2,3},{3,2},{4,5},{5,4},{6,7},{7,6},{8,9},{9,8},{10,11... | collective-permute-start | bytes 98312 | tf_op jit(solution)/shard_map/ppermute | solution.py:435
  12.5 4.8 %copy-start = (bf16[512,64,64]{0,2,1:T(8,128)(2,1)S(1)}, bf16[512,64,64]{0,2,1:T(8,128)(2,1)}, u32[]{:S(2)}) copy-start(bf16[512,64,64]{0,2,1:T(8,128)(2,1)} %param.19) | copy-start | bytes 12582916
  14.6 10.4 %collective-permute-start.3 = (s16[68,16,128]{2,1,0:T(8,128)(2,1)S(1)}, s16[68,16,128]{2,1,0:T(8,128)(2,1)S(1)}, u32[]{:S(2)}, u32[]{:S(2)}) collective-permute-start(s16[68,16,128]{2,1,0:T(8,128)(2,1)S(1)} %get-tuple-element.67), channel_id=1, source_target_pairs={{0,4},{4,0},{8,12},{12,8},{16,20},{20,16},{24,28},{28,24},{1,5},{5... | collective-permute-start | bytes 835592 | tf_op jit(solution)/shard_map/ppermute | solution.py:438
  16.2 8.9 %collective-permute-start.4 = (s16[68,16,128]{2,1,0:T(8,128)(2,1)S(1)}, s16[68,16,128]{2,1,0:T(8,128)(2,1)S(1)}, u32[]{:S(2)}, u32[]{:S(2)}) collective-permute-start(s16[68,16,128]{2,1,0:T(8,128)(2,1)S(1)} %get-tuple-element.68), channel_id=1, source_target_pairs={{0,2},{1,3},{2,0},{3,1},{4,6},{5,7},{6,4},{7,5},{8,10},{9,11},{10,... | collective-permute-start | bytes 835592 | tf_op jit(solution)/shard_map/ppermute | solution.py:435
  21.7 10.3 %collective-permute-start.13 = (bf16[96,16,128]{2,1,0:T(8,128)(2,1)S(1)}, bf16[96,16,128]{2,1,0:T(8,128)(2,1)S(1)}, u32[]{:S(2)}, u32[]{:S(2)}) collective-permute-start(bf16[96,16,128]{2,1,0:T(8,128)(2,1)S(1)} %get-tuple-element.110), channel_id=1, source_target_pairs={{0,8},{4,12},{8,0},{12,4},{16,24},{20,28},{24,16},{28,20},{1,9},{5... | collective-permute-start | bytes 1179656 | tf_op jit(solution)/shard_map/ppermute | solution.py:438
  22.6 5.2 %collective-permute-start.7 = (bf16[32,16,128]{2,1,0:T(8,128)(2,1)S(1)}, bf16[32,16,128]{2,1,0:T(8,128)(2,1)S(1)}, u32[]{:S(2)}, u32[]{:S(2)}) collective-permute-start(bf16[32,16,128]{2,1,0:T(8,128)(2,1)S(1)} %bitcast.24), channel_id=1, source_target_pairs={{0,2},{1,3},{2,0},{3,1},{4,6},{5,7},{6,4},{7,5},{8,10},{9,11},{10,... | collective-permute-start | bytes 393224 | tf_op jit(solution)/shard_map/ppermute | solution.py:435
  25.0 2.8 %collective-permute-start.8 = (f32[16,16,128]{2,1,0:T(8,128)S(1)}, f32[16,16,128]{2,1,0:T(8,128)S(1)}, u32[]{:S(2)}, u32[]{:S(2)}) collective-permute-start(f32[16,16,128]{2,1,0:T(8,128)S(1)} %get-tuple-element.80), channel_id=1, source_target_pairs={{0,1},{1,0},{2,3},{3,2},{4,5},{5,4},{6,7},{7,6},{8,9},{9,8},{10,11... | collective-permute-start | bytes 393224 | tf_op jit(solution)/shard_map/ppermute | solution.py:435
  25.3 6.7 %collective-permute-start.14 = (s16[34,16,128]{2,1,0:T(8,128)(2,1)S(1)}, s16[34,16,128]{2,1,0:T(8,128)(2,1)S(1)}, u32[]{:S(2)}, u32[]{:S(2)}) collective-permute-start(s16[34,16,128]{2,1,0:T(8,128)(2,1)S(1)} %get-tuple-element.70), channel_id=1, source_target_pairs={{0,2},{1,3},{2,0},{3,1},{4,6},{5,7},{6,4},{7,5},{8,10},{9,11},{10,... | collective-permute-start | bytes 417800 | tf_op jit(solution)/shard_map/ppermute | solution.py:435
  26.5 2.0 %collective-permute-start.9 = (f32[16,16,128]{2,1,0:T(8,128)S(1)}, f32[16,16,128]{2,1,0:T(8,128)S(1)}, u32[]{:S(2)}, u32[]{:S(2)}) collective-permute-start(f32[16,16,128]{2,1,0:T(8,128)S(1)} %get-tuple-element.81), channel_id=1, source_target_pairs={{0,1},{1,0},{2,3},{3,2},{4,5},{5,4},{6,7},{7,6},{8,9},{9,8},{10,11... | collective-permute-start | bytes 393224 | tf_op jit(solution)/shard_map/ppermute | solution.py:435
  27.8 1.3 %collective-permute-start.10 = (f32[16,16,128]{2,1,0:T(8,128)S(1)}, f32[16,16,128]{2,1,0:T(8,128)S(1)}, u32[]{:S(2)}, u32[]{:S(2)}) collective-permute-start(f32[16,16,128]{2,1,0:T(8,128)S(1)} %get-tuple-element.82), channel_id=1, source_target_pairs={{0,1},{1,0},{2,3},{3,2},{4,5},{5,4},{6,7},{7,6},{8,9},{9,8},{10,11... | collective-permute-start | bytes 393224 | tf_op jit(solution)/shard_map/ppermute | solution.py:435
  27.8 1.5 %collective-permute-start.11 = (f32[16,16,128]{2,1,0:T(8,128)S(1)}, f32[16,16,128]{2,1,0:T(8,128)S(1)}, u32[]{:S(2)}, u32[]{:S(2)}) collective-permute-start(f32[16,16,128]{2,1,0:T(8,128)S(1)} %get-tuple-element.83), channel_id=1, source_target_pairs={{0,1},{1,0},{2,3},{3,2},{4,5},{5,4},{6,7},{7,6},{8,9},{9,8},{10,11... | collective-permute-start | bytes 393224 | tf_op jit(solution)/shard_map/ppermute | solution.py:435
  29.7 9.0 %collective-permute-start.12 = (s16[68,16,128]{2,1,0:T(8,128)(2,1)S(1)}, s16[68,16,128]{2,1,0:T(8,128)(2,1)S(1)}, u32[]{:S(2)}, u32[]{:S(2)}) collective-permute-start(s16[68,16,128]{2,1,0:T(8,128)(2,1)S(1)} %get-tuple-element.85), channel_id=1, source_target_pairs={{0,4},{4,0},{8,12},{12,8},{16,20},{20,16},{24,28},{28,24},{1,5},{5... | collective-permute-start | bytes 835592 | tf_op jit(solution)/shard_map/ppermute | solution.py:438
  32.0 1.6 %collective-permute-start.15 = (bf16[64,16,128]{2,1,0:T(8,128)(2,1)S(1)}, bf16[64,16,128]{2,1,0:T(8,128)(2,1)S(1)}, u32[]{:S(2)}, u32[]{:S(2)}) collective-permute-start(bf16[64,16,128]{2,1,0:T(8,128)(2,1)S(1)} %bitcast.22), channel_id=1, source_target_pairs={{0,1},{1,0},{2,3},{3,2},{4,5},{5,4},{6,7},{7,6},{8,9},{9,8},{10,11... | collective-permute-start | bytes 786440 | tf_op jit(solution)/shard_map/ppermute | solution.py:435
  32.1 8.8 %collective-permute-start.17 = (bf16[64,16,128]{2,1,0:T(8,128)(2,1)S(1)}, bf16[64,16,128]{2,1,0:T(8,128)(2,1)S(1)}, u32[]{:S(2)}, u32[]{:S(2)}) collective-permute-start(bf16[64,16,128]{2,1,0:T(8,128)(2,1)S(1)} %bitcast.21), channel_id=1, source_target_pairs={{0,2},{1,3},{2,0},{3,1},{4,6},{5,7},{6,4},{7,5},{8,10},{9,11},{10,... | collective-permute-start | bytes 786440 | tf_op jit(solution)/shard_map/ppermute | solution.py:435
  38.9 6.7 %collective-permute-start.16 = (s16[51,16,128]{2,1,0:T(8,128)(2,1)S(1)}, s16[51,16,128]{2,1,0:T(8,128)(2,1)S(1)}, u32[]{:S(2)}, u32[]{:S(2)}) collective-permute-start(s16[51,16,128]{2,1,0:T(8,128)(2,1)S(1)} %get-tuple-element.95), channel_id=1, source_target_pairs={{0,8},{4,12},{8,0},{12,4},{16,24},{20,28},{24,16},{28,20},{1,9},{5... | collective-permute-start | bytes 626696 | tf_op jit(solution)/shard_map/ppermute | solution.py:438
  40.9 9.2 %copy-start.2 = (bf16[16,128,128]{2,1,0:T(8,128)(2,1)S(1)}, bf16[16,128,128]{2,1,0:T(8,128)(2,1)}, u32[]{:S(2)}) copy-start(bf16[16,128,128]{2,1,0:T(8,128)(2,1)} %self_tiles.1) | copy-start | bytes 1572868
  40.9 12.5 %copy-start.1 = (bf16[16,128,64]{1,2,0:T(8,128)(2,1)S(1)}, bf16[16,128,64]{1,2,0:T(8,128)(2,1)}, u32[]{:S(2)}) copy-start(bf16[16,128,64]{1,2,0:T(8,128)(2,1)} %param.13) | copy-start | bytes 786436
  40.9 12.5 %copy-start.3 = (s32[16]{0:T(128)S(1)}, s32[16]{0:T(128)}, u32[]{:S(2)}) copy-start(s32[16]{0:T(128)} %counts.1) | copy-start | bytes 196
  45.8 7.6 %collective-permute-start.18 = (s16[26,16,128]{2,1,0:T(8,128)(2,1)S(1)}, s16[26,16,128]{2,1,0:T(8,128)(2,1)S(1)}, u32[]{:S(2)}, u32[]{:S(2)}) collective-permute-start(s16[26,16,128]{2,1,0:T(8,128)(2,1)S(1)} %get-tuple-element.103), channel_id=1, source_target_pairs={{0,16},{4,20},{8,24},{12,28},{16,0},{20,4},{24,8},{28,12},{1,17},{... | collective-permute-start | bytes 319496 | tf_op jit(solution)/shard_map/ppermute | solution.py:438
  49.1 4.3 %collective-permute-start.19 = (s16[17,16,128]{2,1,0:T(8,128)(2,1)S(1)}, s16[17,16,128]{2,1,0:T(8,128)(2,1)S(1)}, u32[]{:S(2)}, u32[]{:S(2)}) collective-permute-start(s16[17,16,128]{2,1,0:T(8,128)(2,1)S(1)} %get-tuple-element.105), channel_id=1, source_target_pairs={{0,2},{1,3},{2,0},{3,1},{4,6},{5,7},{6,4},{7,5},{8,10},{9,11},{10,... | collective-permute-start | bytes 208904 | tf_op jit(solution)/shard_map/ppermute | solution.py:435
  50.1 1.3 %collective-permute-start.20 = (f32[8,16,128]{2,1,0:T(8,128)S(1)}, f32[8,16,128]{2,1,0:T(8,128)S(1)}, u32[]{:S(2)}, u32[]{:S(2)}) collective-permute-start(f32[8,16,128]{2,1,0:T(8,128)S(1)} %get-tuple-element.90), channel_id=1, source_target_pairs={{0,1},{1,0},{2,3},{3,2},{4,5},{5,4},{6,7},{7,6},{8,9},{9,8},{10,11... | collective-permute-start | bytes 196616 | tf_op jit(solution)/shard_map/ppermute | solution.py:435

commit v8 on v7

--- a/solution.py
+++ b/solution.py
@@ -118,9 +118,9 @@
 
 
 TILE_COPIES = 4
-PITCH = 136
+PITCH = 132
 FAR_UNROLL = 64
-NEAR_UNROLL = 64
+NEAR_UNROLL = 32
 PARTS = 4
 
 

time: 55.1 us -> 55.1 us (level)
  no operation moved by 1% of the time
where the time goes in v8:
time: 55.1 us; the launch traced here: 54.9 us
  Pallas kernels  22.4 us (41%)
  starting transfers between devices  21.8 us (40%)
  waiting for transfers between devices  10.1 us (18%)
    ppermute x7, starting transfers between devices, swap_blk(): return lax.ppermute(x, 'blk', [(i, i ^ 1 << bit) for i in range(blks)])  12.7 us
    ppermute x14, starting transfers between devices, swap_rank(): return lax.ppermute(x, 'rhs', [(i, i ^ d) for i in range(ranks)])  9.08 us
    ppermute x14, waiting for transfers between devices, swap_rank(): return lax.ppermute(x, 'rhs', [(i, i ^ d) for i in range(ranks)])  5.78 us
    ppermute x7, waiting for transfers between devices, swap_blk(): return lax.ppermute(x, 'blk', [(i, i ^ 1 << bit) for i in range(blks)])  4.36 us
    pallas_call x1, Pallas kernels, body(): pl.pallas_call(functools.partial(near_first_kernel, stride, cells, places...  3.79 us
    pallas_call x1, Pallas kernels, body(): pl.pallas_call(functools.partial(far_target_kernel, stride, cells), in_sp...  3.65 us
    pallas_call x1, Pallas kernels, body(): pl.pallas_call(far_source_kernel, in_specs=[SMEM] + [VMEM] * 3, out_specs...  3.53 us
    pallas_call x1, Pallas kernels, body(): pl.pallas_call(near_second_a_kernel, in_specs=[SMEM, VMEM, VMEM, VMEM, HB...  3.16 us
  transfers between devices with their start and end apart: 21, of which 12 were waited for; matrix products, arithmetic and copies ran while one was open for 1% of the time, Pallas kernels for 38%

profile of v8, /device:TPU:0, one launch (start us, length us, event | category | flops | bytes accessed | tf_op | source)
XLA Modules:
  0.0 54.9 jit_solution(9506600553484489754)
XLA Ops:
  0.0 0.5 collective-permute-start.1
  0.5 2.5 %collective-permute-start = (bf16[16,2048]{1,0:T(8,128)(2,1)}, bf16[16,2048]{1,0:T(8,128)(2,1)S(1)}, u32[]{:S(2)}, u32[]{:S(2)}) collective-permute-start(bf16[16,2048]{1,0:T(8,128)(2,1)} %charges_in.1), channel_id=1, source_target_pairs={{0,2},{1,3},{2,0},{3,1},{4,6},{5,7},{6,4},{7,5},{8,10},{9,11},{10,... | collective-permute-start | bytes 196616 | tf_op jit(solution)/shard_map/ppermute | solution.py:435
  2.9 1.8 %prep.1 = (bf16[24,16,128]{2,1,0:T(8,128)(2,1)S(1)}, s32[3,256]{1,0:T(4,128)S(1)}, s32[2,256]{1,0:T(2,128)S(1)}, s32[2,256]{1,0:T(2,128)S(1)}, s32[2,256]{1,0:T(...) custom-call(s32[1,16]{1,0:T(1,128)} %bitcast.19, bf16[16,2048]{1,0:T(8,128)(2,1)} %charges_in.1, ...), custom_call_target="tpu_custom_call" | custom-call | bytes 12582912 | tf_op jit(solution)/shard_map/prep/pallas_call | solution.py:475
  4.8 1.6 %collective-permute-start.2 = (bf16[24,16,128]{2,1,0:T(8,128)(2,1)S(1)}, bf16[24,16,128]{2,1,0:T(8,128)(2,1)S(1)}, u32[]{:S(2)}, u32[]{:S(2)}) collective-permute-start(bf16[24,16,128]{2,1,0:T(8,128)(2,1)S(1)} %get-tuple-element.57), channel_id=1, source_target_pairs={{0,4},{4,0},{8,12},{12,8},{16,20},{20,16},{24,28},{28,24},{1,5},{5... | collective-permute-start | bytes 294920 | tf_op jit(solution)/shard_map/ppermute | solution.py:438
  6.4 3.2 %near_second_a.1 = (f32[128,32,128]{2,1,0:T(8,128)S(1)}, bf16[16,32,128]{2,1,0:T(8,128)(2,1)S(1)}, bf16[64,128,128]{2,1,0:T(8,128)(2,1)S(1)}) custom-call(s32[3,256]{1,0:T(4,128)S(1)} %get-tuple-element.56.idx, bf16[16,16,128]{2,1,0:T(8,128)(2,1)S(1)} %slice.18.mine.moved, ...), custom_call_target="tpu_custom_call", output_to_operand_aliasing={{0}: (5, {})} | custom-call | flops 134217728 | bytes 10485760 | tf_op jit(solution)/shard_map/near_second_a/pallas_call | solution.py:508
  9.6 0.2 collective-permute-done.2
  9.8 0.1 constant_dynamic-update-slice_fusion.7
  9.8 2.7 %collective-permute-start.5 = (bf16[48,16,128]{2,1,0:T(8,128)(2,1)S(1)}, bf16[48,16,128]{2,1,0:T(8,128)(2,1)S(1)}, u32[]{:S(2)}, u32[]{:S(2)}) collective-permute-start(bf16[48,16,128]{2,1,0:T(8,128)(2,1)S(1)} %get-tuple-element.113), channel_id=1, source_target_pairs={{0,16},{4,20},{8,24},{12,28},{16,0},{20,4},{24,8},{28,12},{1,17},{... | collective-permute-start | bytes 589832 | tf_op jit(solution)/shard_map/ppermute | solution.py:438
  12.5 0.0 copy-start
  12.5 2.1 %near_second_b.1 = (f32[128,32,128]{2,1,0:T(8,128)S(1)}, f32[64,16,128]{2,1,0:T(8,128)S(1)}, s16[68,16,128]{2,1,0:T(8,128)(2,1)S(1)}, f32[32,32,128]{2,1,0:T(8,128)S(1)}, s16[68,16,128]{2,1,0:T(8,128)(2,1)S(1)}) custom-call(s32[3,256]{1,0:T(4,128)S(1)} %get-tuple-element.56.idx, ...), custom_call_target="tpu_custom_call", output_to_operand_aliasing={{0}: (3, {})} | custom-call | flops 134217728 | bytes 10485760 | tf_op jit(solution)/shard_map/near_second_b/pallas_call | solution.py:526
  14.6 1.6 %collective-permute-start.3 = (s16[68,16,128]{2,1,0:T(8,128)(2,1)S(1)}, s16[68,16,128]{2,1,0:T(8,128)(2,1)S(1)}, u32[]{:S(2)}, u32[]{:S(2)}) collective-permute-start(s16[68,16,128]{2,1,0:T(8,128)(2,1)S(1)} %get-tuple-element.67), channel_id=1, source_target_pairs={{0,4},{4,0},{8,12},{12,8},{16,20},{20,16},{24,28},{28,24},{1,5},{5... | collective-permute-start | bytes 835592 | tf_op jit(solution)/shard_map/ppermute | solution.py:438
  16.2 1.1 %collective-permute-start.4 = (s16[68,16,128]{2,1,0:T(8,128)(2,1)S(1)}, s16[68,16,128]{2,1,0:T(8,128)(2,1)S(1)}, u32[]{:S(2)}, u32[]{:S(2)}) collective-permute-start(s16[68,16,128]{2,1,0:T(8,128)(2,1)S(1)} %get-tuple-element.68), channel_id=1, source_target_pairs={{0,2},{1,3},{2,0},{3,1},{4,6},{5,7},{6,4},{7,5},{8,10},{9,11},{10,... | collective-permute-start | bytes 835592 | tf_op jit(solution)/shard_map/ppermute | solution.py:435
  17.3 3.5 %far_source.1 = (bf16[256,32,128]{2,1,0:T(8,128)(2,1)S(1)}, f32[128,32,64]{2,1,0:T(8,128)S(1)}) custom-call(s32[2,256]{1,0:T(2,128)S(1)} %get-tuple-element.71.idx, bf16[8,16,128]{2,1,0:T(8,128)(2,1)S(1)} %slice.19.mine, bf16[8,16,128]{2,1,0:T(8,128)(2,1)S(1)} %collective-permute-done.6.theirs, bf16[4096,512]{1,0:T(8,128)(2,1)S(1)} %bitcast.16), custom_call_target="tpu_custom_call" | custom-call | flops 67108864 | bytes 12582912 | tf_op jit(solution)/shard_map/far_source/pallas_call | solution.py:552
  20.8 0.7 %collective-permute-done.5 = bf16[48,16,128]{2,1,0:T(8,128)(2,1)S(1)} collective-permute-done((bf16[48,16,128]{2,1,0:T(8,128)(2,1)S(1)}, bf16[48,16,128]{2,1,0:T(8,128)(2,1)S(1)}, u32[]{:S(2)}, u32[]{:S(2)}) %collective-permute-start.5) | collective-permute-done | bytes 196640 | tf_op jit(solution)/shard_map/ppermute | solution.py:438
  21.6 0.1 constant_dynamic-update-slice_fusion.6
  21.7 0.9 %collective-permute-start.13 = (bf16[96,16,128]{2,1,0:T(8,128)(2,1)S(1)}, bf16[96,16,128]{2,1,0:T(8,128)(2,1)S(1)}, u32[]{:S(2)}, u32[]{:S(2)}) collective-permute-start(bf16[96,16,128]{2,1,0:T(8,128)(2,1)S(1)} %get-tuple-element.110), channel_id=1, source_target_pairs={{0,8},{4,12},{8,0},{12,4},{16,24},{20,28},{24,16},{28,20},{1,9},{5... | collective-permute-start | bytes 1179656 | tf_op jit(solution)/shard_map/ppermute | solution.py:438
  22.6 1.0 %collective-permute-start.7 = (bf16[32,16,128]{2,1,0:T(8,128)(2,1)S(1)}, bf16[32,16,128]{2,1,0:T(8,128)(2,1)S(1)}, u32[]{:S(2)}, u32[]{:S(2)}) collective-permute-start(bf16[32,16,128]{2,1,0:T(8,128)(2,1)S(1)} %bitcast.24), channel_id=1, source_target_pairs={{0,2},{1,3},{2,0},{3,1},{4,6},{5,7},{6,4},{7,5},{8,10},{9,11},{10,... | collective-permute-start | bytes 393224 | tf_op jit(solution)/shard_map/ppermute | solution.py:435
  23.6 1.3 %far_fold.1 = (f32[64,16,128]{2,1,0:T(8,128)S(1)}, f32[16,16,128]{2,1,0:T(8,128)S(1)}, f32[16,16,128]{2,1,0:T(8,128)S(1)}, f32[16,16,128]{2,1,0:T(8,128)S(1)}, f32[16,16,128]{2,1,0:T(8,128)S(1)}) custom-call(f32[128,32,64]{2,1,0:T(8,128)S(1)} %get-tuple-element.78.acc), custom_call_target="tpu_custom_call" | custom-call | flops 67108864 | bytes 12582912 | tf_op jit(solution)/shard_map/far_fold/pallas_call | solution.py:572
  25.0 0.1 collective-permute-start.8
  25.1 0.2 meet_b.1
  25.3 1.2 %collective-permute-start.14 = (s16[34,16,128]{2,1,0:T(8,128)(2,1)S(1)}, s16[34,16,128]{2,1,0:T(8,128)(2,1)S(1)}, u32[]{:S(2)}, u32[]{:S(2)}) collective-permute-start(s16[34,16,128]{2,1,0:T(8,128)(2,1)S(1)} %get-tuple-element.70), channel_id=1, source_target_pairs={{0,2},{1,3},{2,0},{3,1},{4,6},{5,7},{6,4},{7,5},{8,10},{9,11},{10,... | collective-permute-start | bytes 417800 | tf_op jit(solution)/shard_map/ppermute | solution.py:435
  26.5 0.1 collective-permute-start.9
  26.7 1.2 %collective-permute-done.7.refs_0_ = bf16[32,16,128]{2,1,0:T(8,128)(2,1)S(1)} collective-permute-done((bf16[32,16,128]{2,1,0:T(8,128)(2,1)S(1)}, bf16[32,16,128]{2,1,0:T(8,128)(2,1)S(1)}, u32[]{:S(2)}, u32[]{:S(2)}) %collective-permute-start.7) | collective-permute-done | bytes 131104 | tf_op jit(solution)/shard_map/ppermute | solution.py:435
  27.8 0.5 collective-permute-start.11
  28.3 0.1 join.1.mine
  28.5 0.7 %collective-permute-done.10.refs_2_ = f32[16,16,128]{2,1,0:T(8,128)S(1)} collective-permute-done((f32[16,16,128]{2,1,0:T(8,128)S(1)}, f32[16,16,128]{2,1,0:T(8,128)S(1)}, u32[]{:S(2)}, u32[]{:S(2)}) %collective-permute-start.10) | collective-permute-done | bytes 131104 | tf_op jit(solution)/shard_map/ppermute | solution.py:435
  29.2 0.2 collective-permute-done.11.refs_3_
  29.4 0.3 meet_a.1
  29.7 1.1 %collective-permute-start.12 = (s16[68,16,128]{2,1,0:T(8,128)(2,1)S(1)}, s16[68,16,128]{2,1,0:T(8,128)(2,1)S(1)}, u32[]{:S(2)}, u32[]{:S(2)}) collective-permute-start(s16[68,16,128]{2,1,0:T(8,128)(2,1)S(1)} %get-tuple-element.85), channel_id=1, source_target_pairs={{0,4},{4,0},{8,12},{12,8},{16,20},{20,16},{24,28},{28,24},{1,5},{5... | collective-permute-start | bytes 835592 | tf_op jit(solution)/shard_map/ppermute | solution.py:438
  30.7 1.2 %collective-permute-done.13 = bf16[96,16,128]{2,1,0:T(8,128)(2,1)S(1)} collective-permute-done((bf16[96,16,128]{2,1,0:T(8,128)(2,1)S(1)}, bf16[96,16,128]{2,1,0:T(8,128)(2,1)S(1)}, u32[]{:S(2)}, u32[]{:S(2)}) %collective-permute-start.13) | collective-permute-done | bytes 393248 | tf_op jit(solution)/shard_map/ppermute | solution.py:438
  32.0 0.1 constant_dynamic-update-slice_fusion.5.everyone
  32.1 0.1 collective-permute-start.15
  32.2 1.0 %collective-permute-start.17 = (bf16[64,16,128]{2,1,0:T(8,128)(2,1)S(1)}, bf16[64,16,128]{2,1,0:T(8,128)(2,1)S(1)}, u32[]{:S(2)}, u32[]{:S(2)}) collective-permute-start(bf16[64,16,128]{2,1,0:T(8,128)(2,1)S(1)} %bitcast.21), channel_id=1, source_target_pairs={{0,2},{1,3},{2,0},{3,1},{4,6},{5,7},{6,4},{7,5},{8,10},{9,11},{10,... | collective-permute-start | bytes 786440 | tf_op jit(solution)/shard_map/ppermute | solution.py:435
  33.2 0.5 collective-permute-done.15.theirs
  33.7 3.6 %far_target.1 = (f32[8,16,128]{2,1,0:T(8,128)S(1)}, f32[8,16,128]{2,1,0:T(8,128)S(1)}) custom-call(s32[2,256]{1,0:T(2,128)S(1)} %get-tuple-element.87.idx, bf16[192,16,128]{2,1,0:T(8,128)(2,1)S(1)} %constant_dynamic-update-slice_fusion.5.everyone, bf16[64,16,128]{2,1,0:T(8,128)(2,1)S(1)} %collective-permute-done.15.theirs, ...), custom_call_target="tpu_custom_call" | custom-call | bytes 1048576 | tf_op jit(solution)/shard_map/far_target/pallas_call | solution.py:628
  37.3 1.3 %collective-permute-done.12.coded_a = s16[68,16,128]{2,1,0:T(8,128)(2,1)S(1)} collective-permute-done((s16[68,16,128]{2,1,0:T(8,128)(2,1)S(1)}, s16[68,16,128]{2,1,0:T(8,128)(2,1)S(1)}, u32[]{:S(2)}, u32[]{:S(2)}) %collective-permute-start.12) | collective-permute-done | bytes 278560 | tf_op jit(solution)/shard_map/ppermute | solution.py:438
  38.6 0.3 meet.1
  39.0 1.6 %collective-permute-start.16 = (s16[51,16,128]{2,1,0:T(8,128)(2,1)S(1)}, s16[51,16,128]{2,1,0:T(8,128)(2,1)S(1)}, u32[]{:S(2)}, u32[]{:S(2)}) collective-permute-start(s16[51,16,128]{2,1,0:T(8,128)(2,1)S(1)} %get-tuple-element.95), channel_id=1, source_target_pairs={{0,8},{4,12},{8,0},{12,4},{16,24},{20,28},{24,16},{28,20},{1,9},{5... | collective-permute-start | bytes 626696 | tf_op jit(solution)/shard_map/ppermute | solution.py:438
  40.6 0.3 collective-permute-done.17.refs_1_
  40.9 3.8 %near_first.1 = (f32[16,16,128]{2,1,0:T(8,128)S(1)}, s16[17,16,128]{2,1,0:T(8,128)(2,1)S(1)}) custom-call(s32[2,256]{1,0:T(2,128)S(1)} %get-tuple-element.97.idx, bf16[192,16,128]{2,1,0:T(8,128)(2,1)S(1)} %constant_dynamic-update-slice_fusion.5.everyone, bf16[16,32,128]{2,1,0:T(8,128)(2,1)S(1)} %get-tuple-element.60.both, ...), custom_call_target="tpu_custom_call" | custom-call | flops 268435456 | bytes 20971520 | tf_op jit(solution)/shard_map/near_first/pallas_call | solution.py:673
  44.7 0.9 %collective-permute-done.16.coded = s16[51,16,128]{2,1,0:T(8,128)(2,1)S(1)} collective-permute-done((s16[51,16,128]{2,1,0:T(8,128)(2,1)S(1)}, s16[51,16,128]{2,1,0:T(8,128)(2,1)S(1)}, u32[]{:S(2)}, u32[]{:S(2)}) %collective-permute-start.16) | collective-permute-done | bytes 208928 | tf_op jit(solution)/shard_map/ppermute | solution.py:438
  45.6 0.2 add.1
  45.8 3.3 %collective-permute-start.18 = (s16[26,16,128]{2,1,0:T(8,128)(2,1)S(1)}, s16[26,16,128]{2,1,0:T(8,128)(2,1)S(1)}, u32[]{:S(2)}, u32[]{:S(2)}) collective-permute-start(s16[26,16,128]{2,1,0:T(8,128)(2,1)S(1)} %get-tuple-element.103), channel_id=1, source_target_pairs={{0,16},{4,20},{8,24},{12,28},{16,0},{20,4},{24,8},{28,12},{1,17},{... | collective-permute-start | bytes 319496 | tf_op jit(solution)/shard_map/ppermute | solution.py:438
  49.1 1.0 %collective-permute-start.19 = (s16[17,16,128]{2,1,0:T(8,128)(2,1)S(1)}, s16[17,16,128]{2,1,0:T(8,128)(2,1)S(1)}, u32[]{:S(2)}, u32[]{:S(2)}) collective-permute-start(s16[17,16,128]{2,1,0:T(8,128)(2,1)S(1)} %get-tuple-element.105), channel_id=1, source_target_pairs={{0,2},{1,3},{2,0},{3,1},{4,6},{5,7},{6,4},{7,5},{8,10},{9,11},{10,... | collective-permute-start | bytes 208904 | tf_op jit(solution)/shard_map/ppermute | solution.py:435
  50.1 0.4 self.1.own
  50.5 0.9 %collective-permute-done.20.target_other = f32[8,16,128]{2,1,0:T(8,128)S(1)} collective-permute-done((f32[8,16,128]{2,1,0:T(8,128)S(1)}, f32[8,16,128]{2,1,0:T(8,128)S(1)}, u32[]{:S(2)}, u32[]{:S(2)}) %collective-permute-start.20) | collective-permute-done | bytes 65568 | tf_op jit(solution)/shard_map/ppermute | solution.py:435
  51.4 2.0 %collective-permute-done.19.first_other = s16[17,16,128]{2,1,0:T(8,128)(2,1)S(1)} collective-permute-done((s16[17,16,128]{2,1,0:T(8,128)(2,1)S(1)}, s16[17,16,128]{2,1,0:T(8,128)(2,1)S(1)}, u32[]{:S(2)}, u32[]{:S(2)}) %collective-permute-start.19) | collective-permute-done | bytes 69664 | tf_op jit(solution)/shard_map/ppermute | solution.py:435
  53.4 1.5 %final.1 = f32[16,2048]{1,0:T(8,128)} custom-call(s32[16]{0:T(128)S(1)} %copy-done.3, f32[24,16,128]{2,1,0:T(8,128)S(1)} %get-tuple-element.96.mine, s16[26,16,128]{2,1,0:T(8,128)(2,1)S(1)} %collective-permute-done.18.coded, f32[16,16,128]{2,1,0:T(8,128)S(1)} %get-tuple-element.104.first, s16[17,16,128]{2,1,0:T(8,128)(2,1)S(1)} %collective-permute-done.19.first_other, ...), custom_call_target="tpu_custom_call" | custom-call | tf_op jit(solution)/shard_map/final/pallas_call | solution.py:702
  (26 shorter events, 0.2 us)
Async XLA Ops:
  0.0 12.5 %collective-permute-start.1 = (bf16[128,128,128]{2,1,0:T(8,128)(2,1)}, bf16[128,128,128]{2,1,0:T(8,128)(2,1)S(1)}, u32[]{:S(2)}, u32[]{:S(2)}) collective-permute-start(bf16[128,128,128]{2,1,0:T(8,128)(2,1)} %rest.1), channel_id=1, source_target_pairs={{0,1},{1,0},{2,3},{3,2},{4,5},{5,4},{6,7},{7,6},{8,9},{9,8},{10,11... | collective-permute-start | bytes 12582920 | tf_op jit(solution)/shard_map/ppermute | solution.py:435
  0.5 5.9 %collective-permute-start = (bf16[16,2048]{1,0:T(8,128)(2,1)}, bf16[16,2048]{1,0:T(8,128)(2,1)S(1)}, u32[]{:S(2)}, u32[]{:S(2)}) collective-permute-start(bf16[16,2048]{1,0:T(8,128)(2,1)} %charges_in.1), channel_id=1, source_target_pairs={{0,2},{1,3},{2,0},{3,1},{4,6},{5,7},{6,4},{7,5},{8,10},{9,11},{10,... | collective-permute-start | bytes 196616 | tf_op jit(solution)/shard_map/ppermute | solution.py:435
  4.8 5.0 %collective-permute-start.2 = (bf16[24,16,128]{2,1,0:T(8,128)(2,1)S(1)}, bf16[24,16,128]{2,1,0:T(8,128)(2,1)S(1)}, u32[]{:S(2)}, u32[]{:S(2)}) collective-permute-start(bf16[24,16,128]{2,1,0:T(8,128)(2,1)S(1)} %get-tuple-element.57), channel_id=1, source_target_pairs={{0,4},{4,0},{8,12},{12,8},{16,20},{20,16},{24,28},{28,24},{1,5},{5... | collective-permute-start | bytes 294920 | tf_op jit(solution)/shard_map/ppermute | solution.py:438
  9.8 11.8 %collective-permute-start.5 = (bf16[48,16,128]{2,1,0:T(8,128)(2,1)S(1)}, bf16[48,16,128]{2,1,0:T(8,128)(2,1)S(1)}, u32[]{:S(2)}, u32[]{:S(2)}) collective-permute-start(bf16[48,16,128]{2,1,0:T(8,128)(2,1)S(1)} %get-tuple-element.113), channel_id=1, source_target_pairs={{0,16},{4,20},{8,24},{12,28},{16,0},{20,4},{24,8},{28,12},{1,17},{... | collective-permute-start | bytes 589832 | tf_op jit(solution)/shard_map/ppermute | solution.py:438
  12.5 4.8 %collective-permute-start.6 = (bf16[8,16,128]{2,1,0:T(8,128)(2,1)S(1)}, bf16[8,16,128]{2,1,0:T(8,128)(2,1)S(1)}, u32[]{:S(2)}, u32[]{:S(2)}) collective-permute-start(bf16[8,16,128]{2,1,0:T(8,128)(2,1)S(1)} %slice.19.mine), channel_id=1, source_target_pairs={{0,1},{1,0},{2,3},{3,2},{4,5},{5,4},{6,7},{7,6},{8,9},{9,8},{10,11... | collective-permute-start | bytes 98312 | tf_op jit(solution)/shard_map/ppermute | solution.py:435
  12.5 4.8 %copy-start = (bf16[512,64,64]{0,2,1:T(8,128)(2,1)S(1)}, bf16[512,64,64]{0,2,1:T(8,128)(2,1)}, u32[]{:S(2)}) copy-start(bf16[512,64,64]{0,2,1:T(8,128)(2,1)} %param.19) | copy-start | bytes 12582916
  14.6 10.4 %collective-permute-start.3 = (s16[68,16,128]{2,1,0:T(8,128)(2,1)S(1)}, s16[68,16,128]{2,1,0:T(8,128)(2,1)S(1)}, u32[]{:S(2)}, u32[]{:S(2)}) collective-permute-start(s16[68,16,128]{2,1,0:T(8,128)(2,1)S(1)} %get-tuple-element.67), channel_id=1, source_target_pairs={{0,4},{4,0},{8,12},{12,8},{16,20},{20,16},{24,28},{28,24},{1,5},{5... | collective-permute-start | bytes 835592 | tf_op jit(solution)/shard_map/ppermute | solution.py:438
  16.2 8.9 %collective-permute-start.4 = (s16[68,16,128]{2,1,0:T(8,128)(2,1)S(1)}, s16[68,16,128]{2,1,0:T(8,128)(2,1)S(1)}, u32[]{:S(2)}, u32[]{:S(2)}) collective-permute-start(s16[68,16,128]{2,1,0:T(8,128)(2,1)S(1)} %get-tuple-element.68), channel_id=1, source_target_pairs={{0,2},{1,3},{2,0},{3,1},{4,6},{5,7},{6,4},{7,5},{8,10},{9,11},{10,... | collective-permute-start | bytes 835592 | tf_op jit(solution)/shard_map/ppermute | solution.py:435
  21.7 10.3 %collective-permute-start.13 = (bf16[96,16,128]{2,1,0:T(8,128)(2,1)S(1)}, bf16[96,16,128]{2,1,0:T(8,128)(2,1)S(1)}, u32[]{:S(2)}, u32[]{:S(2)}) collective-permute-start(bf16[96,16,128]{2,1,0:T(8,128)(2,1)S(1)} %get-tuple-element.110), channel_id=1, source_target_pairs={{0,8},{4,12},{8,0},{12,4},{16,24},{20,28},{24,16},{28,20},{1,9},{5... | collective-permute-start | bytes 1179656 | tf_op jit(solution)/shard_map/ppermute | solution.py:438
  22.6 5.2 %collective-permute-start.7 = (bf16[32,16,128]{2,1,0:T(8,128)(2,1)S(1)}, bf16[32,16,128]{2,1,0:T(8,128)(2,1)S(1)}, u32[]{:S(2)}, u32[]{:S(2)}) collective-permute-start(bf16[32,16,128]{2,1,0:T(8,128)(2,1)S(1)} %bitcast.24), channel_id=1, source_target_pairs={{0,2},{1,3},{2,0},{3,1},{4,6},{5,7},{6,4},{7,5},{8,10},{9,11},{10,... | collective-permute-start | bytes 393224 | tf_op jit(solution)/shard_map/ppermute | solution.py:435
  25.0 2.8 %collective-permute-start.8 = (f32[16,16,128]{2,1,0:T(8,128)S(1)}, f32[16,16,128]{2,1,0:T(8,128)S(1)}, u32[]{:S(2)}, u32[]{:S(2)}) collective-permute-start(f32[16,16,128]{2,1,0:T(8,128)S(1)} %get-tuple-element.80), channel_id=1, source_target_pairs={{0,1},{1,0},{2,3},{3,2},{4,5},{5,4},{6,7},{7,6},{8,9},{9,8},{10,11... | collective-permute-start | bytes 393224 | tf_op jit(solution)/shard_map/ppermute | solution.py:435
  25.3 6.7 %collective-permute-start.14 = (s16[34,16,128]{2,1,0:T(8,128)(2,1)S(1)}, s16[34,16,128]{2,1,0:T(8,128)(2,1)S(1)}, u32[]{:S(2)}, u32[]{:S(2)}) collective-permute-start(s16[34,16,128]{2,1,0:T(8,128)(2,1)S(1)} %get-tuple-element.70), channel_id=1, source_target_pairs={{0,2},{1,3},{2,0},{3,1},{4,6},{5,7},{6,4},{7,5},{8,10},{9,11},{10,... | collective-permute-start | bytes 417800 | tf_op jit(solution)/shard_map/ppermute | solution.py:435
  26.5 1.9 %collective-permute-start.9 = (f32[16,16,128]{2,1,0:T(8,128)S(1)}, f32[16,16,128]{2,1,0:T(8,128)S(1)}, u32[]{:S(2)}, u32[]{:S(2)}) collective-permute-start(f32[16,16,128]{2,1,0:T(8,128)S(1)} %get-tuple-element.81), channel_id=1, source_target_pairs={{0,1},{1,0},{2,3},{3,2},{4,5},{5,4},{6,7},{7,6},{8,9},{9,8},{10,11... | collective-permute-start | bytes 393224 | tf_op jit(solution)/shard_map/ppermute | solution.py:435
  27.8 1.3 %collective-permute-start.10 = (f32[16,16,128]{2,1,0:T(8,128)S(1)}, f32[16,16,128]{2,1,0:T(8,128)S(1)}, u32[]{:S(2)}, u32[]{:S(2)}) collective-permute-start(f32[16,16,128]{2,1,0:T(8,128)S(1)} %get-tuple-element.82), channel_id=1, source_target_pairs={{0,1},{1,0},{2,3},{3,2},{4,5},{5,4},{6,7},{7,6},{8,9},{9,8},{10,11... | collective-permute-start | bytes 393224 | tf_op jit(solution)/shard_map/ppermute | solution.py:435
  27.8 1.5 %collective-permute-start.11 = (f32[16,16,128]{2,1,0:T(8,128)S(1)}, f32[16,16,128]{2,1,0:T(8,128)S(1)}, u32[]{:S(2)}, u32[]{:S(2)}) collective-permute-start(f32[16,16,128]{2,1,0:T(8,128)S(1)} %get-tuple-element.83), channel_id=1, source_target_pairs={{0,1},{1,0},{2,3},{3,2},{4,5},{5,4},{6,7},{7,6},{8,9},{9,8},{10,11... | collective-permute-start | bytes 393224 | tf_op jit(solution)/shard_map/ppermute | solution.py:435
  29.7 9.0 %collective-permute-start.12 = (s16[68,16,128]{2,1,0:T(8,128)(2,1)S(1)}, s16[68,16,128]{2,1,0:T(8,128)(2,1)S(1)}, u32[]{:S(2)}, u32[]{:S(2)}) collective-permute-start(s16[68,16,128]{2,1,0:T(8,128)(2,1)S(1)} %get-tuple-element.85), channel_id=1, source_target_pairs={{0,4},{4,0},{8,12},{12,8},{16,20},{20,16},{24,28},{28,24},{1,5},{5... | collective-permute-start | bytes 835592 | tf_op jit(solution)/shard_map/ppermute | solution.py:438
  32.1 1.6 %collective-permute-start.15 = (bf16[64,16,128]{2,1,0:T(8,128)(2,1)S(1)}, bf16[64,16,128]{2,1,0:T(8,128)(2,1)S(1)}, u32[]{:S(2)}, u32[]{:S(2)}) collective-permute-start(bf16[64,16,128]{2,1,0:T(8,128)(2,1)S(1)} %bitcast.22), channel_id=1, source_target_pairs={{0,1},{1,0},{2,3},{3,2},{4,5},{5,4},{6,7},{7,6},{8,9},{9,8},{10,11... | collective-permute-start | bytes 786440 | tf_op jit(solution)/shard_map/ppermute | solution.py:435
  32.2 8.8 %collective-permute-start.17 = (bf16[64,16,128]{2,1,0:T(8,128)(2,1)S(1)}, bf16[64,16,128]{2,1,0:T(8,128)(2,1)S(1)}, u32[]{:S(2)}, u32[]{:S(2)}) collective-permute-start(bf16[64,16,128]{2,1,0:T(8,128)(2,1)S(1)} %bitcast.21), channel_id=1, source_target_pairs={{0,2},{1,3},{2,0},{3,1},{4,6},{5,7},{6,4},{7,5},{8,10},{9,11},{10,... | collective-permute-start | bytes 786440 | tf_op jit(solution)/shard_map/ppermute | solution.py:435
  39.0 6.7 %collective-permute-start.16 = (s16[51,16,128]{2,1,0:T(8,128)(2,1)S(1)}, s16[51,16,128]{2,1,0:T(8,128)(2,1)S(1)}, u32[]{:S(2)}, u32[]{:S(2)}) collective-permute-start(s16[51,16,128]{2,1,0:T(8,128)(2,1)S(1)} %get-tuple-element.95), channel_id=1, source_target_pairs={{0,8},{4,12},{8,0},{12,4},{16,24},{20,28},{24,16},{28,20},{1,9},{5... | collective-permute-start | bytes 626696 | tf_op jit(solution)/shard_map/ppermute | solution.py:438
  40.9 9.2 %copy-start.2 = (bf16[16,128,128]{2,1,0:T(8,128)(2,1)S(1)}, bf16[16,128,128]{2,1,0:T(8,128)(2,1)}, u32[]{:S(2)}) copy-start(bf16[16,128,128]{2,1,0:T(8,128)(2,1)} %self_tiles.1) | copy-start | bytes 1572868
  40.9 12.5 %copy-start.1 = (bf16[16,128,64]{1,2,0:T(8,128)(2,1)S(1)}, bf16[16,128,64]{1,2,0:T(8,128)(2,1)}, u32[]{:S(2)}) copy-start(bf16[16,128,64]{1,2,0:T(8,128)(2,1)} %param.13) | copy-start | bytes 786436
  40.9 12.5 %copy-start.3 = (s32[16]{0:T(128)S(1)}, s32[16]{0:T(128)}, u32[]{:S(2)}) copy-start(s32[16]{0:T(128)} %counts.1) | copy-start | bytes 196
  45.8 7.6 %collective-permute-start.18 = (s16[26,16,128]{2,1,0:T(8,128)(2,1)S(1)}, s16[26,16,128]{2,1,0:T(8,128)(2,1)S(1)}, u32[]{:S(2)}, u32[]{:S(2)}) collective-permute-start(s16[26,16,128]{2,1,0:T(8,128)(2,1)S(1)} %get-tuple-element.103), channel_id=1, source_target_pairs={{0,16},{4,20},{8,24},{12,28},{16,0},{20,4},{24,8},{28,12},{1,17},{... | collective-permute-start | bytes 319496 | tf_op jit(solution)/shard_map/ppermute | solution.py:438
  49.1 4.3 %collective-permute-start.19 = (s16[17,16,128]{2,1,0:T(8,128)(2,1)S(1)}, s16[17,16,128]{2,1,0:T(8,128)(2,1)S(1)}, u32[]{:S(2)}, u32[]{:S(2)}) collective-permute-start(s16[17,16,128]{2,1,0:T(8,128)(2,1)S(1)} %get-tuple-element.105), channel_id=1, source_target_pairs={{0,2},{1,3},{2,0},{3,1},{4,6},{5,7},{6,4},{7,5},{8,10},{9,11},{10,... | collective-permute-start | bytes 208904 | tf_op jit(solution)/shard_map/ppermute | solution.py:435
  50.1 1.3 %collective-permute-start.20 = (f32[8,16,128]{2,1,0:T(8,128)S(1)}, f32[8,16,128]{2,1,0:T(8,128)S(1)}, u32[]{:S(2)}, u32[]{:S(2)}) collective-permute-start(f32[8,16,128]{2,1,0:T(8,128)S(1)} %get-tuple-element.90), channel_id=1, source_target_pairs={{0,1},{1,0},{2,3},{3,2},{4,5},{5,4},{6,7},{7,6},{8,9},{9,8},{10,11... | collective-permute-start | bytes 196616 | tf_op jit(solution)/shard_map/ppermute | solution.py:435
